TPU v7x, 256 devices: a whole 4x4x8 slice. The times are simulated.
256 devices in a mesh: dp: 4 (over y_lo, core), blk: 64 (over x, z, y_hi).
Axes of the slice: x: 4, y: 4 (y_hi: 2, y_lo: 2; y = y_hi * 2 + y_lo), z: 8, core: 2. Of those that a mesh axis runs over, the one named last changes fastest.
Arguments:
- gate_pre: bfloat16 [8192, 6912], P('blk', 'dp'), may hold values from -16 to 16
- up_pre: bfloat16 [8192, 6912], P('blk', 'dp'), may hold values from -6 to 6
- down_weight: bfloat16 [6912, 2560], P(('dp', 'blk')), may hold values from -0.078125 to 0.078125
- cotangent: bfloat16 [8192, 2560], P('blk'), may hold values from -6 to 6
Outputs:
- output: bfloat16 [8192, 2560], P('blk')
- grad_weight: float32 [6912, 2560], P(('dp', 'blk'))
- grad_gate: bfloat16 [8192, 6912], P('blk', 'dp')
- grad_up: bfloat16 [8192, 6912], P('blk', 'dp')
All inputs are finite; a program needn't handle non-finite values.
Results may differ from a plain program's by a relative error of at most 0.0049.
Values may be sent and summed in bfloat16 or wider, within the bound.
No kernel may reach another device: no remote copies, remote signals or barrier semaphores. Data moves between devices by JAX's collectives and lax.ppermute only.
A program may use at most 64 MiB of HBM per device.

v0:
```python
import jax
import jax.numpy as jnp
from jax import lax
from jax.sharding import PartitionSpec as P


def from_behind(value, axis, steps):
    count = lax.axis_size(axis)
    pairs = [(source, (source + steps) % count) for source in range(count)]
    return lax.ppermute(value, axis, pairs)


def body(gate_pre, up_pre, down_weight, cotangent):
    gate32 = gate_pre.astype(jnp.float32)
    up32 = up_pre.astype(jnp.float32)
    sig = jax.nn.sigmoid(gate32)
    silu_val = gate32 * sig
    hidden = (silu_val * up32).astype(jnp.bfloat16)
    tok_rows = hidden.shape[0]
    transpose_dims = (((1,), (1,)), ((), ()))
    whole_weight = lax.all_gather(down_weight, "blk", axis=0, tiled=True)
    partial_out = jnp.dot(hidden, whole_weight, preferred_element_type=jnp.float32)
    back = lax.dot_general(
        cotangent, whole_weight, transpose_dims, preferred_element_type=jnp.float32
    )
    output = lax.psum(partial_out, "dp").astype(jnp.bfloat16)
    grad_gate = (back * up32 * (sig * (1.0 + gate32 * (1.0 - sig)))).astype(jnp.bfloat16)
    grad_up = (back * silu_val).astype(jnp.bfloat16)
    count = lax.axis_size("blk")
    scale = float(tok_rows * count) ** (-0.5)
    block_rows = down_weight.shape[0]
    mine = lax.axis_index("blk")
    token_dims = (((0,), (0,)), ((), ()))

    def block_term(block, cot_part):
        start = block * block_rows
        columns = lax.dynamic_slice_in_dim(hidden, start, block_rows, 1)
        return (
            lax.dot_general(columns, cot_part, token_dims, preferred_element_type=jnp.float32)
            * scale
        )

    acc_total = block_term((mine + count - 1) % count, cotangent)

    def turn_one(step, acc):
        acc = from_behind(acc, "blk", 1)
        return acc + block_term((mine + count - 1 - step) % count, cotangent)

    grad_weight = lax.fori_loop(1, count, turn_one, acc_total)
    return (output, grad_weight, grad_gate, grad_up)


def solution(mesh):
    return jax.shard_map(
        body,
        mesh=mesh,
        in_specs=(P("blk", "dp"), P("blk", "dp"), P(("dp", "blk"), None), P("blk", None)),
        out_specs=(P("blk", None), P(("dp", "blk"), None), P("blk", "dp"), P("blk", "dp")),
        check_vma=False,
    )
```

profile of v0, /device:TPU:8, one launch (start us, length us, event | category | flops | bytes accessed | tf_op | source)
XLA Modules:
  0.0 1117.5 jit_solution(5586258651886355740)
XLA Ops:
  7.9 164.4 %all-gather.3.cloned.1.call-done = bf16[64,27,2560]{2,1,0:T(8,128)(2,1)} async-done(((bf16[1,27,2560]{2,1,0:T(8,128)(2,1)}), bf16[64,27,2560]{2,1,0:T(8,128)(2,1)}) %all-gather.3.cloned.1.call-update) | async-done | bytes 8847376 | tf_op jit(solution)/shard_map/all_gather | solution.py:21
  191.6 28.2 %all-reduce.1 = bf16[128,2560]{1,0:T(8,128)(2,1)} all-reduce(f32[128,2560]{1,0:T(8,128)S(1)} %fusion.13), channel_id=1, replica_groups=mesh['dp'=4,'blk'=64] {'dp'}, use_global_device_ids=true, to_apply=%region_0.0 | all-reduce | flops 327680 | bytes 1966080 | tf_op jit(solution)/shard_map/psum | solution.py:26
  220.0 889.9 %while.15 = (s32[]{:T(128)}, f32[27,2560]{1,0:T(8,128)S(1)}, s32[]{:T(128)}, bf16[128,1728]{0,1:T(8,128)(2,1)S(1)}, bf16[128,2560]{1,0:T(8,128)(2,1)S(1)}, /*ind...) while((s32[]{:T(128)}, f32[27,2560]{1,0:T(8,128)S(1)}, s32[]{:T(128)}, ...), condition=%wide.region_2.3_spmd, body=%wide.region_1.2_spmd.sunk | while | flops 17832976 | bytes 2373952 | solution.py:49
  221.1 15.0 %collective-permute-done = f32[27,2560]{1,0:T(8,128)S(1)} collective-permute-done((f32[27,2560]{1,0:T(8,128)S(1)}, f32[27,2560]{1,0:T(8,128)S(1)}, u32[]{:S(2)}, u32[]{:S(2)}) %collective-permute-start) | collective-permute-done | bytes 276512 | tf_op jit(solution)/shard_map/while/body/eval_jaxpr/ppermute | solution.py:10
  236.4 15.1 %collective-permute-done = f32[27,2560]{1,0:T(8,128)S(1)} collective-permute-done((f32[27,2560]{1,0:T(8,128)S(1)}, f32[27,2560]{1,0:T(8,128)S(1)}, u32[]{:S(2)}, u32[]{:S(2)}) %collective-permute-start) | collective-permute-done | bytes 276512 | tf_op jit(solution)/shard_map/while/body/eval_jaxpr/ppermute | solution.py:10
  251.9 14.2 %collective-permute-done = f32[27,2560]{1,0:T(8,128)S(1)} collective-permute-done((f32[27,2560]{1,0:T(8,128)S(1)}, f32[27,2560]{1,0:T(8,128)S(1)}, u32[]{:S(2)}, u32[]{:S(2)}) %collective-permute-start) | collective-permute-done | bytes 276512 | tf_op jit(solution)/shard_map/while/body/eval_jaxpr/ppermute | solution.py:10
  266.4 13.3 %collective-permute-done = f32[27,2560]{1,0:T(8,128)S(1)} collective-permute-done((f32[27,2560]{1,0:T(8,128)S(1)}, f32[27,2560]{1,0:T(8,128)S(1)}, u32[]{:S(2)}, u32[]{:S(2)}) %collective-permute-start) | collective-permute-done | bytes 276512 | tf_op jit(solution)/shard_map/while/body/eval_jaxpr/ppermute | solution.py:10
  280.1 12.8 %collective-permute-done = f32[27,2560]{1,0:T(8,128)S(1)} collective-permute-done((f32[27,2560]{1,0:T(8,128)S(1)}, f32[27,2560]{1,0:T(8,128)S(1)}, u32[]{:S(2)}, u32[]{:S(2)}) %collective-permute-start) | collective-permute-done | bytes 276512 | tf_op jit(solution)/shard_map/while/body/eval_jaxpr/ppermute | solution.py:10
  293.2 12.8 %collective-permute-done = f32[27,2560]{1,0:T(8,128)S(1)} collective-permute-done((f32[27,2560]{1,0:T(8,128)S(1)}, f32[27,2560]{1,0:T(8,128)S(1)}, u32[]{:S(2)}, u32[]{:S(2)}) %collective-permute-start) | collective-permute-done | bytes 276512 | tf_op jit(solution)/shard_map/while/body/eval_jaxpr/ppermute | solution.py:10
  306.3 12.8 %collective-permute-done = f32[27,2560]{1,0:T(8,128)S(1)} collective-permute-done((f32[27,2560]{1,0:T(8,128)S(1)}, f32[27,2560]{1,0:T(8,128)S(1)}, u32[]{:S(2)}, u32[]{:S(2)}) %collective-permute-start) | collective-permute-done | bytes 276512 | tf_op jit(solution)/shard_map/while/body/eval_jaxpr/ppermute | solution.py:10
  319.4 12.8 %collective-permute-done = f32[27,2560]{1,0:T(8,128)S(1)} collective-permute-done((f32[27,2560]{1,0:T(8,128)S(1)}, f32[27,2560]{1,0:T(8,128)S(1)}, u32[]{:S(2)}, u32[]{:S(2)}) %collective-permute-start) | collective-permute-done | bytes 276512 | tf_op jit(solution)/shard_map/while/body/eval_jaxpr/ppermute | solution.py:10
  332.5 12.8 %collective-permute-done = f32[27,2560]{1,0:T(8,128)S(1)} collective-permute-done((f32[27,2560]{1,0:T(8,128)S(1)}, f32[27,2560]{1,0:T(8,128)S(1)}, u32[]{:S(2)}, u32[]{:S(2)}) %collective-permute-start) | collective-permute-done | bytes 276512 | tf_op jit(solution)/shard_map/while/body/eval_jaxpr/ppermute | solution.py:10
  345.6 13.8 %collective-permute-done = f32[27,2560]{1,0:T(8,128)S(1)} collective-permute-done((f32[27,2560]{1,0:T(8,128)S(1)}, f32[27,2560]{1,0:T(8,128)S(1)}, u32[]{:S(2)}, u32[]{:S(2)}) %collective-permute-start) | collective-permute-done | bytes 276512 | tf_op jit(solution)/shard_map/while/body/eval_jaxpr/ppermute | solution.py:10
  359.8 14.9 %collective-permute-done = f32[27,2560]{1,0:T(8,128)S(1)} collective-permute-done((f32[27,2560]{1,0:T(8,128)S(1)}, f32[27,2560]{1,0:T(8,128)S(1)}, u32[]{:S(2)}, u32[]{:S(2)}) %collective-permute-start) | collective-permute-done | bytes 276512 | tf_op jit(solution)/shard_map/while/body/eval_jaxpr/ppermute | solution.py:10
  375.1 16.1 %collective-permute-done = f32[27,2560]{1,0:T(8,128)S(1)} collective-permute-done((f32[27,2560]{1,0:T(8,128)S(1)}, f32[27,2560]{1,0:T(8,128)S(1)}, u32[]{:S(2)}, u32[]{:S(2)}) %collective-permute-start) | collective-permute-done | bytes 276512 | tf_op jit(solution)/shard_map/while/body/eval_jaxpr/ppermute | solution.py:10
  391.6 15.4 %collective-permute-done = f32[27,2560]{1,0:T(8,128)S(1)} collective-permute-done((f32[27,2560]{1,0:T(8,128)S(1)}, f32[27,2560]{1,0:T(8,128)S(1)}, u32[]{:S(2)}, u32[]{:S(2)}) %collective-permute-start) | collective-permute-done | bytes 276512 | tf_op jit(solution)/shard_map/while/body/eval_jaxpr/ppermute | solution.py:10
  407.4 14.6 %collective-permute-done = f32[27,2560]{1,0:T(8,128)S(1)} collective-permute-done((f32[27,2560]{1,0:T(8,128)S(1)}, f32[27,2560]{1,0:T(8,128)S(1)}, u32[]{:S(2)}, u32[]{:S(2)}) %collective-permute-start) | collective-permute-done | bytes 276512 | tf_op jit(solution)/shard_map/while/body/eval_jaxpr/ppermute | solution.py:10
  422.3 13.7 %collective-permute-done = f32[27,2560]{1,0:T(8,128)S(1)} collective-permute-done((f32[27,2560]{1,0:T(8,128)S(1)}, f32[27,2560]{1,0:T(8,128)S(1)}, u32[]{:S(2)}, u32[]{:S(2)}) %collective-permute-start) | collective-permute-done | bytes 276512 | tf_op jit(solution)/shard_map/while/body/eval_jaxpr/ppermute | solution.py:10
  436.3 12.8 %collective-permute-done = f32[27,2560]{1,0:T(8,128)S(1)} collective-permute-done((f32[27,2560]{1,0:T(8,128)S(1)}, f32[27,2560]{1,0:T(8,128)S(1)}, u32[]{:S(2)}, u32[]{:S(2)}) %collective-permute-start) | collective-permute-done | bytes 276512 | tf_op jit(solution)/shard_map/while/body/eval_jaxpr/ppermute | solution.py:10
  449.4 12.8 %collective-permute-done = f32[27,2560]{1,0:T(8,128)S(1)} collective-permute-done((f32[27,2560]{1,0:T(8,128)S(1)}, f32[27,2560]{1,0:T(8,128)S(1)}, u32[]{:S(2)}, u32[]{:S(2)}) %collective-permute-start) | collective-permute-done | bytes 276512 | tf_op jit(solution)/shard_map/while/body/eval_jaxpr/ppermute | solution.py:10
  462.5 12.8 %collective-permute-done = f32[27,2560]{1,0:T(8,128)S(1)} collective-permute-done((f32[27,2560]{1,0:T(8,128)S(1)}, f32[27,2560]{1,0:T(8,128)S(1)}, u32[]{:S(2)}, u32[]{:S(2)}) %collective-permute-start) | collective-permute-done | bytes 276512 | tf_op jit(solution)/shard_map/while/body/eval_jaxpr/ppermute | solution.py:10
  475.6 12.8 %collective-permute-done = f32[27,2560]{1,0:T(8,128)S(1)} collective-permute-done((f32[27,2560]{1,0:T(8,128)S(1)}, f32[27,2560]{1,0:T(8,128)S(1)}, u32[]{:S(2)}, u32[]{:S(2)}) %collective-permute-start) | collective-permute-done | bytes 276512 | tf_op jit(solution)/shard_map/while/body/eval_jaxpr/ppermute | solution.py:10
  488.7 12.8 %collective-permute-done = f32[27,2560]{1,0:T(8,128)S(1)} collective-permute-done((f32[27,2560]{1,0:T(8,128)S(1)}, f32[27,2560]{1,0:T(8,128)S(1)}, u32[]{:S(2)}, u32[]{:S(2)}) %collective-permute-start) | collective-permute-done | bytes 276512 | tf_op jit(solution)/shard_map/while/body/eval_jaxpr/ppermute | solution.py:10
  501.9 13.5 %collective-permute-done = f32[27,2560]{1,0:T(8,128)S(1)} collective-permute-done((f32[27,2560]{1,0:T(8,128)S(1)}, f32[27,2560]{1,0:T(8,128)S(1)}, u32[]{:S(2)}, u32[]{:S(2)}) %collective-permute-start) | collective-permute-done | bytes 276512 | tf_op jit(solution)/shard_map/while/body/eval_jaxpr/ppermute | solution.py:10
  515.7 14.6 %collective-permute-done = f32[27,2560]{1,0:T(8,128)S(1)} collective-permute-done((f32[27,2560]{1,0:T(8,128)S(1)}, f32[27,2560]{1,0:T(8,128)S(1)}, u32[]{:S(2)}, u32[]{:S(2)}) %collective-permute-start) | collective-permute-done | bytes 276512 | tf_op jit(solution)/shard_map/while/body/eval_jaxpr/ppermute | solution.py:10
  530.7 15.8 %collective-permute-done = f32[27,2560]{1,0:T(8,128)S(1)} collective-permute-done((f32[27,2560]{1,0:T(8,128)S(1)}, f32[27,2560]{1,0:T(8,128)S(1)}, u32[]{:S(2)}, u32[]{:S(2)}) %collective-permute-start) | collective-permute-done | bytes 276512 | tf_op jit(solution)/shard_map/while/body/eval_jaxpr/ppermute | solution.py:10
  546.9 15.6 %collective-permute-done = f32[27,2560]{1,0:T(8,128)S(1)} collective-permute-done((f32[27,2560]{1,0:T(8,128)S(1)}, f32[27,2560]{1,0:T(8,128)S(1)}, u32[]{:S(2)}, u32[]{:S(2)}) %collective-permute-start) | collective-permute-done | bytes 276512 | tf_op jit(solution)/shard_map/while/body/eval_jaxpr/ppermute | solution.py:10
  562.8 14.8 %collective-permute-done = f32[27,2560]{1,0:T(8,128)S(1)} collective-permute-done((f32[27,2560]{1,0:T(8,128)S(1)}, f32[27,2560]{1,0:T(8,128)S(1)}, u32[]{:S(2)}, u32[]{:S(2)}) %collective-permute-start) | collective-permute-done | bytes 276512 | tf_op jit(solution)/shard_map/while/body/eval_jaxpr/ppermute | solution.py:10
  577.9 13.8 %collective-permute-done = f32[27,2560]{1,0:T(8,128)S(1)} collective-permute-done((f32[27,2560]{1,0:T(8,128)S(1)}, f32[27,2560]{1,0:T(8,128)S(1)}, u32[]{:S(2)}, u32[]{:S(2)}) %collective-permute-start) | collective-permute-done | bytes 276512 | tf_op jit(solution)/shard_map/while/body/eval_jaxpr/ppermute | solution.py:10
  592.1 12.9 %collective-permute-done = f32[27,2560]{1,0:T(8,128)S(1)} collective-permute-done((f32[27,2560]{1,0:T(8,128)S(1)}, f32[27,2560]{1,0:T(8,128)S(1)}, u32[]{:S(2)}, u32[]{:S(2)}) %collective-permute-start) | collective-permute-done | bytes 276512 | tf_op jit(solution)/shard_map/while/body/eval_jaxpr/ppermute | solution.py:10
  605.3 12.8 %collective-permute-done = f32[27,2560]{1,0:T(8,128)S(1)} collective-permute-done((f32[27,2560]{1,0:T(8,128)S(1)}, f32[27,2560]{1,0:T(8,128)S(1)}, u32[]{:S(2)}, u32[]{:S(2)}) %collective-permute-start) | collective-permute-done | bytes 276512 | tf_op jit(solution)/shard_map/while/body/eval_jaxpr/ppermute | solution.py:10
  618.5 12.8 %collective-permute-done = f32[27,2560]{1,0:T(8,128)S(1)} collective-permute-done((f32[27,2560]{1,0:T(8,128)S(1)}, f32[27,2560]{1,0:T(8,128)S(1)}, u32[]{:S(2)}, u32[]{:S(2)}) %collective-permute-start) | collective-permute-done | bytes 276512 | tf_op jit(solution)/shard_map/while/body/eval_jaxpr/ppermute | solution.py:10
  631.6 12.8 %collective-permute-done = f32[27,2560]{1,0:T(8,128)S(1)} collective-permute-done((f32[27,2560]{1,0:T(8,128)S(1)}, f32[27,2560]{1,0:T(8,128)S(1)}, u32[]{:S(2)}, u32[]{:S(2)}) %collective-permute-start) | collective-permute-done | bytes 276512 | tf_op jit(solution)/shard_map/while/body/eval_jaxpr/ppermute | solution.py:10
  644.7 12.8 %collective-permute-done = f32[27,2560]{1,0:T(8,128)S(1)} collective-permute-done((f32[27,2560]{1,0:T(8,128)S(1)}, f32[27,2560]{1,0:T(8,128)S(1)}, u32[]{:S(2)}, u32[]{:S(2)}) %collective-permute-start) | collective-permute-done | bytes 276512 | tf_op jit(solution)/shard_map/while/body/eval_jaxpr/ppermute | solution.py:10
  657.8 13.1 %collective-permute-done = f32[27,2560]{1,0:T(8,128)S(1)} collective-permute-done((f32[27,2560]{1,0:T(8,128)S(1)}, f32[27,2560]{1,0:T(8,128)S(1)}, u32[]{:S(2)}, u32[]{:S(2)}) %collective-permute-start) | collective-permute-done | bytes 276512 | tf_op jit(solution)/shard_map/while/body/eval_jaxpr/ppermute | solution.py:10
  671.3 14.2 %collective-permute-done = f32[27,2560]{1,0:T(8,128)S(1)} collective-permute-done((f32[27,2560]{1,0:T(8,128)S(1)}, f32[27,2560]{1,0:T(8,128)S(1)}, u32[]{:S(2)}, u32[]{:S(2)}) %collective-permute-start) | collective-permute-done | bytes 276512 | tf_op jit(solution)/shard_map/while/body/eval_jaxpr/ppermute | solution.py:10
  685.8 15.4 %collective-permute-done = f32[27,2560]{1,0:T(8,128)S(1)} collective-permute-done((f32[27,2560]{1,0:T(8,128)S(1)}, f32[27,2560]{1,0:T(8,128)S(1)}, u32[]{:S(2)}, u32[]{:S(2)}) %collective-permute-start) | collective-permute-done | bytes 276512 | tf_op jit(solution)/shard_map/while/body/eval_jaxpr/ppermute | solution.py:10
  701.6 16.0 %collective-permute-done = f32[27,2560]{1,0:T(8,128)S(1)} collective-permute-done((f32[27,2560]{1,0:T(8,128)S(1)}, f32[27,2560]{1,0:T(8,128)S(1)}, u32[]{:S(2)}, u32[]{:S(2)}) %collective-permute-start) | collective-permute-done | bytes 276512 | tf_op jit(solution)/shard_map/while/body/eval_jaxpr/ppermute | solution.py:10
  717.9 15.2 %collective-permute-done = f32[27,2560]{1,0:T(8,128)S(1)} collective-permute-done((f32[27,2560]{1,0:T(8,128)S(1)}, f32[27,2560]{1,0:T(8,128)S(1)}, u32[]{:S(2)}, u32[]{:S(2)}) %collective-permute-start) | collective-permute-done | bytes 276512 | tf_op jit(solution)/shard_map/while/body/eval_jaxpr/ppermute | solution.py:10
  733.4 14.3 %collective-permute-done = f32[27,2560]{1,0:T(8,128)S(1)} collective-permute-done((f32[27,2560]{1,0:T(8,128)S(1)}, f32[27,2560]{1,0:T(8,128)S(1)}, u32[]{:S(2)}, u32[]{:S(2)}) %collective-permute-start) | collective-permute-done | bytes 276512 | tf_op jit(solution)/shard_map/while/body/eval_jaxpr/ppermute | solution.py:10
  748.1 13.4 %collective-permute-done = f32[27,2560]{1,0:T(8,128)S(1)} collective-permute-done((f32[27,2560]{1,0:T(8,128)S(1)}, f32[27,2560]{1,0:T(8,128)S(1)}, u32[]{:S(2)}, u32[]{:S(2)}) %collective-permute-start) | collective-permute-done | bytes 276512 | tf_op jit(solution)/shard_map/while/body/eval_jaxpr/ppermute | solution.py:10
  761.8 12.8 %collective-permute-done = f32[27,2560]{1,0:T(8,128)S(1)} collective-permute-done((f32[27,2560]{1,0:T(8,128)S(1)}, f32[27,2560]{1,0:T(8,128)S(1)}, u32[]{:S(2)}, u32[]{:S(2)}) %collective-permute-start) | collective-permute-done | bytes 276512 | tf_op jit(solution)/shard_map/while/body/eval_jaxpr/ppermute | solution.py:10
  774.9 12.8 %collective-permute-done = f32[27,2560]{1,0:T(8,128)S(1)} collective-permute-done((f32[27,2560]{1,0:T(8,128)S(1)}, f32[27,2560]{1,0:T(8,128)S(1)}, u32[]{:S(2)}, u32[]{:S(2)}) %collective-permute-start) | collective-permute-done | bytes 276512 | tf_op jit(solution)/shard_map/while/body/eval_jaxpr/ppermute | solution.py:10
  788.0 12.8 %collective-permute-done = f32[27,2560]{1,0:T(8,128)S(1)} collective-permute-done((f32[27,2560]{1,0:T(8,128)S(1)}, f32[27,2560]{1,0:T(8,128)S(1)}, u32[]{:S(2)}, u32[]{:S(2)}) %collective-permute-start) | collective-permute-done | bytes 276512 | tf_op jit(solution)/shard_map/while/body/eval_jaxpr/ppermute | solution.py:10
  801.1 12.8 %collective-permute-done = f32[27,2560]{1,0:T(8,128)S(1)} collective-permute-done((f32[27,2560]{1,0:T(8,128)S(1)}, f32[27,2560]{1,0:T(8,128)S(1)}, u32[]{:S(2)}, u32[]{:S(2)}) %collective-permute-start) | collective-permute-done | bytes 276512 | tf_op jit(solution)/shard_map/while/body/eval_jaxpr/ppermute | solution.py:10
  814.2 12.8 %collective-permute-done = f32[27,2560]{1,0:T(8,128)S(1)} collective-permute-done((f32[27,2560]{1,0:T(8,128)S(1)}, f32[27,2560]{1,0:T(8,128)S(1)}, u32[]{:S(2)}, u32[]{:S(2)}) %collective-permute-start) | collective-permute-done | bytes 276512 | tf_op jit(solution)/shard_map/while/body/eval_jaxpr/ppermute | solution.py:10
  827.3 13.8 %collective-permute-done = f32[27,2560]{1,0:T(8,128)S(1)} collective-permute-done((f32[27,2560]{1,0:T(8,128)S(1)}, f32[27,2560]{1,0:T(8,128)S(1)}, u32[]{:S(2)}, u32[]{:S(2)}) %collective-permute-start) | collective-permute-done | bytes 276512 | tf_op jit(solution)/shard_map/while/body/eval_jaxpr/ppermute | solution.py:10
  841.5 14.9 %collective-permute-done = f32[27,2560]{1,0:T(8,128)S(1)} collective-permute-done((f32[27,2560]{1,0:T(8,128)S(1)}, f32[27,2560]{1,0:T(8,128)S(1)}, u32[]{:S(2)}, u32[]{:S(2)}) %collective-permute-start) | collective-permute-done | bytes 276512 | tf_op jit(solution)/shard_map/while/body/eval_jaxpr/ppermute | solution.py:10
  856.8 16.1 %collective-permute-done = f32[27,2560]{1,0:T(8,128)S(1)} collective-permute-done((f32[27,2560]{1,0:T(8,128)S(1)}, f32[27,2560]{1,0:T(8,128)S(1)}, u32[]{:S(2)}, u32[]{:S(2)}) %collective-permute-start) | collective-permute-done | bytes 276512 | tf_op jit(solution)/shard_map/while/body/eval_jaxpr/ppermute | solution.py:10
  873.2 15.4 %collective-permute-done = f32[27,2560]{1,0:T(8,128)S(1)} collective-permute-done((f32[27,2560]{1,0:T(8,128)S(1)}, f32[27,2560]{1,0:T(8,128)S(1)}, u32[]{:S(2)}, u32[]{:S(2)}) %collective-permute-start) | collective-permute-done | bytes 276512 | tf_op jit(solution)/shard_map/while/body/eval_jaxpr/ppermute | solution.py:10
  889.0 14.6 %collective-permute-done = f32[27,2560]{1,0:T(8,128)S(1)} collective-permute-done((f32[27,2560]{1,0:T(8,128)S(1)}, f32[27,2560]{1,0:T(8,128)S(1)}, u32[]{:S(2)}, u32[]{:S(2)}) %collective-permute-start) | collective-permute-done | bytes 276512 | tf_op jit(solution)/shard_map/while/body/eval_jaxpr/ppermute | solution.py:10
  903.9 13.7 %collective-permute-done = f32[27,2560]{1,0:T(8,128)S(1)} collective-permute-done((f32[27,2560]{1,0:T(8,128)S(1)}, f32[27,2560]{1,0:T(8,128)S(1)}, u32[]{:S(2)}, u32[]{:S(2)}) %collective-permute-start) | collective-permute-done | bytes 276512 | tf_op jit(solution)/shard_map/while/body/eval_jaxpr/ppermute | solution.py:10
  917.9 12.8 %collective-permute-done = f32[27,2560]{1,0:T(8,128)S(1)} collective-permute-done((f32[27,2560]{1,0:T(8,128)S(1)}, f32[27,2560]{1,0:T(8,128)S(1)}, u32[]{:S(2)}, u32[]{:S(2)}) %collective-permute-start) | collective-permute-done | bytes 276512 | tf_op jit(solution)/shard_map/while/body/eval_jaxpr/ppermute | solution.py:10
  931.1 12.8 %collective-permute-done = f32[27,2560]{1,0:T(8,128)S(1)} collective-permute-done((f32[27,2560]{1,0:T(8,128)S(1)}, f32[27,2560]{1,0:T(8,128)S(1)}, u32[]{:S(2)}, u32[]{:S(2)}) %collective-permute-start) | collective-permute-done | bytes 276512 | tf_op jit(solution)/shard_map/while/body/eval_jaxpr/ppermute | solution.py:10
  944.2 12.8 %collective-permute-done = f32[27,2560]{1,0:T(8,128)S(1)} collective-permute-done((f32[27,2560]{1,0:T(8,128)S(1)}, f32[27,2560]{1,0:T(8,128)S(1)}, u32[]{:S(2)}, u32[]{:S(2)}) %collective-permute-start) | collective-permute-done | bytes 276512 | tf_op jit(solution)/shard_map/while/body/eval_jaxpr/ppermute | solution.py:10
  957.3 12.8 %collective-permute-done = f32[27,2560]{1,0:T(8,128)S(1)} collective-permute-done((f32[27,2560]{1,0:T(8,128)S(1)}, f32[27,2560]{1,0:T(8,128)S(1)}, u32[]{:S(2)}, u32[]{:S(2)}) %collective-permute-start) | collective-permute-done | bytes 276512 | tf_op jit(solution)/shard_map/while/body/eval_jaxpr/ppermute | solution.py:10
  970.4 12.8 %collective-permute-done = f32[27,2560]{1,0:T(8,128)S(1)} collective-permute-done((f32[27,2560]{1,0:T(8,128)S(1)}, f32[27,2560]{1,0:T(8,128)S(1)}, u32[]{:S(2)}, u32[]{:S(2)}) %collective-permute-start) | collective-permute-done | bytes 276512 | tf_op jit(solution)/shard_map/while/body/eval_jaxpr/ppermute | solution.py:10
  983.5 13.5 %collective-permute-done = f32[27,2560]{1,0:T(8,128)S(1)} collective-permute-done((f32[27,2560]{1,0:T(8,128)S(1)}, f32[27,2560]{1,0:T(8,128)S(1)}, u32[]{:S(2)}, u32[]{:S(2)}) %collective-permute-start) | collective-permute-done | bytes 276512 | tf_op jit(solution)/shard_map/while/body/eval_jaxpr/ppermute | solution.py:10
  997.4 14.6 %collective-permute-done = f32[27,2560]{1,0:T(8,128)S(1)} collective-permute-done((f32[27,2560]{1,0:T(8,128)S(1)}, f32[27,2560]{1,0:T(8,128)S(1)}, u32[]{:S(2)}, u32[]{:S(2)}) %collective-permute-start) | collective-permute-done | bytes 276512 | tf_op jit(solution)/shard_map/while/body/eval_jaxpr/ppermute | solution.py:10
  1012.4 15.8 %collective-permute-done = f32[27,2560]{1,0:T(8,128)S(1)} collective-permute-done((f32[27,2560]{1,0:T(8,128)S(1)}, f32[27,2560]{1,0:T(8,128)S(1)}, u32[]{:S(2)}, u32[]{:S(2)}) %collective-permute-start) | collective-permute-done | bytes 276512 | tf_op jit(solution)/shard_map/while/body/eval_jaxpr/ppermute | solution.py:10
  1028.6 15.5 %collective-permute-done = f32[27,2560]{1,0:T(8,128)S(1)} collective-permute-done((f32[27,2560]{1,0:T(8,128)S(1)}, f32[27,2560]{1,0:T(8,128)S(1)}, u32[]{:S(2)}, u32[]{:S(2)}) %collective-permute-start) | collective-permute-done | bytes 276512 | tf_op jit(solution)/shard_map/while/body/eval_jaxpr/ppermute | solution.py:10
  1044.5 12.8 %collective-permute-done = f32[27,2560]{1,0:T(8,128)S(1)} collective-permute-done((f32[27,2560]{1,0:T(8,128)S(1)}, f32[27,2560]{1,0:T(8,128)S(1)}, u32[]{:S(2)}, u32[]{:S(2)}) %collective-permute-start) | collective-permute-done | bytes 276512 | tf_op jit(solution)/shard_map/while/body/eval_jaxpr/ppermute | solution.py:10
  1057.6 12.8 %collective-permute-done = f32[27,2560]{1,0:T(8,128)S(1)} collective-permute-done((f32[27,2560]{1,0:T(8,128)S(1)}, f32[27,2560]{1,0:T(8,128)S(1)}, u32[]{:S(2)}, u32[]{:S(2)}) %collective-permute-start) | collective-permute-done | bytes 276512 | tf_op jit(solution)/shard_map/while/body/eval_jaxpr/ppermute | solution.py:10
  1070.7 12.8 %collective-permute-done = f32[27,2560]{1,0:T(8,128)S(1)} collective-permute-done((f32[27,2560]{1,0:T(8,128)S(1)}, f32[27,2560]{1,0:T(8,128)S(1)}, u32[]{:S(2)}, u32[]{:S(2)}) %collective-permute-start) | collective-permute-done | bytes 276512 | tf_op jit(solution)/shard_map/while/body/eval_jaxpr/ppermute | solution.py:10
  (144 shorter events, 66.0 us)
Async XLA Ops:
  7.2 165.2 %all-gather.3.cloned.1.call-start = ((), (), s32[]{:S(2)}) async-start(), calls=%async_computation | async-start | bytes 10649600 | tf_op jit(solution)/shard_map/all_gather | solution.py:21
  220.0 16.1 %collective-permute-start = (f32[27,2560]{1,0:T(8,128)S(1)}, f32[27,2560]{1,0:T(8,128)S(1)}, u32[]{:S(2)}, u32[]{:S(2)}) collective-permute-start(f32[27,2560]{1,0:T(8,128)S(1)} %get-tuple-element.213), channel_id=1, source_target_pairs={{0,1},{1,2},{2,3},{3,4},{4,5},{5,6},{6,7},{7,8},{8,9},{9,10},{10,1... | collective-permute-start | bytes 829448 | tf_op jit(solution)/shard_map/while/body/eval_jaxpr/ppermute | solution.py:10
  236.3 15.2 %collective-permute-start = (f32[27,2560]{1,0:T(8,128)S(1)}, f32[27,2560]{1,0:T(8,128)S(1)}, u32[]{:S(2)}, u32[]{:S(2)}) collective-permute-start(f32[27,2560]{1,0:T(8,128)S(1)} %get-tuple-element.213), channel_id=1, source_target_pairs={{0,1},{1,2},{2,3},{3,4},{4,5},{5,6},{6,7},{7,8},{8,9},{9,10},{10,1... | collective-permute-start | bytes 829448 | tf_op jit(solution)/shard_map/while/body/eval_jaxpr/ppermute | solution.py:10
  251.8 14.3 %collective-permute-start = (f32[27,2560]{1,0:T(8,128)S(1)}, f32[27,2560]{1,0:T(8,128)S(1)}, u32[]{:S(2)}, u32[]{:S(2)}) collective-permute-start(f32[27,2560]{1,0:T(8,128)S(1)} %get-tuple-element.213), channel_id=1, source_target_pairs={{0,1},{1,2},{2,3},{3,4},{4,5},{5,6},{6,7},{7,8},{8,9},{9,10},{10,1... | collective-permute-start | bytes 829448 | tf_op jit(solution)/shard_map/while/body/eval_jaxpr/ppermute | solution.py:10
  266.3 13.4 %collective-permute-start = (f32[27,2560]{1,0:T(8,128)S(1)}, f32[27,2560]{1,0:T(8,128)S(1)}, u32[]{:S(2)}, u32[]{:S(2)}) collective-permute-start(f32[27,2560]{1,0:T(8,128)S(1)} %get-tuple-element.213), channel_id=1, source_target_pairs={{0,1},{1,2},{2,3},{3,4},{4,5},{5,6},{6,7},{7,8},{8,9},{9,10},{10,1... | collective-permute-start | bytes 829448 | tf_op jit(solution)/shard_map/while/body/eval_jaxpr/ppermute | solution.py:10
  280.0 12.9 %collective-permute-start = (f32[27,2560]{1,0:T(8,128)S(1)}, f32[27,2560]{1,0:T(8,128)S(1)}, u32[]{:S(2)}, u32[]{:S(2)}) collective-permute-start(f32[27,2560]{1,0:T(8,128)S(1)} %get-tuple-element.213), channel_id=1, source_target_pairs={{0,1},{1,2},{2,3},{3,4},{4,5},{5,6},{6,7},{7,8},{8,9},{9,10},{10,1... | collective-permute-start | bytes 829448 | tf_op jit(solution)/shard_map/while/body/eval_jaxpr/ppermute | solution.py:10
  293.1 12.9 %collective-permute-start = (f32[27,2560]{1,0:T(8,128)S(1)}, f32[27,2560]{1,0:T(8,128)S(1)}, u32[]{:S(2)}, u32[]{:S(2)}) collective-permute-start(f32[27,2560]{1,0:T(8,128)S(1)} %get-tuple-element.213), channel_id=1, source_target_pairs={{0,1},{1,2},{2,3},{3,4},{4,5},{5,6},{6,7},{7,8},{8,9},{9,10},{10,1... | collective-permute-start | bytes 829448 | tf_op jit(solution)/shard_map/while/body/eval_jaxpr/ppermute | solution.py:10
  306.2 12.9 %collective-permute-start = (f32[27,2560]{1,0:T(8,128)S(1)}, f32[27,2560]{1,0:T(8,128)S(1)}, u32[]{:S(2)}, u32[]{:S(2)}) collective-permute-start(f32[27,2560]{1,0:T(8,128)S(1)} %get-tuple-element.213), channel_id=1, source_target_pairs={{0,1},{1,2},{2,3},{3,4},{4,5},{5,6},{6,7},{7,8},{8,9},{9,10},{10,1... | collective-permute-start | bytes 829448 | tf_op jit(solution)/shard_map/while/body/eval_jaxpr/ppermute | solution.py:10
  319.3 12.9 %collective-permute-start = (f32[27,2560]{1,0:T(8,128)S(1)}, f32[27,2560]{1,0:T(8,128)S(1)}, u32[]{:S(2)}, u32[]{:S(2)}) collective-permute-start(f32[27,2560]{1,0:T(8,128)S(1)} %get-tuple-element.213), channel_id=1, source_target_pairs={{0,1},{1,2},{2,3},{3,4},{4,5},{5,6},{6,7},{7,8},{8,9},{9,10},{10,1... | collective-permute-start | bytes 829448 | tf_op jit(solution)/shard_map/while/body/eval_jaxpr/ppermute | solution.py:10
  332.4 12.9 %collective-permute-start = (f32[27,2560]{1,0:T(8,128)S(1)}, f32[27,2560]{1,0:T(8,128)S(1)}, u32[]{:S(2)}, u32[]{:S(2)}) collective-permute-start(f32[27,2560]{1,0:T(8,128)S(1)} %get-tuple-element.213), channel_id=1, source_target_pairs={{0,1},{1,2},{2,3},{3,4},{4,5},{5,6},{6,7},{7,8},{8,9},{9,10},{10,1... | collective-permute-start | bytes 829448 | tf_op jit(solution)/shard_map/while/body/eval_jaxpr/ppermute | solution.py:10
  345.5 14.0 %collective-permute-start = (f32[27,2560]{1,0:T(8,128)S(1)}, f32[27,2560]{1,0:T(8,128)S(1)}, u32[]{:S(2)}, u32[]{:S(2)}) collective-permute-start(f32[27,2560]{1,0:T(8,128)S(1)} %get-tuple-element.213), channel_id=1, source_target_pairs={{0,1},{1,2},{2,3},{3,4},{4,5},{5,6},{6,7},{7,8},{8,9},{9,10},{10,1... | collective-permute-start | bytes 829448 | tf_op jit(solution)/shard_map/while/body/eval_jaxpr/ppermute | solution.py:10
  359.7 15.1 %collective-permute-start = (f32[27,2560]{1,0:T(8,128)S(1)}, f32[27,2560]{1,0:T(8,128)S(1)}, u32[]{:S(2)}, u32[]{:S(2)}) collective-permute-start(f32[27,2560]{1,0:T(8,128)S(1)} %get-tuple-element.213), channel_id=1, source_target_pairs={{0,1},{1,2},{2,3},{3,4},{4,5},{5,6},{6,7},{7,8},{8,9},{9,10},{10,1... | collective-permute-start | bytes 829448 | tf_op jit(solution)/shard_map/while/body/eval_jaxpr/ppermute | solution.py:10
  375.0 16.2 %collective-permute-start = (f32[27,2560]{1,0:T(8,128)S(1)}, f32[27,2560]{1,0:T(8,128)S(1)}, u32[]{:S(2)}, u32[]{:S(2)}) collective-permute-start(f32[27,2560]{1,0:T(8,128)S(1)} %get-tuple-element.213), channel_id=1, source_target_pairs={{0,1},{1,2},{2,3},{3,4},{4,5},{5,6},{6,7},{7,8},{8,9},{9,10},{10,1... | collective-permute-start | bytes 829448 | tf_op jit(solution)/shard_map/while/body/eval_jaxpr/ppermute | solution.py:10
  391.5 15.5 %collective-permute-start = (f32[27,2560]{1,0:T(8,128)S(1)}, f32[27,2560]{1,0:T(8,128)S(1)}, u32[]{:S(2)}, u32[]{:S(2)}) collective-permute-start(f32[27,2560]{1,0:T(8,128)S(1)} %get-tuple-element.213), channel_id=1, source_target_pairs={{0,1},{1,2},{2,3},{3,4},{4,5},{5,6},{6,7},{7,8},{8,9},{9,10},{10,1... | collective-permute-start | bytes 829448 | tf_op jit(solution)/shard_map/while/body/eval_jaxpr/ppermute | solution.py:10
  407.2 14.7 %collective-permute-start = (f32[27,2560]{1,0:T(8,128)S(1)}, f32[27,2560]{1,0:T(8,128)S(1)}, u32[]{:S(2)}, u32[]{:S(2)}) collective-permute-start(f32[27,2560]{1,0:T(8,128)S(1)} %get-tuple-element.213), channel_id=1, source_target_pairs={{0,1},{1,2},{2,3},{3,4},{4,5},{5,6},{6,7},{7,8},{8,9},{9,10},{10,1... | collective-permute-start | bytes 829448 | tf_op jit(solution)/shard_map/while/body/eval_jaxpr/ppermute | solution.py:10
  422.2 13.8 %collective-permute-start = (f32[27,2560]{1,0:T(8,128)S(1)}, f32[27,2560]{1,0:T(8,128)S(1)}, u32[]{:S(2)}, u32[]{:S(2)}) collective-permute-start(f32[27,2560]{1,0:T(8,128)S(1)} %get-tuple-element.213), channel_id=1, source_target_pairs={{0,1},{1,2},{2,3},{3,4},{4,5},{5,6},{6,7},{7,8},{8,9},{9,10},{10,1... | collective-permute-start | bytes 829448 | tf_op jit(solution)/shard_map/while/body/eval_jaxpr/ppermute | solution.py:10
  436.2 12.9 %collective-permute-start = (f32[27,2560]{1,0:T(8,128)S(1)}, f32[27,2560]{1,0:T(8,128)S(1)}, u32[]{:S(2)}, u32[]{:S(2)}) collective-permute-start(f32[27,2560]{1,0:T(8,128)S(1)} %get-tuple-element.213), channel_id=1, source_target_pairs={{0,1},{1,2},{2,3},{3,4},{4,5},{5,6},{6,7},{7,8},{8,9},{9,10},{10,1... | collective-permute-start | bytes 829448 | tf_op jit(solution)/shard_map/while/body/eval_jaxpr/ppermute | solution.py:10
  449.3 12.9 %collective-permute-start = (f32[27,2560]{1,0:T(8,128)S(1)}, f32[27,2560]{1,0:T(8,128)S(1)}, u32[]{:S(2)}, u32[]{:S(2)}) collective-permute-start(f32[27,2560]{1,0:T(8,128)S(1)} %get-tuple-element.213), channel_id=1, source_target_pairs={{0,1},{1,2},{2,3},{3,4},{4,5},{5,6},{6,7},{7,8},{8,9},{9,10},{10,1... | collective-permute-start | bytes 829448 | tf_op jit(solution)/shard_map/while/body/eval_jaxpr/ppermute | solution.py:10
  462.4 12.9 %collective-permute-start = (f32[27,2560]{1,0:T(8,128)S(1)}, f32[27,2560]{1,0:T(8,128)S(1)}, u32[]{:S(2)}, u32[]{:S(2)}) collective-permute-start(f32[27,2560]{1,0:T(8,128)S(1)} %get-tuple-element.213), channel_id=1, source_target_pairs={{0,1},{1,2},{2,3},{3,4},{4,5},{5,6},{6,7},{7,8},{8,9},{9,10},{10,1... | collective-permute-start | bytes 829448 | tf_op jit(solution)/shard_map/while/body/eval_jaxpr/ppermute | solution.py:10
  475.5 12.9 %collective-permute-start = (f32[27,2560]{1,0:T(8,128)S(1)}, f32[27,2560]{1,0:T(8,128)S(1)}, u32[]{:S(2)}, u32[]{:S(2)}) collective-permute-start(f32[27,2560]{1,0:T(8,128)S(1)} %get-tuple-element.213), channel_id=1, source_target_pairs={{0,1},{1,2},{2,3},{3,4},{4,5},{5,6},{6,7},{7,8},{8,9},{9,10},{10,1... | collective-permute-start | bytes 829448 | tf_op jit(solution)/shard_map/while/body/eval_jaxpr/ppermute | solution.py:10
  488.6 12.9 %collective-permute-start = (f32[27,2560]{1,0:T(8,128)S(1)}, f32[27,2560]{1,0:T(8,128)S(1)}, u32[]{:S(2)}, u32[]{:S(2)}) collective-permute-start(f32[27,2560]{1,0:T(8,128)S(1)} %get-tuple-element.213), channel_id=1, source_target_pairs={{0,1},{1,2},{2,3},{3,4},{4,5},{5,6},{6,7},{7,8},{8,9},{9,10},{10,1... | collective-permute-start | bytes 829448 | tf_op jit(solution)/shard_map/while/body/eval_jaxpr/ppermute | solution.py:10
  501.7 13.7 %collective-permute-start = (f32[27,2560]{1,0:T(8,128)S(1)}, f32[27,2560]{1,0:T(8,128)S(1)}, u32[]{:S(2)}, u32[]{:S(2)}) collective-permute-start(f32[27,2560]{1,0:T(8,128)S(1)} %get-tuple-element.213), channel_id=1, source_target_pairs={{0,1},{1,2},{2,3},{3,4},{4,5},{5,6},{6,7},{7,8},{8,9},{9,10},{10,1... | collective-permute-start | bytes 829448 | tf_op jit(solution)/shard_map/while/body/eval_jaxpr/ppermute | solution.py:10
  515.6 14.7 %collective-permute-start = (f32[27,2560]{1,0:T(8,128)S(1)}, f32[27,2560]{1,0:T(8,128)S(1)}, u32[]{:S(2)}, u32[]{:S(2)}) collective-permute-start(f32[27,2560]{1,0:T(8,128)S(1)} %get-tuple-element.213), channel_id=1, source_target_pairs={{0,1},{1,2},{2,3},{3,4},{4,5},{5,6},{6,7},{7,8},{8,9},{9,10},{10,1... | collective-permute-start | bytes 829448 | tf_op jit(solution)/shard_map/while/body/eval_jaxpr/ppermute | solution.py:10
  530.6 16.0 %collective-permute-start = (f32[27,2560]{1,0:T(8,128)S(1)}, f32[27,2560]{1,0:T(8,128)S(1)}, u32[]{:S(2)}, u32[]{:S(2)}) collective-permute-start(f32[27,2560]{1,0:T(8,128)S(1)} %get-tuple-element.213), channel_id=1, source_target_pairs={{0,1},{1,2},{2,3},{3,4},{4,5},{5,6},{6,7},{7,8},{8,9},{9,10},{10,1... | collective-permute-start | bytes 829448 | tf_op jit(solution)/shard_map/while/body/eval_jaxpr/ppermute | solution.py:10
  546.8 15.7 %collective-permute-start = (f32[27,2560]{1,0:T(8,128)S(1)}, f32[27,2560]{1,0:T(8,128)S(1)}, u32[]{:S(2)}, u32[]{:S(2)}) collective-permute-start(f32[27,2560]{1,0:T(8,128)S(1)} %get-tuple-element.213), channel_id=1, source_target_pairs={{0,1},{1,2},{2,3},{3,4},{4,5},{5,6},{6,7},{7,8},{8,9},{9,10},{10,1... | collective-permute-start | bytes 829448 | tf_op jit(solution)/shard_map/while/body/eval_jaxpr/ppermute | solution.py:10
  562.7 14.9 %collective-permute-start = (f32[27,2560]{1,0:T(8,128)S(1)}, f32[27,2560]{1,0:T(8,128)S(1)}, u32[]{:S(2)}, u32[]{:S(2)}) collective-permute-start(f32[27,2560]{1,0:T(8,128)S(1)} %get-tuple-element.213), channel_id=1, source_target_pairs={{0,1},{1,2},{2,3},{3,4},{4,5},{5,6},{6,7},{7,8},{8,9},{9,10},{10,1... | collective-permute-start | bytes 829448 | tf_op jit(solution)/shard_map/while/body/eval_jaxpr/ppermute | solution.py:10
  577.8 13.9 %collective-permute-start = (f32[27,2560]{1,0:T(8,128)S(1)}, f32[27,2560]{1,0:T(8,128)S(1)}, u32[]{:S(2)}, u32[]{:S(2)}) collective-permute-start(f32[27,2560]{1,0:T(8,128)S(1)} %get-tuple-element.213), channel_id=1, source_target_pairs={{0,1},{1,2},{2,3},{3,4},{4,5},{5,6},{6,7},{7,8},{8,9},{9,10},{10,1... | collective-permute-start | bytes 829448 | tf_op jit(solution)/shard_map/while/body/eval_jaxpr/ppermute | solution.py:10
  592.0 13.0 %collective-permute-start = (f32[27,2560]{1,0:T(8,128)S(1)}, f32[27,2560]{1,0:T(8,128)S(1)}, u32[]{:S(2)}, u32[]{:S(2)}) collective-permute-start(f32[27,2560]{1,0:T(8,128)S(1)} %get-tuple-element.213), channel_id=1, source_target_pairs={{0,1},{1,2},{2,3},{3,4},{4,5},{5,6},{6,7},{7,8},{8,9},{9,10},{10,1... | collective-permute-start | bytes 829448 | tf_op jit(solution)/shard_map/while/body/eval_jaxpr/ppermute | solution.py:10
  605.2 12.9 %collective-permute-start = (f32[27,2560]{1,0:T(8,128)S(1)}, f32[27,2560]{1,0:T(8,128)S(1)}, u32[]{:S(2)}, u32[]{:S(2)}) collective-permute-start(f32[27,2560]{1,0:T(8,128)S(1)} %get-tuple-element.213), channel_id=1, source_target_pairs={{0,1},{1,2},{2,3},{3,4},{4,5},{5,6},{6,7},{7,8},{8,9},{9,10},{10,1... | collective-permute-start | bytes 829448 | tf_op jit(solution)/shard_map/while/body/eval_jaxpr/ppermute | solution.py:10
  618.3 12.9 %collective-permute-start = (f32[27,2560]{1,0:T(8,128)S(1)}, f32[27,2560]{1,0:T(8,128)S(1)}, u32[]{:S(2)}, u32[]{:S(2)}) collective-permute-start(f32[27,2560]{1,0:T(8,128)S(1)} %get-tuple-element.213), channel_id=1, source_target_pairs={{0,1},{1,2},{2,3},{3,4},{4,5},{5,6},{6,7},{7,8},{8,9},{9,10},{10,1... | collective-permute-start | bytes 829448 | tf_op jit(solution)/shard_map/while/body/eval_jaxpr/ppermute | solution.py:10
  631.4 12.9 %collective-permute-start = (f32[27,2560]{1,0:T(8,128)S(1)}, f32[27,2560]{1,0:T(8,128)S(1)}, u32[]{:S(2)}, u32[]{:S(2)}) collective-permute-start(f32[27,2560]{1,0:T(8,128)S(1)} %get-tuple-element.213), channel_id=1, source_target_pairs={{0,1},{1,2},{2,3},{3,4},{4,5},{5,6},{6,7},{7,8},{8,9},{9,10},{10,1... | collective-permute-start | bytes 829448 | tf_op jit(solution)/shard_map/while/body/eval_jaxpr/ppermute | solution.py:10
  644.6 12.9 %collective-permute-start = (f32[27,2560]{1,0:T(8,128)S(1)}, f32[27,2560]{1,0:T(8,128)S(1)}, u32[]{:S(2)}, u32[]{:S(2)}) collective-permute-start(f32[27,2560]{1,0:T(8,128)S(1)} %get-tuple-element.213), channel_id=1, source_target_pairs={{0,1},{1,2},{2,3},{3,4},{4,5},{5,6},{6,7},{7,8},{8,9},{9,10},{10,1... | collective-permute-start | bytes 829448 | tf_op jit(solution)/shard_map/while/body/eval_jaxpr/ppermute | solution.py:10
  657.7 13.3 %collective-permute-start = (f32[27,2560]{1,0:T(8,128)S(1)}, f32[27,2560]{1,0:T(8,128)S(1)}, u32[]{:S(2)}, u32[]{:S(2)}) collective-permute-start(f32[27,2560]{1,0:T(8,128)S(1)} %get-tuple-element.213), channel_id=1, source_target_pairs={{0,1},{1,2},{2,3},{3,4},{4,5},{5,6},{6,7},{7,8},{8,9},{9,10},{10,1... | collective-permute-start | bytes 829448 | tf_op jit(solution)/shard_map/while/body/eval_jaxpr/ppermute | solution.py:10
  671.2 14.3 %collective-permute-start = (f32[27,2560]{1,0:T(8,128)S(1)}, f32[27,2560]{1,0:T(8,128)S(1)}, u32[]{:S(2)}, u32[]{:S(2)}) collective-permute-start(f32[27,2560]{1,0:T(8,128)S(1)} %get-tuple-element.213), channel_id=1, source_target_pairs={{0,1},{1,2},{2,3},{3,4},{4,5},{5,6},{6,7},{7,8},{8,9},{9,10},{10,1... | collective-permute-start | bytes 829448 | tf_op jit(solution)/shard_map/while/body/eval_jaxpr/ppermute | solution.py:10
  685.7 15.5 %collective-permute-start = (f32[27,2560]{1,0:T(8,128)S(1)}, f32[27,2560]{1,0:T(8,128)S(1)}, u32[]{:S(2)}, u32[]{:S(2)}) collective-permute-start(f32[27,2560]{1,0:T(8,128)S(1)} %get-tuple-element.213), channel_id=1, source_target_pairs={{0,1},{1,2},{2,3},{3,4},{4,5},{5,6},{6,7},{7,8},{8,9},{9,10},{10,1... | collective-permute-start | bytes 829448 | tf_op jit(solution)/shard_map/while/body/eval_jaxpr/ppermute | solution.py:10
  701.4 16.1 %collective-permute-start = (f32[27,2560]{1,0:T(8,128)S(1)}, f32[27,2560]{1,0:T(8,128)S(1)}, u32[]{:S(2)}, u32[]{:S(2)}) collective-permute-start(f32[27,2560]{1,0:T(8,128)S(1)} %get-tuple-element.213), channel_id=1, source_target_pairs={{0,1},{1,2},{2,3},{3,4},{4,5},{5,6},{6,7},{7,8},{8,9},{9,10},{10,1... | collective-permute-start | bytes 829448 | tf_op jit(solution)/shard_map/while/body/eval_jaxpr/ppermute | solution.py:10
  717.8 15.3 %collective-permute-start = (f32[27,2560]{1,0:T(8,128)S(1)}, f32[27,2560]{1,0:T(8,128)S(1)}, u32[]{:S(2)}, u32[]{:S(2)}) collective-permute-start(f32[27,2560]{1,0:T(8,128)S(1)} %get-tuple-element.213), channel_id=1, source_target_pairs={{0,1},{1,2},{2,3},{3,4},{4,5},{5,6},{6,7},{7,8},{8,9},{9,10},{10,1... | collective-permute-start | bytes 829448 | tf_op jit(solution)/shard_map/while/body/eval_jaxpr/ppermute | solution.py:10
  733.3 14.4 %collective-permute-start = (f32[27,2560]{1,0:T(8,128)S(1)}, f32[27,2560]{1,0:T(8,128)S(1)}, u32[]{:S(2)}, u32[]{:S(2)}) collective-permute-start(f32[27,2560]{1,0:T(8,128)S(1)} %get-tuple-element.213), channel_id=1, source_target_pairs={{0,1},{1,2},{2,3},{3,4},{4,5},{5,6},{6,7},{7,8},{8,9},{9,10},{10,1... | collective-permute-start | bytes 829448 | tf_op jit(solution)/shard_map/while/body/eval_jaxpr/ppermute | solution.py:10
  747.9 13.5 %collective-permute-start = (f32[27,2560]{1,0:T(8,128)S(1)}, f32[27,2560]{1,0:T(8,128)S(1)}, u32[]{:S(2)}, u32[]{:S(2)}) collective-permute-start(f32[27,2560]{1,0:T(8,128)S(1)} %get-tuple-element.213), channel_id=1, source_target_pairs={{0,1},{1,2},{2,3},{3,4},{4,5},{5,6},{6,7},{7,8},{8,9},{9,10},{10,1... | collective-permute-start | bytes 829448 | tf_op jit(solution)/shard_map/while/body/eval_jaxpr/ppermute | solution.py:10
  761.6 12.9 %collective-permute-start = (f32[27,2560]{1,0:T(8,128)S(1)}, f32[27,2560]{1,0:T(8,128)S(1)}, u32[]{:S(2)}, u32[]{:S(2)}) collective-permute-start(f32[27,2560]{1,0:T(8,128)S(1)} %get-tuple-element.213), channel_id=1, source_target_pairs={{0,1},{1,2},{2,3},{3,4},{4,5},{5,6},{6,7},{7,8},{8,9},{9,10},{10,1... | collective-permute-start | bytes 829448 | tf_op jit(solution)/shard_map/while/body/eval_jaxpr/ppermute | solution.py:10
  774.8 12.9 %collective-permute-start = (f32[27,2560]{1,0:T(8,128)S(1)}, f32[27,2560]{1,0:T(8,128)S(1)}, u32[]{:S(2)}, u32[]{:S(2)}) collective-permute-start(f32[27,2560]{1,0:T(8,128)S(1)} %get-tuple-element.213), channel_id=1, source_target_pairs={{0,1},{1,2},{2,3},{3,4},{4,5},{5,6},{6,7},{7,8},{8,9},{9,10},{10,1... | collective-permute-start | bytes 829448 | tf_op jit(solution)/shard_map/while/body/eval_jaxpr/ppermute | solution.py:10
  787.9 12.9 %collective-permute-start = (f32[27,2560]{1,0:T(8,128)S(1)}, f32[27,2560]{1,0:T(8,128)S(1)}, u32[]{:S(2)}, u32[]{:S(2)}) collective-permute-start(f32[27,2560]{1,0:T(8,128)S(1)} %get-tuple-element.213), channel_id=1, source_target_pairs={{0,1},{1,2},{2,3},{3,4},{4,5},{5,6},{6,7},{7,8},{8,9},{9,10},{10,1... | collective-permute-start | bytes 829448 | tf_op jit(solution)/shard_map/while/body/eval_jaxpr/ppermute | solution.py:10
  801.0 12.9 %collective-permute-start = (f32[27,2560]{1,0:T(8,128)S(1)}, f32[27,2560]{1,0:T(8,128)S(1)}, u32[]{:S(2)}, u32[]{:S(2)}) collective-permute-start(f32[27,2560]{1,0:T(8,128)S(1)} %get-tuple-element.213), channel_id=1, source_target_pairs={{0,1},{1,2},{2,3},{3,4},{4,5},{5,6},{6,7},{7,8},{8,9},{9,10},{10,1... | collective-permute-start | bytes 829448 | tf_op jit(solution)/shard_map/while/body/eval_jaxpr/ppermute | solution.py:10
  814.1 12.9 %collective-permute-start = (f32[27,2560]{1,0:T(8,128)S(1)}, f32[27,2560]{1,0:T(8,128)S(1)}, u32[]{:S(2)}, u32[]{:S(2)}) collective-permute-start(f32[27,2560]{1,0:T(8,128)S(1)} %get-tuple-element.213), channel_id=1, source_target_pairs={{0,1},{1,2},{2,3},{3,4},{4,5},{5,6},{6,7},{7,8},{8,9},{9,10},{10,1... | collective-permute-start | bytes 829448 | tf_op jit(solution)/shard_map/while/body/eval_jaxpr/ppermute | solution.py:10
  827.2 14.0 %collective-permute-start = (f32[27,2560]{1,0:T(8,128)S(1)}, f32[27,2560]{1,0:T(8,128)S(1)}, u32[]{:S(2)}, u32[]{:S(2)}) collective-permute-start(f32[27,2560]{1,0:T(8,128)S(1)} %get-tuple-element.213), channel_id=1, source_target_pairs={{0,1},{1,2},{2,3},{3,4},{4,5},{5,6},{6,7},{7,8},{8,9},{9,10},{10,1... | collective-permute-start | bytes 829448 | tf_op jit(solution)/shard_map/while/body/eval_jaxpr/ppermute | solution.py:10
  841.4 15.1 %collective-permute-start = (f32[27,2560]{1,0:T(8,128)S(1)}, f32[27,2560]{1,0:T(8,128)S(1)}, u32[]{:S(2)}, u32[]{:S(2)}) collective-permute-start(f32[27,2560]{1,0:T(8,128)S(1)} %get-tuple-element.213), channel_id=1, source_target_pairs={{0,1},{1,2},{2,3},{3,4},{4,5},{5,6},{6,7},{7,8},{8,9},{9,10},{10,1... | collective-permute-start | bytes 829448 | tf_op jit(solution)/shard_map/while/body/eval_jaxpr/ppermute | solution.py:10
  856.7 16.2 %collective-permute-start = (f32[27,2560]{1,0:T(8,128)S(1)}, f32[27,2560]{1,0:T(8,128)S(1)}, u32[]{:S(2)}, u32[]{:S(2)}) collective-permute-start(f32[27,2560]{1,0:T(8,128)S(1)} %get-tuple-element.213), channel_id=1, source_target_pairs={{0,1},{1,2},{2,3},{3,4},{4,5},{5,6},{6,7},{7,8},{8,9},{9,10},{10,1... | collective-permute-start | bytes 829448 | tf_op jit(solution)/shard_map/while/body/eval_jaxpr/ppermute | solution.py:10
  873.1 15.5 %collective-permute-start = (f32[27,2560]{1,0:T(8,128)S(1)}, f32[27,2560]{1,0:T(8,128)S(1)}, u32[]{:S(2)}, u32[]{:S(2)}) collective-permute-start(f32[27,2560]{1,0:T(8,128)S(1)} %get-tuple-element.213), channel_id=1, source_target_pairs={{0,1},{1,2},{2,3},{3,4},{4,5},{5,6},{6,7},{7,8},{8,9},{9,10},{10,1... | collective-permute-start | bytes 829448 | tf_op jit(solution)/shard_map/while/body/eval_jaxpr/ppermute | solution.py:10
  888.9 14.7 %collective-permute-start = (f32[27,2560]{1,0:T(8,128)S(1)}, f32[27,2560]{1,0:T(8,128)S(1)}, u32[]{:S(2)}, u32[]{:S(2)}) collective-permute-start(f32[27,2560]{1,0:T(8,128)S(1)} %get-tuple-element.213), channel_id=1, source_target_pairs={{0,1},{1,2},{2,3},{3,4},{4,5},{5,6},{6,7},{7,8},{8,9},{9,10},{10,1... | collective-permute-start | bytes 829448 | tf_op jit(solution)/shard_map/while/body/eval_jaxpr/ppermute | solution.py:10
  903.8 13.8 %collective-permute-start = (f32[27,2560]{1,0:T(8,128)S(1)}, f32[27,2560]{1,0:T(8,128)S(1)}, u32[]{:S(2)}, u32[]{:S(2)}) collective-permute-start(f32[27,2560]{1,0:T(8,128)S(1)} %get-tuple-element.213), channel_id=1, source_target_pairs={{0,1},{1,2},{2,3},{3,4},{4,5},{5,6},{6,7},{7,8},{8,9},{9,10},{10,1... | collective-permute-start | bytes 829448 | tf_op jit(solution)/shard_map/while/body/eval_jaxpr/ppermute | solution.py:10
  917.8 12.9 %collective-permute-start = (f32[27,2560]{1,0:T(8,128)S(1)}, f32[27,2560]{1,0:T(8,128)S(1)}, u32[]{:S(2)}, u32[]{:S(2)}) collective-permute-start(f32[27,2560]{1,0:T(8,128)S(1)} %get-tuple-element.213), channel_id=1, source_target_pairs={{0,1},{1,2},{2,3},{3,4},{4,5},{5,6},{6,7},{7,8},{8,9},{9,10},{10,1... | collective-permute-start | bytes 829448 | tf_op jit(solution)/shard_map/while/body/eval_jaxpr/ppermute | solution.py:10
  930.9 12.9 %collective-permute-start = (f32[27,2560]{1,0:T(8,128)S(1)}, f32[27,2560]{1,0:T(8,128)S(1)}, u32[]{:S(2)}, u32[]{:S(2)}) collective-permute-start(f32[27,2560]{1,0:T(8,128)S(1)} %get-tuple-element.213), channel_id=1, source_target_pairs={{0,1},{1,2},{2,3},{3,4},{4,5},{5,6},{6,7},{7,8},{8,9},{9,10},{10,1... | collective-permute-start | bytes 829448 | tf_op jit(solution)/shard_map/while/body/eval_jaxpr/ppermute | solution.py:10
  944.0 12.9 %collective-permute-start = (f32[27,2560]{1,0:T(8,128)S(1)}, f32[27,2560]{1,0:T(8,128)S(1)}, u32[]{:S(2)}, u32[]{:S(2)}) collective-permute-start(f32[27,2560]{1,0:T(8,128)S(1)} %get-tuple-element.213), channel_id=1, source_target_pairs={{0,1},{1,2},{2,3},{3,4},{4,5},{5,6},{6,7},{7,8},{8,9},{9,10},{10,1... | collective-permute-start | bytes 829448 | tf_op jit(solution)/shard_map/while/body/eval_jaxpr/ppermute | solution.py:10
  957.2 12.9 %collective-permute-start = (f32[27,2560]{1,0:T(8,128)S(1)}, f32[27,2560]{1,0:T(8,128)S(1)}, u32[]{:S(2)}, u32[]{:S(2)}) collective-permute-start(f32[27,2560]{1,0:T(8,128)S(1)} %get-tuple-element.213), channel_id=1, source_target_pairs={{0,1},{1,2},{2,3},{3,4},{4,5},{5,6},{6,7},{7,8},{8,9},{9,10},{10,1... | collective-permute-start | bytes 829448 | tf_op jit(solution)/shard_map/while/body/eval_jaxpr/ppermute | solution.py:10
  970.3 12.9 %collective-permute-start = (f32[27,2560]{1,0:T(8,128)S(1)}, f32[27,2560]{1,0:T(8,128)S(1)}, u32[]{:S(2)}, u32[]{:S(2)}) collective-permute-start(f32[27,2560]{1,0:T(8,128)S(1)} %get-tuple-element.213), channel_id=1, source_target_pairs={{0,1},{1,2},{2,3},{3,4},{4,5},{5,6},{6,7},{7,8},{8,9},{9,10},{10,1... | collective-permute-start | bytes 829448 | tf_op jit(solution)/shard_map/while/body/eval_jaxpr/ppermute | solution.py:10
  983.4 13.6 %collective-permute-start = (f32[27,2560]{1,0:T(8,128)S(1)}, f32[27,2560]{1,0:T(8,128)S(1)}, u32[]{:S(2)}, u32[]{:S(2)}) collective-permute-start(f32[27,2560]{1,0:T(8,128)S(1)} %get-tuple-element.213), channel_id=1, source_target_pairs={{0,1},{1,2},{2,3},{3,4},{4,5},{5,6},{6,7},{7,8},{8,9},{9,10},{10,1... | collective-permute-start | bytes 829448 | tf_op jit(solution)/shard_map/while/body/eval_jaxpr/ppermute | solution.py:10
  997.3 14.7 %collective-permute-start = (f32[27,2560]{1,0:T(8,128)S(1)}, f32[27,2560]{1,0:T(8,128)S(1)}, u32[]{:S(2)}, u32[]{:S(2)}) collective-permute-start(f32[27,2560]{1,0:T(8,128)S(1)} %get-tuple-element.213), channel_id=1, source_target_pairs={{0,1},{1,2},{2,3},{3,4},{4,5},{5,6},{6,7},{7,8},{8,9},{9,10},{10,1... | collective-permute-start | bytes 829448 | tf_op jit(solution)/shard_map/while/body/eval_jaxpr/ppermute | solution.py:10
  1012.2 16.0 %collective-permute-start = (f32[27,2560]{1,0:T(8,128)S(1)}, f32[27,2560]{1,0:T(8,128)S(1)}, u32[]{:S(2)}, u32[]{:S(2)}) collective-permute-start(f32[27,2560]{1,0:T(8,128)S(1)} %get-tuple-element.213), channel_id=1, source_target_pairs={{0,1},{1,2},{2,3},{3,4},{4,5},{5,6},{6,7},{7,8},{8,9},{9,10},{10,1... | collective-permute-start | bytes 829448 | tf_op jit(solution)/shard_map/while/body/eval_jaxpr/ppermute | solution.py:10
  1028.4 15.7 %collective-permute-start = (f32[27,2560]{1,0:T(8,128)S(1)}, f32[27,2560]{1,0:T(8,128)S(1)}, u32[]{:S(2)}, u32[]{:S(2)}) collective-permute-start(f32[27,2560]{1,0:T(8,128)S(1)} %get-tuple-element.213), channel_id=1, source_target_pairs={{0,1},{1,2},{2,3},{3,4},{4,5},{5,6},{6,7},{7,8},{8,9},{9,10},{10,1... | collective-permute-start | bytes 829448 | tf_op jit(solution)/shard_map/while/body/eval_jaxpr/ppermute | solution.py:10
  1044.3 12.9 %collective-permute-start = (f32[27,2560]{1,0:T(8,128)S(1)}, f32[27,2560]{1,0:T(8,128)S(1)}, u32[]{:S(2)}, u32[]{:S(2)}) collective-permute-start(f32[27,2560]{1,0:T(8,128)S(1)} %get-tuple-element.213), channel_id=1, source_target_pairs={{0,1},{1,2},{2,3},{3,4},{4,5},{5,6},{6,7},{7,8},{8,9},{9,10},{10,1... | collective-permute-start | bytes 829448 | tf_op jit(solution)/shard_map/while/body/eval_jaxpr/ppermute | solution.py:10
  1057.4 12.9 %collective-permute-start = (f32[27,2560]{1,0:T(8,128)S(1)}, f32[27,2560]{1,0:T(8,128)S(1)}, u32[]{:S(2)}, u32[]{:S(2)}) collective-permute-start(f32[27,2560]{1,0:T(8,128)S(1)} %get-tuple-element.213), channel_id=1, source_target_pairs={{0,1},{1,2},{2,3},{3,4},{4,5},{5,6},{6,7},{7,8},{8,9},{9,10},{10,1... | collective-permute-start | bytes 829448 | tf_op jit(solution)/shard_map/while/body/eval_jaxpr/ppermute | solution.py:10
  1070.6 12.9 %collective-permute-start = (f32[27,2560]{1,0:T(8,128)S(1)}, f32[27,2560]{1,0:T(8,128)S(1)}, u32[]{:S(2)}, u32[]{:S(2)}) collective-permute-start(f32[27,2560]{1,0:T(8,128)S(1)} %get-tuple-element.213), channel_id=1, source_target_pairs={{0,1},{1,2},{2,3},{3,4},{4,5},{5,6},{6,7},{7,8},{8,9},{9,10},{10,1... | collective-permute-start | bytes 829448 | tf_op jit(solution)/shard_map/while/body/eval_jaxpr/ppermute | solution.py:10
  1083.7 12.9 %collective-permute-start = (f32[27,2560]{1,0:T(8,128)S(1)}, f32[27,2560]{1,0:T(8,128)S(1)}, u32[]{:S(2)}, u32[]{:S(2)}) collective-permute-start(f32[27,2560]{1,0:T(8,128)S(1)} %get-tuple-element.213), channel_id=1, source_target_pairs={{0,1},{1,2},{2,3},{3,4},{4,5},{5,6},{6,7},{7,8},{8,9},{9,10},{10,1... | collective-permute-start | bytes 829448 | tf_op jit(solution)/shard_map/while/body/eval_jaxpr/ppermute | solution.py:10
  1096.8 12.9 %collective-permute-start = (f32[27,2560]{1,0:T(8,128)S(1)}, f32[27,2560]{1,0:T(8,128)S(1)}, u32[]{:S(2)}, u32[]{:S(2)}) collective-permute-start(f32[27,2560]{1,0:T(8,128)S(1)} %get-tuple-element.213), channel_id=1, source_target_pairs={{0,1},{1,2},{2,3},{3,4},{4,5},{5,6},{6,7},{7,8},{8,9},{9,10},{10,1... | collective-permute-start | bytes 829448 | tf_op jit(solution)/shard_map/while/body/eval_jaxpr/ppermute | solution.py:10
  (5 other events, 533.1 us)
Sparse Core Ops, SparseCore 0:
  11.5 160.8 all-gather.2
where the time goes:
time: 1120 us
  waiting for transfers between devices  1030 us (92%)
  blocking collectives  28.2 us (3%)
  matrix products  22.2 us (2%)
  between operations  14.1 us (1%)
  local copies, waits for them, and re-layouts  11.3 us (1%)
    ppermute x63, waiting for transfers between devices, from_behind(): return lax.ppermute(value, axis, pairs)  867 us
    all_gather x1, waiting for transfers between devices, body(): whole_weight = lax.all_gather(down_weight, 'blk', axis=0, tiled=True)  164 us
    psum x1, blocking collectives, body(): output = lax.psum(partial_out, 'dp').astype(jnp.bfloat16)  28.2 us
  transfers between devices with their start and end apart: 64, of which 64 were waited for; matrix products, arithmetic and copies ran while one was open for 0% of the time, Pallas kernels for 0%

commit v1 on v0

v1 whole, which is shorter than its diff:
```python
import jax
import jax.numpy as jnp
from jax import lax
from jax.sharding import Mesh, PartitionSpec as P

BF16 = jnp.bfloat16
F32 = jnp.float32
NX, NZ = 4, 8


def shift(value, axis, steps):
    count = lax.axis_size(axis)
    return lax.ppermute(value, axis, [(i, (i + steps) % count) for i in range(count)])


def pick(stacked, index):
    return lax.dynamic_index_in_dim(stacked, index, 0, keepdims=False)


def swapped(value, core):
    half = value.shape[-1] // 2
    left, right = value[..., :half], value[..., half:]
    first = core == 0
    return jnp.concatenate([jnp.where(first, left, right), jnp.where(first, right, left)], -1)


def body(gate_pre, up_pre, down_weight, cotangent):
    x, z, yh, core = (lax.axis_index(a) for a in ("x", "z", "yh", "core"))
    rows, units = gate_pre.shape
    block, width = down_weight.shape
    half = width // 2
    part = units // NX

    w_mine = swapped(down_weight, core)
    w_other = shift(w_mine, "yh", 1)
    low = yh == 0
    w0 = jnp.concatenate([jnp.where(low, w_mine, w_other), jnp.where(low, w_other, w_mine)], 0)
    fwd, bwd = [w0], [w0]
    for _ in range(3):
        fwd.append(shift(fwd[-1], "z", 1))
        bwd.append(shift(bwd[-1], "z", -1))
    far = jnp.concatenate(
        [shift(fwd[3][:, :half], "z", 1), shift(bwd[3][:, half:], "z", -1)], 1
    )
    by_distance = [w0, fwd[1], fwd[2], fwd[3], far, bwd[3], bwd[2], bwd[1]]
    weight = jnp.zeros((NZ,) + w0.shape, BF16)
    for distance, piece in enumerate(by_distance):
        weight = lax.dynamic_update_index_in_dim(weight, piece, (z - distance) % NZ, 0)
    weight = weight.reshape(NZ * 2 * block, width)

    gate32, up32 = gate_pre.astype(F32), up_pre.astype(F32)
    sig = jax.nn.sigmoid(gate32)
    silu_val = gate32 * sig
    hidden = (silu_val * up32).astype(BF16)
    slices = hidden.reshape(rows, NX, part).transpose(1, 0, 2)
    cot_own = swapped(cotangent, core)
    got = []
    for k in (1, 2, 3):
        message = jnp.concatenate([cot_own[:, :half], pick(slices, (x + k) % NX)], 1)
        got.append(shift(message, "x", k))
    near = jnp.concatenate([g[:, :half] for g in got], 0)
    cot = jnp.concatenate([cot_own, jnp.concatenate([near, shift(near, "core", 1)], 1)], 0)
    hid = jnp.concatenate([pick(slices, x)] + [g[:, half:] for g in got], 0)

    scale = float(rows * NX * NZ * 2) ** (-0.5)
    grad_part = lax.dot_general(hid, cot, (((0,), (0,)), ((), ())), preferred_element_type=F32)
    grad_part = (grad_part * scale).reshape(NZ, 2 * block, width)
    farthest = pick(grad_part, (z + 4) % NZ)
    to_fwd = farthest[:, :half].astype(BF16)
    to_bwd = farthest[:, half:].astype(BF16)
    to_fwd, to_bwd = shift(to_fwd, "z", 1), shift(to_bwd, "z", -1)
    pad_fwd = jnp.pad(to_fwd.astype(F32), ((0, 0), (0, half)))
    pad_bwd = jnp.pad(to_bwd.astype(F32), ((0, 0), (half, 0)))
    to_fwd = (pick(grad_part, (z + 3) % NZ) + pad_fwd).astype(BF16)
    to_bwd = (pick(grad_part, (z - 3) % NZ) + pad_bwd).astype(BF16)
    for distance in (2, 1):
        to_fwd, to_bwd = shift(to_fwd, "z", 1), shift(to_bwd, "z", -1)
        to_fwd = (pick(grad_part, (z + distance) % NZ) + to_fwd.astype(F32)).astype(BF16)
        to_bwd = (pick(grad_part, (z - distance) % NZ) + to_bwd.astype(F32)).astype(BF16)
    to_fwd, to_bwd = shift(to_fwd, "z", 1), shift(to_bwd, "z", -1)
    grad = pick(grad_part, z) + (to_fwd.astype(F32) + to_bwd.astype(F32))
    keep = jnp.where(low, grad[:block], grad[block:])
    give = jnp.where(low, grad[block:], grad[:block]).astype(BF16)
    grad_weight = swapped(keep + shift(give, "yh", 1).astype(F32), core)

    back = lax.dot_general(cot, weight, (((1,), (1,)), ((), ())), preferred_element_type=F32)
    back = back.astype(BF16)
    out_other = jnp.dot(hid, weight[:, half:], preferred_element_type=F32).astype(BF16)
    out_mine = jnp.dot(hid, weight[:, :half], preferred_element_type=F32)
    out_mine = out_mine + shift(out_other, "core", 1).astype(F32)
    total = out_mine[:rows]
    back_own = jnp.zeros((NX, rows, part), BF16)
    back_own = lax.dynamic_update_index_in_dim(back_own, back[:rows], x, 0)
    for k in (1, 2, 3):
        here = slice(k * rows, (k + 1) * rows)
        message = jnp.concatenate([out_mine[here].astype(BF16), back[here]], 1)
        message = shift(message, "x", -k)
        total = total + message[:, :half].astype(F32)
        back_own = lax.dynamic_update_index_in_dim(back_own, message[:, half:], (x + k) % NX, 0)
    rounded = total.astype(BF16)
    out_half = (rounded.astype(F32) + shift(rounded, "yl", 1).astype(F32)).astype(BF16)
    output = swapped(jnp.concatenate([out_half, shift(out_half, "core", 1)], 1), core)

    back32 = back_own.transpose(1, 0, 2).reshape(rows, units).astype(F32)
    grad_gate = (back32 * up32 * (sig * (1.0 + gate32 * (1.0 - sig)))).astype(BF16)
    grad_up = (back32 * silu_val).astype(BF16)
    return output, grad_weight, grad_gate, grad_up


def solution(mesh):
    fine = Mesh(mesh.devices.reshape(2, 2, NX, NZ, 2), ("yl", "core", "x", "z", "yh"))
    blk, dp = ("x", "z", "yh"), ("yl", "core")
    return jax.shard_map(
        body,
        mesh=fine,
        in_specs=(P(blk, dp), P(blk, dp), P(dp + blk, None), P(blk, None)),
        out_specs=(P(blk, None), P(dp + blk, None), P(blk, dp), P(blk, dp)),
        check_vma=False,
    )
```

time: 1120 us -> 153 us (0.14)
  the two profiles are of different devices: /device:TPU:8 before, /device:TPU:1 now
where the time goes in v1:
time: 153 us; the launch traced here: 152 us
  waiting for transfers between devices  57.5 us (38%)
  starting transfers between devices  45.9 us (30%)
  local copies, waits for them, and re-layouts  20.9 us (14%)
  other arithmetic  15.5 us (10%)
  matrix products  11.3 us (7%)
    ppermute x28, waiting for transfers between devices, shift(): lax.ppermute(value, axis, [(i, (i + steps) % count) for i in range(count)])  57.5 us
    ppermute x28, starting transfers between devices, shift(): lax.ppermute(value, axis, [(i, (i + steps) % count) for i in range(count)])  45.9 us
    unnamed x42, local copies, waits for them, and re-layouts  5.27 us
    reshape x1, local copies, waits for them, and re-layouts, body(): grad_part = (grad_part * scale).reshape(NZ, 2 * block, width)  4 us
    dot_general x1, matrix products, body(): lax.dot_general(hid, cot, (((0,), (0,)), ((), ())), preferred_element_typ...  3.46 us
    dot_general x1, matrix products, body(): lax.dot_general(cot, weight, (((1,), (1,)), ((), ())), preferred_element_...  3.16 us
  transfers between devices with their start and end apart: 28, of which 11 were waited for; matrix products, arithmetic and copies ran while one was open for 20% of the time, Pallas kernels for 0%

profile of v1, /device:TPU:1, one launch (start us, length us, event | category | flops | bytes accessed | tf_op | source)
XLA Modules:
  0.0 152.4 jit_solution(16083509303605380546)
XLA Ops:
  0.6 0.9 broadcast_select_fusion.7
  1.6 3.8 %collective-permute-start.3 = (bf16[27,2560]{1,0:T(8,128)(2,1)S(1)}, bf16[27,2560]{1,0:T(8,128)(2,1)S(1)}, u32[]{:S(2)}, u32[]{:S(2)}) collective-permute-start(bf16[27,2560]{1,0:T(8,128)(2,1)S(1)} %pad_maximum_fusion.11), channel_id=1, source_target_pairs={{0,1},{1,0},{2,3},{3,2},{4,5},{5,4},{6,7},{7,6},{8,9},{9,8},{10,11... | collective-permute-start | bytes 414728 | tf_op jit(solution)/shard_map/ppermute | solution.py:13
  5.4 1.8 %broadcast_select_fusion.2 = (bf16[128,1280]{1,0:T(8,128)(2,1)}, bf16[128,1280]{1,0:T(8,128)(2,1)S(1)}) fusion(pred[]{:T(512)S(6)} %eq.31, bf16[128,2560]{1,0:T(8,128)(2,1)} %param.7), kind=kLoop, calls=%fused_computation.55 | loop fusion | flops 327680 | bytes 1310721 | tf_op jit(solution)/shard_map/jit(_where)/select_n | solution.py:24
  7.3 1.5 %fusion.2 = bf16[128,1728]{0,1:T(8,128)(2,1)S(1)} fusion(bf16[128,1728]{0,1:T(8,128)(2,1)} %param.5, bf16[128,1728]{0,1:T(8,128)(2,1)} %param.4), kind=kLoop, calls=%fused_computation.13 | loop fusion | flops 1769472 | bytes 1327104 | tf_op jit(solution)/shard_map/convert_element_type | solution.py:54
  9.1 0.8 bitcast_dynamic-update-slice_fusion.6
  9.9 1.8 %collective-permute-start.4 = (bf16[54,2560]{1,0:T(8,128)(2,1)}, bf16[54,2560]{1,0:T(8,128)(2,1)}, u32[]{:S(2)}, u32[]{:S(2)}) collective-permute-start(bf16[54,2560]{1,0:T(8,128)(2,1)} %get-tuple-element.5), channel_id=1, source_target_pairs={{0,2},{2,4},{4,6},{6,8},{8,10},{10,12},{12,14},{14,0},{1,3},{3,5},... | collective-permute-start | bytes 829448 | tf_op jit(solution)/shard_map/ppermute | solution.py:13
  11.7 3.9 %collective-permute-start.8 = (bf16[54,2560]{1,0:T(8,128)(2,1)}, bf16[54,2560]{1,0:T(8,128)(2,1)}, u32[]{:S(2)}, u32[]{:S(2)}) collective-permute-start(bf16[54,2560]{1,0:T(8,128)(2,1)} %get-tuple-element.5), channel_id=1, source_target_pairs={{0,14},{2,0},{4,2},{6,4},{8,6},{10,8},{12,10},{14,12},{1,15},{3,1}... | collective-permute-start | bytes 829448 | tf_op jit(solution)/shard_map/ppermute | solution.py:13
  15.7 0.7 constant_dynamic-slice_fusion.3
  16.7 1.2 pad_maximum_fusion.5
  17.9 1.2 collective-permute-start
  19.1 2.5 %collective-permute-start.1 = (bf16[128,1712]{1,0:T(8,128)(2,1)}, bf16[128,1712]{1,0:T(8,128)(2,1)S(1)}, u32[]{:S(2)}, u32[]{:S(2)}) collective-permute-start(bf16[128,1712]{1,0:T(8,128)(2,1)} %get-tuple-element.27), channel_id=1, source_target_pairs={{0,32},{16,48},{32,0},{48,16},{1,33},{17,49},{33,1},{49,17},{2,34}... | collective-permute-start | bytes 1314824 | tf_op jit(solution)/shard_map/ppermute | solution.py:13
  21.5 1.2 collective-permute-start.2
  22.7 1.6 %copy.23 = bf16[128,1,432]{2,0,1:T(8,128)(2,1)} copy(bf16[128,1,432]{0,2,1:T(8,128)(2,1)} %get-tuple-element.20) | data formatting | bytes 221184
  24.4 2.7 %collective-permute-start.9 = (bf16[54,2560]{1,0:T(8,128)(2,1)}, bf16[54,2560]{1,0:T(8,128)(2,1)S(1)}, u32[]{:S(2)}, u32[]{:S(2)}) collective-permute-start(bf16[54,2560]{1,0:T(8,128)(2,1)} %collective-permute-done.8), channel_id=1, source_target_pairs={{0,14},{2,0},{4,2},{6,4},{8,6},{10,8},{12,10},{14,12},{1,15},{3,1}... | collective-permute-start | bytes 829448 | tf_op jit(solution)/shard_map/ppermute | solution.py:13
  27.0 1.0 bitcast_dynamic-update-slice_fusion.5
  28.0 1.5 collective-permute-done
  29.5 0.8 copy-done.11
  30.3 10.0 %collective-permute-done.1 = bf16[128,1712]{1,0:T(8,128)(2,1)S(1)} collective-permute-done((bf16[128,1712]{1,0:T(8,128)(2,1)}, bf16[128,1712]{1,0:T(8,128)(2,1)S(1)}, u32[]{:S(2)}, u32[]{:S(2)}) %collective-permute-start.1) | collective-permute-done | bytes 438304 | tf_op jit(solution)/shard_map/ppermute | solution.py:13
  40.3 0.7 copy-done.12
  41.2 1.0 slice.154
  42.3 2.7 %collective-permute-start.13 = (bf16[384,1280]{1,0:T(8,128)(2,1)S(1)}, bf16[384,1280]{1,0:T(8,128)(2,1)S(1)}, u32[]{:S(2)}, u32[]{:S(2)}) collective-permute-start(bf16[384,1280]{1,0:T(8,128)(2,1)S(1)} %pad_maximum_fusion), channel_id=1, source_target_pairs={{0,64},{64,0},{1,65},{65,1},{2,66},{66,2},{3,67},{67,3},{4,68},{68... | collective-permute-start | bytes 2949128 | tf_op jit(solution)/shard_map/ppermute | solution.py:13
  45.0 0.9 slice.143
  45.9 0.9 slice.144
  46.9 0.9 slice.145
  47.9 2.7 %collective-permute-start.10 = (bf16[54,2560]{1,0:T(8,128)(2,1)S(1)}, bf16[54,2560]{1,0:T(8,128)(2,1)S(1)}, u32[]{:S(2)}, u32[]{:S(2)}) collective-permute-start(bf16[54,2560]{1,0:T(8,128)(2,1)S(1)} %collective-permute-done.9), channel_id=1, source_target_pairs={{0,14},{2,0},{4,2},{6,4},{8,6},{10,8},{12,10},{14,12},{1,15},{3,1}... | collective-permute-start | bytes 829448 | tf_op jit(solution)/shard_map/ppermute | solution.py:13
  50.6 6.9 %collective-permute-done.6 = bf16[54,2560]{1,0:T(8,128)(2,1)S(1)} collective-permute-done((bf16[54,2560]{1,0:T(8,128)(2,1)S(1)}, bf16[54,2560]{1,0:T(8,128)(2,1)S(1)}, u32[]{:S(2)}, u32[]{:S(2)}) %collective-permute-start.6) | collective-permute-done | bytes 276512 | tf_op jit(solution)/shard_map/ppermute | solution.py:13
  57.6 2.9 %collective-permute-start.11 = (bf16[54,1280]{1,0:T(8,128)(2,1)S(1)}, bf16[54,1280]{1,0:T(8,128)(2,1)S(1)}, u32[]{:S(2)}, u32[]{:S(2)}) collective-permute-start(bf16[54,1280]{1,0:T(8,128)(2,1)S(1)} %slice.147), channel_id=1, source_target_pairs={{0,14},{2,0},{4,2},{6,4},{8,6},{10,8},{12,10},{14,12},{1,15},{3,1}... | collective-permute-start | bytes 414728 | tf_op jit(solution)/shard_map/ppermute | solution.py:13
  60.5 2.6 %collective-permute-done.7 = bf16[54,1280]{1,0:T(8,128)(2,1)S(1)} collective-permute-done((bf16[54,1280]{1,0:T(8,128)(2,1)S(1)}, bf16[54,1280]{1,0:T(8,128)(2,1)S(1)}, u32[]{:S(2)}, u32[]{:S(2)}) %collective-permute-start.7) | collective-permute-done | bytes 138272 | tf_op jit(solution)/shard_map/ppermute | solution.py:13
  63.3 0.9 copy-done.17
  64.3 3.5 %convolution_multiply_fusion = f32[432,2560]{1,0:T(8,128)} fusion(bf16[128,432]{1,0:T(8,128)(2,1)S(1)} %slice.145, bf16[128,432]{1,0:T(8,128)(2,1)S(1)} %slice.144, bf16[128,432]{1,0:T(8,128)(2,1)S(1)} %slice.143, bf16[128,432]{1,0:T(8,128)(2,1)S(1)} %bitcast.78, bf16[384,1280]{1,0:T(8,128)(2,1)S(1)} %collective-permute-done.13, ...), kind=kOutput, calls=%fused_computation | convolution fusion | flops 1151066112 | bytes 7487488 | tf_op jit(solution)/shard_map/dot_general | solution.py:66
  67.7 4.0 %reshape.30 = f32[8,54,2560]{2,1,0:T(8,128)} reshape(f32[432,2560]{1,0:T(8,128)} %convolution_multiply_fusion) | data formatting | bytes 8847360 | tf_op jit(solution)/shard_map/reshape | solution.py:67
  71.7 1.1 fusion.20
  72.8 0.7 fusion.27
  73.6 1.0 bitcast_dynamic-update-slice_fusion
  74.5 1.7 %reshape.29 = bf16[432,2560]{1,0:T(8,128)(2,1)} reshape(bf16[8,54,2560]{2,1,0:T(8,128)(2,1)S(1)} %bitcast_dynamic-update-slice_fusion) | data formatting | bytes 4423680 | tf_op jit(solution)/shard_map/reshape | solution.py:49
  76.2 2.8 %collective-permute-done.19 = bf16[54,1280]{1,0:T(8,128)(2,1)} collective-permute-done((bf16[54,1280]{1,0:T(8,128)(2,1)}, bf16[54,1280]{1,0:T(8,128)(2,1)}, u32[]{:S(2)}, u32[]{:S(2)}) %collective-permute-start.19) | collective-permute-done | bytes 138272 | tf_op jit(solution)/shard_map/ppermute | solution.py:13
  79.0 1.2 fusion.17
  80.3 2.4 %convolution_convert_fusion = bf16[512,1280]{1,0:T(8,128)(2,1)S(1)} fusion(bf16[432,2560]{1,0:T(8,128)(2,1)} %reshape.29, bf16[128,432]{1,0:T(8,128)(2,1)} %copy-done.7, bf16[128,432]{1,0:T(8,128)(2,1)S(1)} %slice.144, bf16[128,432]{1,0:T(8,128)(2,1)S(1)} %slice.143, bf16[128,432]{1,0:T(8,128)(2,1)} %bitcast.77), kind=kOutput, calls=%fused_computation.2 | convolution fusion | flops 568655872 | bytes 2899968 | tf_op jit(solution)/shard_map/dot_general | solution.py:88
  82.7 3.1 %collective-permute-start.12 = (bf16[512,1280]{1,0:T(8,128)(2,1)S(1)}, bf16[512,1280]{1,0:T(8,128)(2,1)S(1)}, u32[]{:S(2)}, u32[]{:S(2)}) collective-permute-start(bf16[512,1280]{1,0:T(8,128)(2,1)S(1)} %convolution_convert_fusion), channel_id=1, source_target_pairs={{0,64},{64,0},{1,65},{65,1},{2,66},{66,2},{3,67},{67,3},{4,68},{68... | collective-permute-start | bytes 3932168 | tf_op jit(solution)/shard_map/ppermute | solution.py:13
  85.8 3.3 %collective-permute-start.23 = (bf16[54,1280]{1,0:T(8,128)(2,1)S(1)}, bf16[54,1280]{1,0:T(8,128)(2,1)S(1)}, u32[]{:S(2)}, u32[]{:S(2)}) collective-permute-start(bf16[54,1280]{1,0:T(8,128)(2,1)S(1)} %copy-done.16), channel_id=1, source_target_pairs={{0,14},{2,0},{4,2},{6,4},{8,6},{10,8},{12,10},{14,12},{1,15},{3,1}... | collective-permute-start | bytes 414728 | tf_op jit(solution)/shard_map/ppermute | solution.py:13
  89.3 3.2 %convolution_convert_fusion.1 = bf16[512,432]{1,0:T(8,128)(2,1)S(1)} fusion(bf16[432,2560]{1,0:T(8,128)(2,1)} %reshape.29, bf16[384,1280]{1,0:T(8,128)(2,1)S(1)} %copy-done.18, bf16[128,1280]{1,0:T(8,128)(2,1)S(1)} %slice.154, bf16[128,1280]{1,0:T(8,128)(2,1)S(1)} %slice.153, bf16[128,1280]{1,0:T(8,128)(2,1)S(1)} %slice.152, ...), kind=kOutput, calls=%fused_computation.7 | convolution fusion | flops 1148411904 | bytes 5275648 | tf_op jit(solution)/shard_map/dot_general | solution.py:86
  92.5 4.2 %collective-permute-done.21 = bf16[54,2560]{1,0:T(8,128)(2,1)S(1)} collective-permute-done((bf16[54,2560]{1,0:T(8,128)(2,1)S(1)}, bf16[54,2560]{1,0:T(8,128)(2,1)S(1)}, u32[]{:S(2)}, u32[]{:S(2)}) %collective-permute-start.21) | collective-permute-done | bytes 276512 | tf_op jit(solution)/shard_map/ppermute | solution.py:13
  96.7 0.8 fusion.19
  97.6 1.5 %collective-permute-start.22 = (bf16[54,2560]{1,0:T(8,128)(2,1)}, bf16[54,2560]{1,0:T(8,128)(2,1)}, u32[]{:S(2)}, u32[]{:S(2)}) collective-permute-start(bf16[54,2560]{1,0:T(8,128)(2,1)} %get-tuple-element.6), channel_id=1, source_target_pairs={{0,2},{2,4},{4,6},{6,8},{8,10},{10,12},{12,14},{14,0},{1,3},{3,5},... | collective-permute-start | bytes 829448 | tf_op jit(solution)/shard_map/ppermute | solution.py:13
  99.2 3.8 %collective-permute-done.24 = bf16[54,2560]{1,0:T(8,128)(2,1)S(1)} collective-permute-done((bf16[54,2560]{1,0:T(8,128)(2,1)S(1)}, bf16[54,2560]{1,0:T(8,128)(2,1)S(1)}, u32[]{:S(2)}, u32[]{:S(2)}) %collective-permute-start.24) | collective-permute-done | bytes 276512 | tf_op jit(solution)/shard_map/ppermute | solution.py:13
  103.1 1.3 collective-permute-start.25
  104.4 2.3 %fusion.28 = (bf16[512,1280]{1,0:T(8,128)(2,1)S(1)}, f32[512,1280]{1,0:T(8,128)}) fusion(bf16[512,1280]{1,0:T(8,128)(2,1)S(1)} %collective-permute-done.12, bf16[432,2560]{1,0:T(8,128)(2,1)S(1)} %copy-done.1, bf16[128,432]{1,0:T(8,128)(2,1)S(1)} %copy-done.8, bf16[128,432]{1,0:T(8,128)(2,1)S(1)} %slice.144, bf16[128,432]{1,0:T(8,128)(2,1)S(1)} %slice.143, ...), kind=kOutput, calls=%fused_computation.90 | convolution fusion | flops 569966592 | bytes 6873088 | tf_op jit(solution)/shard_map/dot_general | solution.py:89
  106.8 1.8 %collective-permute-start.15 = (bf16[128,1712]{1,0:T(8,128)(2,1)S(1)}, bf16[128,1712]{1,0:T(8,128)(2,1)S(1)}, u32[]{:S(2)}, u32[]{:S(2)}) collective-permute-start(bf16[128,1712]{1,0:T(8,128)(2,1)S(1)} %pad_maximum_fusion.7), channel_id=1, source_target_pairs={{0,32},{16,48},{32,0},{48,16},{1,33},{17,49},{33,1},{49,17},{2,34}... | collective-permute-start | bytes 1314824 | tf_op jit(solution)/shard_map/ppermute | solution.py:13
  109.0 2.8 %collective-permute-start.14 = (bf16[128,1712]{1,0:T(8,128)(2,1)S(1)}, bf16[128,1712]{1,0:T(8,128)(2,1)}, u32[]{:S(2)}, u32[]{:S(2)}) collective-permute-start(bf16[128,1712]{1,0:T(8,128)(2,1)S(1)} %pad_maximum_fusion.6), channel_id=1, source_target_pairs={{0,48},{16,0},{32,16},{48,32},{1,49},{17,1},{33,17},{49,33},{2,50}... | collective-permute-start | bytes 1314824 | tf_op jit(solution)/shard_map/ppermute | solution.py:13
  111.8 0.8 fusion.16
  112.6 17.5 %collective-permute-done.16 = bf16[128,1712]{1,0:T(8,128)(2,1)S(1)} collective-permute-done((bf16[128,1712]{1,0:T(8,128)(2,1)S(1)}, bf16[128,1712]{1,0:T(8,128)(2,1)S(1)}, u32[]{:S(2)}, u32[]{:S(2)}) %collective-permute-start.16) | collective-permute-done | bytes 438304 | tf_op jit(solution)/shard_map/ppermute | solution.py:13
  130.1 0.8 copy-done.13
  131.0 0.9 fusion.23
  132.0 1.5 fusion.13
  133.5 0.3 copy.20
  133.8 1.4 collective-permute-start.17
  135.2 1.3 bitcast_add_fusion.6
  136.6 2.7 %collective-permute-start.27 = (bf16[27,2560]{1,0:T(8,128)(2,1)S(1)}, bf16[27,2560]{1,0:T(8,128)(2,1)S(1)}, u32[]{:S(2)}, u32[]{:S(2)}) collective-permute-start(bf16[27,2560]{1,0:T(8,128)(2,1)S(1)} %select_convert_fusion), channel_id=1, source_target_pairs={{0,1},{1,0},{2,3},{3,2},{4,5},{5,4},{6,7},{7,6},{8,9},{9,8},{10,11... | collective-permute-start | bytes 414728 | tf_op jit(solution)/shard_map/ppermute | solution.py:13
  139.3 1.4 fusion.10
  140.7 7.3 %collective-permute-done.27 = bf16[27,2560]{1,0:T(8,128)(2,1)S(1)} collective-permute-done((bf16[27,2560]{1,0:T(8,128)(2,1)S(1)}, bf16[27,2560]{1,0:T(8,128)(2,1)S(1)}, u32[]{:S(2)}, u32[]{:S(2)}) %collective-permute-start.27) | collective-permute-done | bytes 138272 | tf_op jit(solution)/shard_map/ppermute | solution.py:13
  148.1 2.1 %collective-permute-start.18 = (bf16[128,1280]{1,0:T(8,128)(2,1)S(1)}, bf16[128,1280]{1,0:T(8,128)(2,1)S(1)}, u32[]{:S(2)}, u32[]{:S(2)}) collective-permute-start(bf16[128,1280]{1,0:T(8,128)(2,1)S(1)} %add_convert_fusion), channel_id=1, source_target_pairs={{0,64},{64,0},{1,65},{65,1},{2,66},{66,2},{3,67},{67,3},{4,68},{68... | collective-permute-start | bytes 983048 | tf_op jit(solution)/shard_map/ppermute | solution.py:13
  150.2 0.7 pad_maximum_fusion.9
  151.0 0.5 collective-permute-done.18
  151.5 0.9 pad_maximum_fusion.1
  (95 shorter events, 2.6 us)
Async XLA Ops:
  1.6 7.3 %collective-permute-start.3 = (bf16[27,2560]{1,0:T(8,128)(2,1)S(1)}, bf16[27,2560]{1,0:T(8,128)(2,1)S(1)}, u32[]{:S(2)}, u32[]{:S(2)}) collective-permute-start(bf16[27,2560]{1,0:T(8,128)(2,1)S(1)} %pad_maximum_fusion.11), channel_id=1, source_target_pairs={{0,1},{1,0},{2,3},{3,2},{4,5},{5,4},{6,7},{7,6},{8,9},{9,8},{10,11... | collective-permute-start | bytes 414728 | tf_op jit(solution)/shard_map/ppermute | solution.py:13
  7.3 9.4 %copy-start.4 = (bf16[128,1280]{1,0:T(8,128)(2,1)}, bf16[128,1280]{1,0:T(8,128)(2,1)S(1)}, u32[]{:S(2)}) copy-start(bf16[128,1280]{1,0:T(8,128)(2,1)S(1)} %get-tuple-element.16) | copy-start | bytes 983044
  9.9 14.5 %collective-permute-start.4 = (bf16[54,2560]{1,0:T(8,128)(2,1)}, bf16[54,2560]{1,0:T(8,128)(2,1)}, u32[]{:S(2)}, u32[]{:S(2)}) collective-permute-start(bf16[54,2560]{1,0:T(8,128)(2,1)} %get-tuple-element.5), channel_id=1, source_target_pairs={{0,2},{2,4},{4,6},{6,8},{8,10},{10,12},{12,14},{14,0},{1,3},{3,5},... | collective-permute-start | bytes 829448 | tf_op jit(solution)/shard_map/ppermute | solution.py:13
  11.7 12.6 %collective-permute-start.8 = (bf16[54,2560]{1,0:T(8,128)(2,1)}, bf16[54,2560]{1,0:T(8,128)(2,1)}, u32[]{:S(2)}, u32[]{:S(2)}) collective-permute-start(bf16[54,2560]{1,0:T(8,128)(2,1)} %get-tuple-element.5), channel_id=1, source_target_pairs={{0,14},{2,0},{4,2},{6,4},{8,6},{10,8},{12,10},{14,12},{1,15},{3,1}... | collective-permute-start | bytes 829448 | tf_op jit(solution)/shard_map/ppermute | solution.py:13
  17.9 11.6 %collective-permute-start = (bf16[128,1712]{1,0:T(8,128)(2,1)}, bf16[128,1712]{1,0:T(8,128)(2,1)S(1)}, u32[]{:S(2)}, u32[]{:S(2)}) collective-permute-start(bf16[128,1712]{1,0:T(8,128)(2,1)} %get-tuple-element.26), channel_id=1, source_target_pairs={{0,16},{16,32},{32,48},{48,0},{1,17},{17,33},{33,49},{49,1},{2,18}... | collective-permute-start | bytes 1314824 | tf_op jit(solution)/shard_map/ppermute | solution.py:13
  19.1 21.2 %collective-permute-start.1 = (bf16[128,1712]{1,0:T(8,128)(2,1)}, bf16[128,1712]{1,0:T(8,128)(2,1)S(1)}, u32[]{:S(2)}, u32[]{:S(2)}) collective-permute-start(bf16[128,1712]{1,0:T(8,128)(2,1)} %get-tuple-element.27), channel_id=1, source_target_pairs={{0,32},{16,48},{32,0},{48,16},{1,33},{17,49},{33,1},{49,17},{2,34}... | collective-permute-start | bytes 1314824 | tf_op jit(solution)/shard_map/ppermute | solution.py:13
  21.5 19.7 %collective-permute-start.2 = (bf16[128,1712]{1,0:T(8,128)(2,1)}, bf16[128,1712]{1,0:T(8,128)(2,1)}, u32[]{:S(2)}, u32[]{:S(2)}) collective-permute-start(bf16[128,1712]{1,0:T(8,128)(2,1)} %get-tuple-element.28), channel_id=1, source_target_pairs={{0,48},{16,0},{32,16},{48,32},{1,49},{17,1},{33,17},{49,33},{2,50}... | collective-permute-start | bytes 1314824 | tf_op jit(solution)/shard_map/ppermute | solution.py:13
  24.3 23.4 %collective-permute-start.5 = (bf16[54,2560]{1,0:T(8,128)(2,1)}, bf16[54,2560]{1,0:T(8,128)(2,1)S(1)}, u32[]{:S(2)}, u32[]{:S(2)}) collective-permute-start(bf16[54,2560]{1,0:T(8,128)(2,1)} %collective-permute-done.4), channel_id=1, source_target_pairs={{0,2},{2,4},{4,6},{6,8},{8,10},{10,12},{12,14},{14,0},{1,3},{3,5},... | collective-permute-start | bytes 829448 | tf_op jit(solution)/shard_map/ppermute | solution.py:13
  24.4 23.5 %collective-permute-start.9 = (bf16[54,2560]{1,0:T(8,128)(2,1)}, bf16[54,2560]{1,0:T(8,128)(2,1)S(1)}, u32[]{:S(2)}, u32[]{:S(2)}) collective-permute-start(bf16[54,2560]{1,0:T(8,128)(2,1)} %collective-permute-done.8), channel_id=1, source_target_pairs={{0,14},{2,0},{4,2},{6,4},{8,6},{10,8},{12,10},{14,12},{1,15},{3,1}... | collective-permute-start | bytes 829448 | tf_op jit(solution)/shard_map/ppermute | solution.py:13
  29.5 0.8 copy-start.11
  40.3 0.8 copy-start.12
  42.2 22.0 %copy-start.5 = (bf16[128,1280]{1,0:T(8,128)(2,1)S(1)}, bf16[128,1280]{1,0:T(8,128)(2,1)}, u32[]{:S(2)}) copy-start(bf16[128,1280]{1,0:T(8,128)(2,1)} %copy-done.4) | copy-start | bytes 983044
  42.2 22.0 %copy-start.9 = (bf16[128,1,432]{2,0,1:T(8,128)(2,1)S(1)}, bf16[128,1,432]{2,0,1:T(8,128)(2,1)}, u32[]{:S(2)}) copy-start(bf16[128,1,432]{2,0,1:T(8,128)(2,1)} %copy.23) | copy-start | bytes 331780
  42.3 22.0 %copy-start.14 = (bf16[128,1280]{1,0:T(8,128)(2,1)S(1)}, bf16[128,1280]{1,0:T(8,128)(2,1)}, u32[]{:S(2)}) copy-start(bf16[128,1280]{1,0:T(8,128)(2,1)} %get-tuple-element.15) | copy-start | bytes 983044
  42.3 20.9 %collective-permute-start.13 = (bf16[384,1280]{1,0:T(8,128)(2,1)S(1)}, bf16[384,1280]{1,0:T(8,128)(2,1)S(1)}, u32[]{:S(2)}, u32[]{:S(2)}) collective-permute-start(bf16[384,1280]{1,0:T(8,128)(2,1)S(1)} %pad_maximum_fusion), channel_id=1, source_target_pairs={{0,64},{64,0},{1,65},{65,1},{2,66},{66,2},{3,67},{67,3},{4,68},{68... | collective-permute-start | bytes 2949128 | tf_op jit(solution)/shard_map/ppermute | solution.py:13
  47.8 15.5 %copy-start.7 = (bf16[128,432]{1,0:T(8,128)(2,1)}, bf16[128,432]{1,0:T(8,128)(2,1)S(1)}, u32[]{:S(2)}) copy-start(bf16[128,432]{1,0:T(8,128)(2,1)S(1)} %slice.145) | copy-start | bytes 331780
  47.8 9.7 %collective-permute-start.6 = (bf16[54,2560]{1,0:T(8,128)(2,1)S(1)}, bf16[54,2560]{1,0:T(8,128)(2,1)S(1)}, u32[]{:S(2)}, u32[]{:S(2)}) collective-permute-start(bf16[54,2560]{1,0:T(8,128)(2,1)S(1)} %collective-permute-done.5), channel_id=1, source_target_pairs={{0,2},{2,4},{4,6},{6,8},{8,10},{10,12},{12,14},{14,0},{1,3},{3,5},... | collective-permute-start | bytes 829448 | tf_op jit(solution)/shard_map/ppermute | solution.py:13
  47.9 9.7 %collective-permute-start.10 = (bf16[54,2560]{1,0:T(8,128)(2,1)S(1)}, bf16[54,2560]{1,0:T(8,128)(2,1)S(1)}, u32[]{:S(2)}, u32[]{:S(2)}) collective-permute-start(bf16[54,2560]{1,0:T(8,128)(2,1)S(1)} %collective-permute-done.9), channel_id=1, source_target_pairs={{0,14},{2,0},{4,2},{6,4},{8,6},{10,8},{12,10},{14,12},{1,15},{3,1}... | collective-permute-start | bytes 829448 | tf_op jit(solution)/shard_map/ppermute | solution.py:13
  57.5 5.7 %collective-permute-start.7 = (bf16[54,1280]{1,0:T(8,128)(2,1)S(1)}, bf16[54,1280]{1,0:T(8,128)(2,1)S(1)}, u32[]{:S(2)}, u32[]{:S(2)}) collective-permute-start(bf16[54,1280]{1,0:T(8,128)(2,1)S(1)} %slice.146), channel_id=1, source_target_pairs={{0,2},{2,4},{4,6},{6,8},{8,10},{10,12},{12,14},{14,0},{1,3},{3,5},... | collective-permute-start | bytes 414728 | tf_op jit(solution)/shard_map/ppermute | solution.py:13
  57.6 5.6 %collective-permute-start.11 = (bf16[54,1280]{1,0:T(8,128)(2,1)S(1)}, bf16[54,1280]{1,0:T(8,128)(2,1)S(1)}, u32[]{:S(2)}, u32[]{:S(2)}) collective-permute-start(bf16[54,1280]{1,0:T(8,128)(2,1)S(1)} %slice.147), channel_id=1, source_target_pairs={{0,14},{2,0},{4,2},{6,4},{8,6},{10,8},{12,10},{14,12},{1,15},{3,1}... | collective-permute-start | bytes 414728 | tf_op jit(solution)/shard_map/ppermute | solution.py:13
  63.3 1.0 copy-start.17
  73.6 5.5 %collective-permute-start.19 = (bf16[54,1280]{1,0:T(8,128)(2,1)}, bf16[54,1280]{1,0:T(8,128)(2,1)}, u32[]{:S(2)}, u32[]{:S(2)}) collective-permute-start(bf16[54,1280]{1,0:T(8,128)(2,1)} %get-tuple-element.31), channel_id=1, source_target_pairs={{0,2},{2,4},{4,6},{6,8},{8,10},{10,12},{12,14},{14,0},{1,3},{3,5},... | collective-permute-start | bytes 414728 | tf_op jit(solution)/shard_map/ppermute | solution.py:13
  79.0 6.7 %copy-start.16 = (bf16[54,1280]{1,0:T(8,128)(2,1)S(1)}, bf16[54,1280]{1,0:T(8,128)(2,1)}, u32[]{:S(2)}) copy-start(bf16[54,1280]{1,0:T(8,128)(2,1)} %get-tuple-element.32) | copy-start | bytes 414724
  80.2 8.9 %copy-start = (f32[8,54,2560]{2,1,0:T(8,128)S(1)}, f32[8,54,2560]{2,1,0:T(8,128)}, u32[]{:S(2)}) copy-start(f32[8,54,2560]{2,1,0:T(8,128)} %reshape.30) | copy-start | bytes 13271044
  80.2 9.0 %copy-start.6 = (bf16[128,1280]{1,0:T(8,128)(2,1)S(1)}, bf16[128,1280]{1,0:T(8,128)(2,1)}, u32[]{:S(2)}) copy-start(bf16[128,1280]{1,0:T(8,128)(2,1)} %copy-done.4) | copy-start | bytes 983044
  80.2 9.0 %copy-start.15 = (bf16[128,1280]{1,0:T(8,128)(2,1)S(1)}, bf16[128,1280]{1,0:T(8,128)(2,1)}, u32[]{:S(2)}) copy-start(bf16[128,1280]{1,0:T(8,128)(2,1)} %get-tuple-element.15) | copy-start | bytes 983044
  80.2 9.0 %copy-start.18 = (bf16[384,1280]{1,0:T(8,128)(2,1)S(1)}, bf16[384,1280]{1,0:T(8,128)(2,1)}, u32[]{:S(2)}) copy-start(bf16[384,1280]{1,0:T(8,128)(2,1)} %copy-done.17) | copy-start | bytes 2949124
  80.2 8.9 %collective-permute-start.20 = (bf16[54,2560]{1,0:T(8,128)(2,1)S(1)}, bf16[54,2560]{1,0:T(8,128)(2,1)S(1)}, u32[]{:S(2)}, u32[]{:S(2)}) collective-permute-start(bf16[54,2560]{1,0:T(8,128)(2,1)S(1)} %fusion.17), channel_id=1, source_target_pairs={{0,2},{2,4},{4,6},{6,8},{8,10},{10,12},{12,14},{14,0},{1,3},{3,5},... | collective-permute-start | bytes 829448 | tf_op jit(solution)/shard_map/ppermute | solution.py:13
  82.7 21.7 %collective-permute-start.12 = (bf16[512,1280]{1,0:T(8,128)(2,1)S(1)}, bf16[512,1280]{1,0:T(8,128)(2,1)S(1)}, u32[]{:S(2)}, u32[]{:S(2)}) collective-permute-start(bf16[512,1280]{1,0:T(8,128)(2,1)S(1)} %convolution_convert_fusion), channel_id=1, source_target_pairs={{0,64},{64,0},{1,65},{65,1},{2,66},{66,2},{3,67},{67,3},{4,68},{68... | collective-permute-start | bytes 3932168 | tf_op jit(solution)/shard_map/ppermute | solution.py:13
  85.8 6.7 %collective-permute-start.23 = (bf16[54,1280]{1,0:T(8,128)(2,1)S(1)}, bf16[54,1280]{1,0:T(8,128)(2,1)S(1)}, u32[]{:S(2)}, u32[]{:S(2)}) collective-permute-start(bf16[54,1280]{1,0:T(8,128)(2,1)S(1)} %copy-done.16), channel_id=1, source_target_pairs={{0,14},{2,0},{4,2},{6,4},{8,6},{10,8},{12,10},{14,12},{1,15},{3,1}... | collective-permute-start | bytes 414728 | tf_op jit(solution)/shard_map/ppermute | solution.py:13
  89.1 7.6 %collective-permute-start.21 = (bf16[54,2560]{1,0:T(8,128)(2,1)S(1)}, bf16[54,2560]{1,0:T(8,128)(2,1)S(1)}, u32[]{:S(2)}, u32[]{:S(2)}) collective-permute-start(bf16[54,2560]{1,0:T(8,128)(2,1)S(1)} %fusion.18), channel_id=1, source_target_pairs={{0,2},{2,4},{4,6},{6,8},{8,10},{10,12},{12,14},{14,0},{1,3},{3,5},... | collective-permute-start | bytes 829448 | tf_op jit(solution)/shard_map/ppermute | solution.py:13
  92.4 11.9 %copy-start.1 = (bf16[432,2560]{1,0:T(8,128)(2,1)S(1)}, bf16[432,2560]{1,0:T(8,128)(2,1)}, u32[]{:S(2)}) copy-start(bf16[432,2560]{1,0:T(8,128)(2,1)} %reshape.29) | copy-start | bytes 6635524
  92.4 11.9 %copy-start.8 = (bf16[128,432]{1,0:T(8,128)(2,1)S(1)}, bf16[128,432]{1,0:T(8,128)(2,1)}, u32[]{:S(2)}) copy-start(bf16[128,432]{1,0:T(8,128)(2,1)} %copy-done.7) | copy-start | bytes 331780
  92.5 11.9 %copy-start.10 = (bf16[128,1,432]{2,0,1:T(8,128)(2,1)S(1)}, bf16[128,1,432]{2,0,1:T(8,128)(2,1)}, u32[]{:S(2)}) copy-start(bf16[128,1,432]{2,0,1:T(8,128)(2,1)} %copy.23) | copy-start | bytes 331780
  97.5 5.5 %collective-permute-start.24 = (bf16[54,2560]{1,0:T(8,128)(2,1)S(1)}, bf16[54,2560]{1,0:T(8,128)(2,1)S(1)}, u32[]{:S(2)}, u32[]{:S(2)}) collective-permute-start(bf16[54,2560]{1,0:T(8,128)(2,1)S(1)} %get-tuple-element.7), channel_id=1, source_target_pairs={{0,14},{2,0},{4,2},{6,4},{8,6},{10,8},{12,10},{14,12},{1,15},{3,1}... | collective-permute-start | bytes 829448 | tf_op jit(solution)/shard_map/ppermute | solution.py:13
  97.6 37.5 %collective-permute-start.22 = (bf16[54,2560]{1,0:T(8,128)(2,1)}, bf16[54,2560]{1,0:T(8,128)(2,1)}, u32[]{:S(2)}, u32[]{:S(2)}) collective-permute-start(bf16[54,2560]{1,0:T(8,128)(2,1)} %get-tuple-element.6), channel_id=1, source_target_pairs={{0,2},{2,4},{4,6},{6,8},{8,10},{10,12},{12,14},{14,0},{1,3},{3,5},... | collective-permute-start | bytes 829448 | tf_op jit(solution)/shard_map/ppermute | solution.py:13
  103.1 8.7 %collective-permute-start.25 = (bf16[54,2560]{1,0:T(8,128)(2,1)S(1)}, bf16[54,2560]{1,0:T(8,128)(2,1)S(1)}, u32[]{:S(2)}, u32[]{:S(2)}) collective-permute-start(bf16[54,2560]{1,0:T(8,128)(2,1)S(1)} %fusion.15), channel_id=1, source_target_pairs={{0,14},{2,0},{4,2},{6,4},{8,6},{10,8},{12,10},{14,12},{1,15},{3,1}... | collective-permute-start | bytes 829448 | tf_op jit(solution)/shard_map/ppermute | solution.py:13
  106.8 25.1 %collective-permute-start.15 = (bf16[128,1712]{1,0:T(8,128)(2,1)S(1)}, bf16[128,1712]{1,0:T(8,128)(2,1)S(1)}, u32[]{:S(2)}, u32[]{:S(2)}) collective-permute-start(bf16[128,1712]{1,0:T(8,128)(2,1)S(1)} %pad_maximum_fusion.7), channel_id=1, source_target_pairs={{0,32},{16,48},{32,0},{48,16},{1,33},{17,49},{33,1},{49,17},{2,34}... | collective-permute-start | bytes 1314824 | tf_op jit(solution)/shard_map/ppermute | solution.py:13
  108.7 21.4 %collective-permute-start.16 = (bf16[128,1712]{1,0:T(8,128)(2,1)S(1)}, bf16[128,1712]{1,0:T(8,128)(2,1)S(1)}, u32[]{:S(2)}, u32[]{:S(2)}) collective-permute-start(bf16[128,1712]{1,0:T(8,128)(2,1)S(1)} %pad_maximum_fusion.8), channel_id=1, source_target_pairs={{0,16},{16,32},{32,48},{48,0},{1,17},{17,33},{33,49},{49,1},{2,18}... | collective-permute-start | bytes 1314824 | tf_op jit(solution)/shard_map/ppermute | solution.py:13
  109.0 22.1 %collective-permute-start.14 = (bf16[128,1712]{1,0:T(8,128)(2,1)S(1)}, bf16[128,1712]{1,0:T(8,128)(2,1)}, u32[]{:S(2)}, u32[]{:S(2)}) collective-permute-start(bf16[128,1712]{1,0:T(8,128)(2,1)S(1)} %pad_maximum_fusion.6), channel_id=1, source_target_pairs={{0,48},{16,0},{32,16},{48,32},{1,49},{17,1},{33,17},{49,33},{2,50}... | collective-permute-start | bytes 1314824 | tf_op jit(solution)/shard_map/ppermute | solution.py:13
  112.5 22.6 %collective-permute-start.26 = (bf16[54,2560]{1,0:T(8,128)(2,1)}, bf16[54,2560]{1,0:T(8,128)(2,1)}, u32[]{:S(2)}, u32[]{:S(2)}) collective-permute-start(bf16[54,2560]{1,0:T(8,128)(2,1)} %fusion.16), channel_id=1, source_target_pairs={{0,14},{2,0},{4,2},{6,4},{8,6},{10,8},{12,10},{14,12},{1,15},{3,1}... | collective-permute-start | bytes 829448 | tf_op jit(solution)/shard_map/ppermute | solution.py:13
  130.1 0.8 copy-start.13
  132.0 7.3 %copy-start.2 = (bf16[128,1728]{0,1:T(8,128)(2,1)S(1)}, bf16[128,1728]{0,1:T(8,128)(2,1)}, u32[]{:S(2)}) copy-start(bf16[128,1728]{0,1:T(8,128)(2,1)} %param.5) | copy-start | bytes 1327108
  132.0 7.3 %copy-start.3 = (bf16[128,1728]{0,1:T(8,128)(2,1)S(1)}, bf16[128,1728]{0,1:T(8,128)(2,1)}, u32[]{:S(2)}) copy-start(bf16[128,1728]{0,1:T(8,128)(2,1)} %param.4) | copy-start | bytes 1327108
  133.8 14.3 %collective-permute-start.17 = (bf16[128,1280]{1,0:T(8,128)(2,1)S(1)}, bf16[128,1280]{1,0:T(8,128)(2,1)S(1)}, u32[]{:S(2)}, u32[]{:S(2)}) collective-permute-start(bf16[128,1280]{1,0:T(8,128)(2,1)S(1)} %fusion.13), channel_id=1, source_target_pairs={{0,128},{128,0},{1,129},{129,1},{2,130},{130,2},{3,131},{131,3},{4... | collective-permute-start | bytes 983048 | tf_op jit(solution)/shard_map/ppermute | solution.py:13
  136.6 11.4 %collective-permute-start.27 = (bf16[27,2560]{1,0:T(8,128)(2,1)S(1)}, bf16[27,2560]{1,0:T(8,128)(2,1)S(1)}, u32[]{:S(2)}, u32[]{:S(2)}) collective-permute-start(bf16[27,2560]{1,0:T(8,128)(2,1)S(1)} %select_convert_fusion), channel_id=1, source_target_pairs={{0,1},{1,0},{2,3},{3,2},{4,5},{5,4},{6,7},{7,6},{8,9},{9,8},{10,11... | collective-permute-start | bytes 414728 | tf_op jit(solution)/shard_map/ppermute | solution.py:13
  148.1 3.3 %collective-permute-start.18 = (bf16[128,1280]{1,0:T(8,128)(2,1)S(1)}, bf16[128,1280]{1,0:T(8,128)(2,1)S(1)}, u32[]{:S(2)}, u32[]{:S(2)}) collective-permute-start(bf16[128,1280]{1,0:T(8,128)(2,1)S(1)} %add_convert_fusion), channel_id=1, source_target_pairs={{0,64},{64,0},{1,65},{65,1},{2,66},{66,2},{3,67},{67,3},{4,68},{68... | collective-permute-start | bytes 983048 | tf_op jit(solution)/shard_map/ppermute | solution.py:13

commit v2 on v0

v2 whole, which is shorter than its diff:
```python
import functools

import jax
import jax.numpy as jnp
from jax import lax
from jax.experimental import pallas as pl
from jax.experimental.pallas import tpu as pltpu
from jax.sharding import Mesh, PartitionSpec as P

BF16 = jnp.bfloat16
F32 = jnp.float32
NX, NZ = 4, 8
SLOT = 64
SENT = 56
TILE = 256


def shift(value, axis, steps):
    count = lax.axis_size(axis)
    return lax.ppermute(value, axis, [(i, (i + steps) % count) for i in range(count)])


def after(value, *others):
    return lax.optimization_barrier((value, others))[0]


def call(kernel, outs, *args, scratch=(), limit=24, flops=0, moved=None):
    whole = pl.BlockSpec(memory_space=pltpu.VMEM)
    if moved is None:
        moved = sum(a.size * a.dtype.itemsize for a in args + tuple(outs))
    return pl.pallas_call(
        kernel,
        out_shape=outs,
        in_specs=[whole] * len(args),
        out_specs=[whole] * len(outs),
        scratch_shapes=list(scratch),
        compiler_params=pltpu.CompilerParams(vmem_limit_bytes=limit * 2**20),
        cost_estimate=pl.CostEstimate(flops=flops, bytes_accessed=moved, transcendentals=0),
    )(*args)


def like(shape, dtype=BF16):
    return jax.ShapeDtypeStruct(shape, dtype)


def store_swapped(core, out, value):
    half = value.shape[1] // 2

    @pl.when(core == 0)
    def _():
        out[...] = value

    @pl.when(core != 0)
    def _():
        out[:, :half] = value[:, half:]
        out[:, half:] = value[:, :half]


def pack_weight(mine, other, out):
    rows = mine.shape[0]
    yh = lax.axis_index("yh")
    to = lax.broadcasted_iota(jnp.int32, (SENT, rows), 0)
    row = lax.broadcasted_iota(jnp.int32, (SENT, rows), 1)
    place = jnp.where(to == row + rows * yh, 1.0, 0.0).astype(BF16)
    place_other = jnp.where(to == row + rows * (1 - yh), 1.0, 0.0).astype(BF16)
    both = jnp.dot(place, mine[...], preferred_element_type=F32)
    both = both + jnp.dot(place_other, other[...], preferred_element_type=F32)
    store_swapped(lax.axis_index("core"), out, both.astype(BF16))


def prepare(gate, up, cot, m1, m2, m3, hid_own, cot_own, hidden):
    gate32, up32 = gate[...].astype(F32), up[...].astype(F32)
    units, rows = gate.shape
    half = cot.shape[1] // 2
    used = units // (NX * NZ)
    hidden[:units] = (gate32 * jax.nn.sigmoid(gate32) * up32).astype(BF16).astype(F32)
    inside = lax.broadcasted_iota(jnp.int32, (SLOT, rows), 0) < used
    padded = [
        jnp.where(inside, hidden[used * b : used * b + SLOT], 0.0).astype(BF16)
        for b in range(NX * NZ)
    ]
    for x in range(NX):

        @pl.when(lax.axis_index("x") == x)
        def _(x=x):
            for k, out in enumerate((hid_own, m1, m2, m3)):
                for block in range(NZ):
                    value = padded[(x + k) % NX * NZ + block]
                    if k == 0:
                        out[block * SLOT : (block + 1) * SLOT] = value
                    else:
                        row, column = block * SLOT % rows, half + block * SLOT // rows * rows
                        out[row : row + SLOT, column : column + rows] = value

    core = lax.axis_index("core")
    store_swapped(core, cot_own, cot[...])
    for out in (m1, m2, m3):
        out[:, :half] = cot_own[:, :half]


def stack_halves(g1, g2, g3, out):
    rows, half = g1.shape[0], out.shape[1]
    for k, got in enumerate((g1, g2, g3)):
        out[k * rows : (k + 1) * rows] = got[:, :half]


def add_up(own, h1, h2, h3, out):
    half = own.shape[1]
    total = own[...]
    for got in (h1, h2, h3):
        total = total + got[:, :half].astype(F32)
    out[...] = total.astype(BF16)


def weight_gradient(scale, cot_own, hid_own, g1, g2, g3, far, pieces, to_fwd, to_bwd, cot, hid, hid_t):
    rows, half = cot_own.shape[0], cot_own.shape[1] // 2
    cot[:rows] = cot_own[...]
    hid_t[:, :rows] = hid_own[...]
    for k, got in enumerate((g1, g2, g3)):
        here = slice((k + 1) * rows, (k + 2) * rows)
        cot[here, :half] = got[:, :half]
        cot[here, half:] = far[k * rows : (k + 1) * rows]
        for i in range(NZ * SLOT // rows):
            from_column = half + i * rows
            hid_t[i * rows : (i + 1) * rows, here] = got[:, from_column : from_column + rows]
    z = lax.axis_index("z")

    @pl.loop(0, cot.shape[1] // TILE)
    def _(t):
        columns = pl.ds(pl.multiple_of(t * TILE, TILE), TILE)
        product = jnp.dot(hid_t[...], cot[:, columns], preferred_element_type=F32) * scale
        for block in range(NZ):
            distance = lax.rem(block - z + NZ, NZ)
            pieces[distance, :, columns] = product[block * SLOT : block * SLOT + SENT]

    to_fwd[...] = pieces[4, :, :half].astype(BF16)
    to_bwd[...] = pieces[4, :, half:].astype(BF16)
    hid[...] = hid_t[...].T


def output_other(w0, f1, f2, f3, f4, b4, b3, b2, b1, hid, out, weight):
    z = lax.axis_index("z")
    half = w0.shape[1] // 2
    for distance, piece in enumerate((w0, f1, f2, f3, None, b3, b2, b1)):
        to = lax.rem(z - distance + NZ, NZ)
        if piece is None:
            weight[to, :SENT, :half] = f4[...]
            weight[to, :SENT, half:] = b4[...]
        else:
            weight[to, :SENT] = piece[...]
        weight[to, SENT:] = jnp.zeros((SLOT - SENT, w0.shape[1]), BF16)

    @pl.loop(0, half // TILE)
    def _(t):
        columns = pl.ds(pl.multiple_of(half + t * TILE, TILE), TILE)
        rhs = weight[:, :, columns].reshape(NZ * SLOT, TILE)
        product = jnp.dot(hid[...], rhs, preferred_element_type=F32)
        out[:, pl.ds(pl.multiple_of(t * TILE, TILE), TILE)] = product.astype(BF16)


def output_mine(hid, cot, weight, out, back):
    half = weight.shape[2] // 2

    @pl.loop(0, half // TILE)
    def _(t):
        columns = pl.ds(pl.multiple_of(t * TILE, TILE), TILE)
        rhs = weight[:, :, columns].reshape(NZ * SLOT, TILE)
        out[:, columns] = jnp.dot(hid[...], rhs, preferred_element_type=F32)

    slots = TILE // SLOT

    @pl.loop(0, NZ // slots)
    def _(t):
        some = weight[pl.ds(t * slots, slots)].reshape(TILE, weight.shape[2])
        product = lax.dot_general(
            some, cot[...], (((1,), (1,)), ((), ())), preferred_element_type=F32
        )
        back[pl.ds(pl.multiple_of(t * TILE, TILE), TILE)] = product.astype(BF16)


def pack_output(mine, crossed, back, total, back_own, m1, m2, m3):
    rows, half = total.shape
    total[...] = mine[:rows] + crossed[:rows].astype(F32)
    back_own[...] = back[:, :rows]
    for k, out in enumerate((m1, m2, m3)):
        here = slice((k + 1) * rows, (k + 2) * rows)
        out[:, :half] = (mine[here] + crossed[here].astype(F32)).astype(BF16)
        for i in range(NZ * SLOT // rows):
            to_column = half + i * rows
            out[:, to_column : to_column + rows] = back[i * rows : (i + 1) * rows, here]


def activation_gradients(gate, up, back_own, h1, h2, h3, grad_gate, grad_up, back32):
    units, rows = gate.shape
    half = h1.shape[1] - back_own.shape[0]
    used = units // (NX * NZ)
    for x in range(NX):

        @pl.when(lax.axis_index("x") == x)
        def _(x=x):
            for s in range(NX):
                source = (back_own, h1, h2, h3)[(s - x) % NX]
                for block in range(NZ):
                    row, column = block * SLOT, 0
                    if s != x:
                        row, column = row % rows, half + row // rows * rows
                    value = source[row : row + SLOT, column : column + rows].astype(F32)
                    start = (s * NZ + block) * used
                    back32[start : start + used] = value[:used]

    gate32, up32 = gate[...].astype(F32), up[...].astype(F32)
    sig = jax.nn.sigmoid(gate32)
    grad_gate[...] = (back32[...] * up32 * (sig * (1.0 + gate32 * (1.0 - sig)))).astype(BF16)
    grad_up[...] = (back32[...] * (gate32 * sig)).astype(BF16)


def add_pieces(distance, pieces, fwd, bwd, to_fwd, to_bwd):
    some = fwd.shape[1]
    to_fwd[:, :some] = (pieces[distance, :, :some] + fwd[...].astype(F32)).astype(BF16)
    to_bwd[:, -some:] = (pieces[NZ - distance, :, -some:] + bwd[...].astype(F32)).astype(BF16)
    if some < to_fwd.shape[1]:
        to_fwd[:, some:] = pieces[distance, :, some:].astype(BF16)
        to_bwd[:, :-some] = pieces[NZ - distance, :, :-some].astype(BF16)


def finish_rows(pieces, fwd, bwd, keep, give, total):
    rows, half = keep.shape[0], keep.shape[1] // 2
    core, yh = lax.axis_index("core"), lax.axis_index("yh")
    store_swapped(core, total, pieces[0] + (fwd[...].astype(F32) + bwd[...].astype(F32)))

    @pl.when(yh == 0)
    def _():
        keep[...] = total[:rows]
        give[...] = total[rows : 2 * rows].astype(BF16)

    @pl.when(yh != 0)
    def _():
        keep[...] = total[rows : 2 * rows]
        give[...] = total[:rows].astype(BF16)


def place_output(mine, other, out):
    half = mine.shape[1]

    @pl.when(lax.axis_index("core") == 0)
    def _():
        out[:, :half] = mine[...]
        out[:, half:] = other[...]

    @pl.when(lax.axis_index("core") != 0)
    def _():
        out[:, :half] = other[...]
        out[:, half:] = mine[...]


def body(gate_pre, up_pre, down_weight, cotangent):
    gate, up = gate_pre.T, up_pre.T
    units, rows = gate.shape
    block, width = down_weight.shape
    half = width // 2
    slots = NZ * SLOT
    tokens = NX * rows
    wide = half + slots

    w_other = shift(down_weight, "yh", 1)
    m1, m2, m3, hid_own, cot_own = call(
        prepare,
        [like((rows, wide))] * 3 + [like((slots, rows)), like((rows, width))],
        gate, up, cotangent,
        scratch=[pltpu.VMEM((units + SLOT, rows), F32)],
    )
    w_other = after(w_other, m1, m2, m3)
    (w0,) = call(pack_weight, [like((SENT, width))], down_weight, w_other)
    got = [shift(m, "x", k) for k, m in ((1, m1), (2, m2), (3, m3))]

    (near,) = call(stack_halves, [like(((NX - 1) * rows, half))], *got, flops=2 * 10**9)

    fwd, bwd = [w0], [w0]
    for step in range(3):
        f, b = shift(fwd[-1], "z", 1), shift(bwd[-1], "z", -1)
        if step == 1:
            f, b, near = lax.optimization_barrier((f, b, near))
        else:
            f, b = lax.optimization_barrier((f, b))
        fwd.append(f)
        bwd.append(b)
    far = shift(near, "core", 1)
    scale = float(tokens * NZ * 2) ** (-0.5)
    pieces, to_fwd, to_bwd, cot, hid = call(
        functools.partial(weight_gradient, scale),
        [like((NZ, SENT, width), F32)] + [like((SENT, half))] * 2 + [like((tokens, width)), like((tokens, slots))],
        cot_own, hid_own, *got, far,
        scratch=[pltpu.VMEM((slots, tokens), BF16)],
        flops=2 * slots * tokens * width,
    )

    def added(distance, ring):
        kernel = functools.partial(add_pieces, distance)
        return call(kernel, [like((SENT, width))] * 2, pieces, *ring, moved=0)

    to_fwd, to_bwd = after((to_fwd, to_bwd), fwd[3], bwd[3])
    f4, b4 = shift(fwd[3][:, :half], "z", 1), shift(bwd[3][:, half:], "z", -1)
    ring = (shift(to_fwd, "z", 1), shift(to_bwd, "z", -1))
    f4, b4, ring = lax.optimization_barrier((f4, b4, ring))
    to_fwd, to_bwd = added(3, ring)
    ring = (shift(to_fwd, "z", 1), shift(to_bwd, "z", -1))

    f4, b4 = after((f4, b4), to_fwd, to_bwd)
    out_other, weight = call(
        output_other,
        [like((tokens, half)), like((NZ, SLOT, width))],
        *fwd, f4, b4, *reversed(bwd[1:]), hid,
        flops=2 * slots * tokens * half,
    )
    crossed = shift(out_other, "core", 1)
    out_mine, back = call(
        output_mine,
        [like((tokens, half), F32), like((slots, tokens))],
        hid, cot, weight,
        flops=6 * slots * tokens * half,
    )
    crossed = after(crossed, back)
    total, back_own, m1, m2, m3 = call(
        pack_output,
        [like((rows, half), F32), like((slots, rows))] + [like((rows, wide))] * 3,
        out_mine, crossed, back,
    )
    got_back = [shift(m, "x", -k) for k, m in ((1, m1), (2, m2), (3, m3))]
    ring = after(ring, m1, m2, m3)
    to_fwd, to_bwd = added(2, ring)
    ring = lax.optimization_barrier((shift(to_fwd, "z", 1), shift(to_bwd, "z", -1)))
    to_fwd, to_bwd = added(1, ring)
    got_back = after(got_back, to_fwd, to_bwd)
    ring = (shift(to_fwd, "z", 1), shift(to_bwd, "z", -1))
    (rounded,) = call(add_up, [like((rows, half))], total, *got_back, moved=0)
    across = shift(rounded, "yl", 1)
    ring = after(ring, rounded)
    keep, give = call(
        finish_rows,
        [like((block, width), F32), like((block, width))],
        pieces, *ring,
        scratch=[pltpu.VMEM((SENT, width), F32)],
    )
    taken = shift(give, "yh", 1)
    got_back = after(got_back, give)
    grad_gate, grad_up = call(
        activation_gradients,
        [like((units, rows))] * 2,
        gate, up, back_own, *got_back,
        scratch=[pltpu.VMEM((units, rows), F32)],
        flops=15 * 10**8,
    )
    across = after(across, give)
    out_half = (rounded.astype(F32) + across.astype(F32)).astype(BF16)
    (output,) = call(place_output, [like((rows, width))], out_half, shift(out_half, "core", 1))
    grad_weight = keep + taken.astype(F32)
    return output, grad_weight, grad_gate.T, grad_up.T


def solution(mesh):
    fine = Mesh(mesh.devices.reshape(2, 2, NX, NZ, 2), ("yl", "core", "x", "z", "yh"))
    blk, dp = ("x", "z", "yh"), ("yl", "core")
    return jax.shard_map(
        body,
        mesh=fine,
        in_specs=(P(blk, dp), P(blk, dp), P(dp + blk, None), P(blk, None)),
        out_specs=(P(blk, None), P(dp + blk, None), P(blk, dp), P(blk, dp)),
        check_vma=False,
    )
```

time: 1120 us -> 110 us (0.10)
  the two profiles are of different devices: /device:TPU:8 before, /device:TPU:1 now
where the time goes in v2:
time: 110 us; the launch traced here: 109 us
  starting transfers between devices  47.4 us (43%)
  waiting for transfers between devices  43.6 us (40%)
  Pallas kernels  12.7 us (12%)
  local copies, waits for them, and re-layouts  4.06 us (4%)
    ppermute x28, starting transfers between devices, shift(): lax.ppermute(value, axis, [(i, (i + steps) % count) for i in range(count)])  47.4 us
    ppermute x28, waiting for transfers between devices, shift(): lax.ppermute(value, axis, [(i, (i + steps) % count) for i in range(count)])  43.6 us
    pallas_call x14, Pallas kernels, call(): pl.pallas_call(kernel, out_shape=outs, in_specs=[whole] * len(args), out_...  12.7 us
    unnamed x12, local copies, waits for them, and re-layouts  4.04 us
  transfers between devices with their start and end apart: 28, of which 11 were waited for; matrix products, arithmetic and copies ran while one was open for 1% of the time, Pallas kernels for 9%

profile of v2, /device:TPU:1, one launch (start us, length us, event | category | flops | bytes accessed | tf_op | source)
XLA Modules:
  0.0 109.3 jit_solution(14513030656727309280)
XLA Ops:
  0.6 3.8 %collective-permute-start.3 = (bf16[27,2560]{1,0:T(8,128)(2,1)}, bf16[27,2560]{1,0:T(8,128)(2,1)S(1)}, u32[]{:S(2)}, u32[]{:S(2)}) collective-permute-start(bf16[27,2560]{1,0:T(8,128)(2,1)} %mine.1), channel_id=1, source_target_pairs={{0,1},{1,0},{2,3},{3,2},{4,5},{5,4},{6,7},{7,6},{8,9},{9,8},{10,11... | collective-permute-start | bytes 414728 | tf_op jit(solution)/shard_map/ppermute | solution.py:20
  4.5 1.1 copy-done
  5.6 1.0 copy-done.1
  6.6 1.0 copy-done.3
  7.6 0.6 shard_map.75
  8.2 1.3 %collective-permute-start = (bf16[128,1792]{1,0:T(8,128)(2,1)S(1)}, bf16[128,1792]{1,0:T(8,128)(2,1)S(1)}, u32[]{:S(2)}, u32[]{:S(2)}) collective-permute-start(bf16[128,1792]{1,0:T(8,128)(2,1)S(1)} %get-tuple-element.65), channel_id=1, source_target_pairs={{0,16},{16,32},{32,48},{48,0},{1,17},{17,33},{33,49},{49,1},{2,18}... | collective-permute-start | bytes 1376264 | tf_op jit(solution)/shard_map/ppermute | solution.py:20
  9.5 2.5 %collective-permute-start.1 = (bf16[128,1792]{1,0:T(8,128)(2,1)S(1)}, bf16[128,1792]{1,0:T(8,128)(2,1)S(1)}, u32[]{:S(2)}, u32[]{:S(2)}) collective-permute-start(bf16[128,1792]{1,0:T(8,128)(2,1)S(1)} %get-tuple-element.66), channel_id=1, source_target_pairs={{0,32},{16,48},{32,0},{48,16},{1,33},{17,49},{33,1},{49,17},{2,34}... | collective-permute-start | bytes 1376264 | tf_op jit(solution)/shard_map/ppermute | solution.py:20
  12.0 1.2 %collective-permute-start.2 = (bf16[128,1792]{1,0:T(8,128)(2,1)S(1)}, bf16[128,1792]{1,0:T(8,128)(2,1)S(1)}, u32[]{:S(2)}, u32[]{:S(2)}) collective-permute-start(bf16[128,1792]{1,0:T(8,128)(2,1)S(1)} %get-tuple-element.67), channel_id=1, source_target_pairs={{0,48},{16,0},{32,16},{48,32},{1,49},{17,1},{33,17},{49,33},{2,50}... | collective-permute-start | bytes 1376264 | tf_op jit(solution)/shard_map/ppermute | solution.py:20
  13.1 0.0 collective-permute-done.3.other
  13.1 0.9 copy-done.5
  14.0 0.3 shard_map.76.w0
  14.4 5.7 %collective-permute-start.5 = (bf16[56,2560]{1,0:T(8,128)(2,1)S(1)}, bf16[56,2560]{1,0:T(8,128)(2,1)S(1)}, u32[]{:S(2)}, u32[]{:S(2)}) collective-permute-start(bf16[56,2560]{1,0:T(8,128)(2,1)S(1)} %shard_map.76.w0), channel_id=1, source_target_pairs={{0,14},{2,0},{4,2},{6,4},{8,6},{10,8},{12,10},{14,12},{1,15},{3,1}... | collective-permute-start | bytes 860168 | tf_op jit(solution)/shard_map/ppermute | solution.py:20
  20.0 4.3 %collective-permute-done.5.b1 = bf16[56,2560]{1,0:T(8,128)(2,1)S(1)} collective-permute-done((bf16[56,2560]{1,0:T(8,128)(2,1)S(1)}, bf16[56,2560]{1,0:T(8,128)(2,1)S(1)}, u32[]{:S(2)}, u32[]{:S(2)}) %collective-permute-start.5) | collective-permute-done | bytes 286752 | tf_op jit(solution)/shard_map/ppermute | solution.py:20
  24.3 3.1 %collective-permute-done.4.f1 = bf16[56,2560]{1,0:T(8,128)(2,1)S(1)} collective-permute-done((bf16[56,2560]{1,0:T(8,128)(2,1)S(1)}, bf16[56,2560]{1,0:T(8,128)(2,1)S(1)}, u32[]{:S(2)}, u32[]{:S(2)}) %collective-permute-start.4) | collective-permute-done | bytes 286752 | tf_op jit(solution)/shard_map/ppermute | solution.py:20
  27.5 0.0 collective-permute-start.6
  27.5 2.7 %collective-permute-start.7 = (bf16[56,2560]{1,0:T(8,128)(2,1)S(1)}, bf16[56,2560]{1,0:T(8,128)(2,1)S(1)}, u32[]{:S(2)}, u32[]{:S(2)}) collective-permute-start(bf16[56,2560]{1,0:T(8,128)(2,1)S(1)} %collective-permute-done.5.b1), channel_id=1, source_target_pairs={{0,14},{2,0},{4,2},{6,4},{8,6},{10,8},{12,10},{14,12},{1,15},{3,1}... | collective-permute-start | bytes 860168 | tf_op jit(solution)/shard_map/ppermute | solution.py:20
  30.1 0.0 collective-permute-done.g1
  30.1 1.2 %collective-permute-done.1.g2 = bf16[128,1792]{1,0:T(8,128)(2,1)S(1)} collective-permute-done((bf16[128,1792]{1,0:T(8,128)(2,1)S(1)}, bf16[128,1792]{1,0:T(8,128)(2,1)S(1)}, u32[]{:S(2)}, u32[]{:S(2)}) %collective-permute-start.1) | collective-permute-done | bytes 458784 | tf_op jit(solution)/shard_map/ppermute | solution.py:20
  31.4 0.1 shard_map.77
  31.5 2.7 %collective-permute-done.6.f2 = bf16[56,2560]{1,0:T(8,128)(2,1)S(1)} collective-permute-done((bf16[56,2560]{1,0:T(8,128)(2,1)S(1)}, bf16[56,2560]{1,0:T(8,128)(2,1)S(1)}, u32[]{:S(2)}, u32[]{:S(2)}) %collective-permute-start.6) | collective-permute-done | bytes 286752 | tf_op jit(solution)/shard_map/ppermute | solution.py:20
  34.2 0.0 collective-permute-done.7.b2
  34.2 4.2 %collective-permute-start.8 = (bf16[384,1280]{1,0:T(8,128)(2,1)S(1)}, bf16[384,1280]{1,0:T(8,128)(2,1)S(1)}, u32[]{:S(2)}, u32[]{:S(2)}) collective-permute-start(bf16[384,1280]{1,0:T(8,128)(2,1)S(1)} %shard_map.77), channel_id=1, source_target_pairs={{0,64},{64,0},{1,65},{65,1},{2,66},{66,2},{3,67},{67,3},{4,68},{68... | collective-permute-start | bytes 2949128 | tf_op jit(solution)/shard_map/ppermute | solution.py:20
  38.3 3.0 %collective-permute-start.10 = (bf16[56,2560]{1,0:T(8,128)(2,1)S(1)}, bf16[56,2560]{1,0:T(8,128)(2,1)S(1)}, u32[]{:S(2)}, u32[]{:S(2)}) collective-permute-start(bf16[56,2560]{1,0:T(8,128)(2,1)S(1)} %collective-permute-done.7.b2), channel_id=1, source_target_pairs={{0,14},{2,0},{4,2},{6,4},{8,6},{10,8},{12,10},{14,12},{1,15},{3,1}... | collective-permute-start | bytes 860168 | tf_op jit(solution)/shard_map/ppermute | solution.py:20
  41.3 7.2 %collective-permute-done.9.f3 = bf16[56,2560]{1,0:T(8,128)(2,1)S(1)} collective-permute-done((bf16[56,2560]{1,0:T(8,128)(2,1)S(1)}, bf16[56,2560]{1,0:T(8,128)(2,1)S(1)}, u32[]{:S(2)}, u32[]{:S(2)}) %collective-permute-start.9) | collective-permute-done | bytes 286752 | tf_op jit(solution)/shard_map/ppermute | solution.py:20
  48.5 2.5 %collective-permute-start.12 = (bf16[56,1280]{1,0:T(8,128)(2,1)S(1)}, bf16[56,1280]{1,0:T(8,128)(2,1)S(1)}, u32[]{:S(2)}, u32[]{:S(2)}) collective-permute-start(bf16[56,1280]{1,0:T(8,128)(2,1)S(1)} %slice.7), channel_id=1, source_target_pairs={{0,14},{2,0},{4,2},{6,4},{8,6},{10,8},{12,10},{14,12},{1,15},{3,1}... | collective-permute-start | bytes 430088 | tf_op jit(solution)/shard_map/ppermute | solution.py:20
  51.1 0.0 collective-permute-done.8.far
  51.1 3.4 %shard_map.78 = (f32[8,56,2560]{2,1,0:T(8,128)S(1)}, bf16[56,1280]{1,0:T(8,128)(2,1)S(1)}, bf16[56,1280]{1,0:T(8,128)(2,1)S(1)}, bf16[512,2560]{1,0:T(8,128)(2,1)S(1)}, bf16[512,512]{1,0:T(8,128)(2,1)S(1)}) custom-call(bf16[128,2560]{1,0:T(8,128)(2,1)S(1)} %get-tuple-element.63.cot_own, bf16[512,128]{1,0:T(8,128)(2,1)S(1)} %get-tuple-element.64.hid_own, ...), custom_call_target="tpu_custom_call" | custom-call | flops 1342177280 | bytes 11165696 | tf_op jit(solution)/shard_map/pallas_call | solution.py:31
  54.5 0.1 collective-permute-start.13
  54.6 2.9 %collective-permute-start.14 = (bf16[56,1280]{1,0:T(8,128)(2,1)S(1)}, bf16[56,1280]{1,0:T(8,128)(2,1)S(1)}, u32[]{:S(2)}, u32[]{:S(2)}) collective-permute-start(bf16[56,1280]{1,0:T(8,128)(2,1)S(1)} %get-tuple-element.81), channel_id=1, source_target_pairs={{0,14},{2,0},{4,2},{6,4},{8,6},{10,8},{12,10},{14,12},{1,15},{3,1}... | collective-permute-start | bytes 430088 | tf_op jit(solution)/shard_map/ppermute | solution.py:20
  57.5 2.2 %collective-permute-done.13.fwd = bf16[56,1280]{1,0:T(8,128)(2,1)S(1)} collective-permute-done((bf16[56,1280]{1,0:T(8,128)(2,1)S(1)}, bf16[56,1280]{1,0:T(8,128)(2,1)S(1)}, u32[]{:S(2)}, u32[]{:S(2)}) %collective-permute-start.13) | collective-permute-done | bytes 143392 | tf_op jit(solution)/shard_map/ppermute | solution.py:20
  59.7 0.1 shard_map.79
  59.8 1.7 %shard_map.80 = (bf16[512,1280]{1,0:T(8,128)(2,1)S(1)}, bf16[8,64,2560]{2,1,0:T(8,128)(2,1)S(1)}) custom-call(bf16[56,2560]{1,0:T(8,128)(2,1)S(1)} %shard_map.76.w0, bf16[56,2560]{1,0:T(8,128)(2,1)S(1)} %collective-permute-done.4.f1, bf16[56,2560]{1,0:T(8,128)(2,1)S(1)} %collective-permute-done.6.f2, bf16[56,2560]{1,0:T(8,128)(2,1)S(1)} %collective-permute-done.9.f3, ...), custom_call_target="tpu_custom_call" | custom-call | flops 671088640 | bytes 6750208 | tf_op jit(solution)/shard_map/pallas_call | solution.py:31
  61.5 2.3 %collective-permute-start.15 = (bf16[512,1280]{1,0:T(8,128)(2,1)S(1)}, bf16[512,1280]{1,0:T(8,128)(2,1)S(1)}, u32[]{:S(2)}, u32[]{:S(2)}) collective-permute-start(bf16[512,1280]{1,0:T(8,128)(2,1)S(1)} %get-tuple-element.93), channel_id=1, source_target_pairs={{0,64},{64,0},{1,65},{65,1},{2,66},{66,2},{3,67},{67,3},{4,68},{68... | collective-permute-start | bytes 3932168 | tf_op jit(solution)/shard_map/ppermute | solution.py:20
  63.9 0.2 collective-permute-start.19
  64.1 3.0 %collective-permute-start.20 = (bf16[56,2560]{1,0:T(8,128)(2,1)S(1)}, bf16[56,2560]{1,0:T(8,128)(2,1)S(1)}, u32[]{:S(2)}, u32[]{:S(2)}) collective-permute-start(bf16[56,2560]{1,0:T(8,128)(2,1)S(1)} %get-tuple-element.88), channel_id=1, source_target_pairs={{0,14},{2,0},{4,2},{6,4},{8,6},{10,8},{12,10},{14,12},{1,15},{3,1}... | collective-permute-start | bytes 860168 | tf_op jit(solution)/shard_map/ppermute | solution.py:20
  67.1 3.2 %shard_map.81 = (f32[512,1280]{1,0:T(8,128)S(1)}, bf16[512,512]{1,0:T(8,128)(2,1)S(1)}) custom-call(bf16[512,512]{1,0:T(8,128)(2,1)S(1)} %get-tuple-element.72.hid, bf16[512,2560]{1,0:T(8,128)(2,1)S(1)} %get-tuple-element.73.cot, bf16[8,64,2560]{2,1,0:T(8,128)(2,1)S(1)} %get-tuple-element.91.weight), custom_call_target="tpu_custom_call" | custom-call | flops 2013265920 | bytes 8912896 | tf_op jit(solution)/shard_map/pallas_call | solution.py:31
  70.3 0.0 collective-permute-done.15.crossed
  70.3 0.4 shard_map.82
  70.7 0.1 collective-permute-start.16
  70.8 2.1 %collective-permute-start.17 = (bf16[128,1792]{1,0:T(8,128)(2,1)S(1)}, bf16[128,1792]{1,0:T(8,128)(2,1)S(1)}, u32[]{:S(2)}, u32[]{:S(2)}) collective-permute-start(bf16[128,1792]{1,0:T(8,128)(2,1)S(1)} %get-tuple-element.98), channel_id=1, source_target_pairs={{0,32},{16,48},{32,0},{48,16},{1,33},{17,49},{33,1},{49,17},{2,34}... | collective-permute-start | bytes 1376264 | tf_op jit(solution)/shard_map/ppermute | solution.py:20
  72.9 0.0 collective-permute-start.18
  72.9 1.3 %collective-permute-done.19.fwd = bf16[56,2560]{1,0:T(8,128)(2,1)S(1)} collective-permute-done((bf16[56,2560]{1,0:T(8,128)(2,1)S(1)}, bf16[56,2560]{1,0:T(8,128)(2,1)S(1)}, u32[]{:S(2)}, u32[]{:S(2)}) %collective-permute-start.19) | collective-permute-done | bytes 286752 | tf_op jit(solution)/shard_map/ppermute | solution.py:20
  74.2 0.0 collective-permute-done.20.bwd
  74.2 0.1 shard_map.83
  74.3 0.1 collective-permute-start.21
  74.4 2.7 %collective-permute-start.22 = (bf16[56,2560]{1,0:T(8,128)(2,1)S(1)}, bf16[56,2560]{1,0:T(8,128)(2,1)S(1)}, u32[]{:S(2)}, u32[]{:S(2)}) collective-permute-start(bf16[56,2560]{1,0:T(8,128)(2,1)S(1)} %get-tuple-element.103), channel_id=1, source_target_pairs={{0,14},{2,0},{4,2},{6,4},{8,6},{10,8},{12,10},{14,12},{1,15},{3,1}... | collective-permute-start | bytes 860168 | tf_op jit(solution)/shard_map/ppermute | solution.py:20
  77.1 6.2 %collective-permute-done.21.fwd = bf16[56,2560]{1,0:T(8,128)(2,1)S(1)} collective-permute-done((bf16[56,2560]{1,0:T(8,128)(2,1)S(1)}, bf16[56,2560]{1,0:T(8,128)(2,1)S(1)}, u32[]{:S(2)}, u32[]{:S(2)}) %collective-permute-start.21) | collective-permute-done | bytes 286752 | tf_op jit(solution)/shard_map/ppermute | solution.py:20
  83.3 0.1 shard_map.84
  83.4 0.1 collective-permute-start.24
  83.5 2.7 %collective-permute-start.25 = (bf16[56,2560]{1,0:T(8,128)(2,1)S(1)}, bf16[56,2560]{1,0:T(8,128)(2,1)S(1)}, u32[]{:S(2)}, u32[]{:S(2)}) collective-permute-start(bf16[56,2560]{1,0:T(8,128)(2,1)S(1)} %get-tuple-element.107), channel_id=1, source_target_pairs={{0,14},{2,0},{4,2},{6,4},{8,6},{10,8},{12,10},{14,12},{1,15},{3,1}... | collective-permute-start | bytes 860168 | tf_op jit(solution)/shard_map/ppermute | solution.py:20
  86.2 8.5 %collective-permute-done.18.h3 = bf16[128,1792]{1,0:T(8,128)(2,1)S(1)} collective-permute-done((bf16[128,1792]{1,0:T(8,128)(2,1)S(1)}, bf16[128,1792]{1,0:T(8,128)(2,1)S(1)}, u32[]{:S(2)}, u32[]{:S(2)}) %collective-permute-start.18) | collective-permute-done | bytes 458784 | tf_op jit(solution)/shard_map/ppermute | solution.py:20
  94.7 0.1 shard_map.85
  94.8 0.0 copy-start.2
  94.8 0.0 copy-start.4
  94.8 0.5 collective-permute-start.23
  95.3 0.3 shard_map.86
  95.6 1.6 %collective-permute-start.27 = (bf16[27,2560]{1,0:T(8,128)(2,1)S(1)}, bf16[27,2560]{1,0:T(8,128)(2,1)S(1)}, u32[]{:S(2)}, u32[]{:S(2)}) collective-permute-start(bf16[27,2560]{1,0:T(8,128)(2,1)S(1)} %get-tuple-element.113), channel_id=1, source_target_pairs={{0,1},{1,0},{2,3},{3,2},{4,5},{5,4},{6,7},{7,6},{8,9},{9,8},{10,11... | collective-permute-start | bytes 414728 | tf_op jit(solution)/shard_map/ppermute | solution.py:20
  97.2 1.3 %shard_map.88 = (bf16[1728,128]{1,0:T(8,128)(2,1)}, bf16[1728,128]{1,0:T(8,128)(2,1)}) custom-call(bf16[1728,128]{1,0:T(8,128)(2,1)S(1)} %bitcast.5, bf16[1728,128]{1,0:T(8,128)(2,1)S(1)} %bitcast.7, bf16[512,128]{1,0:T(8,128)(2,1)S(1)} %get-tuple-element.116.back_own, bf16[128,1792]{1,0:T(8,128)(2,1)S(1)} %collective-permute-done.16.h1, ...), custom_call_target="tpu_custom_call" | custom-call | flops 1500000000 | bytes 3276800 | tf_op jit(solution)/shard_map/pallas_call | solution.py:31
  98.5 5.2 %collective-permute-done.23 = bf16[128,1280]{1,0:T(8,128)(2,1)S(1)} collective-permute-done((bf16[128,1280]{1,0:T(8,128)(2,1)S(1)}, bf16[128,1280]{1,0:T(8,128)(2,1)S(1)}, u32[]{:S(2)}, u32[]{:S(2)}) %collective-permute-start.23) | collective-permute-done | bytes 327712 | tf_op jit(solution)/shard_map/ppermute | solution.py:20
  103.7 0.1 add_convert_fusion.mine
  103.8 2.4 %collective-permute-start.26 = (bf16[128,1280]{1,0:T(8,128)(2,1)S(1)}, bf16[128,1280]{1,0:T(8,128)(2,1)S(1)}, u32[]{:S(2)}, u32[]{:S(2)}) collective-permute-start(bf16[128,1280]{1,0:T(8,128)(2,1)S(1)} %add_convert_fusion.mine), channel_id=1, source_target_pairs={{0,64},{64,0},{1,65},{65,1},{2,66},{66,2},{3,67},{67,3},{4,68},{68... | collective-permute-start | bytes 983048 | tf_op jit(solution)/shard_map/ppermute | solution.py:20
  106.1 1.6 %collective-permute-done.27 = bf16[27,2560]{1,0:T(8,128)(2,1)S(1)} collective-permute-done((bf16[27,2560]{1,0:T(8,128)(2,1)S(1)}, bf16[27,2560]{1,0:T(8,128)(2,1)S(1)}, u32[]{:S(2)}, u32[]{:S(2)}) %collective-permute-start.27) | collective-permute-done | bytes 138272 | tf_op jit(solution)/shard_map/ppermute | solution.py:20
  107.7 0.8 convert_add_fusion
  108.5 0.9 shard_map.87
  (22 shorter events, 0.1 us)
Async XLA Ops:
  0.6 12.5 %collective-permute-start.3 = (bf16[27,2560]{1,0:T(8,128)(2,1)}, bf16[27,2560]{1,0:T(8,128)(2,1)S(1)}, u32[]{:S(2)}, u32[]{:S(2)}) collective-permute-start(bf16[27,2560]{1,0:T(8,128)(2,1)} %mine.1), channel_id=1, source_target_pairs={{0,1},{1,0},{2,3},{3,2},{4,5},{5,4},{6,7},{7,6},{8,9},{9,8},{10,11... | collective-permute-start | bytes 414728 | tf_op jit(solution)/shard_map/ppermute | solution.py:20
  4.5 1.1 copy-start
  5.5 1.0 copy-start.1
  6.6 1.0 copy-start.3
  8.2 21.9 %collective-permute-start = (bf16[128,1792]{1,0:T(8,128)(2,1)S(1)}, bf16[128,1792]{1,0:T(8,128)(2,1)S(1)}, u32[]{:S(2)}, u32[]{:S(2)}) collective-permute-start(bf16[128,1792]{1,0:T(8,128)(2,1)S(1)} %get-tuple-element.65), channel_id=1, source_target_pairs={{0,16},{16,32},{32,48},{48,0},{1,17},{17,33},{33,49},{49,1},{2,18}... | collective-permute-start | bytes 1376264 | tf_op jit(solution)/shard_map/ppermute | solution.py:20
  9.5 21.9 %collective-permute-start.1 = (bf16[128,1792]{1,0:T(8,128)(2,1)S(1)}, bf16[128,1792]{1,0:T(8,128)(2,1)S(1)}, u32[]{:S(2)}, u32[]{:S(2)}) collective-permute-start(bf16[128,1792]{1,0:T(8,128)(2,1)S(1)} %get-tuple-element.66), channel_id=1, source_target_pairs={{0,32},{16,48},{32,0},{48,16},{1,33},{17,49},{33,1},{49,17},{2,34}... | collective-permute-start | bytes 1376264 | tf_op jit(solution)/shard_map/ppermute | solution.py:20
  12.0 19.4 %collective-permute-start.2 = (bf16[128,1792]{1,0:T(8,128)(2,1)S(1)}, bf16[128,1792]{1,0:T(8,128)(2,1)S(1)}, u32[]{:S(2)}, u32[]{:S(2)}) collective-permute-start(bf16[128,1792]{1,0:T(8,128)(2,1)S(1)} %get-tuple-element.67), channel_id=1, source_target_pairs={{0,48},{16,0},{32,16},{48,32},{1,49},{17,1},{33,17},{49,33},{2,50}... | collective-permute-start | bytes 1376264 | tf_op jit(solution)/shard_map/ppermute | solution.py:20
  13.1 0.9 copy-start.5
  14.4 10.0 %collective-permute-start.5 = (bf16[56,2560]{1,0:T(8,128)(2,1)S(1)}, bf16[56,2560]{1,0:T(8,128)(2,1)S(1)}, u32[]{:S(2)}, u32[]{:S(2)}) collective-permute-start(bf16[56,2560]{1,0:T(8,128)(2,1)S(1)} %shard_map.76.w0), channel_id=1, source_target_pairs={{0,14},{2,0},{4,2},{6,4},{8,6},{10,8},{12,10},{14,12},{1,15},{3,1}... | collective-permute-start | bytes 860168 | tf_op jit(solution)/shard_map/ppermute | solution.py:20
  20.0 7.4 %collective-permute-start.4 = (bf16[56,2560]{1,0:T(8,128)(2,1)S(1)}, bf16[56,2560]{1,0:T(8,128)(2,1)S(1)}, u32[]{:S(2)}, u32[]{:S(2)}) collective-permute-start(bf16[56,2560]{1,0:T(8,128)(2,1)S(1)} %shard_map.76.w0), channel_id=1, source_target_pairs={{0,2},{2,4},{4,6},{6,8},{8,10},{10,12},{12,14},{14,0},{1,3},{3,5},... | collective-permute-start | bytes 860168 | tf_op jit(solution)/shard_map/ppermute | solution.py:20
  27.5 6.7 %collective-permute-start.6 = (bf16[56,2560]{1,0:T(8,128)(2,1)S(1)}, bf16[56,2560]{1,0:T(8,128)(2,1)S(1)}, u32[]{:S(2)}, u32[]{:S(2)}) collective-permute-start(bf16[56,2560]{1,0:T(8,128)(2,1)S(1)} %collective-permute-done.4.f1), channel_id=1, source_target_pairs={{0,2},{2,4},{4,6},{6,8},{8,10},{10,12},{12,14},{14,0},{1,3},{3,5},... | collective-permute-start | bytes 860168 | tf_op jit(solution)/shard_map/ppermute | solution.py:20
  27.5 6.7 %collective-permute-start.7 = (bf16[56,2560]{1,0:T(8,128)(2,1)S(1)}, bf16[56,2560]{1,0:T(8,128)(2,1)S(1)}, u32[]{:S(2)}, u32[]{:S(2)}) collective-permute-start(bf16[56,2560]{1,0:T(8,128)(2,1)S(1)} %collective-permute-done.5.b1), channel_id=1, source_target_pairs={{0,14},{2,0},{4,2},{6,4},{8,6},{10,8},{12,10},{14,12},{1,15},{3,1}... | collective-permute-start | bytes 860168 | tf_op jit(solution)/shard_map/ppermute | solution.py:20
  34.2 16.9 %collective-permute-start.8 = (bf16[384,1280]{1,0:T(8,128)(2,1)S(1)}, bf16[384,1280]{1,0:T(8,128)(2,1)S(1)}, u32[]{:S(2)}, u32[]{:S(2)}) collective-permute-start(bf16[384,1280]{1,0:T(8,128)(2,1)S(1)} %shard_map.77), channel_id=1, source_target_pairs={{0,64},{64,0},{1,65},{65,1},{2,66},{66,2},{3,67},{67,3},{4,68},{68... | collective-permute-start | bytes 2949128 | tf_op jit(solution)/shard_map/ppermute | solution.py:20
  38.3 10.2 %collective-permute-start.9 = (bf16[56,2560]{1,0:T(8,128)(2,1)S(1)}, bf16[56,2560]{1,0:T(8,128)(2,1)S(1)}, u32[]{:S(2)}, u32[]{:S(2)}) collective-permute-start(bf16[56,2560]{1,0:T(8,128)(2,1)S(1)} %collective-permute-done.6.f2), channel_id=1, source_target_pairs={{0,2},{2,4},{4,6},{6,8},{8,10},{10,12},{12,14},{14,0},{1,3},{3,5},... | collective-permute-start | bytes 860168 | tf_op jit(solution)/shard_map/ppermute | solution.py:20
  38.3 10.2 %collective-permute-start.10 = (bf16[56,2560]{1,0:T(8,128)(2,1)S(1)}, bf16[56,2560]{1,0:T(8,128)(2,1)S(1)}, u32[]{:S(2)}, u32[]{:S(2)}) collective-permute-start(bf16[56,2560]{1,0:T(8,128)(2,1)S(1)} %collective-permute-done.7.b2), channel_id=1, source_target_pairs={{0,14},{2,0},{4,2},{6,4},{8,6},{10,8},{12,10},{14,12},{1,15},{3,1}... | collective-permute-start | bytes 860168 | tf_op jit(solution)/shard_map/ppermute | solution.py:20
  48.5 9.0 %collective-permute-start.12 = (bf16[56,1280]{1,0:T(8,128)(2,1)S(1)}, bf16[56,1280]{1,0:T(8,128)(2,1)S(1)}, u32[]{:S(2)}, u32[]{:S(2)}) collective-permute-start(bf16[56,1280]{1,0:T(8,128)(2,1)S(1)} %slice.7), channel_id=1, source_target_pairs={{0,14},{2,0},{4,2},{6,4},{8,6},{10,8},{12,10},{14,12},{1,15},{3,1}... | collective-permute-start | bytes 430088 | tf_op jit(solution)/shard_map/ppermute | solution.py:20
  51.1 6.5 %collective-permute-start.11 = (bf16[56,1280]{1,0:T(8,128)(2,1)S(1)}, bf16[56,1280]{1,0:T(8,128)(2,1)S(1)}, u32[]{:S(2)}, u32[]{:S(2)}) collective-permute-start(bf16[56,1280]{1,0:T(8,128)(2,1)S(1)} %slice.6), channel_id=1, source_target_pairs={{0,2},{2,4},{4,6},{6,8},{8,10},{10,12},{12,14},{14,0},{1,3},{3,5},... | collective-permute-start | bytes 430088 | tf_op jit(solution)/shard_map/ppermute | solution.py:20
  54.5 5.2 %collective-permute-start.13 = (bf16[56,1280]{1,0:T(8,128)(2,1)S(1)}, bf16[56,1280]{1,0:T(8,128)(2,1)S(1)}, u32[]{:S(2)}, u32[]{:S(2)}) collective-permute-start(bf16[56,1280]{1,0:T(8,128)(2,1)S(1)} %get-tuple-element.80), channel_id=1, source_target_pairs={{0,2},{2,4},{4,6},{6,8},{8,10},{10,12},{12,14},{14,0},{1,3},{3,5},... | collective-permute-start | bytes 430088 | tf_op jit(solution)/shard_map/ppermute | solution.py:20
  54.6 5.2 %collective-permute-start.14 = (bf16[56,1280]{1,0:T(8,128)(2,1)S(1)}, bf16[56,1280]{1,0:T(8,128)(2,1)S(1)}, u32[]{:S(2)}, u32[]{:S(2)}) collective-permute-start(bf16[56,1280]{1,0:T(8,128)(2,1)S(1)} %get-tuple-element.81), channel_id=1, source_target_pairs={{0,14},{2,0},{4,2},{6,4},{8,6},{10,8},{12,10},{14,12},{1,15},{3,1}... | collective-permute-start | bytes 430088 | tf_op jit(solution)/shard_map/ppermute | solution.py:20
  61.5 8.8 %collective-permute-start.15 = (bf16[512,1280]{1,0:T(8,128)(2,1)S(1)}, bf16[512,1280]{1,0:T(8,128)(2,1)S(1)}, u32[]{:S(2)}, u32[]{:S(2)}) collective-permute-start(bf16[512,1280]{1,0:T(8,128)(2,1)S(1)} %get-tuple-element.93), channel_id=1, source_target_pairs={{0,64},{64,0},{1,65},{65,1},{2,66},{66,2},{3,67},{67,3},{4,68},{68... | collective-permute-start | bytes 3932168 | tf_op jit(solution)/shard_map/ppermute | solution.py:20
  63.9 10.3 %collective-permute-start.19 = (bf16[56,2560]{1,0:T(8,128)(2,1)S(1)}, bf16[56,2560]{1,0:T(8,128)(2,1)S(1)}, u32[]{:S(2)}, u32[]{:S(2)}) collective-permute-start(bf16[56,2560]{1,0:T(8,128)(2,1)S(1)} %get-tuple-element.87), channel_id=1, source_target_pairs={{0,2},{2,4},{4,6},{6,8},{8,10},{10,12},{12,14},{14,0},{1,3},{3,5},... | collective-permute-start | bytes 860168 | tf_op jit(solution)/shard_map/ppermute | solution.py:20
  64.1 10.1 %collective-permute-start.20 = (bf16[56,2560]{1,0:T(8,128)(2,1)S(1)}, bf16[56,2560]{1,0:T(8,128)(2,1)S(1)}, u32[]{:S(2)}, u32[]{:S(2)}) collective-permute-start(bf16[56,2560]{1,0:T(8,128)(2,1)S(1)} %get-tuple-element.88), channel_id=1, source_target_pairs={{0,14},{2,0},{4,2},{6,4},{8,6},{10,8},{12,10},{14,12},{1,15},{3,1}... | collective-permute-start | bytes 860168 | tf_op jit(solution)/shard_map/ppermute | solution.py:20
  70.7 15.5 %collective-permute-start.16 = (bf16[128,1792]{1,0:T(8,128)(2,1)S(1)}, bf16[128,1792]{1,0:T(8,128)(2,1)S(1)}, u32[]{:S(2)}, u32[]{:S(2)}) collective-permute-start(bf16[128,1792]{1,0:T(8,128)(2,1)S(1)} %get-tuple-element.97), channel_id=1, source_target_pairs={{0,48},{16,0},{32,16},{48,32},{1,49},{17,1},{33,17},{49,33},{2,50}... | collective-permute-start | bytes 1376264 | tf_op jit(solution)/shard_map/ppermute | solution.py:20
  70.8 15.4 %collective-permute-start.17 = (bf16[128,1792]{1,0:T(8,128)(2,1)S(1)}, bf16[128,1792]{1,0:T(8,128)(2,1)S(1)}, u32[]{:S(2)}, u32[]{:S(2)}) collective-permute-start(bf16[128,1792]{1,0:T(8,128)(2,1)S(1)} %get-tuple-element.98), channel_id=1, source_target_pairs={{0,32},{16,48},{32,0},{48,16},{1,33},{17,49},{33,1},{49,17},{2,34}... | collective-permute-start | bytes 1376264 | tf_op jit(solution)/shard_map/ppermute | solution.py:20
  72.9 21.8 %collective-permute-start.18 = (bf16[128,1792]{1,0:T(8,128)(2,1)S(1)}, bf16[128,1792]{1,0:T(8,128)(2,1)S(1)}, u32[]{:S(2)}, u32[]{:S(2)}) collective-permute-start(bf16[128,1792]{1,0:T(8,128)(2,1)S(1)} %get-tuple-element.99), channel_id=1, source_target_pairs={{0,16},{16,32},{32,48},{48,0},{1,17},{17,33},{33,49},{49,1},{2,18}... | collective-permute-start | bytes 1376264 | tf_op jit(solution)/shard_map/ppermute | solution.py:20
  74.3 9.0 %collective-permute-start.21 = (bf16[56,2560]{1,0:T(8,128)(2,1)S(1)}, bf16[56,2560]{1,0:T(8,128)(2,1)S(1)}, u32[]{:S(2)}, u32[]{:S(2)}) collective-permute-start(bf16[56,2560]{1,0:T(8,128)(2,1)S(1)} %get-tuple-element.102), channel_id=1, source_target_pairs={{0,2},{2,4},{4,6},{6,8},{8,10},{10,12},{12,14},{14,0},{1,3},{3,5},... | collective-permute-start | bytes 860168 | tf_op jit(solution)/shard_map/ppermute | solution.py:20
  74.4 8.9 %collective-permute-start.22 = (bf16[56,2560]{1,0:T(8,128)(2,1)S(1)}, bf16[56,2560]{1,0:T(8,128)(2,1)S(1)}, u32[]{:S(2)}, u32[]{:S(2)}) collective-permute-start(bf16[56,2560]{1,0:T(8,128)(2,1)S(1)} %get-tuple-element.103), channel_id=1, source_target_pairs={{0,14},{2,0},{4,2},{6,4},{8,6},{10,8},{12,10},{14,12},{1,15},{3,1}... | collective-permute-start | bytes 860168 | tf_op jit(solution)/shard_map/ppermute | solution.py:20
  83.4 11.9 %collective-permute-start.24 = (bf16[56,2560]{1,0:T(8,128)(2,1)S(1)}, bf16[56,2560]{1,0:T(8,128)(2,1)S(1)}, u32[]{:S(2)}, u32[]{:S(2)}) collective-permute-start(bf16[56,2560]{1,0:T(8,128)(2,1)S(1)} %get-tuple-element.106), channel_id=1, source_target_pairs={{0,2},{2,4},{4,6},{6,8},{8,10},{10,12},{12,14},{14,0},{1,3},{3,5},... | collective-permute-start | bytes 860168 | tf_op jit(solution)/shard_map/ppermute | solution.py:20
  83.5 11.8 %collective-permute-start.25 = (bf16[56,2560]{1,0:T(8,128)(2,1)S(1)}, bf16[56,2560]{1,0:T(8,128)(2,1)S(1)}, u32[]{:S(2)}, u32[]{:S(2)}) collective-permute-start(bf16[56,2560]{1,0:T(8,128)(2,1)S(1)} %get-tuple-element.107), channel_id=1, source_target_pairs={{0,14},{2,0},{4,2},{6,4},{8,6},{10,8},{12,10},{14,12},{1,15},{3,1}... | collective-permute-start | bytes 860168 | tf_op jit(solution)/shard_map/ppermute | solution.py:20
  94.8 2.4 %copy-start.2 = (bf16[128,1728]{0,1:T(8,128)(2,1)S(1)}, bf16[128,1728]{0,1:T(8,128)(2,1)}, u32[]{:S(2)}) copy-start(bf16[128,1728]{0,1:T(8,128)(2,1)} %param.4) | copy-start | bytes 1327108
  94.8 2.4 %copy-start.4 = (bf16[128,1728]{0,1:T(8,128)(2,1)S(1)}, bf16[128,1728]{0,1:T(8,128)(2,1)}, u32[]{:S(2)}) copy-start(bf16[128,1728]{0,1:T(8,128)(2,1)} %param.5) | copy-start | bytes 1327108
  94.8 8.9 %collective-permute-start.23 = (bf16[128,1280]{1,0:T(8,128)(2,1)S(1)}, bf16[128,1280]{1,0:T(8,128)(2,1)S(1)}, u32[]{:S(2)}, u32[]{:S(2)}) collective-permute-start(bf16[128,1280]{1,0:T(8,128)(2,1)S(1)} %shard_map.85), channel_id=1, source_target_pairs={{0,128},{128,0},{1,129},{129,1},{2,130},{130,2},{3,131},{131,3},{4... | collective-permute-start | bytes 983048 | tf_op jit(solution)/shard_map/ppermute | solution.py:20
  95.6 12.1 %collective-permute-start.27 = (bf16[27,2560]{1,0:T(8,128)(2,1)S(1)}, bf16[27,2560]{1,0:T(8,128)(2,1)S(1)}, u32[]{:S(2)}, u32[]{:S(2)}) collective-permute-start(bf16[27,2560]{1,0:T(8,128)(2,1)S(1)} %get-tuple-element.113), channel_id=1, source_target_pairs={{0,1},{1,0},{2,3},{3,2},{4,5},{5,4},{6,7},{7,6},{8,9},{9,8},{10,11... | collective-permute-start | bytes 414728 | tf_op jit(solution)/shard_map/ppermute | solution.py:20
  103.8 4.7 %collective-permute-start.26 = (bf16[128,1280]{1,0:T(8,128)(2,1)S(1)}, bf16[128,1280]{1,0:T(8,128)(2,1)S(1)}, u32[]{:S(2)}, u32[]{:S(2)}) collective-permute-start(bf16[128,1280]{1,0:T(8,128)(2,1)S(1)} %add_convert_fusion.mine), channel_id=1, source_target_pairs={{0,64},{64,0},{1,65},{65,1},{2,66},{66,2},{3,67},{67,3},{4,68},{68... | collective-permute-start | bytes 983048 | tf_op jit(solution)/shard_map/ppermute | solution.py:20

commit v3 on v2

--- a/solution.py
+++ b/solution.py
@@ -105,14 +105,13 @@
 
 
 def add_up(own, h1, h2, h3, out):
-    half = own.shape[1]
     total = own[...]
     for got in (h1, h2, h3):
-        total = total + got[:, :half].astype(F32)
+        total = total + got[...].astype(F32)
     out[...] = total.astype(BF16)
 
 
-def weight_gradient(scale, cot_own, hid_own, g1, g2, g3, far, pieces, to_fwd, to_bwd, cot, hid, hid_t):
+def weight_gradient(scale, cot_own, hid_own, g1, g2, g3, far, pieces, to_bwd, cot, hid, hid_t):
     rows, half = cot_own.shape[0], cot_own.shape[1] // 2
     cot[:rows] = cot_own[...]
     hid_t[:, :rows] = hid_own[...]
@@ -133,21 +132,20 @@
             distance = lax.rem(block - z + NZ, NZ)
             pieces[distance, :, columns] = product[block * SLOT : block * SLOT + SENT]
 
-    to_fwd[...] = pieces[4, :, :half].astype(BF16)
-    to_bwd[...] = pieces[4, :, half:].astype(BF16)
+    to_bwd[...] = pieces[NZ // 2].astype(BF16)
     hid[...] = hid_t[...].T
 
 
-def output_other(w0, f1, f2, f3, f4, b4, b3, b2, b1, hid, out, weight):
+def first_rows(value, out):
+    out[...] = value[: out.shape[0], : out.shape[1]]
+
+
+def output_other(w0, f1, f2, f3, f4, b3, b2, b1, hid, mark, out, weight):
     z = lax.axis_index("z")
     half = w0.shape[1] // 2
-    for distance, piece in enumerate((w0, f1, f2, f3, None, b3, b2, b1)):
+    for distance, piece in enumerate((w0, f1, f2, f3, f4, b3, b2, b1)):
         to = lax.rem(z - distance + NZ, NZ)
-        if piece is None:
-            weight[to, :SENT, :half] = f4[...]
-            weight[to, :SENT, half:] = b4[...]
-        else:
-            weight[to, :SENT] = piece[...]
+        weight[to, :SENT] = piece[...]
         weight[to, SENT:] = jnp.zeros((SLOT - SENT, w0.shape[1]), BF16)
 
     @pl.loop(0, half // TILE)
@@ -158,7 +156,7 @@
         out[:, pl.ds(pl.multiple_of(t * TILE, TILE), TILE)] = product.astype(BF16)
 
 
-def output_mine(hid, cot, weight, out, back):
+def output_mine(hid, weight, out):
     half = weight.shape[2] // 2
 
     @pl.loop(0, half // TILE)
@@ -167,7 +165,10 @@
         rhs = weight[:, :, columns].reshape(NZ * SLOT, TILE)
         out[:, columns] = jnp.dot(hid[...], rhs, preferred_element_type=F32)
 
+
+def back_parts(cot, weight, *parts):
     slots = TILE // SLOT
+    rows = parts[0].shape[1]
 
     @pl.loop(0, NZ // slots)
     def _(t):
@@ -175,36 +176,31 @@
         product = lax.dot_general(
             some, cot[...], (((1,), (1,)), ((), ())), preferred_element_type=F32
         )
-        back[pl.ds(pl.multiple_of(t * TILE, TILE), TILE)] = product.astype(BF16)
-
-
-def pack_output(mine, crossed, back, total, back_own, m1, m2, m3):
-    rows, half = total.shape
+        for k, part in enumerate(parts):
+            part[pl.ds(pl.multiple_of(t * TILE, TILE), TILE)] = product[
+                :, k * rows : (k + 1) * rows
+            ].astype(BF16)
+
+
+def pack_output(mine, crossed, total, m1, m2, m3):
+    rows = total.shape[0]
     total[...] = mine[:rows] + crossed[:rows].astype(F32)
-    back_own[...] = back[:, :rows]
     for k, out in enumerate((m1, m2, m3)):
         here = slice((k + 1) * rows, (k + 2) * rows)
-        out[:, :half] = (mine[here] + crossed[here].astype(F32)).astype(BF16)
-        for i in range(NZ * SLOT // rows):
-            to_column = half + i * rows
-            out[:, to_column : to_column + rows] = back[i * rows : (i + 1) * rows, here]
-
-
-def activation_gradients(gate, up, back_own, h1, h2, h3, grad_gate, grad_up, back32):
+        out[...] = (mine[here] + crossed[here].astype(F32)).astype(BF16)
+
+
+def activation_gradients(gate, up, b0, b1, b2, b3, grad_gate, grad_up, back32):
     units, rows = gate.shape
-    half = h1.shape[1] - back_own.shape[0]
     used = units // (NX * NZ)
     for x in range(NX):
 
         @pl.when(lax.axis_index("x") == x)
         def _(x=x):
             for s in range(NX):
-                source = (back_own, h1, h2, h3)[(s - x) % NX]
+                source = (b0, b1, b2, b3)[(s - x) % NX]
                 for block in range(NZ):
-                    row, column = block * SLOT, 0
-                    if s != x:
-                        row, column = row % rows, half + row // rows * rows
-                    value = source[row : row + SLOT, column : column + rows].astype(F32)
+                    value = source[block * SLOT : (block + 1) * SLOT].astype(F32)
                     start = (s * NZ + block) * used
                     back32[start : start + used] = value[:used]
 
@@ -214,13 +210,13 @@
     grad_up[...] = (back32[...] * (gate32 * sig)).astype(BF16)
 
 
-def add_pieces(distance, pieces, fwd, bwd, to_fwd, to_bwd):
-    some = fwd.shape[1]
-    to_fwd[:, :some] = (pieces[distance, :, :some] + fwd[...].astype(F32)).astype(BF16)
-    to_bwd[:, -some:] = (pieces[NZ - distance, :, -some:] + bwd[...].astype(F32)).astype(BF16)
-    if some < to_fwd.shape[1]:
-        to_fwd[:, some:] = pieces[distance, :, some:].astype(BF16)
-        to_bwd[:, :-some] = pieces[NZ - distance, :, :-some].astype(BF16)
+def add_pieces(distance, pieces, *refs):
+    *sums, to_fwd, to_bwd = refs
+    here = pieces[distance]
+    if len(sums) > 1:
+        here = here + sums[0][...].astype(F32)
+    to_fwd[...] = here.astype(BF16)
+    to_bwd[...] = (pieces[NZ - distance] + sums[-1][...].astype(F32)).astype(BF16)
 
 
 def finish_rows(pieces, fwd, bwd, keep, give, total):
@@ -286,9 +282,9 @@
         bwd.append(b)
     far = shift(near, "core", 1)
     scale = float(tokens * NZ * 2) ** (-0.5)
-    pieces, to_fwd, to_bwd, cot, hid = call(
+    pieces, to_bwd, cot, hid = call(
         functools.partial(weight_gradient, scale),
-        [like((NZ, SENT, width), F32)] + [like((SENT, half))] * 2 + [like((tokens, width)), like((tokens, slots))],
+        [like((NZ, SENT, width), F32), like((SENT, width)), like((tokens, width)), like((tokens, slots))],
         cot_own, hid_own, *got, far,
         scratch=[pltpu.VMEM((slots, tokens), BF16)],
         flops=2 * slots * tokens * width,
@@ -298,41 +294,42 @@
         kernel = functools.partial(add_pieces, distance)
         return call(kernel, [like((SENT, width))] * 2, pieces, *ring, moved=0)
 
-    to_fwd, to_bwd = after((to_fwd, to_bwd), fwd[3], bwd[3])
-    f4, b4 = shift(fwd[3][:, :half], "z", 1), shift(bwd[3][:, half:], "z", -1)
-    ring = (shift(to_fwd, "z", 1), shift(to_bwd, "z", -1))
-    f4, b4, ring = lax.optimization_barrier((f4, b4, ring))
+    f4 = shift(fwd[3], "z", 1)
+    ring = (shift(to_bwd, "z", -1),)
     to_fwd, to_bwd = added(3, ring)
     ring = (shift(to_fwd, "z", 1), shift(to_bwd, "z", -1))
 
-    f4, b4 = after((f4, b4), to_fwd, to_bwd)
+    (mark,) = call(first_rows, [like((16, 128))], to_fwd, flops=2 * 10**9)
     out_other, weight = call(
         output_other,
         [like((tokens, half)), like((NZ, SLOT, width))],
-        *fwd, f4, b4, *reversed(bwd[1:]), hid,
+        *fwd, f4, *reversed(bwd[1:]), hid, mark,
         flops=2 * slots * tokens * half,
     )
     crossed = shift(out_other, "core", 1)
-    out_mine, back = call(
-        output_mine,
-        [like((tokens, half), F32), like((slots, tokens))],
-        hid, cot, weight,
-        flops=6 * slots * tokens * half,
-    )
-    crossed = after(crossed, back)
-    total, back_own, m1, m2, m3 = call(
+    (out_mine,) = call(
+        output_mine, [like((tokens, half), F32)], hid, weight, flops=14 * 10**9
+    )
+    crossed = after(crossed, out_mine)
+    total, m1, m2, m3 = call(
         pack_output,
-        [like((rows, half), F32), like((slots, rows))] + [like((rows, wide))] * 3,
-        out_mine, crossed, back,
-    )
-    got_back = [shift(m, "x", -k) for k, m in ((1, m1), (2, m2), (3, m3))]
-    ring = after(ring, m1, m2, m3)
+        [like((rows, half), F32)] + [like((rows, half))] * 3,
+        out_mine, crossed,
+        flops=4 * 10**9,
+    )
+    got_out = [shift(m, "x", -k) for k, m in ((1, m1), (2, m2), (3, m3))]
+    back_own, *backs = call(
+        back_parts, [like((slots, rows))] * NX, after(cot, m1), weight, moved=0
+    )
+    back1, back2, back3 = backs
+    got_back1, got_back3 = shift(back1, "x", -1), shift(back3, "x", -3)
+    ring = after(ring, back1, back2, back3)
     to_fwd, to_bwd = added(2, ring)
     ring = lax.optimization_barrier((shift(to_fwd, "z", 1), shift(to_bwd, "z", -1)))
     to_fwd, to_bwd = added(1, ring)
-    got_back = after(got_back, to_fwd, to_bwd)
+    got_out = after(got_out, to_fwd, to_bwd)
     ring = (shift(to_fwd, "z", 1), shift(to_bwd, "z", -1))
-    (rounded,) = call(add_up, [like((rows, half))], total, *got_back, moved=0)
+    (rounded,) = call(add_up, [like((rows, half))], total, *got_out, moved=0)
     across = shift(rounded, "yl", 1)
     ring = after(ring, rounded)
     keep, give = call(
@@ -340,15 +337,18 @@
         [like((block, width), F32), like((block, width))],
         pieces, *ring,
         scratch=[pltpu.VMEM((SENT, width), F32)],
+        flops=60 * 10**7,
+        moved=0,
     )
     taken = shift(give, "yh", 1)
-    got_back = after(got_back, give)
+    got_back2 = shift(after(back2, give), "x", -2)
     grad_gate, grad_up = call(
         activation_gradients,
         [like((units, rows))] * 2,
-        gate, up, back_own, *got_back,
+        gate, up, back_own, got_back1, got_back2, got_back3,
         scratch=[pltpu.VMEM((units, rows), F32)],
-        flops=15 * 10**8,
+        flops=60 * 10**7,
+        moved=0,
     )
     across = after(across, give)
     out_half = (rounded.astype(F32) + across.astype(F32)).astype(BF16)

time: 110 us -> 97 us (0.88)
  waiting for transfers between devices: 43.6 us -> 31.8 us
    ppermute x28 -> x29, waiting for transfers between devices: 43.6 us -> 31.8 us  [shift(): lax.ppermute(value, axis, [(i, (i + steps) % count) for i in range(count)])]
    ppermute x28 -> x29, starting transfers between devices: 47.4 us -> 46.5 us  [shift(): lax.ppermute(value, axis, [(i, (i + steps) % count) for i in range(count)])]
    pallas_call x14 -> x16, Pallas kernels: 12.7 us -> 12.6 us  [call(): pl.pallas_call(kernel, out_shape=outs, in_specs=[whole] * len(args), out_...]
  transfers between devices with their start and end apart: 28 -> 29, of which waited for: 11 -> 13; matrix products, arithmetic and copies ran while one was open for 1% -> 1% of each run, Pallas kernels for 9% -> 12%
where the time goes in v3:
time: 97 us; the launch traced here: 96.6 us
  starting transfers between devices  46.5 us (48%)
  waiting for transfers between devices  31.8 us (33%)
  Pallas kernels  12.6 us (13%)
  local copies, waits for them, and re-layouts  4.04 us (4%)
    ppermute x29, starting transfers between devices, shift(): lax.ppermute(value, axis, [(i, (i + steps) % count) for i in range(count)])  46.5 us
    ppermute x29, waiting for transfers between devices, shift(): lax.ppermute(value, axis, [(i, (i + steps) % count) for i in range(count)])  31.8 us
    pallas_call x16, Pallas kernels, call(): pl.pallas_call(kernel, out_shape=outs, in_specs=[whole] * len(args), out_...  12.6 us
    unnamed x12, local copies, waits for them, and re-layouts  4.04 us
  transfers between devices with their start and end apart: 29, of which 13 were waited for; matrix products, arithmetic and copies ran while one was open for 1% of the time, Pallas kernels for 12%

profile of v3, /device:TPU:1, one launch (start us, length us, event | category | flops | bytes accessed | tf_op | source)
XLA Modules:
  0.0 96.6 jit_solution(18066416403859526743)
XLA Ops:
  0.6 3.8 %collective-permute-start.3 = (bf16[27,2560]{1,0:T(8,128)(2,1)}, bf16[27,2560]{1,0:T(8,128)(2,1)S(1)}, u32[]{:S(2)}, u32[]{:S(2)}) collective-permute-start(bf16[27,2560]{1,0:T(8,128)(2,1)} %mine.1), channel_id=1, source_target_pairs={{0,1},{1,0},{2,3},{3,2},{4,5},{5,4},{6,7},{7,6},{8,9},{9,8},{10,11... | collective-permute-start | bytes 414728 | tf_op jit(solution)/shard_map/ppermute | solution.py:20
  4.5 1.1 %copy-done = bf16[128,2560]{1,0:T(8,128)(2,1)S(1)} copy-done((bf16[128,2560]{1,0:T(8,128)(2,1)S(1)}, bf16[128,2560]{1,0:T(8,128)(2,1)}, u32[]{:S(2)}) %copy-start) | copy-done | bytes 655384
  5.6 1.0 %copy-done.1 = bf16[128,1728]{0,1:T(8,128)(2,1)S(1)} copy-done((bf16[128,1728]{0,1:T(8,128)(2,1)S(1)}, bf16[128,1728]{0,1:T(8,128)(2,1)}, u32[]{:S(2)}) %copy-start.1) | copy-done | bytes 442392
  6.6 1.0 %copy-done.3 = bf16[128,1728]{0,1:T(8,128)(2,1)S(1)} copy-done((bf16[128,1728]{0,1:T(8,128)(2,1)S(1)}, bf16[128,1728]{0,1:T(8,128)(2,1)}, u32[]{:S(2)}) %copy-start.3) | copy-done | bytes 442392
  7.6 0.6 shard_map.75
  8.2 1.3 %collective-permute-start = (bf16[128,1792]{1,0:T(8,128)(2,1)S(1)}, bf16[128,1792]{1,0:T(8,128)(2,1)S(1)}, u32[]{:S(2)}, u32[]{:S(2)}) collective-permute-start(bf16[128,1792]{1,0:T(8,128)(2,1)S(1)} %get-tuple-element.56), channel_id=1, source_target_pairs={{0,16},{16,32},{32,48},{48,0},{1,17},{17,33},{33,49},{49,1},{2,18}... | collective-permute-start | bytes 1376264 | tf_op jit(solution)/shard_map/ppermute | solution.py:20
  9.5 2.5 %collective-permute-start.1 = (bf16[128,1792]{1,0:T(8,128)(2,1)S(1)}, bf16[128,1792]{1,0:T(8,128)(2,1)S(1)}, u32[]{:S(2)}, u32[]{:S(2)}) collective-permute-start(bf16[128,1792]{1,0:T(8,128)(2,1)S(1)} %get-tuple-element.57), channel_id=1, source_target_pairs={{0,32},{16,48},{32,0},{48,16},{1,33},{17,49},{33,1},{49,17},{2,34}... | collective-permute-start | bytes 1376264 | tf_op jit(solution)/shard_map/ppermute | solution.py:20
  12.0 1.2 %collective-permute-start.2 = (bf16[128,1792]{1,0:T(8,128)(2,1)S(1)}, bf16[128,1792]{1,0:T(8,128)(2,1)S(1)}, u32[]{:S(2)}, u32[]{:S(2)}) collective-permute-start(bf16[128,1792]{1,0:T(8,128)(2,1)S(1)} %get-tuple-element.58), channel_id=1, source_target_pairs={{0,48},{16,0},{32,16},{48,32},{1,49},{17,1},{33,17},{49,33},{2,50}... | collective-permute-start | bytes 1376264 | tf_op jit(solution)/shard_map/ppermute | solution.py:20
  13.1 0.0 collective-permute-done.3.other
  13.1 0.9 copy-done.5
  14.0 0.3 shard_map.76.w0
  14.4 5.7 %collective-permute-start.5 = (bf16[56,2560]{1,0:T(8,128)(2,1)S(1)}, bf16[56,2560]{1,0:T(8,128)(2,1)S(1)}, u32[]{:S(2)}, u32[]{:S(2)}) collective-permute-start(bf16[56,2560]{1,0:T(8,128)(2,1)S(1)} %shard_map.76.w0), channel_id=1, source_target_pairs={{0,14},{2,0},{4,2},{6,4},{8,6},{10,8},{12,10},{14,12},{1,15},{3,1}... | collective-permute-start | bytes 860168 | tf_op jit(solution)/shard_map/ppermute | solution.py:20
  20.0 0.0 collective-permute-start.4
  20.0 4.3 %collective-permute-done.5.b1 = bf16[56,2560]{1,0:T(8,128)(2,1)S(1)} collective-permute-done((bf16[56,2560]{1,0:T(8,128)(2,1)S(1)}, bf16[56,2560]{1,0:T(8,128)(2,1)S(1)}, u32[]{:S(2)}, u32[]{:S(2)}) %collective-permute-start.5) | collective-permute-done | bytes 286752 | tf_op jit(solution)/shard_map/ppermute | solution.py:20
  24.3 3.1 %collective-permute-done.4.f1 = bf16[56,2560]{1,0:T(8,128)(2,1)S(1)} collective-permute-done((bf16[56,2560]{1,0:T(8,128)(2,1)S(1)}, bf16[56,2560]{1,0:T(8,128)(2,1)S(1)}, u32[]{:S(2)}, u32[]{:S(2)}) %collective-permute-start.4) | collective-permute-done | bytes 286752 | tf_op jit(solution)/shard_map/ppermute | solution.py:20
  27.5 2.7 %collective-permute-start.7 = (bf16[56,2560]{1,0:T(8,128)(2,1)S(1)}, bf16[56,2560]{1,0:T(8,128)(2,1)S(1)}, u32[]{:S(2)}, u32[]{:S(2)}) collective-permute-start(bf16[56,2560]{1,0:T(8,128)(2,1)S(1)} %collective-permute-done.5.b1), channel_id=1, source_target_pairs={{0,14},{2,0},{4,2},{6,4},{8,6},{10,8},{12,10},{14,12},{1,15},{3,1}... | collective-permute-start | bytes 860168 | tf_op jit(solution)/shard_map/ppermute | solution.py:20
  30.1 0.0 collective-permute-done.g1
  30.1 1.2 %collective-permute-done.1.g2 = bf16[128,1792]{1,0:T(8,128)(2,1)S(1)} collective-permute-done((bf16[128,1792]{1,0:T(8,128)(2,1)S(1)}, bf16[128,1792]{1,0:T(8,128)(2,1)S(1)}, u32[]{:S(2)}, u32[]{:S(2)}) %collective-permute-start.1) | collective-permute-done | bytes 458784 | tf_op jit(solution)/shard_map/ppermute | solution.py:20
  31.4 0.1 shard_map.77
  31.5 2.7 %collective-permute-done.6.f2 = bf16[56,2560]{1,0:T(8,128)(2,1)S(1)} collective-permute-done((bf16[56,2560]{1,0:T(8,128)(2,1)S(1)}, bf16[56,2560]{1,0:T(8,128)(2,1)S(1)}, u32[]{:S(2)}, u32[]{:S(2)}) %collective-permute-start.6) | collective-permute-done | bytes 286752 | tf_op jit(solution)/shard_map/ppermute | solution.py:20
  34.2 4.2 %collective-permute-start.8 = (bf16[384,1280]{1,0:T(8,128)(2,1)S(1)}, bf16[384,1280]{1,0:T(8,128)(2,1)S(1)}, u32[]{:S(2)}, u32[]{:S(2)}) collective-permute-start(bf16[384,1280]{1,0:T(8,128)(2,1)S(1)} %shard_map.77), channel_id=1, source_target_pairs={{0,64},{64,0},{1,65},{65,1},{2,66},{66,2},{3,67},{67,3},{4,68},{68... | collective-permute-start | bytes 2949128 | tf_op jit(solution)/shard_map/ppermute | solution.py:20
  38.3 3.0 %collective-permute-start.10 = (bf16[56,2560]{1,0:T(8,128)(2,1)S(1)}, bf16[56,2560]{1,0:T(8,128)(2,1)S(1)}, u32[]{:S(2)}, u32[]{:S(2)}) collective-permute-start(bf16[56,2560]{1,0:T(8,128)(2,1)S(1)} %collective-permute-done.7.b2), channel_id=1, source_target_pairs={{0,14},{2,0},{4,2},{6,4},{8,6},{10,8},{12,10},{14,12},{1,15},{3,1}... | collective-permute-start | bytes 860168 | tf_op jit(solution)/shard_map/ppermute | solution.py:20
  41.3 3.4 %shard_map.78 = (f32[8,56,2560]{2,1,0:T(8,128)S(1)}, bf16[56,2560]{1,0:T(8,128)(2,1)S(1)}, bf16[512,2560]{1,0:T(8,128)(2,1)S(1)}, bf16[512,512]{1,0:T(8,128)(2,1)S(1)}) custom-call(bf16[128,2560]{1,0:T(8,128)(2,1)S(1)} %get-tuple-element.54.cot_own, bf16[512,128]{1,0:T(8,128)(2,1)S(1)} %get-tuple-element.55.hid_own, ...), custom_call_target="tpu_custom_call" | custom-call | flops 1342177280 | bytes 11165696 | tf_op jit(solution)/shard_map/pallas_call | solution.py:31
  44.7 2.3 %collective-permute-start.12 = (bf16[56,2560]{1,0:T(8,128)(2,1)S(1)}, bf16[56,2560]{1,0:T(8,128)(2,1)S(1)}, u32[]{:S(2)}, u32[]{:S(2)}) collective-permute-start(bf16[56,2560]{1,0:T(8,128)(2,1)S(1)} %get-tuple-element.69), channel_id=1, source_target_pairs={{0,14},{2,0},{4,2},{6,4},{8,6},{10,8},{12,10},{14,12},{1,15},{3,1}... | collective-permute-start | bytes 860168 | tf_op jit(solution)/shard_map/ppermute | solution.py:20
  47.0 1.5 %collective-permute-done.9.f3 = bf16[56,2560]{1,0:T(8,128)(2,1)S(1)} collective-permute-done((bf16[56,2560]{1,0:T(8,128)(2,1)S(1)}, bf16[56,2560]{1,0:T(8,128)(2,1)S(1)}, u32[]{:S(2)}, u32[]{:S(2)}) %collective-permute-start.9) | collective-permute-done | bytes 286752 | tf_op jit(solution)/shard_map/ppermute | solution.py:20
  48.5 5.1 %collective-permute-done.12.refs_0_ = bf16[56,2560]{1,0:T(8,128)(2,1)S(1)} collective-permute-done((bf16[56,2560]{1,0:T(8,128)(2,1)S(1)}, bf16[56,2560]{1,0:T(8,128)(2,1)S(1)}, u32[]{:S(2)}, u32[]{:S(2)}) %collective-permute-start.12) | collective-permute-done | bytes 286752 | tf_op jit(solution)/shard_map/ppermute | solution.py:20
  53.6 0.1 shard_map.79
  53.7 3.5 %collective-permute-start.18 = (bf16[56,2560]{1,0:T(8,128)(2,1)S(1)}, bf16[56,2560]{1,0:T(8,128)(2,1)S(1)}, u32[]{:S(2)}, u32[]{:S(2)}) collective-permute-start(bf16[56,2560]{1,0:T(8,128)(2,1)S(1)} %get-tuple-element.78), channel_id=1, source_target_pairs={{0,14},{2,0},{4,2},{6,4},{8,6},{10,8},{12,10},{14,12},{1,15},{3,1}... | collective-permute-start | bytes 860168 | tf_op jit(solution)/shard_map/ppermute | solution.py:20
  57.2 0.0 collective-permute-start.17
  57.2 0.2 collective-permute-done.11.f4
  57.4 1.7 %shard_map.81 = (bf16[512,1280]{1,0:T(8,128)(2,1)S(1)}, bf16[8,64,2560]{2,1,0:T(8,128)(2,1)S(1)}) custom-call(bf16[56,2560]{1,0:T(8,128)(2,1)S(1)} %shard_map.76.w0, bf16[56,2560]{1,0:T(8,128)(2,1)S(1)} %collective-permute-done.4.f1, bf16[56,2560]{1,0:T(8,128)(2,1)S(1)} %collective-permute-done.6.f2, bf16[56,2560]{1,0:T(8,128)(2,1)S(1)} %collective-permute-done.9.f3, ...), custom_call_target="tpu_custom_call" | custom-call | flops 671088640 | bytes 6754304 | tf_op jit(solution)/shard_map/pallas_call | solution.py:31
  59.1 1.6 %collective-permute-start.13 = (bf16[512,1280]{1,0:T(8,128)(2,1)S(1)}, bf16[512,1280]{1,0:T(8,128)(2,1)S(1)}, u32[]{:S(2)}, u32[]{:S(2)}) collective-permute-start(bf16[512,1280]{1,0:T(8,128)(2,1)S(1)} %get-tuple-element.72), channel_id=1, source_target_pairs={{0,64},{64,0},{1,65},{65,1},{2,66},{66,2},{3,67},{67,3},{4,68},{68... | collective-permute-start | bytes 3932168 | tf_op jit(solution)/shard_map/ppermute | solution.py:20
  60.7 1.5 %shard_map.82.mine = f32[512,1280]{1,0:T(8,128)S(1)} custom-call(bf16[512,512]{1,0:T(8,128)(2,1)S(1)} %get-tuple-element.63.hid, bf16[8,64,2560]{2,1,0:T(8,128)(2,1)S(1)} %get-tuple-element.71.weight), custom_call_target="tpu_custom_call" | custom-call | flops 14000000000 | bytes 5767168 | tf_op jit(solution)/shard_map/pallas_call | solution.py:31
  62.2 1.2 %collective-permute-done.13.crossed = bf16[512,1280]{1,0:T(8,128)(2,1)S(1)} collective-permute-done((bf16[512,1280]{1,0:T(8,128)(2,1)S(1)}, bf16[512,1280]{1,0:T(8,128)(2,1)S(1)}, u32[]{:S(2)}, u32[]{:S(2)}) %collective-permute-start.13) | collective-permute-done | bytes 1310752 | tf_op jit(solution)/shard_map/ppermute | solution.py:20
  63.4 0.2 shard_map.83
  63.6 0.3 collective-permute-start.15
  64.0 0.3 collective-permute-start.16
  64.3 2.3 %collective-permute-start.14 = (bf16[128,1280]{1,0:T(8,128)(2,1)S(1)}, bf16[128,1280]{1,0:T(8,128)(2,1)S(1)}, u32[]{:S(2)}, u32[]{:S(2)}) collective-permute-start(bf16[128,1280]{1,0:T(8,128)(2,1)S(1)} %get-tuple-element.75), channel_id=1, source_target_pairs={{0,48},{16,0},{32,16},{48,32},{1,49},{17,1},{33,17},{49,33},{2,50}... | collective-permute-start | bytes 983048 | tf_op jit(solution)/shard_map/ppermute | solution.py:20
  66.6 1.7 %shard_map.84 = (bf16[512,128]{1,0:T(8,128)(2,1)S(1)}, bf16[512,128]{1,0:T(8,128)(2,1)S(1)}, bf16[512,128]{1,0:T(8,128)(2,1)S(1)}, bf16[512,128]{1,0:T(8,128)(2,1)S(1)}) custom-call(bf16[512,2560]{1,0:T(8,128)(2,1)S(1)} %get-tuple-element.80.cot, bf16[8,64,2560]{2,1,0:T(8,128)(2,1)S(1)} %get-tuple-element.71.weight), custom_call_target="tpu_custom_call" | custom-call | tf_op jit(solution)/shard_map/pallas_call | solution.py:31
  68.4 0.1 shard_map.85
  68.5 0.1 collective-permute-start.19
  68.6 2.7 %collective-permute-start.20 = (bf16[56,2560]{1,0:T(8,128)(2,1)S(1)}, bf16[56,2560]{1,0:T(8,128)(2,1)S(1)}, u32[]{:S(2)}, u32[]{:S(2)}) collective-permute-start(bf16[56,2560]{1,0:T(8,128)(2,1)S(1)} %get-tuple-element.87), channel_id=1, source_target_pairs={{0,14},{2,0},{4,2},{6,4},{8,6},{10,8},{12,10},{14,12},{1,15},{3,1}... | collective-permute-start | bytes 860168 | tf_op jit(solution)/shard_map/ppermute | solution.py:20
  71.3 5.6 %collective-permute-done.19.refs_0_ = bf16[56,2560]{1,0:T(8,128)(2,1)S(1)} collective-permute-done((bf16[56,2560]{1,0:T(8,128)(2,1)S(1)}, bf16[56,2560]{1,0:T(8,128)(2,1)S(1)}, u32[]{:S(2)}, u32[]{:S(2)}) %collective-permute-start.19) | collective-permute-done | bytes 286752 | tf_op jit(solution)/shard_map/ppermute | solution.py:20
  76.9 0.1 shard_map.86
  77.1 1.8 %collective-permute-start.22 = (bf16[56,2560]{1,0:T(8,128)(2,1)S(1)}, bf16[56,2560]{1,0:T(8,128)(2,1)S(1)}, u32[]{:S(2)}, u32[]{:S(2)}) collective-permute-start(bf16[56,2560]{1,0:T(8,128)(2,1)S(1)} %get-tuple-element.90), channel_id=1, source_target_pairs={{0,2},{2,4},{4,6},{6,8},{8,10},{10,12},{12,14},{14,0},{1,3},{3,5},... | collective-permute-start | bytes 860168 | tf_op jit(solution)/shard_map/ppermute | solution.py:20
  78.9 0.9 collective-permute-start.23
  79.8 1.9 %collective-permute-done.16.h3 = bf16[128,1280]{1,0:T(8,128)(2,1)S(1)} collective-permute-done((bf16[128,1280]{1,0:T(8,128)(2,1)S(1)}, bf16[128,1280]{1,0:T(8,128)(2,1)S(1)}, u32[]{:S(2)}, u32[]{:S(2)}) %collective-permute-start.16) | collective-permute-done | bytes 327712 | tf_op jit(solution)/shard_map/ppermute | solution.py:20
  81.8 0.2 shard_map.87
  81.9 0.0 copy-start.2
  81.9 0.0 copy-start.4
  81.9 0.5 collective-permute-start.21
  82.4 0.1 collective-permute-start.26
  82.5 1.4 %collective-permute-start.28 = (bf16[512,128]{1,0:T(8,128)(2,1)S(1)}, bf16[512,128]{1,0:T(8,128)(2,1)S(1)}, u32[]{:S(2)}, u32[]{:S(2)}) collective-permute-start(bf16[512,128]{1,0:T(8,128)(2,1)S(1)} %get-tuple-element.83), channel_id=1, source_target_pairs={{0,16},{16,32},{32,48},{48,0},{1,17},{17,33},{33,49},{49,1},{2,18}... | collective-permute-start | bytes 393224 | tf_op jit(solution)/shard_map/ppermute | solution.py:20
  83.9 0.6 collective-permute-done.22.fwd
  84.5 0.2 collective-permute-done.23.bwd
  84.8 0.3 shard_map.88
  85.1 0.7 collective-permute-start.25
  85.8 0.8 collective-permute-start.27
  86.6 3.9 %collective-permute-done.21 = bf16[128,1280]{1,0:T(8,128)(2,1)S(1)} collective-permute-done((bf16[128,1280]{1,0:T(8,128)(2,1)S(1)}, bf16[128,1280]{1,0:T(8,128)(2,1)S(1)}, u32[]{:S(2)}, u32[]{:S(2)}) %collective-permute-start.21) | collective-permute-done | bytes 327712 | tf_op jit(solution)/shard_map/ppermute | solution.py:20
  90.5 0.1 add_convert_fusion.mine
  90.6 3.0 %collective-permute-start.24 = (bf16[128,1280]{1,0:T(8,128)(2,1)S(1)}, bf16[128,1280]{1,0:T(8,128)(2,1)S(1)}, u32[]{:S(2)}, u32[]{:S(2)}) collective-permute-start(bf16[128,1280]{1,0:T(8,128)(2,1)S(1)} %add_convert_fusion.mine), channel_id=1, source_target_pairs={{0,64},{64,0},{1,65},{65,1},{2,66},{66,2},{3,67},{67,3},{4,68},{68... | collective-permute-start | bytes 983048 | tf_op jit(solution)/shard_map/ppermute | solution.py:20
  93.6 1.3 %shard_map.90 = (bf16[1728,128]{1,0:T(8,128)(2,1)}, bf16[1728,128]{1,0:T(8,128)(2,1)}) custom-call(bf16[1728,128]{1,0:T(8,128)(2,1)S(1)} %bitcast.5, bf16[1728,128]{1,0:T(8,128)(2,1)S(1)} %bitcast.7, bf16[512,128]{1,0:T(8,128)(2,1)S(1)} %get-tuple-element.100.b0, bf16[512,128]{1,0:T(8,128)(2,1)S(1)} %collective-permute-done.26.b1, ...), custom_call_target="tpu_custom_call" | custom-call | flops 600000000 | tf_op jit(solution)/shard_map/pallas_call | solution.py:31
  94.9 0.8 convert_add_fusion
  95.7 0.9 shard_map.89
  (24 shorter events, 0.1 us)
Async XLA Ops:
  0.6 12.5 %collective-permute-start.3 = (bf16[27,2560]{1,0:T(8,128)(2,1)}, bf16[27,2560]{1,0:T(8,128)(2,1)S(1)}, u32[]{:S(2)}, u32[]{:S(2)}) collective-permute-start(bf16[27,2560]{1,0:T(8,128)(2,1)} %mine.1), channel_id=1, source_target_pairs={{0,1},{1,0},{2,3},{3,2},{4,5},{5,4},{6,7},{7,6},{8,9},{9,8},{10,11... | collective-permute-start | bytes 414728 | tf_op jit(solution)/shard_map/ppermute | solution.py:20
  4.5 1.1 %copy-start = (bf16[128,2560]{1,0:T(8,128)(2,1)S(1)}, bf16[128,2560]{1,0:T(8,128)(2,1)}, u32[]{:S(2)}) copy-start(bf16[128,2560]{1,0:T(8,128)(2,1)} %cot.1) | copy-start | bytes 1966084
  5.5 1.0 %copy-start.1 = (bf16[128,1728]{0,1:T(8,128)(2,1)S(1)}, bf16[128,1728]{0,1:T(8,128)(2,1)}, u32[]{:S(2)}) copy-start(bf16[128,1728]{0,1:T(8,128)(2,1)} %param.4) | copy-start | bytes 1327108
  6.6 1.0 %copy-start.3 = (bf16[128,1728]{0,1:T(8,128)(2,1)S(1)}, bf16[128,1728]{0,1:T(8,128)(2,1)}, u32[]{:S(2)}) copy-start(bf16[128,1728]{0,1:T(8,128)(2,1)} %param.5) | copy-start | bytes 1327108
  8.2 21.9 %collective-permute-start = (bf16[128,1792]{1,0:T(8,128)(2,1)S(1)}, bf16[128,1792]{1,0:T(8,128)(2,1)S(1)}, u32[]{:S(2)}, u32[]{:S(2)}) collective-permute-start(bf16[128,1792]{1,0:T(8,128)(2,1)S(1)} %get-tuple-element.56), channel_id=1, source_target_pairs={{0,16},{16,32},{32,48},{48,0},{1,17},{17,33},{33,49},{49,1},{2,18}... | collective-permute-start | bytes 1376264 | tf_op jit(solution)/shard_map/ppermute | solution.py:20
  9.5 21.9 %collective-permute-start.1 = (bf16[128,1792]{1,0:T(8,128)(2,1)S(1)}, bf16[128,1792]{1,0:T(8,128)(2,1)S(1)}, u32[]{:S(2)}, u32[]{:S(2)}) collective-permute-start(bf16[128,1792]{1,0:T(8,128)(2,1)S(1)} %get-tuple-element.57), channel_id=1, source_target_pairs={{0,32},{16,48},{32,0},{48,16},{1,33},{17,49},{33,1},{49,17},{2,34}... | collective-permute-start | bytes 1376264 | tf_op jit(solution)/shard_map/ppermute | solution.py:20
  12.0 19.4 %collective-permute-start.2 = (bf16[128,1792]{1,0:T(8,128)(2,1)S(1)}, bf16[128,1792]{1,0:T(8,128)(2,1)S(1)}, u32[]{:S(2)}, u32[]{:S(2)}) collective-permute-start(bf16[128,1792]{1,0:T(8,128)(2,1)S(1)} %get-tuple-element.58), channel_id=1, source_target_pairs={{0,48},{16,0},{32,16},{48,32},{1,49},{17,1},{33,17},{49,33},{2,50}... | collective-permute-start | bytes 1376264 | tf_op jit(solution)/shard_map/ppermute | solution.py:20
  13.1 0.9 copy-start.5
  14.4 10.0 %collective-permute-start.5 = (bf16[56,2560]{1,0:T(8,128)(2,1)S(1)}, bf16[56,2560]{1,0:T(8,128)(2,1)S(1)}, u32[]{:S(2)}, u32[]{:S(2)}) collective-permute-start(bf16[56,2560]{1,0:T(8,128)(2,1)S(1)} %shard_map.76.w0), channel_id=1, source_target_pairs={{0,14},{2,0},{4,2},{6,4},{8,6},{10,8},{12,10},{14,12},{1,15},{3,1}... | collective-permute-start | bytes 860168 | tf_op jit(solution)/shard_map/ppermute | solution.py:20
  20.0 7.4 %collective-permute-start.4 = (bf16[56,2560]{1,0:T(8,128)(2,1)S(1)}, bf16[56,2560]{1,0:T(8,128)(2,1)S(1)}, u32[]{:S(2)}, u32[]{:S(2)}) collective-permute-start(bf16[56,2560]{1,0:T(8,128)(2,1)S(1)} %shard_map.76.w0), channel_id=1, source_target_pairs={{0,2},{2,4},{4,6},{6,8},{8,10},{10,12},{12,14},{14,0},{1,3},{3,5},... | collective-permute-start | bytes 860168 | tf_op jit(solution)/shard_map/ppermute | solution.py:20
  27.5 6.7 %collective-permute-start.6 = (bf16[56,2560]{1,0:T(8,128)(2,1)S(1)}, bf16[56,2560]{1,0:T(8,128)(2,1)S(1)}, u32[]{:S(2)}, u32[]{:S(2)}) collective-permute-start(bf16[56,2560]{1,0:T(8,128)(2,1)S(1)} %collective-permute-done.4.f1), channel_id=1, source_target_pairs={{0,2},{2,4},{4,6},{6,8},{8,10},{10,12},{12,14},{14,0},{1,3},{3,5},... | collective-permute-start | bytes 860168 | tf_op jit(solution)/shard_map/ppermute | solution.py:20
  27.5 6.7 %collective-permute-start.7 = (bf16[56,2560]{1,0:T(8,128)(2,1)S(1)}, bf16[56,2560]{1,0:T(8,128)(2,1)S(1)}, u32[]{:S(2)}, u32[]{:S(2)}) collective-permute-start(bf16[56,2560]{1,0:T(8,128)(2,1)S(1)} %collective-permute-done.5.b1), channel_id=1, source_target_pairs={{0,14},{2,0},{4,2},{6,4},{8,6},{10,8},{12,10},{14,12},{1,15},{3,1}... | collective-permute-start | bytes 860168 | tf_op jit(solution)/shard_map/ppermute | solution.py:20
  34.2 7.1 %collective-permute-start.8 = (bf16[384,1280]{1,0:T(8,128)(2,1)S(1)}, bf16[384,1280]{1,0:T(8,128)(2,1)S(1)}, u32[]{:S(2)}, u32[]{:S(2)}) collective-permute-start(bf16[384,1280]{1,0:T(8,128)(2,1)S(1)} %shard_map.77), channel_id=1, source_target_pairs={{0,64},{64,0},{1,65},{65,1},{2,66},{66,2},{3,67},{67,3},{4,68},{68... | collective-permute-start | bytes 2949128 | tf_op jit(solution)/shard_map/ppermute | solution.py:20
  38.3 10.2 %collective-permute-start.9 = (bf16[56,2560]{1,0:T(8,128)(2,1)S(1)}, bf16[56,2560]{1,0:T(8,128)(2,1)S(1)}, u32[]{:S(2)}, u32[]{:S(2)}) collective-permute-start(bf16[56,2560]{1,0:T(8,128)(2,1)S(1)} %collective-permute-done.6.f2), channel_id=1, source_target_pairs={{0,2},{2,4},{4,6},{6,8},{8,10},{10,12},{12,14},{14,0},{1,3},{3,5},... | collective-permute-start | bytes 860168 | tf_op jit(solution)/shard_map/ppermute | solution.py:20
  38.3 10.2 %collective-permute-start.10 = (bf16[56,2560]{1,0:T(8,128)(2,1)S(1)}, bf16[56,2560]{1,0:T(8,128)(2,1)S(1)}, u32[]{:S(2)}, u32[]{:S(2)}) collective-permute-start(bf16[56,2560]{1,0:T(8,128)(2,1)S(1)} %collective-permute-done.7.b2), channel_id=1, source_target_pairs={{0,14},{2,0},{4,2},{6,4},{8,6},{10,8},{12,10},{14,12},{1,15},{3,1}... | collective-permute-start | bytes 860168 | tf_op jit(solution)/shard_map/ppermute | solution.py:20
  44.7 8.9 %collective-permute-start.12 = (bf16[56,2560]{1,0:T(8,128)(2,1)S(1)}, bf16[56,2560]{1,0:T(8,128)(2,1)S(1)}, u32[]{:S(2)}, u32[]{:S(2)}) collective-permute-start(bf16[56,2560]{1,0:T(8,128)(2,1)S(1)} %get-tuple-element.69), channel_id=1, source_target_pairs={{0,14},{2,0},{4,2},{6,4},{8,6},{10,8},{12,10},{14,12},{1,15},{3,1}... | collective-permute-start | bytes 860168 | tf_op jit(solution)/shard_map/ppermute | solution.py:20
  48.5 8.9 %collective-permute-start.11 = (bf16[56,2560]{1,0:T(8,128)(2,1)S(1)}, bf16[56,2560]{1,0:T(8,128)(2,1)S(1)}, u32[]{:S(2)}, u32[]{:S(2)}) collective-permute-start(bf16[56,2560]{1,0:T(8,128)(2,1)S(1)} %collective-permute-done.9.f3), channel_id=1, source_target_pairs={{0,2},{2,4},{4,6},{6,8},{8,10},{10,12},{12,14},{14,0},{1,3},{3,5},... | collective-permute-start | bytes 860168 | tf_op jit(solution)/shard_map/ppermute | solution.py:20
  53.7 14.7 %collective-permute-start.18 = (bf16[56,2560]{1,0:T(8,128)(2,1)S(1)}, bf16[56,2560]{1,0:T(8,128)(2,1)S(1)}, u32[]{:S(2)}, u32[]{:S(2)}) collective-permute-start(bf16[56,2560]{1,0:T(8,128)(2,1)S(1)} %get-tuple-element.78), channel_id=1, source_target_pairs={{0,14},{2,0},{4,2},{6,4},{8,6},{10,8},{12,10},{14,12},{1,15},{3,1}... | collective-permute-start | bytes 860168 | tf_op jit(solution)/shard_map/ppermute | solution.py:20
  57.2 11.2 %collective-permute-start.17 = (bf16[56,2560]{1,0:T(8,128)(2,1)S(1)}, bf16[56,2560]{1,0:T(8,128)(2,1)S(1)}, u32[]{:S(2)}, u32[]{:S(2)}) collective-permute-start(bf16[56,2560]{1,0:T(8,128)(2,1)S(1)} %get-tuple-element.70.value), channel_id=1, source_target_pairs={{0,2},{2,4},{4,6},{6,8},{8,10},{10,12},{12,14},{14,0},{1,3},{3,5},... | collective-permute-start | bytes 860168 | tf_op jit(solution)/shard_map/ppermute | solution.py:20
  59.1 4.3 %collective-permute-start.13 = (bf16[512,1280]{1,0:T(8,128)(2,1)S(1)}, bf16[512,1280]{1,0:T(8,128)(2,1)S(1)}, u32[]{:S(2)}, u32[]{:S(2)}) collective-permute-start(bf16[512,1280]{1,0:T(8,128)(2,1)S(1)} %get-tuple-element.72), channel_id=1, source_target_pairs={{0,64},{64,0},{1,65},{65,1},{2,66},{66,2},{3,67},{67,3},{4,68},{68... | collective-permute-start | bytes 3932168 | tf_op jit(solution)/shard_map/ppermute | solution.py:20
  63.6 16.2 %collective-permute-start.15 = (bf16[128,1280]{1,0:T(8,128)(2,1)S(1)}, bf16[128,1280]{1,0:T(8,128)(2,1)S(1)}, u32[]{:S(2)}, u32[]{:S(2)}) collective-permute-start(bf16[128,1280]{1,0:T(8,128)(2,1)S(1)} %get-tuple-element.76), channel_id=1, source_target_pairs={{0,32},{16,48},{32,0},{48,16},{1,33},{17,49},{33,1},{49,17},{2,34}... | collective-permute-start | bytes 983048 | tf_op jit(solution)/shard_map/ppermute | solution.py:20
  64.0 17.8 %collective-permute-start.16 = (bf16[128,1280]{1,0:T(8,128)(2,1)S(1)}, bf16[128,1280]{1,0:T(8,128)(2,1)S(1)}, u32[]{:S(2)}, u32[]{:S(2)}) collective-permute-start(bf16[128,1280]{1,0:T(8,128)(2,1)S(1)} %get-tuple-element.77), channel_id=1, source_target_pairs={{0,16},{16,32},{32,48},{48,0},{1,17},{17,33},{33,49},{49,1},{2,18}... | collective-permute-start | bytes 983048 | tf_op jit(solution)/shard_map/ppermute | solution.py:20
  64.3 17.5 %collective-permute-start.14 = (bf16[128,1280]{1,0:T(8,128)(2,1)S(1)}, bf16[128,1280]{1,0:T(8,128)(2,1)S(1)}, u32[]{:S(2)}, u32[]{:S(2)}) collective-permute-start(bf16[128,1280]{1,0:T(8,128)(2,1)S(1)} %get-tuple-element.75), channel_id=1, source_target_pairs={{0,48},{16,0},{32,16},{48,32},{1,49},{17,1},{33,17},{49,33},{2,50}... | collective-permute-start | bytes 983048 | tf_op jit(solution)/shard_map/ppermute | solution.py:20
  68.5 8.4 %collective-permute-start.19 = (bf16[56,2560]{1,0:T(8,128)(2,1)S(1)}, bf16[56,2560]{1,0:T(8,128)(2,1)S(1)}, u32[]{:S(2)}, u32[]{:S(2)}) collective-permute-start(bf16[56,2560]{1,0:T(8,128)(2,1)S(1)} %get-tuple-element.86), channel_id=1, source_target_pairs={{0,2},{2,4},{4,6},{6,8},{8,10},{10,12},{12,14},{14,0},{1,3},{3,5},... | collective-permute-start | bytes 860168 | tf_op jit(solution)/shard_map/ppermute | solution.py:20
  68.6 8.3 %collective-permute-start.20 = (bf16[56,2560]{1,0:T(8,128)(2,1)S(1)}, bf16[56,2560]{1,0:T(8,128)(2,1)S(1)}, u32[]{:S(2)}, u32[]{:S(2)}) collective-permute-start(bf16[56,2560]{1,0:T(8,128)(2,1)S(1)} %get-tuple-element.87), channel_id=1, source_target_pairs={{0,14},{2,0},{4,2},{6,4},{8,6},{10,8},{12,10},{14,12},{1,15},{3,1}... | collective-permute-start | bytes 860168 | tf_op jit(solution)/shard_map/ppermute | solution.py:20
  77.1 7.5 %collective-permute-start.22 = (bf16[56,2560]{1,0:T(8,128)(2,1)S(1)}, bf16[56,2560]{1,0:T(8,128)(2,1)S(1)}, u32[]{:S(2)}, u32[]{:S(2)}) collective-permute-start(bf16[56,2560]{1,0:T(8,128)(2,1)S(1)} %get-tuple-element.90), channel_id=1, source_target_pairs={{0,2},{2,4},{4,6},{6,8},{8,10},{10,12},{12,14},{14,0},{1,3},{3,5},... | collective-permute-start | bytes 860168 | tf_op jit(solution)/shard_map/ppermute | solution.py:20
  78.9 5.9 %collective-permute-start.23 = (bf16[56,2560]{1,0:T(8,128)(2,1)S(1)}, bf16[56,2560]{1,0:T(8,128)(2,1)S(1)}, u32[]{:S(2)}, u32[]{:S(2)}) collective-permute-start(bf16[56,2560]{1,0:T(8,128)(2,1)S(1)} %get-tuple-element.91), channel_id=1, source_target_pairs={{0,14},{2,0},{4,2},{6,4},{8,6},{10,8},{12,10},{14,12},{1,15},{3,1}... | collective-permute-start | bytes 860168 | tf_op jit(solution)/shard_map/ppermute | solution.py:20
  81.9 11.7 %copy-start.2 = (bf16[128,1728]{0,1:T(8,128)(2,1)S(1)}, bf16[128,1728]{0,1:T(8,128)(2,1)}, u32[]{:S(2)}) copy-start(bf16[128,1728]{0,1:T(8,128)(2,1)} %param.4) | copy-start | bytes 1327108
  81.9 11.7 %copy-start.4 = (bf16[128,1728]{0,1:T(8,128)(2,1)S(1)}, bf16[128,1728]{0,1:T(8,128)(2,1)}, u32[]{:S(2)}) copy-start(bf16[128,1728]{0,1:T(8,128)(2,1)} %param.5) | copy-start | bytes 1327108
  81.9 8.6 %collective-permute-start.21 = (bf16[128,1280]{1,0:T(8,128)(2,1)S(1)}, bf16[128,1280]{1,0:T(8,128)(2,1)S(1)}, u32[]{:S(2)}, u32[]{:S(2)}) collective-permute-start(bf16[128,1280]{1,0:T(8,128)(2,1)S(1)} %shard_map.87), channel_id=1, source_target_pairs={{0,128},{128,0},{1,129},{129,1},{2,130},{130,2},{3,131},{131,3},{4... | collective-permute-start | bytes 983048 | tf_op jit(solution)/shard_map/ppermute | solution.py:20
  82.4 11.2 %collective-permute-start.26 = (bf16[512,128]{1,0:T(8,128)(2,1)S(1)}, bf16[512,128]{1,0:T(8,128)(2,1)S(1)}, u32[]{:S(2)}, u32[]{:S(2)}) collective-permute-start(bf16[512,128]{1,0:T(8,128)(2,1)S(1)} %get-tuple-element.81), channel_id=1, source_target_pairs={{0,48},{16,0},{32,16},{48,32},{1,49},{17,1},{33,17},{49,33},{2,50}... | collective-permute-start | bytes 393224 | tf_op jit(solution)/shard_map/ppermute | solution.py:20
  82.5 11.1 %collective-permute-start.28 = (bf16[512,128]{1,0:T(8,128)(2,1)S(1)}, bf16[512,128]{1,0:T(8,128)(2,1)S(1)}, u32[]{:S(2)}, u32[]{:S(2)}) collective-permute-start(bf16[512,128]{1,0:T(8,128)(2,1)S(1)} %get-tuple-element.83), channel_id=1, source_target_pairs={{0,16},{16,32},{32,48},{48,0},{1,17},{17,33},{33,49},{49,1},{2,18}... | collective-permute-start | bytes 393224 | tf_op jit(solution)/shard_map/ppermute | solution.py:20
  85.1 9.9 %collective-permute-start.25 = (bf16[27,2560]{1,0:T(8,128)(2,1)S(1)}, bf16[27,2560]{1,0:T(8,128)(2,1)S(1)}, u32[]{:S(2)}, u32[]{:S(2)}) collective-permute-start(bf16[27,2560]{1,0:T(8,128)(2,1)S(1)} %get-tuple-element.97), channel_id=1, source_target_pairs={{0,1},{1,0},{2,3},{3,2},{4,5},{5,4},{6,7},{7,6},{8,9},{9,8},{10,11... | collective-permute-start | bytes 414728 | tf_op jit(solution)/shard_map/ppermute | solution.py:20
  85.8 7.8 %collective-permute-start.27 = (bf16[512,128]{1,0:T(8,128)(2,1)S(1)}, bf16[512,128]{1,0:T(8,128)(2,1)S(1)}, u32[]{:S(2)}, u32[]{:S(2)}) collective-permute-start(bf16[512,128]{1,0:T(8,128)(2,1)S(1)} %get-tuple-element.101), channel_id=1, source_target_pairs={{0,32},{16,48},{32,0},{48,16},{1,33},{17,49},{33,1},{49,17},{2,34}... | collective-permute-start | bytes 393224 | tf_op jit(solution)/shard_map/ppermute | solution.py:20
  90.6 5.1 %collective-permute-start.24 = (bf16[128,1280]{1,0:T(8,128)(2,1)S(1)}, bf16[128,1280]{1,0:T(8,128)(2,1)S(1)}, u32[]{:S(2)}, u32[]{:S(2)}) collective-permute-start(bf16[128,1280]{1,0:T(8,128)(2,1)S(1)} %add_convert_fusion.mine), channel_id=1, source_target_pairs={{0,64},{64,0},{1,65},{65,1},{2,66},{66,2},{3,67},{67,3},{4,68},{68... | collective-permute-start | bytes 983048 | tf_op jit(solution)/shard_map/ppermute | solution.py:20

commit v4 on v3

--- a/solution.py
+++ b/solution.py
@@ -24,15 +24,14 @@
     return lax.optimization_barrier((value, others))[0]
 
 
-def call(kernel, outs, *args, scratch=(), limit=24, flops=0, moved=None):
-    whole = pl.BlockSpec(memory_space=pltpu.VMEM)
+def call(kernel, outs, *args, scratch=(), limit=24, flops=0, moved=None, space=pltpu.VMEM, out_space=pltpu.VMEM):
     if moved is None:
         moved = sum(a.size * a.dtype.itemsize for a in args + tuple(outs))
     return pl.pallas_call(
         kernel,
         out_shape=outs,
-        in_specs=[whole] * len(args),
-        out_specs=[whole] * len(outs),
+        in_specs=[pl.BlockSpec(memory_space=space)] * len(args),
+        out_specs=[pl.BlockSpec(memory_space=out_space)] * len(outs),
         scratch_shapes=list(scratch),
         compiler_params=pltpu.CompilerParams(vmem_limit_bytes=limit * 2**20),
         cost_estimate=pl.CostEstimate(flops=flops, bytes_accessed=moved, transcendentals=0),
@@ -68,34 +67,53 @@
     store_swapped(lax.axis_index("core"), out, both.astype(BF16))
 
 
-def prepare(gate, up, cot, m1, m2, m3, hid_own, cot_own, hidden):
-    gate32, up32 = gate[...].astype(F32), up[...].astype(F32)
+def prepare(gate_hbm, up_hbm, cot_hbm, m1, m2, m3, hid_own, cot_own, cot, gate, up, hidden, slots, sems):
     units, rows = gate.shape
-    half = cot.shape[1] // 2
-    used = units // (NX * NZ)
-    hidden[:units] = (gate32 * jax.nn.sigmoid(gate32) * up32).astype(BF16).astype(F32)
+    half = cot_hbm.shape[1] // 2
+    part = units // NX
+    used = part // NZ
+    x, core = lax.axis_index("x"), lax.axis_index("core")
+    started = []
+
+    def copy(source, to):
+        started.append(pltpu.make_async_copy(source, to, sems.at[len(started)]))
+        started[-1].start()
+        return started[-1]
+
+    cot_loads = []
+    for s in range(NX):
+        here = pl.ds(s * (rows // NX), rows // NX)
+        cot_loads.append(copy(cot_hbm.at[here], cot.at[here]))
+    loads = []
+    for s in range(NX):
+        here = pl.ds(s * part, part)
+        loads.append([copy(gate_hbm.at[here], gate.at[here]), copy(up_hbm.at[here], up.at[here])])
+    for load in cot_loads:
+        load.wait()
+    mine = cot.at[:, pl.ds(pl.multiple_of(core * half, half), half)]
+    other = cot.at[:, pl.ds(pl.multiple_of((1 - core) * half, half), half)]
+    for out in (m1, m2, m3, cot_own):
+        copy(mine, out.at[:, pl.ds(0, half)])
+    copy(other, cot_own.at[:, pl.ds(half, half)])
     inside = lax.broadcasted_iota(jnp.int32, (SLOT, rows), 0) < used
-    padded = [
-        jnp.where(inside, hidden[used * b : used * b + SLOT], 0.0).astype(BF16)
-        for b in range(NX * NZ)
-    ]
-    for x in range(NX):
-
-        @pl.when(lax.axis_index("x") == x)
-        def _(x=x):
-            for k, out in enumerate((hid_own, m1, m2, m3)):
-                for block in range(NZ):
-                    value = padded[(x + k) % NX * NZ + block]
-                    if k == 0:
-                        out[block * SLOT : (block + 1) * SLOT] = value
-                    else:
-                        row, column = block * SLOT % rows, half + block * SLOT // rows * rows
-                        out[row : row + SLOT, column : column + rows] = value
-
-    core = lax.axis_index("core")
-    store_swapped(core, cot_own, cot[...])
-    for out in (m1, m2, m3):
-        out[:, :half] = cot_own[:, :half]
+    for s in range(NX):
+        for load in loads[s]:
+            load.wait()
+        here = slice(s * part, (s + 1) * part)
+        gate32, up32 = gate[here].astype(F32), up[here].astype(F32)
+        hidden[here] = (gate32 * jax.nn.sigmoid(gate32) * up32).astype(BF16).astype(F32)
+        for block in range(NZ):
+            start = s * part + used * block
+            value = jnp.where(inside, hidden[start : start + SLOT], 0.0).astype(BF16)
+            row, column = block * SLOT % rows, block * SLOT // rows * rows
+            slots[s, row : row + SLOT, column : column + rows] = value
+    for k, out in enumerate((m1, m2, m3)):
+        copy(slots.at[lax.rem(x + k + 1, NX)], out.at[:, pl.ds(half, NZ * SLOT)])
+    for i in range(NZ * SLOT // rows):
+        here = pl.ds(i * rows, rows)
+        copy(slots.at[x, :, here], hid_own.at[here])
+    for last in started[3 * NX :]:
+        last.wait()
 
 
 def stack_halves(g1, g2, g3, out):
@@ -136,50 +154,67 @@
     hid[...] = hid_t[...].T
 
 
-def first_rows(value, out):
-    out[...] = value[: out.shape[0], : out.shape[1]]
-
-
-def output_other(w0, f1, f2, f3, f4, b3, b2, b1, hid, mark, out, weight):
+def near_blocks(w0, f1, f2, f3, b3, b2, b1, hid, weight, product, opposite, mark):
     z = lax.axis_index("z")
-    half = w0.shape[1] // 2
-    for distance, piece in enumerate((w0, f1, f2, f3, f4, b3, b2, b1)):
+    width = w0.shape[1]
+    for distance, piece in enumerate((w0, f1, f2, f3, None, b3, b2, b1)):
         to = lax.rem(z - distance + NZ, NZ)
-        weight[to, :SENT] = piece[...]
-        weight[to, SENT:] = jnp.zeros((SLOT - SENT, w0.shape[1]), BF16)
-
-    @pl.loop(0, half // TILE)
-    def _(t):
-        columns = pl.ds(pl.multiple_of(half + t * TILE, TILE), TILE)
-        rhs = weight[:, :, columns].reshape(NZ * SLOT, TILE)
-        product = jnp.dot(hid[...], rhs, preferred_element_type=F32)
-        out[:, pl.ds(pl.multiple_of(t * TILE, TILE), TILE)] = product.astype(BF16)
-
-
-def output_mine(hid, weight, out):
-    half = weight.shape[2] // 2
-
-    @pl.loop(0, half // TILE)
+        if piece is None:
+            weight[to] = jnp.zeros((SLOT, width), BF16)
+        else:
+            weight[to, :SENT] = piece[...]
+            weight[to, SENT:] = jnp.zeros((SLOT - SENT, width), BF16)
+
+    @pl.loop(0, width // TILE)
     def _(t):
         columns = pl.ds(pl.multiple_of(t * TILE, TILE), TILE)
         rhs = weight[:, :, columns].reshape(NZ * SLOT, TILE)
-        out[:, columns] = jnp.dot(hid[...], rhs, preferred_element_type=F32)
-
-
-def back_parts(cot, weight, *parts):
+        product[:, columns] = jnp.dot(hid[...], rhs, preferred_element_type=F32)
+
+    for block in range(NZ):
+
+        @pl.when(z == (block + NZ // 2) % NZ)
+        def _(block=block):
+            opposite[...] = hid[:, block * SLOT : (block + 1) * SLOT]
+
+    mark[...] = w0[: mark.shape[0], : mark.shape[1]]
+
+
+def with_opposite(first, product, opposite, block, out):
+    rhs = jnp.concatenate([block[...], jnp.zeros((SLOT - SENT, block.shape[1]), BF16)], 0)
+    width = out.shape[1]
+    for t in range(width // TILE):
+        to = slice(t * TILE, (t + 1) * TILE)
+        here = slice(first + t * TILE, first + (t + 1) * TILE)
+        more = jnp.dot(opposite[...], rhs[:, here], preferred_element_type=F32)
+        out[:, to] = (product[:, here] + more).astype(out.dtype)
+
+
+def first_rows(value, out):
+    out[...] = value[: out.shape[0], : out.shape[1]]
+
+
+def back_parts(cot, weight, block, *parts):
     slots = TILE // SLOT
     rows = parts[0].shape[1]
+    dims = (((1,), (1,)), ((), ()))
 
     @pl.loop(0, NZ // slots)
     def _(t):
         some = weight[pl.ds(t * slots, slots)].reshape(TILE, weight.shape[2])
-        product = lax.dot_general(
-            some, cot[...], (((1,), (1,)), ((), ())), preferred_element_type=F32
-        )
+        product = lax.dot_general(some, cot[...], dims, preferred_element_type=F32)
         for k, part in enumerate(parts):
             part[pl.ds(pl.multiple_of(t * TILE, TILE), TILE)] = product[
                 :, k * rows : (k + 1) * rows
             ].astype(BF16)
+
+    opposite = lax.rem(lax.axis_index("z") + NZ // 2, NZ)
+    rhs = jnp.concatenate([block[...], jnp.zeros((SLOT - SENT, block.shape[1]), BF16)], 0)
+    product = lax.dot_general(rhs, cot[...], dims, preferred_element_type=F32)
+    for k, part in enumerate(parts):
+        part[pl.ds(pl.multiple_of(opposite * SLOT, SLOT), SLOT)] = product[
+            :, k * rows : (k + 1) * rows
+        ].astype(BF16)
 
 
 def pack_output(mine, crossed, total, m1, m2, m3):
@@ -210,8 +245,8 @@
     grad_up[...] = (back32[...] * (gate32 * sig)).astype(BF16)
 
 
-def add_pieces(distance, pieces, *refs):
-    *sums, to_fwd, to_bwd = refs
+def add_pieces(distance, others, pieces, *refs):
+    *sums, to_fwd, to_bwd = refs[others:]
     here = pieces[distance]
     if len(sums) > 1:
         here = here + sums[0][...].astype(F32)
@@ -235,7 +270,7 @@
         give[...] = total[:rows].astype(BF16)
 
 
-def place_output(mine, other, out):
+def finish(mine, other, keep, taken, out, grad):
     half = mine.shape[1]
 
     @pl.when(lax.axis_index("core") == 0)
@@ -247,6 +282,8 @@
     def _():
         out[:, :half] = other[...]
         out[:, half:] = mine[...]
+
+    grad[...] = keep[...] + taken[...].astype(F32)
 
 
 def body(gate_pre, up_pre, down_weight, cotangent):
@@ -263,7 +300,13 @@
         prepare,
         [like((rows, wide))] * 3 + [like((slots, rows)), like((rows, width))],
         gate, up, cotangent,
-        scratch=[pltpu.VMEM((units + SLOT, rows), F32)],
+        scratch=[pltpu.VMEM((rows, width), BF16)]
+        + [pltpu.VMEM((units, rows), BF16)] * 2
+        + [pltpu.VMEM((units + SLOT, rows), F32), pltpu.VMEM((NX, rows, slots), BF16)]
+        + [pltpu.SemaphoreType.DMA((3 * NX + 8 + slots // rows,))],
+        out_space=pltpu.HBM,
+        space=pltpu.HBM,
+        limit=56,
     )
     w_other = after(w_other, m1, m2, m3)
     (w0,) = call(pack_weight, [like((SENT, width))], down_weight, w_other)
@@ -290,42 +333,53 @@
         flops=2 * slots * tokens * width,
     )
 
-    def added(distance, ring):
-        kernel = functools.partial(add_pieces, distance)
-        return call(kernel, [like((SENT, width))] * 2, pieces, *ring, moved=0)
+    def added(distance, ring, *others):
+        kernel = functools.partial(add_pieces, distance, len(others))
+        return call(kernel, [like((SENT, width))] * 2, pieces, *others, *ring, moved=0)
 
     f4 = shift(fwd[3], "z", 1)
     ring = (shift(to_bwd, "z", -1),)
-    to_fwd, to_bwd = added(3, ring)
+
+    weight, product, opposite, early = call(
+        near_blocks,
+        [like((NZ, SLOT, width)), like((tokens, width), F32), like((tokens, SLOT)), like((16, 128))],
+        *fwd, *reversed(bwd[1:]), hid,
+        moved=0,
+    )
+    to_fwd, to_bwd = added(3, ring, early)
     ring = (shift(to_fwd, "z", 1), shift(to_bwd, "z", -1))
 
     (mark,) = call(first_rows, [like((16, 128))], to_fwd, flops=2 * 10**9)
-    out_other, weight = call(
-        output_other,
-        [like((tokens, half)), like((NZ, SLOT, width))],
-        *fwd, f4, *reversed(bwd[1:]), hid, mark,
+    (out_other,) = call(
+        lambda product, opposite, block, mark, out: with_opposite(half, product, opposite, block, out),
+        [like((tokens, half))],
+        product, opposite, f4, mark,
         flops=2 * slots * tokens * half,
     )
     crossed = shift(out_other, "core", 1)
     (out_mine,) = call(
-        output_mine, [like((tokens, half), F32)], hid, weight, flops=14 * 10**9
+        functools.partial(with_opposite, 0),
+        [like((tokens, half), F32)],
+        product, opposite, f4,
+        flops=14 * 10**9,
     )
     crossed = after(crossed, out_mine)
     total, m1, m2, m3 = call(
         pack_output,
         [like((rows, half), F32)] + [like((rows, half))] * 3,
         out_mine, crossed,
-        flops=4 * 10**9,
+        flops=2 * 10**9,
     )
     got_out = [shift(m, "x", -k) for k, m in ((1, m1), (2, m2), (3, m3))]
     back_own, *backs = call(
-        back_parts, [like((slots, rows))] * NX, after(cot, m1), weight, moved=0
+        back_parts, [like((slots, rows))] * NX, after(cot, m1), weight, f4, moved=0
     )
     back1, back2, back3 = backs
+    ring = after(ring, m1, m2, m3)
+    to_fwd, to_bwd = added(2, ring)
+    ring = (shift(to_fwd, "z", 1), shift(to_bwd, "z", -1))
+    *ring, back1, back2, back3 = lax.optimization_barrier((*ring, back1, back2, back3))
     got_back1, got_back3 = shift(back1, "x", -1), shift(back3, "x", -3)
-    ring = after(ring, back1, back2, back3)
-    to_fwd, to_bwd = added(2, ring)
-    ring = lax.optimization_barrier((shift(to_fwd, "z", 1), shift(to_bwd, "z", -1)))
     to_fwd, to_bwd = added(1, ring)
     got_out = after(got_out, to_fwd, to_bwd)
     ring = (shift(to_fwd, "z", 1), shift(to_bwd, "z", -1))
@@ -347,13 +401,16 @@
         [like((units, rows))] * 2,
         gate, up, back_own, got_back1, got_back2, got_back3,
         scratch=[pltpu.VMEM((units, rows), F32)],
-        flops=60 * 10**7,
+        flops=400 * 10**7,
         moved=0,
     )
     across = after(across, give)
     out_half = (rounded.astype(F32) + across.astype(F32)).astype(BF16)
-    (output,) = call(place_output, [like((rows, width))], out_half, shift(out_half, "core", 1))
-    grad_weight = keep + taken.astype(F32)
+    output, grad_weight = call(
+        finish,
+        [like((rows, width)), like((block, width), F32)],
+        out_half, shift(out_half, "core", 1), keep, taken,
+    )
     return output, grad_weight, grad_gate.T, grad_up.T
 
 

time: 97 us -> 93.8 us (0.967)
  waiting for transfers between devices: 31.8 us -> 27.7 us
  Pallas kernels: 12.6 us -> 16.6 us
  local copies, waits for them, and re-layouts: 4.04 us -> 0.94 us
  starting transfers between devices: 46.5 us -> 47.5 us
    ppermute x29, waiting for transfers between devices: 31.8 us -> 27.7 us  [shift(): lax.ppermute(value, axis, [(i, (i + steps) % count) for i in range(count)])]
    pallas_call x16 -> x17, Pallas kernels: 12.6 us -> 16.6 us  [call(): pl.pallas_call(kernel, out_shape=outs, in_specs=[pl.BlockSpec(memory_spac...]
    unnamed x12 -> x10, local copies, waits for them, and re-layouts: 4.04 us -> 0.94 us
    ppermute x29, starting transfers between devices: 46.5 us -> 47.5 us  [shift(): lax.ppermute(value, axis, [(i, (i + steps) % count) for i in range(count)])]
  transfers between devices with their start and end apart: 29 -> 29, of which waited for: 13 -> 13; matrix products, arithmetic and copies ran while one was open for 1% -> 0% of each run, Pallas kernels for 12% -> 17%
where the time goes in v4:
time: 93.8 us; the launch traced here: 93.7 us
  starting transfers between devices  47.5 us (51%)
  waiting for transfers between devices  27.7 us (30%)
  Pallas kernels  16.6 us (18%)
  local copies, waits for them, and re-layouts  0.94 us (1%)
    ppermute x29, starting transfers between devices, shift(): lax.ppermute(value, axis, [(i, (i + steps) % count) for i in range(count)])  47.5 us
    ppermute x29, waiting for transfers between devices, shift(): lax.ppermute(value, axis, [(i, (i + steps) % count) for i in range(count)])  27.7 us
    pallas_call x17, Pallas kernels, call(): pl.pallas_call(kernel, out_shape=outs, in_specs=[pl.BlockSpec(memory_spac...  16.6 us
  transfers between devices with their start and end apart: 29, of which 13 were waited for; matrix products, arithmetic and copies ran while one was open for 0% of the time, Pallas kernels for 17%

profile of v4, /device:TPU:1, one launch (start us, length us, event | category | flops | bytes accessed | tf_op | source)
XLA Modules:
  0.0 93.7 jit_solution(2536686652842602371)
XLA Ops:
  0.6 3.8 %collective-permute-start = (bf16[27,2560]{1,0:T(8,128)(2,1)}, bf16[27,2560]{1,0:T(8,128)(2,1)S(1)}, u32[]{:S(2)}, u32[]{:S(2)}) collective-permute-start(bf16[27,2560]{1,0:T(8,128)(2,1)} %mine.1), channel_id=1, source_target_pairs={{0,1},{1,0},{2,3},{3,2},{4,5},{5,4},{6,7},{7,6},{8,9},{9,8},{10,11... | collective-permute-start | bytes 414728 | tf_op jit(solution)/shard_map/ppermute | solution.py:20
  4.5 2.7 %shard_map.75 = (bf16[128,1792]{1,0:T(8,128)(2,1)}, bf16[128,1792]{1,0:T(8,128)(2,1)}, bf16[128,1792]{1,0:T(8,128)(2,1)}, bf16[512,128]{1,0:T(8,128)(2,1)}, bf16[128,2560]{1,0:T(8,128)(2,1)}) custom-call(bf16[1728,128]{1,0:T(8,128)(2,1)} %bitcast.4, bf16[1728,128]{1,0:T(8,128)(2,1)} %bitcast.6, bf16[128,2560]{1,0:T(8,128)(2,1)} %cot_hbm.1), custom_call_target="tpu_custom_call" | custom-call | bytes 3702784 | tf_op jit(solution)/shard_map/pallas_call | solution.py:30
  7.1 1.3 %collective-permute-start.5 = (bf16[128,1792]{1,0:T(8,128)(2,1)}, bf16[128,1792]{1,0:T(8,128)(2,1)S(1)}, u32[]{:S(2)}, u32[]{:S(2)}) collective-permute-start(bf16[128,1792]{1,0:T(8,128)(2,1)} %get-tuple-element.61), channel_id=1, source_target_pairs={{0,16},{16,32},{32,48},{48,0},{1,17},{17,33},{33,49},{49,1},{2,18}... | collective-permute-start | bytes 1376264 | tf_op jit(solution)/shard_map/ppermute | solution.py:20
  8.4 2.5 %collective-permute-start.6 = (bf16[128,1792]{1,0:T(8,128)(2,1)}, bf16[128,1792]{1,0:T(8,128)(2,1)S(1)}, u32[]{:S(2)}, u32[]{:S(2)}) collective-permute-start(bf16[128,1792]{1,0:T(8,128)(2,1)} %get-tuple-element.62), channel_id=1, source_target_pairs={{0,32},{16,48},{32,0},{48,16},{1,33},{17,49},{33,1},{49,17},{2,34}... | collective-permute-start | bytes 1376264 | tf_op jit(solution)/shard_map/ppermute | solution.py:20
  10.9 1.2 %collective-permute-start.7 = (bf16[128,1792]{1,0:T(8,128)(2,1)}, bf16[128,1792]{1,0:T(8,128)(2,1)S(1)}, u32[]{:S(2)}, u32[]{:S(2)}) collective-permute-start(bf16[128,1792]{1,0:T(8,128)(2,1)} %get-tuple-element.63), channel_id=1, source_target_pairs={{0,48},{16,0},{32,16},{48,32},{1,49},{17,1},{33,17},{49,33},{2,50}... | collective-permute-start | bytes 1376264 | tf_op jit(solution)/shard_map/ppermute | solution.py:20
  12.0 0.0 collective-permute-done.other
  12.0 0.9 copy-done.2
  13.0 0.3 shard_map.76.w0
  13.3 0.0 copy-start.3
  13.3 0.0 copy-start.4
  13.3 5.7 %collective-permute-start.2 = (bf16[56,2560]{1,0:T(8,128)(2,1)S(1)}, bf16[56,2560]{1,0:T(8,128)(2,1)S(1)}, u32[]{:S(2)}, u32[]{:S(2)}) collective-permute-start(bf16[56,2560]{1,0:T(8,128)(2,1)S(1)} %shard_map.76.w0), channel_id=1, source_target_pairs={{0,14},{2,0},{4,2},{6,4},{8,6},{10,8},{12,10},{14,12},{1,15},{3,1}... | collective-permute-start | bytes 860168 | tf_op jit(solution)/shard_map/ppermute | solution.py:20
  19.0 0.0 collective-permute-start.1
  19.0 4.3 %collective-permute-done.2.b1 = bf16[56,2560]{1,0:T(8,128)(2,1)S(1)} collective-permute-done((bf16[56,2560]{1,0:T(8,128)(2,1)S(1)}, bf16[56,2560]{1,0:T(8,128)(2,1)S(1)}, u32[]{:S(2)}, u32[]{:S(2)}) %collective-permute-start.2) | collective-permute-done | bytes 286752 | tf_op jit(solution)/shard_map/ppermute | solution.py:20
  23.3 3.1 %collective-permute-done.1.f1 = bf16[56,2560]{1,0:T(8,128)(2,1)S(1)} collective-permute-done((bf16[56,2560]{1,0:T(8,128)(2,1)S(1)}, bf16[56,2560]{1,0:T(8,128)(2,1)S(1)}, u32[]{:S(2)}, u32[]{:S(2)}) %collective-permute-start.1) | collective-permute-done | bytes 286752 | tf_op jit(solution)/shard_map/ppermute | solution.py:20
  26.4 0.0 collective-permute-start.3
  26.4 2.7 %collective-permute-start.4 = (bf16[56,2560]{1,0:T(8,128)(2,1)S(1)}, bf16[56,2560]{1,0:T(8,128)(2,1)S(1)}, u32[]{:S(2)}, u32[]{:S(2)}) collective-permute-start(bf16[56,2560]{1,0:T(8,128)(2,1)S(1)} %collective-permute-done.2.b1), channel_id=1, source_target_pairs={{0,14},{2,0},{4,2},{6,4},{8,6},{10,8},{12,10},{14,12},{1,15},{3,1}... | collective-permute-start | bytes 860168 | tf_op jit(solution)/shard_map/ppermute | solution.py:20
  29.1 1.4 %collective-permute-done.6.g2 = bf16[128,1792]{1,0:T(8,128)(2,1)S(1)} collective-permute-done((bf16[128,1792]{1,0:T(8,128)(2,1)}, bf16[128,1792]{1,0:T(8,128)(2,1)S(1)}, u32[]{:S(2)}, u32[]{:S(2)}) %collective-permute-start.6) | collective-permute-done | bytes 458784 | tf_op jit(solution)/shard_map/ppermute | solution.py:20
  30.5 0.1 collective-permute-done.7.g3
  30.6 0.1 shard_map.77
  30.6 2.5 %collective-permute-done.3.f2 = bf16[56,2560]{1,0:T(8,128)(2,1)S(1)} collective-permute-done((bf16[56,2560]{1,0:T(8,128)(2,1)S(1)}, bf16[56,2560]{1,0:T(8,128)(2,1)S(1)}, u32[]{:S(2)}, u32[]{:S(2)}) %collective-permute-start.3) | collective-permute-done | bytes 286752 | tf_op jit(solution)/shard_map/ppermute | solution.py:20
  33.1 4.2 %collective-permute-start.10 = (bf16[384,1280]{1,0:T(8,128)(2,1)S(1)}, bf16[384,1280]{1,0:T(8,128)(2,1)S(1)}, u32[]{:S(2)}, u32[]{:S(2)}) collective-permute-start(bf16[384,1280]{1,0:T(8,128)(2,1)S(1)} %shard_map.77), channel_id=1, source_target_pairs={{0,64},{64,0},{1,65},{65,1},{2,66},{66,2},{3,67},{67,3},{4,68},{68... | collective-permute-start | bytes 2949128 | tf_op jit(solution)/shard_map/ppermute | solution.py:20
  37.3 0.0 collective-permute-start.8
  37.3 3.0 %collective-permute-start.9 = (bf16[56,2560]{1,0:T(8,128)(2,1)S(1)}, bf16[56,2560]{1,0:T(8,128)(2,1)S(1)}, u32[]{:S(2)}, u32[]{:S(2)}) collective-permute-start(bf16[56,2560]{1,0:T(8,128)(2,1)S(1)} %collective-permute-done.4.b2), channel_id=1, source_target_pairs={{0,14},{2,0},{4,2},{6,4},{8,6},{10,8},{12,10},{14,12},{1,15},{3,1}... | collective-permute-start | bytes 860168 | tf_op jit(solution)/shard_map/ppermute | solution.py:20
  40.2 0.0 collective-permute-done.10.far
  40.2 3.4 %shard_map.78 = (f32[8,56,2560]{2,1,0:T(8,128)S(1)}, bf16[56,2560]{1,0:T(8,128)(2,1)S(1)}, bf16[512,2560]{1,0:T(8,128)(2,1)S(1)}, bf16[512,512]{1,0:T(8,128)(2,1)S(1)}) custom-call(bf16[128,2560]{1,0:T(8,128)(2,1)S(1)} %copy-done.3, bf16[512,128]{1,0:T(8,128)(2,1)S(1)} %copy-done.4, bf16[128,1792]{1,0:T(8,128)(2,1)S(1)} %collective-permute-done.5.g1, ...), custom_call_target="tpu_custom_call" | custom-call | flops 1342177280 | bytes 11165696 | tf_op jit(solution)/shard_map/pallas_call | solution.py:30
  43.7 2.3 %collective-permute-start.12 = (bf16[56,2560]{1,0:T(8,128)(2,1)S(1)}, bf16[56,2560]{1,0:T(8,128)(2,1)S(1)}, u32[]{:S(2)}, u32[]{:S(2)}) collective-permute-start(bf16[56,2560]{1,0:T(8,128)(2,1)S(1)} %get-tuple-element.79), channel_id=1, source_target_pairs={{0,14},{2,0},{4,2},{6,4},{8,6},{10,8},{12,10},{14,12},{1,15},{3,1}... | collective-permute-start | bytes 860168 | tf_op jit(solution)/shard_map/ppermute | solution.py:20
  45.9 1.5 %collective-permute-done.8.f3 = bf16[56,2560]{1,0:T(8,128)(2,1)S(1)} collective-permute-done((bf16[56,2560]{1,0:T(8,128)(2,1)S(1)}, bf16[56,2560]{1,0:T(8,128)(2,1)S(1)}, u32[]{:S(2)}, u32[]{:S(2)}) %collective-permute-start.8) | collective-permute-done | bytes 286752 | tf_op jit(solution)/shard_map/ppermute | solution.py:20
  47.4 3.2 %shard_map.79 = (bf16[8,64,2560]{2,1,0:T(8,128)(2,1)S(1)}, f32[512,2560]{1,0:T(8,128)S(1)}, bf16[512,64]{1,0:T(8,128)(2,1)S(1)}, bf16[16,128]{1,0:T(8,128)(2,1)S(1)}) custom-call(bf16[56,2560]{1,0:T(8,128)(2,1)S(1)} %shard_map.76.w0, bf16[56,2560]{1,0:T(8,128)(2,1)S(1)} %collective-permute-done.1.f1, bf16[56,2560]{1,0:T(8,128)(2,1)S(1)} %collective-permute-done.3.f2, ...), custom_call_target="tpu_custom_call" | custom-call | tf_op jit(solution)/shard_map/pallas_call | solution.py:30
  50.7 1.9 %collective-permute-done.12.refs_1_ = bf16[56,2560]{1,0:T(8,128)(2,1)S(1)} collective-permute-done((bf16[56,2560]{1,0:T(8,128)(2,1)S(1)}, bf16[56,2560]{1,0:T(8,128)(2,1)S(1)}, u32[]{:S(2)}, u32[]{:S(2)}) %collective-permute-start.12) | collective-permute-done | bytes 286752 | tf_op jit(solution)/shard_map/ppermute | solution.py:20
  52.6 0.1 shard_map.81
  52.7 3.7 %collective-permute-start.18 = (bf16[56,2560]{1,0:T(8,128)(2,1)S(1)}, bf16[56,2560]{1,0:T(8,128)(2,1)S(1)}, u32[]{:S(2)}, u32[]{:S(2)}) collective-permute-start(bf16[56,2560]{1,0:T(8,128)(2,1)S(1)} %get-tuple-element.86), channel_id=1, source_target_pairs={{0,14},{2,0},{4,2},{6,4},{8,6},{10,8},{12,10},{14,12},{1,15},{3,1}... | collective-permute-start | bytes 860168 | tf_op jit(solution)/shard_map/ppermute | solution.py:20
  56.3 0.5 shard_map.83
  56.8 1.6 %collective-permute-start.13 = (bf16[512,1280]{1,0:T(8,128)(2,1)S(1)}, bf16[512,1280]{1,0:T(8,128)(2,1)S(1)}, u32[]{:S(2)}, u32[]{:S(2)}) collective-permute-start(bf16[512,1280]{1,0:T(8,128)(2,1)S(1)} %shard_map.83), channel_id=1, source_target_pairs={{0,64},{64,0},{1,65},{65,1},{2,66},{66,2},{3,67},{67,3},{4,68},{68... | collective-permute-start | bytes 3932168 | tf_op jit(solution)/shard_map/ppermute | solution.py:20
  58.5 0.5 shard_map.80.mine
  58.9 2.2 %collective-permute-done.13.crossed = bf16[512,1280]{1,0:T(8,128)(2,1)S(1)} collective-permute-done((bf16[512,1280]{1,0:T(8,128)(2,1)S(1)}, bf16[512,1280]{1,0:T(8,128)(2,1)S(1)}, u32[]{:S(2)}, u32[]{:S(2)}) %collective-permute-start.13) | collective-permute-done | bytes 1310752 | tf_op jit(solution)/shard_map/ppermute | solution.py:20
  61.1 0.2 shard_map.84
  61.3 0.3 collective-permute-start.15
  61.6 0.4 collective-permute-start.16
  62.0 2.3 %collective-permute-start.14 = (bf16[128,1280]{1,0:T(8,128)(2,1)S(1)}, bf16[128,1280]{1,0:T(8,128)(2,1)S(1)}, u32[]{:S(2)}, u32[]{:S(2)}) collective-permute-start(bf16[128,1280]{1,0:T(8,128)(2,1)S(1)} %get-tuple-element.83), channel_id=1, source_target_pairs={{0,48},{16,0},{32,16},{48,32},{1,49},{17,1},{33,17},{49,33},{2,50}... | collective-permute-start | bytes 983048 | tf_op jit(solution)/shard_map/ppermute | solution.py:20
  64.3 0.4 collective-permute-done.17.refs_0_
  64.7 0.1 shard_map.85
  64.9 0.1 collective-permute-start.19
  64.9 2.7 %collective-permute-start.20 = (bf16[56,2560]{1,0:T(8,128)(2,1)S(1)}, bf16[56,2560]{1,0:T(8,128)(2,1)S(1)}, u32[]{:S(2)}, u32[]{:S(2)}) collective-permute-start(bf16[56,2560]{1,0:T(8,128)(2,1)S(1)} %get-tuple-element.90), channel_id=1, source_target_pairs={{0,14},{2,0},{4,2},{6,4},{8,6},{10,8},{12,10},{14,12},{1,15},{3,1}... | collective-permute-start | bytes 860168 | tf_op jit(solution)/shard_map/ppermute | solution.py:20
  67.6 2.6 %shard_map.86 = (bf16[512,128]{1,0:T(8,128)(2,1)S(1)}, bf16[512,128]{1,0:T(8,128)(2,1)S(1)}, bf16[512,128]{1,0:T(8,128)(2,1)S(1)}, bf16[512,128]{1,0:T(8,128)(2,1)S(1)}) custom-call(bf16[512,2560]{1,0:T(8,128)(2,1)S(1)} %get-tuple-element.92.cot, bf16[8,64,2560]{2,1,0:T(8,128)(2,1)S(1)} %get-tuple-element.93.weight, ...), custom_call_target="tpu_custom_call" | custom-call | tf_op jit(solution)/shard_map/pallas_call | solution.py:30
  70.3 2.2 %collective-permute-done.19.refs_0_ = bf16[56,2560]{1,0:T(8,128)(2,1)S(1)} collective-permute-done((bf16[56,2560]{1,0:T(8,128)(2,1)S(1)}, bf16[56,2560]{1,0:T(8,128)(2,1)S(1)}, u32[]{:S(2)}, u32[]{:S(2)}) %collective-permute-start.19) | collective-permute-done | bytes 286752 | tf_op jit(solution)/shard_map/ppermute | solution.py:20
  72.4 0.1 shard_map.87
  72.6 2.6 %collective-permute-start.22 = (bf16[56,2560]{1,0:T(8,128)(2,1)S(1)}, bf16[56,2560]{1,0:T(8,128)(2,1)S(1)}, u32[]{:S(2)}, u32[]{:S(2)}) collective-permute-start(bf16[56,2560]{1,0:T(8,128)(2,1)S(1)} %get-tuple-element.99), channel_id=1, source_target_pairs={{0,2},{2,4},{4,6},{6,8},{8,10},{10,12},{12,14},{14,0},{1,3},{3,5},... | collective-permute-start | bytes 860168 | tf_op jit(solution)/shard_map/ppermute | solution.py:20
  75.2 0.1 collective-permute-start.23
  75.3 4.1 %collective-permute-done.16.h3 = bf16[128,1280]{1,0:T(8,128)(2,1)S(1)} collective-permute-done((bf16[128,1280]{1,0:T(8,128)(2,1)S(1)}, bf16[128,1280]{1,0:T(8,128)(2,1)S(1)}, u32[]{:S(2)}, u32[]{:S(2)}) %collective-permute-start.16) | collective-permute-done | bytes 327712 | tf_op jit(solution)/shard_map/ppermute | solution.py:20
  79.4 0.1 shard_map.88
  79.6 0.0 copy-start
  79.6 0.0 copy-start.1
  79.6 0.5 collective-permute-start.21
  80.1 0.2 collective-permute-start.26
  80.2 1.3 %collective-permute-start.28 = (bf16[512,128]{1,0:T(8,128)(2,1)S(1)}, bf16[512,128]{1,0:T(8,128)(2,1)S(1)}, u32[]{:S(2)}, u32[]{:S(2)}) collective-permute-start(bf16[512,128]{1,0:T(8,128)(2,1)S(1)} %get-tuple-element.115), channel_id=1, source_target_pairs={{0,16},{16,32},{32,48},{48,0},{1,17},{17,33},{33,49},{49,1},{2,18}... | collective-permute-start | bytes 393224 | tf_op jit(solution)/shard_map/ppermute | solution.py:20
  81.5 0.3 shard_map.89
  81.8 1.8 %collective-permute-start.25 = (bf16[27,2560]{1,0:T(8,128)(2,1)S(1)}, bf16[27,2560]{1,0:T(8,128)(2,1)S(1)}, u32[]{:S(2)}, u32[]{:S(2)}) collective-permute-start(bf16[27,2560]{1,0:T(8,128)(2,1)S(1)} %get-tuple-element.106), channel_id=1, source_target_pairs={{0,1},{1,0},{2,3},{3,2},{4,5},{5,4},{6,7},{7,6},{8,9},{9,8},{10,11... | collective-permute-start | bytes 414728 | tf_op jit(solution)/shard_map/ppermute | solution.py:20
  83.6 1.0 %collective-permute-start.27 = (bf16[512,128]{1,0:T(8,128)(2,1)S(1)}, bf16[512,128]{1,0:T(8,128)(2,1)S(1)}, u32[]{:S(2)}, u32[]{:S(2)}) collective-permute-start(bf16[512,128]{1,0:T(8,128)(2,1)S(1)} %get-tuple-element.114), channel_id=1, source_target_pairs={{0,32},{16,48},{32,0},{48,16},{1,33},{17,49},{33,1},{49,17},{2,34}... | collective-permute-start | bytes 393224 | tf_op jit(solution)/shard_map/ppermute | solution.py:20
  84.6 3.7 %collective-permute-done.21 = bf16[128,1280]{1,0:T(8,128)(2,1)S(1)} collective-permute-done((bf16[128,1280]{1,0:T(8,128)(2,1)S(1)}, bf16[128,1280]{1,0:T(8,128)(2,1)S(1)}, u32[]{:S(2)}, u32[]{:S(2)}) %collective-permute-start.21) | collective-permute-done | bytes 327712 | tf_op jit(solution)/shard_map/ppermute | solution.py:20
  88.4 0.1 add_convert_fusion.mine
  88.5 2.5 %collective-permute-start.24 = (bf16[128,1280]{1,0:T(8,128)(2,1)S(1)}, bf16[128,1280]{1,0:T(8,128)(2,1)S(1)}, u32[]{:S(2)}, u32[]{:S(2)}) collective-permute-start(bf16[128,1280]{1,0:T(8,128)(2,1)S(1)} %add_convert_fusion.mine), channel_id=1, source_target_pairs={{0,64},{64,0},{1,65},{65,1},{2,66},{66,2},{3,67},{67,3},{4,68},{68... | collective-permute-start | bytes 983048 | tf_op jit(solution)/shard_map/ppermute | solution.py:20
  91.0 1.3 %shard_map.91 = (bf16[1728,128]{1,0:T(8,128)(2,1)}, bf16[1728,128]{1,0:T(8,128)(2,1)}) custom-call(bf16[1728,128]{1,0:T(8,128)(2,1)S(1)} %bitcast.5, bf16[1728,128]{1,0:T(8,128)(2,1)S(1)} %bitcast.7, bf16[512,128]{1,0:T(8,128)(2,1)S(1)} %get-tuple-element.111.b0, bf16[512,128]{1,0:T(8,128)(2,1)S(1)} %collective-permute-done.26.b1, ...), custom_call_target="tpu_custom_call" | custom-call | flops 4000000000 | tf_op jit(solution)/shard_map/pallas_call | solution.py:30
  92.4 0.3 collective-permute-done.25.taken
  92.6 1.0 %shard_map.90 = (bf16[128,2560]{1,0:T(8,128)(2,1)}, f32[27,2560]{1,0:T(8,128)}) custom-call(bf16[128,1280]{1,0:T(8,128)(2,1)S(1)} %add_convert_fusion.mine, bf16[128,1280]{1,0:T(8,128)(2,1)S(1)} %collective-permute-done.24.other, f32[27,2560]{1,0:T(8,128)S(1)} %get-tuple-element.108.keep, bf16[27,2560]{1,0:T(8,128)(2,1)S(1)} %collective-permute-done.25.taken), custom_call_target="tpu_custom_call" | custom-call | bytes 2001920 | tf_op jit(solution)/shard_map/pallas_call | solution.py:30
  (22 shorter events, 0.1 us)
Async XLA Ops:
  0.6 11.4 %collective-permute-start = (bf16[27,2560]{1,0:T(8,128)(2,1)}, bf16[27,2560]{1,0:T(8,128)(2,1)S(1)}, u32[]{:S(2)}, u32[]{:S(2)}) collective-permute-start(bf16[27,2560]{1,0:T(8,128)(2,1)} %mine.1), channel_id=1, source_target_pairs={{0,1},{1,0},{2,3},{3,2},{4,5},{5,4},{6,7},{7,6},{8,9},{9,8},{10,11... | collective-permute-start | bytes 414728 | tf_op jit(solution)/shard_map/ppermute | solution.py:20
  7.1 22.0 %collective-permute-start.5 = (bf16[128,1792]{1,0:T(8,128)(2,1)}, bf16[128,1792]{1,0:T(8,128)(2,1)S(1)}, u32[]{:S(2)}, u32[]{:S(2)}) collective-permute-start(bf16[128,1792]{1,0:T(8,128)(2,1)} %get-tuple-element.61), channel_id=1, source_target_pairs={{0,16},{16,32},{32,48},{48,0},{1,17},{17,33},{33,49},{49,1},{2,18}... | collective-permute-start | bytes 1376264 | tf_op jit(solution)/shard_map/ppermute | solution.py:20
  8.4 22.1 %collective-permute-start.6 = (bf16[128,1792]{1,0:T(8,128)(2,1)}, bf16[128,1792]{1,0:T(8,128)(2,1)S(1)}, u32[]{:S(2)}, u32[]{:S(2)}) collective-permute-start(bf16[128,1792]{1,0:T(8,128)(2,1)} %get-tuple-element.62), channel_id=1, source_target_pairs={{0,32},{16,48},{32,0},{48,16},{1,33},{17,49},{33,1},{49,17},{2,34}... | collective-permute-start | bytes 1376264 | tf_op jit(solution)/shard_map/ppermute | solution.py:20
  10.9 19.7 %collective-permute-start.7 = (bf16[128,1792]{1,0:T(8,128)(2,1)}, bf16[128,1792]{1,0:T(8,128)(2,1)S(1)}, u32[]{:S(2)}, u32[]{:S(2)}) collective-permute-start(bf16[128,1792]{1,0:T(8,128)(2,1)} %get-tuple-element.63), channel_id=1, source_target_pairs={{0,48},{16,0},{32,16},{48,32},{1,49},{17,1},{33,17},{49,33},{2,50}... | collective-permute-start | bytes 1376264 | tf_op jit(solution)/shard_map/ppermute | solution.py:20
  12.0 0.9 copy-start.2
  13.3 26.9 %copy-start.3 = (bf16[128,2560]{1,0:T(8,128)(2,1)S(1)}, bf16[128,2560]{1,0:T(8,128)(2,1)}, u32[]{:S(2)}) copy-start(bf16[128,2560]{1,0:T(8,128)(2,1)} %get-tuple-element.71.cot_own) | copy-start | bytes 1966084
  13.3 26.9 %copy-start.4 = (bf16[512,128]{1,0:T(8,128)(2,1)S(1)}, bf16[512,128]{1,0:T(8,128)(2,1)}, u32[]{:S(2)}) copy-start(bf16[512,128]{1,0:T(8,128)(2,1)} %get-tuple-element.72.hid_own) | copy-start | bytes 393220
  13.3 10.0 %collective-permute-start.2 = (bf16[56,2560]{1,0:T(8,128)(2,1)S(1)}, bf16[56,2560]{1,0:T(8,128)(2,1)S(1)}, u32[]{:S(2)}, u32[]{:S(2)}) collective-permute-start(bf16[56,2560]{1,0:T(8,128)(2,1)S(1)} %shard_map.76.w0), channel_id=1, source_target_pairs={{0,14},{2,0},{4,2},{6,4},{8,6},{10,8},{12,10},{14,12},{1,15},{3,1}... | collective-permute-start | bytes 860168 | tf_op jit(solution)/shard_map/ppermute | solution.py:20
  19.0 7.5 %collective-permute-start.1 = (bf16[56,2560]{1,0:T(8,128)(2,1)S(1)}, bf16[56,2560]{1,0:T(8,128)(2,1)S(1)}, u32[]{:S(2)}, u32[]{:S(2)}) collective-permute-start(bf16[56,2560]{1,0:T(8,128)(2,1)S(1)} %shard_map.76.w0), channel_id=1, source_target_pairs={{0,2},{2,4},{4,6},{6,8},{8,10},{10,12},{12,14},{14,0},{1,3},{3,5},... | collective-permute-start | bytes 860168 | tf_op jit(solution)/shard_map/ppermute | solution.py:20
  26.4 6.7 %collective-permute-start.3 = (bf16[56,2560]{1,0:T(8,128)(2,1)S(1)}, bf16[56,2560]{1,0:T(8,128)(2,1)S(1)}, u32[]{:S(2)}, u32[]{:S(2)}) collective-permute-start(bf16[56,2560]{1,0:T(8,128)(2,1)S(1)} %collective-permute-done.1.f1), channel_id=1, source_target_pairs={{0,2},{2,4},{4,6},{6,8},{8,10},{10,12},{12,14},{14,0},{1,3},{3,5},... | collective-permute-start | bytes 860168 | tf_op jit(solution)/shard_map/ppermute | solution.py:20
  26.4 6.7 %collective-permute-start.4 = (bf16[56,2560]{1,0:T(8,128)(2,1)S(1)}, bf16[56,2560]{1,0:T(8,128)(2,1)S(1)}, u32[]{:S(2)}, u32[]{:S(2)}) collective-permute-start(bf16[56,2560]{1,0:T(8,128)(2,1)S(1)} %collective-permute-done.2.b1), channel_id=1, source_target_pairs={{0,14},{2,0},{4,2},{6,4},{8,6},{10,8},{12,10},{14,12},{1,15},{3,1}... | collective-permute-start | bytes 860168 | tf_op jit(solution)/shard_map/ppermute | solution.py:20
  33.1 7.1 %collective-permute-start.10 = (bf16[384,1280]{1,0:T(8,128)(2,1)S(1)}, bf16[384,1280]{1,0:T(8,128)(2,1)S(1)}, u32[]{:S(2)}, u32[]{:S(2)}) collective-permute-start(bf16[384,1280]{1,0:T(8,128)(2,1)S(1)} %shard_map.77), channel_id=1, source_target_pairs={{0,64},{64,0},{1,65},{65,1},{2,66},{66,2},{3,67},{67,3},{4,68},{68... | collective-permute-start | bytes 2949128 | tf_op jit(solution)/shard_map/ppermute | solution.py:20
  37.3 10.2 %collective-permute-start.8 = (bf16[56,2560]{1,0:T(8,128)(2,1)S(1)}, bf16[56,2560]{1,0:T(8,128)(2,1)S(1)}, u32[]{:S(2)}, u32[]{:S(2)}) collective-permute-start(bf16[56,2560]{1,0:T(8,128)(2,1)S(1)} %collective-permute-done.3.f2), channel_id=1, source_target_pairs={{0,2},{2,4},{4,6},{6,8},{8,10},{10,12},{12,14},{14,0},{1,3},{3,5},... | collective-permute-start | bytes 860168 | tf_op jit(solution)/shard_map/ppermute | solution.py:20
  37.3 10.2 %collective-permute-start.9 = (bf16[56,2560]{1,0:T(8,128)(2,1)S(1)}, bf16[56,2560]{1,0:T(8,128)(2,1)S(1)}, u32[]{:S(2)}, u32[]{:S(2)}) collective-permute-start(bf16[56,2560]{1,0:T(8,128)(2,1)S(1)} %collective-permute-done.4.b2), channel_id=1, source_target_pairs={{0,14},{2,0},{4,2},{6,4},{8,6},{10,8},{12,10},{14,12},{1,15},{3,1}... | collective-permute-start | bytes 860168 | tf_op jit(solution)/shard_map/ppermute | solution.py:20
  43.7 8.9 %collective-permute-start.12 = (bf16[56,2560]{1,0:T(8,128)(2,1)S(1)}, bf16[56,2560]{1,0:T(8,128)(2,1)S(1)}, u32[]{:S(2)}, u32[]{:S(2)}) collective-permute-start(bf16[56,2560]{1,0:T(8,128)(2,1)S(1)} %get-tuple-element.79), channel_id=1, source_target_pairs={{0,14},{2,0},{4,2},{6,4},{8,6},{10,8},{12,10},{14,12},{1,15},{3,1}... | collective-permute-start | bytes 860168 | tf_op jit(solution)/shard_map/ppermute | solution.py:20
  47.4 8.9 %collective-permute-start.11 = (bf16[56,2560]{1,0:T(8,128)(2,1)S(1)}, bf16[56,2560]{1,0:T(8,128)(2,1)S(1)}, u32[]{:S(2)}, u32[]{:S(2)}) collective-permute-start(bf16[56,2560]{1,0:T(8,128)(2,1)S(1)} %collective-permute-done.8.f3), channel_id=1, source_target_pairs={{0,2},{2,4},{4,6},{6,8},{8,10},{10,12},{12,14},{14,0},{1,3},{3,5},... | collective-permute-start | bytes 860168 | tf_op jit(solution)/shard_map/ppermute | solution.py:20
  52.7 11.7 %collective-permute-start.18 = (bf16[56,2560]{1,0:T(8,128)(2,1)S(1)}, bf16[56,2560]{1,0:T(8,128)(2,1)S(1)}, u32[]{:S(2)}, u32[]{:S(2)}) collective-permute-start(bf16[56,2560]{1,0:T(8,128)(2,1)S(1)} %get-tuple-element.86), channel_id=1, source_target_pairs={{0,14},{2,0},{4,2},{6,4},{8,6},{10,8},{12,10},{14,12},{1,15},{3,1}... | collective-permute-start | bytes 860168 | tf_op jit(solution)/shard_map/ppermute | solution.py:20
  56.3 8.4 %collective-permute-start.17 = (bf16[56,2560]{1,0:T(8,128)(2,1)S(1)}, bf16[56,2560]{1,0:T(8,128)(2,1)S(1)}, u32[]{:S(2)}, u32[]{:S(2)}) collective-permute-start(bf16[56,2560]{1,0:T(8,128)(2,1)S(1)} %get-tuple-element.80.value), channel_id=1, source_target_pairs={{0,2},{2,4},{4,6},{6,8},{8,10},{10,12},{12,14},{14,0},{1,3},{3,5},... | collective-permute-start | bytes 860168 | tf_op jit(solution)/shard_map/ppermute | solution.py:20
  56.8 4.3 %collective-permute-start.13 = (bf16[512,1280]{1,0:T(8,128)(2,1)S(1)}, bf16[512,1280]{1,0:T(8,128)(2,1)S(1)}, u32[]{:S(2)}, u32[]{:S(2)}) collective-permute-start(bf16[512,1280]{1,0:T(8,128)(2,1)S(1)} %shard_map.83), channel_id=1, source_target_pairs={{0,64},{64,0},{1,65},{65,1},{2,66},{66,2},{3,67},{67,3},{4,68},{68... | collective-permute-start | bytes 3932168 | tf_op jit(solution)/shard_map/ppermute | solution.py:20
  61.3 14.0 %collective-permute-start.15 = (bf16[128,1280]{1,0:T(8,128)(2,1)S(1)}, bf16[128,1280]{1,0:T(8,128)(2,1)S(1)}, u32[]{:S(2)}, u32[]{:S(2)}) collective-permute-start(bf16[128,1280]{1,0:T(8,128)(2,1)S(1)} %get-tuple-element.84), channel_id=1, source_target_pairs={{0,32},{16,48},{32,0},{48,16},{1,33},{17,49},{33,1},{49,17},{2,34}... | collective-permute-start | bytes 983048 | tf_op jit(solution)/shard_map/ppermute | solution.py:20
  61.6 17.8 %collective-permute-start.16 = (bf16[128,1280]{1,0:T(8,128)(2,1)S(1)}, bf16[128,1280]{1,0:T(8,128)(2,1)S(1)}, u32[]{:S(2)}, u32[]{:S(2)}) collective-permute-start(bf16[128,1280]{1,0:T(8,128)(2,1)S(1)} %get-tuple-element.85), channel_id=1, source_target_pairs={{0,16},{16,32},{32,48},{48,0},{1,17},{17,33},{33,49},{49,1},{2,18}... | collective-permute-start | bytes 983048 | tf_op jit(solution)/shard_map/ppermute | solution.py:20
  62.0 17.4 %collective-permute-start.14 = (bf16[128,1280]{1,0:T(8,128)(2,1)S(1)}, bf16[128,1280]{1,0:T(8,128)(2,1)S(1)}, u32[]{:S(2)}, u32[]{:S(2)}) collective-permute-start(bf16[128,1280]{1,0:T(8,128)(2,1)S(1)} %get-tuple-element.83), channel_id=1, source_target_pairs={{0,48},{16,0},{32,16},{48,32},{1,49},{17,1},{33,17},{49,33},{2,50}... | collective-permute-start | bytes 983048 | tf_op jit(solution)/shard_map/ppermute | solution.py:20
  64.9 7.6 %collective-permute-start.19 = (bf16[56,2560]{1,0:T(8,128)(2,1)S(1)}, bf16[56,2560]{1,0:T(8,128)(2,1)S(1)}, u32[]{:S(2)}, u32[]{:S(2)}) collective-permute-start(bf16[56,2560]{1,0:T(8,128)(2,1)S(1)} %get-tuple-element.89), channel_id=1, source_target_pairs={{0,2},{2,4},{4,6},{6,8},{8,10},{10,12},{12,14},{14,0},{1,3},{3,5},... | collective-permute-start | bytes 860168 | tf_op jit(solution)/shard_map/ppermute | solution.py:20
  64.9 7.5 %collective-permute-start.20 = (bf16[56,2560]{1,0:T(8,128)(2,1)S(1)}, bf16[56,2560]{1,0:T(8,128)(2,1)S(1)}, u32[]{:S(2)}, u32[]{:S(2)}) collective-permute-start(bf16[56,2560]{1,0:T(8,128)(2,1)S(1)} %get-tuple-element.90), channel_id=1, source_target_pairs={{0,14},{2,0},{4,2},{6,4},{8,6},{10,8},{12,10},{14,12},{1,15},{3,1}... | collective-permute-start | bytes 860168 | tf_op jit(solution)/shard_map/ppermute | solution.py:20
  72.6 9.0 %collective-permute-start.22 = (bf16[56,2560]{1,0:T(8,128)(2,1)S(1)}, bf16[56,2560]{1,0:T(8,128)(2,1)S(1)}, u32[]{:S(2)}, u32[]{:S(2)}) collective-permute-start(bf16[56,2560]{1,0:T(8,128)(2,1)S(1)} %get-tuple-element.99), channel_id=1, source_target_pairs={{0,2},{2,4},{4,6},{6,8},{8,10},{10,12},{12,14},{14,0},{1,3},{3,5},... | collective-permute-start | bytes 860168 | tf_op jit(solution)/shard_map/ppermute | solution.py:20
  75.2 6.3 %collective-permute-start.23 = (bf16[56,2560]{1,0:T(8,128)(2,1)S(1)}, bf16[56,2560]{1,0:T(8,128)(2,1)S(1)}, u32[]{:S(2)}, u32[]{:S(2)}) collective-permute-start(bf16[56,2560]{1,0:T(8,128)(2,1)S(1)} %get-tuple-element.100), channel_id=1, source_target_pairs={{0,14},{2,0},{4,2},{6,4},{8,6},{10,8},{12,10},{14,12},{1,15},{3,1}... | collective-permute-start | bytes 860168 | tf_op jit(solution)/shard_map/ppermute | solution.py:20
  79.6 11.5 %copy-start = (bf16[128,1728]{0,1:T(8,128)(2,1)S(1)}, bf16[128,1728]{0,1:T(8,128)(2,1)}, u32[]{:S(2)}) copy-start(bf16[128,1728]{0,1:T(8,128)(2,1)} %param.4) | copy-start | bytes 1327108
  79.6 11.5 %copy-start.1 = (bf16[128,1728]{0,1:T(8,128)(2,1)S(1)}, bf16[128,1728]{0,1:T(8,128)(2,1)}, u32[]{:S(2)}) copy-start(bf16[128,1728]{0,1:T(8,128)(2,1)} %param.5) | copy-start | bytes 1327108
  79.6 8.8 %collective-permute-start.21 = (bf16[128,1280]{1,0:T(8,128)(2,1)S(1)}, bf16[128,1280]{1,0:T(8,128)(2,1)S(1)}, u32[]{:S(2)}, u32[]{:S(2)}) collective-permute-start(bf16[128,1280]{1,0:T(8,128)(2,1)S(1)} %shard_map.88), channel_id=1, source_target_pairs={{0,128},{128,0},{1,129},{129,1},{2,130},{130,2},{3,131},{131,3},{4... | collective-permute-start | bytes 983048 | tf_op jit(solution)/shard_map/ppermute | solution.py:20
  80.1 10.9 %collective-permute-start.26 = (bf16[512,128]{1,0:T(8,128)(2,1)S(1)}, bf16[512,128]{1,0:T(8,128)(2,1)S(1)}, u32[]{:S(2)}, u32[]{:S(2)}) collective-permute-start(bf16[512,128]{1,0:T(8,128)(2,1)S(1)} %get-tuple-element.112), channel_id=1, source_target_pairs={{0,48},{16,0},{32,16},{48,32},{1,49},{17,1},{33,17},{49,33},{2,50}... | collective-permute-start | bytes 393224 | tf_op jit(solution)/shard_map/ppermute | solution.py:20
  80.2 10.8 %collective-permute-start.28 = (bf16[512,128]{1,0:T(8,128)(2,1)S(1)}, bf16[512,128]{1,0:T(8,128)(2,1)S(1)}, u32[]{:S(2)}, u32[]{:S(2)}) collective-permute-start(bf16[512,128]{1,0:T(8,128)(2,1)S(1)} %get-tuple-element.115), channel_id=1, source_target_pairs={{0,16},{16,32},{32,48},{48,0},{1,17},{17,33},{33,49},{49,1},{2,18}... | collective-permute-start | bytes 393224 | tf_op jit(solution)/shard_map/ppermute | solution.py:20
  81.8 10.8 %collective-permute-start.25 = (bf16[27,2560]{1,0:T(8,128)(2,1)S(1)}, bf16[27,2560]{1,0:T(8,128)(2,1)S(1)}, u32[]{:S(2)}, u32[]{:S(2)}) collective-permute-start(bf16[27,2560]{1,0:T(8,128)(2,1)S(1)} %get-tuple-element.106), channel_id=1, source_target_pairs={{0,1},{1,0},{2,3},{3,2},{4,5},{5,4},{6,7},{7,6},{8,9},{9,8},{10,11... | collective-permute-start | bytes 414728 | tf_op jit(solution)/shard_map/ppermute | solution.py:20
  83.6 7.4 %collective-permute-start.27 = (bf16[512,128]{1,0:T(8,128)(2,1)S(1)}, bf16[512,128]{1,0:T(8,128)(2,1)S(1)}, u32[]{:S(2)}, u32[]{:S(2)}) collective-permute-start(bf16[512,128]{1,0:T(8,128)(2,1)S(1)} %get-tuple-element.114), channel_id=1, source_target_pairs={{0,32},{16,48},{32,0},{48,16},{1,33},{17,49},{33,1},{49,17},{2,34}... | collective-permute-start | bytes 393224 | tf_op jit(solution)/shard_map/ppermute | solution.py:20
  88.5 4.2 %collective-permute-start.24 = (bf16[128,1280]{1,0:T(8,128)(2,1)S(1)}, bf16[128,1280]{1,0:T(8,128)(2,1)S(1)}, u32[]{:S(2)}, u32[]{:S(2)}) collective-permute-start(bf16[128,1280]{1,0:T(8,128)(2,1)S(1)} %add_convert_fusion.mine), channel_id=1, source_target_pairs={{0,64},{64,0},{1,65},{65,1},{2,66},{66,2},{3,67},{67,3},{4,68},{68... | collective-permute-start | bytes 983048 | tf_op jit(solution)/shard_map/ppermute | solution.py:20

commit v5 on v4

--- a/solution.py
+++ b/solution.py
@@ -154,16 +154,21 @@
     hid[...] = hid_t[...].T
 
 
-def near_blocks(w0, f1, f2, f3, b3, b2, b1, hid, weight, product, opposite, mark):
+def padded(piece):
+    rows, width = piece.shape
+    return jnp.concatenate([piece[...].astype(F32), jnp.zeros((SLOT - rows, width), F32)], 0).astype(BF16)
+
+
+def near_blocks(w0, f1, f2, f3, b3, b2, b1, hid, weight, product, opposite, other, mark):
     z = lax.axis_index("z")
     width = w0.shape[1]
+    half = width // 2
     for distance, piece in enumerate((w0, f1, f2, f3, None, b3, b2, b1)):
         to = lax.rem(z - distance + NZ, NZ)
         if piece is None:
             weight[to] = jnp.zeros((SLOT, width), BF16)
         else:
-            weight[to, :SENT] = piece[...]
-            weight[to, SENT:] = jnp.zeros((SLOT - SENT, width), BF16)
+            weight[to] = padded(piece)
 
     @pl.loop(0, width // TILE)
     def _(t):
@@ -171,23 +176,34 @@
         rhs = weight[:, :, columns].reshape(NZ * SLOT, TILE)
         product[:, columns] = jnp.dot(hid[...], rhs, preferred_element_type=F32)
 
+    other[:, :half] = product[:, half:].astype(BF16)
     for block in range(NZ):
 
         @pl.when(z == (block + NZ // 2) % NZ)
         def _(block=block):
-            opposite[...] = hid[:, block * SLOT : (block + 1) * SLOT]
+            some = hid[:, block * SLOT : (block + 1) * SLOT]
+            opposite[...] = some
+            other[:, half:] = jnp.concatenate([some, jnp.zeros_like(some)], 1)
 
     mark[...] = w0[: mark.shape[0], : mark.shape[1]]
 
 
-def with_opposite(first, product, opposite, block, out):
-    rhs = jnp.concatenate([block[...], jnp.zeros((SLOT - SENT, block.shape[1]), BF16)], 0)
-    width = out.shape[1]
-    for t in range(width // TILE):
-        to = slice(t * TILE, (t + 1) * TILE)
-        here = slice(first + t * TILE, first + (t + 1) * TILE)
-        more = jnp.dot(opposite[...], rhs[:, here], preferred_element_type=F32)
-        out[:, to] = (product[:, here] + more).astype(out.dtype)
+def other_half(block, mark, out):
+    out[...] = block[:, out.shape[1] :]
+
+
+def output_parts(product, crossed, opposite, block, block_other, total, m1, m2, m3):
+    rows, half = total.shape
+    own, far = padded(block.at[:, :half]), padded(block_other)
+    far_hidden = crossed[:, half : half + SLOT]
+    for t in range(half // TILE):
+        here = slice(t * TILE, (t + 1) * TILE)
+        value = product[:, here] + crossed[:, here].astype(F32)
+        value = value + jnp.dot(opposite[...], own[:, here], preferred_element_type=F32)
+        value = value + jnp.dot(far_hidden, far[:, here], preferred_element_type=F32)
+        total[:, here] = value[:rows]
+        for k, out in enumerate((m1, m2, m3)):
+            out[:, here] = value[(k + 1) * rows : (k + 2) * rows].astype(BF16)
 
 
 def first_rows(value, out):
@@ -209,20 +225,11 @@
             ].astype(BF16)
 
     opposite = lax.rem(lax.axis_index("z") + NZ // 2, NZ)
-    rhs = jnp.concatenate([block[...], jnp.zeros((SLOT - SENT, block.shape[1]), BF16)], 0)
-    product = lax.dot_general(rhs, cot[...], dims, preferred_element_type=F32)
+    product = lax.dot_general(padded(block), cot[...], dims, preferred_element_type=F32)
     for k, part in enumerate(parts):
         part[pl.ds(pl.multiple_of(opposite * SLOT, SLOT), SLOT)] = product[
             :, k * rows : (k + 1) * rows
         ].astype(BF16)
-
-
-def pack_output(mine, crossed, total, m1, m2, m3):
-    rows = total.shape[0]
-    total[...] = mine[:rows] + crossed[:rows].astype(F32)
-    for k, out in enumerate((m1, m2, m3)):
-        here = slice((k + 1) * rows, (k + 2) * rows)
-        out[...] = (mine[here] + crossed[here].astype(F32)).astype(BF16)
 
 
 def activation_gradients(gate, up, b0, b1, b2, b3, grad_gate, grad_up, back32):
@@ -340,35 +347,25 @@
     f4 = shift(fwd[3], "z", 1)
     ring = (shift(to_bwd, "z", -1),)
 
-    weight, product, opposite, early = call(
+    weight, product, opposite, other, early = call(
         near_blocks,
-        [like((NZ, SLOT, width)), like((tokens, width), F32), like((tokens, SLOT)), like((16, 128))],
+        [like((NZ, SLOT, width)), like((tokens, width), F32), like((tokens, SLOT))]
+        + [like((tokens, half + 2 * SLOT)), like((16, 128))],
         *fwd, *reversed(bwd[1:]), hid,
         moved=0,
     )
+    crossed = shift(other, "core", 1)
     to_fwd, to_bwd = added(3, ring, early)
     ring = (shift(to_fwd, "z", 1), shift(to_bwd, "z", -1))
 
     (mark,) = call(first_rows, [like((16, 128))], to_fwd, flops=2 * 10**9)
-    (out_other,) = call(
-        lambda product, opposite, block, mark, out: with_opposite(half, product, opposite, block, out),
-        [like((tokens, half))],
-        product, opposite, f4, mark,
-        flops=2 * slots * tokens * half,
-    )
-    crossed = shift(out_other, "core", 1)
-    (out_mine,) = call(
-        functools.partial(with_opposite, 0),
-        [like((tokens, half), F32)],
-        product, opposite, f4,
-        flops=14 * 10**9,
-    )
-    crossed = after(crossed, out_mine)
+    (block_half,) = call(other_half, [like((SENT, half))], f4, mark, flops=14 * 10**9)
     total, m1, m2, m3 = call(
-        pack_output,
+        output_parts,
         [like((rows, half), F32)] + [like((rows, half))] * 3,
-        out_mine, crossed,
-        flops=2 * 10**9,
+        product, crossed, opposite, f4, shift(block_half, "core", 1),
+        flops=1 * 10**9,
+        moved=0,
     )
     got_out = [shift(m, "x", -k) for k, m in ((1, m1), (2, m2), (3, m3))]
     back_own, *backs = call(

time: 93.8 us -> 92.1 us (0.982)
  waiting for transfers between devices: 27.7 us -> 25.1 us
  starting transfers between devices: 47.5 us -> 48.5 us
    ppermute x29 -> x30, waiting for transfers between devices: 27.7 us -> 25.1 us  [shift(): lax.ppermute(value, axis, [(i, (i + steps) % count) for i in range(count)])]
    ppermute x29 -> x30, starting transfers between devices: 47.5 us -> 48.5 us  [shift(): lax.ppermute(value, axis, [(i, (i + steps) % count) for i in range(count)])]
    pallas_call x17 -> x16, Pallas kernels: 16.6 us -> 16.5 us  [call(): pl.pallas_call(kernel, out_shape=outs, in_specs=[pl.BlockSpec(memory_spac...]
  transfers between devices with their start and end apart: 29 -> 30, of which waited for: 13 -> 13; matrix products, arithmetic and copies ran while one was open for 0% -> 0% of each run, Pallas kernels for 17% -> 17%
where the time goes in v5:
time: 92.1 us; the launch traced here: 92 us
  starting transfers between devices  48.5 us (53%)
  waiting for transfers between devices  25.1 us (27%)
  Pallas kernels  16.5 us (18%)
  local copies, waits for them, and re-layouts  0.94 us (1%)
    ppermute x30, starting transfers between devices, shift(): lax.ppermute(value, axis, [(i, (i + steps) % count) for i in range(count)])  48.5 us
    ppermute x30, waiting for transfers between devices, shift(): lax.ppermute(value, axis, [(i, (i + steps) % count) for i in range(count)])  25.1 us
    pallas_call x16, Pallas kernels, call(): pl.pallas_call(kernel, out_shape=outs, in_specs=[pl.BlockSpec(memory_spac...  16.5 us
  transfers between devices with their start and end apart: 30, of which 13 were waited for; matrix products, arithmetic and copies ran while one was open for 0% of the time, Pallas kernels for 17%

profile of v5, /device:TPU:1, one launch (start us, length us, event | category | flops | bytes accessed | tf_op | source)
XLA Modules:
  0.0 92.0 jit_solution(2008049367860831529)
XLA Ops:
  0.6 3.8 %collective-permute-start = (bf16[27,2560]{1,0:T(8,128)(2,1)}, bf16[27,2560]{1,0:T(8,128)(2,1)S(1)}, u32[]{:S(2)}, u32[]{:S(2)}) collective-permute-start(bf16[27,2560]{1,0:T(8,128)(2,1)} %mine.1), channel_id=1, source_target_pairs={{0,1},{1,0},{2,3},{3,2},{4,5},{5,4},{6,7},{7,6},{8,9},{9,8},{10,11... | collective-permute-start | bytes 414728 | tf_op jit(solution)/shard_map/ppermute | solution.py:20
  4.5 2.7 %shard_map.75 = (bf16[128,1792]{1,0:T(8,128)(2,1)}, bf16[128,1792]{1,0:T(8,128)(2,1)}, bf16[128,1792]{1,0:T(8,128)(2,1)}, bf16[512,128]{1,0:T(8,128)(2,1)}, bf16[128,2560]{1,0:T(8,128)(2,1)}) custom-call(bf16[1728,128]{1,0:T(8,128)(2,1)} %bitcast.4, bf16[1728,128]{1,0:T(8,128)(2,1)} %bitcast.6, bf16[128,2560]{1,0:T(8,128)(2,1)} %cot_hbm.1), custom_call_target="tpu_custom_call" | custom-call | bytes 3702784 | tf_op jit(solution)/shard_map/pallas_call | solution.py:30
  7.1 1.3 %collective-permute-start.5 = (bf16[128,1792]{1,0:T(8,128)(2,1)}, bf16[128,1792]{1,0:T(8,128)(2,1)S(1)}, u32[]{:S(2)}, u32[]{:S(2)}) collective-permute-start(bf16[128,1792]{1,0:T(8,128)(2,1)} %get-tuple-element.61), channel_id=1, source_target_pairs={{0,16},{16,32},{32,48},{48,0},{1,17},{17,33},{33,49},{49,1},{2,18}... | collective-permute-start | bytes 1376264 | tf_op jit(solution)/shard_map/ppermute | solution.py:20
  8.4 2.5 %collective-permute-start.6 = (bf16[128,1792]{1,0:T(8,128)(2,1)}, bf16[128,1792]{1,0:T(8,128)(2,1)S(1)}, u32[]{:S(2)}, u32[]{:S(2)}) collective-permute-start(bf16[128,1792]{1,0:T(8,128)(2,1)} %get-tuple-element.62), channel_id=1, source_target_pairs={{0,32},{16,48},{32,0},{48,16},{1,33},{17,49},{33,1},{49,17},{2,34}... | collective-permute-start | bytes 1376264 | tf_op jit(solution)/shard_map/ppermute | solution.py:20
  10.9 1.2 %collective-permute-start.7 = (bf16[128,1792]{1,0:T(8,128)(2,1)}, bf16[128,1792]{1,0:T(8,128)(2,1)S(1)}, u32[]{:S(2)}, u32[]{:S(2)}) collective-permute-start(bf16[128,1792]{1,0:T(8,128)(2,1)} %get-tuple-element.63), channel_id=1, source_target_pairs={{0,48},{16,0},{32,16},{48,32},{1,49},{17,1},{33,17},{49,33},{2,50}... | collective-permute-start | bytes 1376264 | tf_op jit(solution)/shard_map/ppermute | solution.py:20
  12.0 0.9 copy-done.2
  13.0 0.3 shard_map.76.w0
  13.3 0.0 copy-start.3
  13.3 0.0 copy-start.4
  13.3 1.7 %collective-permute-start.1 = (bf16[56,2560]{1,0:T(8,128)(2,1)S(1)}, bf16[56,2560]{1,0:T(8,128)(2,1)S(1)}, u32[]{:S(2)}, u32[]{:S(2)}) collective-permute-start(bf16[56,2560]{1,0:T(8,128)(2,1)S(1)} %shard_map.76.w0), channel_id=1, source_target_pairs={{0,2},{2,4},{4,6},{6,8},{8,10},{10,12},{12,14},{14,0},{1,3},{3,5},... | collective-permute-start | bytes 860168 | tf_op jit(solution)/shard_map/ppermute | solution.py:20
  15.0 4.0 %collective-permute-start.2 = (bf16[56,2560]{1,0:T(8,128)(2,1)S(1)}, bf16[56,2560]{1,0:T(8,128)(2,1)S(1)}, u32[]{:S(2)}, u32[]{:S(2)}) collective-permute-start(bf16[56,2560]{1,0:T(8,128)(2,1)S(1)} %shard_map.76.w0), channel_id=1, source_target_pairs={{0,14},{2,0},{4,2},{6,4},{8,6},{10,8},{12,10},{14,12},{1,15},{3,1}... | collective-permute-start | bytes 860168 | tf_op jit(solution)/shard_map/ppermute | solution.py:20
  19.1 5.3 %collective-permute-done.1.f1 = bf16[56,2560]{1,0:T(8,128)(2,1)S(1)} collective-permute-done((bf16[56,2560]{1,0:T(8,128)(2,1)S(1)}, bf16[56,2560]{1,0:T(8,128)(2,1)S(1)}, u32[]{:S(2)}, u32[]{:S(2)}) %collective-permute-start.1) | collective-permute-done | bytes 286752 | tf_op jit(solution)/shard_map/ppermute | solution.py:20
  24.3 0.0 collective-permute-done.2.b1
  24.3 0.0 collective-permute-start.3
  24.3 2.7 %collective-permute-start.4 = (bf16[56,2560]{1,0:T(8,128)(2,1)S(1)}, bf16[56,2560]{1,0:T(8,128)(2,1)S(1)}, u32[]{:S(2)}, u32[]{:S(2)}) collective-permute-start(bf16[56,2560]{1,0:T(8,128)(2,1)S(1)} %collective-permute-done.2.b1), channel_id=1, source_target_pairs={{0,14},{2,0},{4,2},{6,4},{8,6},{10,8},{12,10},{14,12},{1,15},{3,1}... | collective-permute-start | bytes 860168 | tf_op jit(solution)/shard_map/ppermute | solution.py:20
  27.0 0.0 collective-permute-done.5.g1
  27.0 3.5 %collective-permute-done.6.g2 = bf16[128,1792]{1,0:T(8,128)(2,1)S(1)} collective-permute-done((bf16[128,1792]{1,0:T(8,128)(2,1)}, bf16[128,1792]{1,0:T(8,128)(2,1)S(1)}, u32[]{:S(2)}, u32[]{:S(2)}) %collective-permute-start.6) | collective-permute-done | bytes 458784 | tf_op jit(solution)/shard_map/ppermute | solution.py:20
  30.5 0.1 collective-permute-done.7.g3
  30.6 0.1 shard_map.77
  30.6 0.8 collective-permute-done.3.f2
  31.4 3.4 %collective-permute-start.10 = (bf16[384,1280]{1,0:T(8,128)(2,1)S(1)}, bf16[384,1280]{1,0:T(8,128)(2,1)S(1)}, u32[]{:S(2)}, u32[]{:S(2)}) collective-permute-start(bf16[384,1280]{1,0:T(8,128)(2,1)S(1)} %shard_map.77), channel_id=1, source_target_pairs={{0,64},{64,0},{1,65},{65,1},{2,66},{66,2},{3,67},{67,3},{4,68},{68... | collective-permute-start | bytes 2949128 | tf_op jit(solution)/shard_map/ppermute | solution.py:20
  34.8 2.0 %collective-permute-start.8 = (bf16[56,2560]{1,0:T(8,128)(2,1)S(1)}, bf16[56,2560]{1,0:T(8,128)(2,1)S(1)}, u32[]{:S(2)}, u32[]{:S(2)}) collective-permute-start(bf16[56,2560]{1,0:T(8,128)(2,1)S(1)} %collective-permute-done.3.f2), channel_id=1, source_target_pairs={{0,2},{2,4},{4,6},{6,8},{8,10},{10,12},{12,14},{14,0},{1,3},{3,5},... | collective-permute-start | bytes 860168 | tf_op jit(solution)/shard_map/ppermute | solution.py:20
  36.8 1.4 %collective-permute-start.9 = (bf16[56,2560]{1,0:T(8,128)(2,1)S(1)}, bf16[56,2560]{1,0:T(8,128)(2,1)S(1)}, u32[]{:S(2)}, u32[]{:S(2)}) collective-permute-start(bf16[56,2560]{1,0:T(8,128)(2,1)S(1)} %collective-permute-done.4.b2), channel_id=1, source_target_pairs={{0,14},{2,0},{4,2},{6,4},{8,6},{10,8},{12,10},{14,12},{1,15},{3,1}... | collective-permute-start | bytes 860168 | tf_op jit(solution)/shard_map/ppermute | solution.py:20
  38.2 3.4 %shard_map.78 = (f32[8,56,2560]{2,1,0:T(8,128)S(1)}, bf16[56,2560]{1,0:T(8,128)(2,1)S(1)}, bf16[512,2560]{1,0:T(8,128)(2,1)S(1)}, bf16[512,512]{1,0:T(8,128)(2,1)S(1)}) custom-call(bf16[128,2560]{1,0:T(8,128)(2,1)S(1)} %copy-done.3, bf16[512,128]{1,0:T(8,128)(2,1)S(1)} %copy-done.4, bf16[128,1792]{1,0:T(8,128)(2,1)S(1)} %collective-permute-done.5.g1, ...), custom_call_target="tpu_custom_call" | custom-call | flops 1342177280 | bytes 11165696 | tf_op jit(solution)/shard_map/pallas_call | solution.py:30
  41.6 2.3 %collective-permute-start.13 = (bf16[56,2560]{1,0:T(8,128)(2,1)S(1)}, bf16[56,2560]{1,0:T(8,128)(2,1)S(1)}, u32[]{:S(2)}, u32[]{:S(2)}) collective-permute-start(bf16[56,2560]{1,0:T(8,128)(2,1)S(1)} %get-tuple-element.80), channel_id=1, source_target_pairs={{0,14},{2,0},{4,2},{6,4},{8,6},{10,8},{12,10},{14,12},{1,15},{3,1}... | collective-permute-start | bytes 860168 | tf_op jit(solution)/shard_map/ppermute | solution.py:20
  43.9 1.4 %collective-permute-done.8.f3 = bf16[56,2560]{1,0:T(8,128)(2,1)S(1)} collective-permute-done((bf16[56,2560]{1,0:T(8,128)(2,1)S(1)}, bf16[56,2560]{1,0:T(8,128)(2,1)S(1)}, u32[]{:S(2)}, u32[]{:S(2)}) %collective-permute-start.8) | collective-permute-done | bytes 286752 | tf_op jit(solution)/shard_map/ppermute | solution.py:20
  45.3 0.3 collective-permute-done.9.b3
  45.5 1.1 %collective-permute-start.12 = (bf16[56,2560]{1,0:T(8,128)(2,1)S(1)}, bf16[56,2560]{1,0:T(8,128)(2,1)S(1)}, u32[]{:S(2)}, u32[]{:S(2)}) collective-permute-start(bf16[56,2560]{1,0:T(8,128)(2,1)S(1)} %collective-permute-done.8.f3), channel_id=1, source_target_pairs={{0,2},{2,4},{4,6},{6,8},{8,10},{10,12},{12,14},{14,0},{1,3},{3,5},... | collective-permute-start | bytes 860168 | tf_op jit(solution)/shard_map/ppermute | solution.py:20
  46.7 3.4 %shard_map.79 = (bf16[8,64,2560]{2,1,0:T(8,128)(2,1)S(1)}, f32[512,2560]{1,0:T(8,128)S(1)}, bf16[512,64]{1,0:T(8,128)(2,1)S(1)}, bf16[512,1408]{1,0:T(8,128)(2,1)S(1)}, bf16[16,128]{1,0:T(8,128)(2,1)S(1)}) custom-call(bf16[56,2560]{1,0:T(8,128)(2,1)S(1)} %shard_map.76.w0, bf16[56,2560]{1,0:T(8,128)(2,1)S(1)} %collective-permute-done.1.f1, ...), custom_call_target="tpu_custom_call" | custom-call | tf_op jit(solution)/shard_map/pallas_call | solution.py:30
  50.1 2.3 %collective-permute-start.11 = (bf16[512,1408]{1,0:T(8,128)(2,1)S(1)}, bf16[512,1408]{1,0:T(8,128)(2,1)S(1)}, u32[]{:S(2)}, u32[]{:S(2)}) collective-permute-start(bf16[512,1408]{1,0:T(8,128)(2,1)S(1)} %get-tuple-element.76), channel_id=1, source_target_pairs={{0,64},{64,0},{1,65},{65,1},{2,66},{66,2},{3,67},{67,3},{4,68},{68... | collective-permute-start | bytes 4325384 | tf_op jit(solution)/shard_map/ppermute | solution.py:20
  52.4 0.1 shard_map.80
  52.5 1.4 %collective-permute-start.18 = (bf16[56,2560]{1,0:T(8,128)(2,1)S(1)}, bf16[56,2560]{1,0:T(8,128)(2,1)S(1)}, u32[]{:S(2)}, u32[]{:S(2)}) collective-permute-start(bf16[56,2560]{1,0:T(8,128)(2,1)S(1)} %get-tuple-element.81.value), channel_id=1, source_target_pairs={{0,2},{2,4},{4,6},{6,8},{8,10},{10,12},{12,14},{14,0},{1,3},{3,5},... | collective-permute-start | bytes 860168 | tf_op jit(solution)/shard_map/ppermute | solution.py:20
  53.9 1.3 %collective-permute-start.19 = (bf16[56,2560]{1,0:T(8,128)(2,1)S(1)}, bf16[56,2560]{1,0:T(8,128)(2,1)S(1)}, u32[]{:S(2)}, u32[]{:S(2)}) collective-permute-start(bf16[56,2560]{1,0:T(8,128)(2,1)S(1)} %get-tuple-element.86), channel_id=1, source_target_pairs={{0,14},{2,0},{4,2},{6,4},{8,6},{10,8},{12,10},{14,12},{1,15},{3,1}... | collective-permute-start | bytes 860168 | tf_op jit(solution)/shard_map/ppermute | solution.py:20
  55.3 0.8 collective-permute-start.14
  56.1 1.0 %collective-permute-done.14.block_other = bf16[56,1280]{1,0:T(8,128)(2,1)S(1)} collective-permute-done((bf16[56,1280]{1,0:T(8,128)(2,1)S(1)}, bf16[56,1280]{1,0:T(8,128)(2,1)S(1)}, u32[]{:S(2)}, u32[]{:S(2)}) %collective-permute-start.14) | collective-permute-done | bytes 143392 | tf_op jit(solution)/shard_map/ppermute | solution.py:20
  57.1 0.9 shard_map.83
  58.0 1.8 %collective-permute-start.15 = (bf16[128,1280]{1,0:T(8,128)(2,1)S(1)}, bf16[128,1280]{1,0:T(8,128)(2,1)S(1)}, u32[]{:S(2)}, u32[]{:S(2)}) collective-permute-start(bf16[128,1280]{1,0:T(8,128)(2,1)S(1)} %get-tuple-element.83), channel_id=1, source_target_pairs={{0,48},{16,0},{32,16},{48,32},{1,49},{17,1},{33,17},{49,33},{2,50}... | collective-permute-start | bytes 983048 | tf_op jit(solution)/shard_map/ppermute | solution.py:20
  59.8 0.9 collective-permute-start.16
  60.6 0.4 collective-permute-start.17
  61.0 1.2 %collective-permute-done.18.refs_0_ = bf16[56,2560]{1,0:T(8,128)(2,1)S(1)} collective-permute-done((bf16[56,2560]{1,0:T(8,128)(2,1)S(1)}, bf16[56,2560]{1,0:T(8,128)(2,1)S(1)}, u32[]{:S(2)}, u32[]{:S(2)}) %collective-permute-start.18) | collective-permute-done | bytes 286752 | tf_op jit(solution)/shard_map/ppermute | solution.py:20
  62.2 0.3 collective-permute-done.19.refs_1_
  62.5 0.1 shard_map.84
  62.7 1.4 %collective-permute-start.20 = (bf16[56,2560]{1,0:T(8,128)(2,1)S(1)}, bf16[56,2560]{1,0:T(8,128)(2,1)S(1)}, u32[]{:S(2)}, u32[]{:S(2)}) collective-permute-start(bf16[56,2560]{1,0:T(8,128)(2,1)S(1)} %get-tuple-element.89), channel_id=1, source_target_pairs={{0,2},{2,4},{4,6},{6,8},{8,10},{10,12},{12,14},{14,0},{1,3},{3,5},... | collective-permute-start | bytes 860168 | tf_op jit(solution)/shard_map/ppermute | solution.py:20
  64.0 1.4 %collective-permute-start.21 = (bf16[56,2560]{1,0:T(8,128)(2,1)S(1)}, bf16[56,2560]{1,0:T(8,128)(2,1)S(1)}, u32[]{:S(2)}, u32[]{:S(2)}) collective-permute-start(bf16[56,2560]{1,0:T(8,128)(2,1)S(1)} %get-tuple-element.90), channel_id=1, source_target_pairs={{0,14},{2,0},{4,2},{6,4},{8,6},{10,8},{12,10},{14,12},{1,15},{3,1}... | collective-permute-start | bytes 860168 | tf_op jit(solution)/shard_map/ppermute | solution.py:20
  65.4 2.6 %shard_map.85 = (bf16[512,128]{1,0:T(8,128)(2,1)S(1)}, bf16[512,128]{1,0:T(8,128)(2,1)S(1)}, bf16[512,128]{1,0:T(8,128)(2,1)S(1)}, bf16[512,128]{1,0:T(8,128)(2,1)S(1)}) custom-call(bf16[512,2560]{1,0:T(8,128)(2,1)S(1)} %get-tuple-element.92.cot, bf16[8,64,2560]{2,1,0:T(8,128)(2,1)S(1)} %get-tuple-element.93.weight, ...), custom_call_target="tpu_custom_call" | custom-call | tf_op jit(solution)/shard_map/pallas_call | solution.py:30
  68.1 3.3 %collective-permute-done.20.refs_0_ = bf16[56,2560]{1,0:T(8,128)(2,1)S(1)} collective-permute-done((bf16[56,2560]{1,0:T(8,128)(2,1)S(1)}, bf16[56,2560]{1,0:T(8,128)(2,1)S(1)}, u32[]{:S(2)}, u32[]{:S(2)}) %collective-permute-start.20) | collective-permute-done | bytes 286752 | tf_op jit(solution)/shard_map/ppermute | solution.py:20
  71.4 0.1 shard_map.86
  71.5 0.1 collective-permute-start.23
  71.6 2.7 %collective-permute-start.24 = (bf16[56,2560]{1,0:T(8,128)(2,1)S(1)}, bf16[56,2560]{1,0:T(8,128)(2,1)S(1)}, u32[]{:S(2)}, u32[]{:S(2)}) collective-permute-start(bf16[56,2560]{1,0:T(8,128)(2,1)S(1)} %get-tuple-element.100), channel_id=1, source_target_pairs={{0,14},{2,0},{4,2},{6,4},{8,6},{10,8},{12,10},{14,12},{1,15},{3,1}... | collective-permute-start | bytes 860168 | tf_op jit(solution)/shard_map/ppermute | solution.py:20
  74.3 3.6 %collective-permute-done.17.h3 = bf16[128,1280]{1,0:T(8,128)(2,1)S(1)} collective-permute-done((bf16[128,1280]{1,0:T(8,128)(2,1)S(1)}, bf16[128,1280]{1,0:T(8,128)(2,1)S(1)}, u32[]{:S(2)}, u32[]{:S(2)}) %collective-permute-start.17) | collective-permute-done | bytes 327712 | tf_op jit(solution)/shard_map/ppermute | solution.py:20
  77.9 0.1 shard_map.87
  78.1 0.0 copy-start
  78.1 0.0 copy-start.1
  78.1 0.5 collective-permute-start.22
  78.6 1.5 %collective-permute-start.29 = (bf16[512,128]{1,0:T(8,128)(2,1)S(1)}, bf16[512,128]{1,0:T(8,128)(2,1)S(1)}, u32[]{:S(2)}, u32[]{:S(2)}) collective-permute-start(bf16[512,128]{1,0:T(8,128)(2,1)S(1)} %get-tuple-element.115), channel_id=1, source_target_pairs={{0,16},{16,32},{32,48},{48,0},{1,17},{17,33},{33,49},{49,1},{2,18}... | collective-permute-start | bytes 393224 | tf_op jit(solution)/shard_map/ppermute | solution.py:20
  80.0 0.3 shard_map.88
  80.3 1.6 %collective-permute-start.26 = (bf16[27,2560]{1,0:T(8,128)(2,1)S(1)}, bf16[27,2560]{1,0:T(8,128)(2,1)S(1)}, u32[]{:S(2)}, u32[]{:S(2)}) collective-permute-start(bf16[27,2560]{1,0:T(8,128)(2,1)S(1)} %get-tuple-element.106), channel_id=1, source_target_pairs={{0,1},{1,0},{2,3},{3,2},{4,5},{5,4},{6,7},{7,6},{8,9},{9,8},{10,11... | collective-permute-start | bytes 414728 | tf_op jit(solution)/shard_map/ppermute | solution.py:20
  82.0 0.9 collective-permute-start.28
  82.8 4.1 %collective-permute-done.22 = bf16[128,1280]{1,0:T(8,128)(2,1)S(1)} collective-permute-done((bf16[128,1280]{1,0:T(8,128)(2,1)S(1)}, bf16[128,1280]{1,0:T(8,128)(2,1)S(1)}, u32[]{:S(2)}, u32[]{:S(2)}) %collective-permute-start.22) | collective-permute-done | bytes 327712 | tf_op jit(solution)/shard_map/ppermute | solution.py:20
  87.0 0.1 add_convert_fusion.mine
  87.1 2.4 %collective-permute-start.25 = (bf16[128,1280]{1,0:T(8,128)(2,1)S(1)}, bf16[128,1280]{1,0:T(8,128)(2,1)S(1)}, u32[]{:S(2)}, u32[]{:S(2)}) collective-permute-start(bf16[128,1280]{1,0:T(8,128)(2,1)S(1)} %add_convert_fusion.mine), channel_id=1, source_target_pairs={{0,64},{64,0},{1,65},{65,1},{2,66},{66,2},{3,67},{67,3},{4,68},{68... | collective-permute-start | bytes 983048 | tf_op jit(solution)/shard_map/ppermute | solution.py:20
  89.5 1.3 %shard_map.90 = (bf16[1728,128]{1,0:T(8,128)(2,1)}, bf16[1728,128]{1,0:T(8,128)(2,1)}) custom-call(bf16[1728,128]{1,0:T(8,128)(2,1)S(1)} %bitcast.5, bf16[1728,128]{1,0:T(8,128)(2,1)S(1)} %bitcast.7, bf16[512,128]{1,0:T(8,128)(2,1)S(1)} %get-tuple-element.111.b0, bf16[512,128]{1,0:T(8,128)(2,1)S(1)} %collective-permute-done.27.b1, ...), custom_call_target="tpu_custom_call" | custom-call | flops 4000000000 | tf_op jit(solution)/shard_map/pallas_call | solution.py:30
  90.8 0.2 collective-permute-done.26.taken
  91.0 1.0 %shard_map.89 = (bf16[128,2560]{1,0:T(8,128)(2,1)}, f32[27,2560]{1,0:T(8,128)}) custom-call(bf16[128,1280]{1,0:T(8,128)(2,1)S(1)} %add_convert_fusion.mine, bf16[128,1280]{1,0:T(8,128)(2,1)S(1)} %collective-permute-done.25.other, f32[27,2560]{1,0:T(8,128)S(1)} %get-tuple-element.108.keep, bf16[27,2560]{1,0:T(8,128)(2,1)S(1)} %collective-permute-done.26.taken), custom_call_target="tpu_custom_call" | custom-call | bytes 2001920 | tf_op jit(solution)/shard_map/pallas_call | solution.py:30
  (23 shorter events, 0.1 us)
Async XLA Ops:
  0.6 11.4 %collective-permute-start = (bf16[27,2560]{1,0:T(8,128)(2,1)}, bf16[27,2560]{1,0:T(8,128)(2,1)S(1)}, u32[]{:S(2)}, u32[]{:S(2)}) collective-permute-start(bf16[27,2560]{1,0:T(8,128)(2,1)} %mine.1), channel_id=1, source_target_pairs={{0,1},{1,0},{2,3},{3,2},{4,5},{5,4},{6,7},{7,6},{8,9},{9,8},{10,11... | collective-permute-start | bytes 414728 | tf_op jit(solution)/shard_map/ppermute | solution.py:20
  7.1 19.9 %collective-permute-start.5 = (bf16[128,1792]{1,0:T(8,128)(2,1)}, bf16[128,1792]{1,0:T(8,128)(2,1)S(1)}, u32[]{:S(2)}, u32[]{:S(2)}) collective-permute-start(bf16[128,1792]{1,0:T(8,128)(2,1)} %get-tuple-element.61), channel_id=1, source_target_pairs={{0,16},{16,32},{32,48},{48,0},{1,17},{17,33},{33,49},{49,1},{2,18}... | collective-permute-start | bytes 1376264 | tf_op jit(solution)/shard_map/ppermute | solution.py:20
  8.4 22.1 %collective-permute-start.6 = (bf16[128,1792]{1,0:T(8,128)(2,1)}, bf16[128,1792]{1,0:T(8,128)(2,1)S(1)}, u32[]{:S(2)}, u32[]{:S(2)}) collective-permute-start(bf16[128,1792]{1,0:T(8,128)(2,1)} %get-tuple-element.62), channel_id=1, source_target_pairs={{0,32},{16,48},{32,0},{48,16},{1,33},{17,49},{33,1},{49,17},{2,34}... | collective-permute-start | bytes 1376264 | tf_op jit(solution)/shard_map/ppermute | solution.py:20
  10.9 19.7 %collective-permute-start.7 = (bf16[128,1792]{1,0:T(8,128)(2,1)}, bf16[128,1792]{1,0:T(8,128)(2,1)S(1)}, u32[]{:S(2)}, u32[]{:S(2)}) collective-permute-start(bf16[128,1792]{1,0:T(8,128)(2,1)} %get-tuple-element.63), channel_id=1, source_target_pairs={{0,48},{16,0},{32,16},{48,32},{1,49},{17,1},{33,17},{49,33},{2,50}... | collective-permute-start | bytes 1376264 | tf_op jit(solution)/shard_map/ppermute | solution.py:20
  12.0 0.9 copy-start.2
  13.3 24.9 %copy-start.3 = (bf16[128,2560]{1,0:T(8,128)(2,1)S(1)}, bf16[128,2560]{1,0:T(8,128)(2,1)}, u32[]{:S(2)}) copy-start(bf16[128,2560]{1,0:T(8,128)(2,1)} %get-tuple-element.71.cot_own) | copy-start | bytes 1966084
  13.3 24.9 %copy-start.4 = (bf16[512,128]{1,0:T(8,128)(2,1)S(1)}, bf16[512,128]{1,0:T(8,128)(2,1)}, u32[]{:S(2)}) copy-start(bf16[512,128]{1,0:T(8,128)(2,1)} %get-tuple-element.72.hid_own) | copy-start | bytes 393220
  13.3 11.0 %collective-permute-start.1 = (bf16[56,2560]{1,0:T(8,128)(2,1)S(1)}, bf16[56,2560]{1,0:T(8,128)(2,1)S(1)}, u32[]{:S(2)}, u32[]{:S(2)}) collective-permute-start(bf16[56,2560]{1,0:T(8,128)(2,1)S(1)} %shard_map.76.w0), channel_id=1, source_target_pairs={{0,2},{2,4},{4,6},{6,8},{8,10},{10,12},{12,14},{14,0},{1,3},{3,5},... | collective-permute-start | bytes 860168 | tf_op jit(solution)/shard_map/ppermute | solution.py:20
  15.0 9.3 %collective-permute-start.2 = (bf16[56,2560]{1,0:T(8,128)(2,1)S(1)}, bf16[56,2560]{1,0:T(8,128)(2,1)S(1)}, u32[]{:S(2)}, u32[]{:S(2)}) collective-permute-start(bf16[56,2560]{1,0:T(8,128)(2,1)S(1)} %shard_map.76.w0), channel_id=1, source_target_pairs={{0,14},{2,0},{4,2},{6,4},{8,6},{10,8},{12,10},{14,12},{1,15},{3,1}... | collective-permute-start | bytes 860168 | tf_op jit(solution)/shard_map/ppermute | solution.py:20
  24.3 7.1 %collective-permute-start.3 = (bf16[56,2560]{1,0:T(8,128)(2,1)S(1)}, bf16[56,2560]{1,0:T(8,128)(2,1)S(1)}, u32[]{:S(2)}, u32[]{:S(2)}) collective-permute-start(bf16[56,2560]{1,0:T(8,128)(2,1)S(1)} %collective-permute-done.1.f1), channel_id=1, source_target_pairs={{0,2},{2,4},{4,6},{6,8},{8,10},{10,12},{12,14},{14,0},{1,3},{3,5},... | collective-permute-start | bytes 860168 | tf_op jit(solution)/shard_map/ppermute | solution.py:20
  24.3 7.1 %collective-permute-start.4 = (bf16[56,2560]{1,0:T(8,128)(2,1)S(1)}, bf16[56,2560]{1,0:T(8,128)(2,1)S(1)}, u32[]{:S(2)}, u32[]{:S(2)}) collective-permute-start(bf16[56,2560]{1,0:T(8,128)(2,1)S(1)} %collective-permute-done.2.b1), channel_id=1, source_target_pairs={{0,14},{2,0},{4,2},{6,4},{8,6},{10,8},{12,10},{14,12},{1,15},{3,1}... | collective-permute-start | bytes 860168 | tf_op jit(solution)/shard_map/ppermute | solution.py:20
  31.4 6.7 %collective-permute-start.10 = (bf16[384,1280]{1,0:T(8,128)(2,1)S(1)}, bf16[384,1280]{1,0:T(8,128)(2,1)S(1)}, u32[]{:S(2)}, u32[]{:S(2)}) collective-permute-start(bf16[384,1280]{1,0:T(8,128)(2,1)S(1)} %shard_map.77), channel_id=1, source_target_pairs={{0,64},{64,0},{1,65},{65,1},{2,66},{66,2},{3,67},{67,3},{4,68},{68... | collective-permute-start | bytes 2949128 | tf_op jit(solution)/shard_map/ppermute | solution.py:20
  34.8 10.5 %collective-permute-start.8 = (bf16[56,2560]{1,0:T(8,128)(2,1)S(1)}, bf16[56,2560]{1,0:T(8,128)(2,1)S(1)}, u32[]{:S(2)}, u32[]{:S(2)}) collective-permute-start(bf16[56,2560]{1,0:T(8,128)(2,1)S(1)} %collective-permute-done.3.f2), channel_id=1, source_target_pairs={{0,2},{2,4},{4,6},{6,8},{8,10},{10,12},{12,14},{14,0},{1,3},{3,5},... | collective-permute-start | bytes 860168 | tf_op jit(solution)/shard_map/ppermute | solution.py:20
  36.8 8.7 %collective-permute-start.9 = (bf16[56,2560]{1,0:T(8,128)(2,1)S(1)}, bf16[56,2560]{1,0:T(8,128)(2,1)S(1)}, u32[]{:S(2)}, u32[]{:S(2)}) collective-permute-start(bf16[56,2560]{1,0:T(8,128)(2,1)S(1)} %collective-permute-done.4.b2), channel_id=1, source_target_pairs={{0,14},{2,0},{4,2},{6,4},{8,6},{10,8},{12,10},{14,12},{1,15},{3,1}... | collective-permute-start | bytes 860168 | tf_op jit(solution)/shard_map/ppermute | solution.py:20
  41.6 10.8 %collective-permute-start.13 = (bf16[56,2560]{1,0:T(8,128)(2,1)S(1)}, bf16[56,2560]{1,0:T(8,128)(2,1)S(1)}, u32[]{:S(2)}, u32[]{:S(2)}) collective-permute-start(bf16[56,2560]{1,0:T(8,128)(2,1)S(1)} %get-tuple-element.80), channel_id=1, source_target_pairs={{0,14},{2,0},{4,2},{6,4},{8,6},{10,8},{12,10},{14,12},{1,15},{3,1}... | collective-permute-start | bytes 860168 | tf_op jit(solution)/shard_map/ppermute | solution.py:20
  45.5 9.7 %collective-permute-start.12 = (bf16[56,2560]{1,0:T(8,128)(2,1)S(1)}, bf16[56,2560]{1,0:T(8,128)(2,1)S(1)}, u32[]{:S(2)}, u32[]{:S(2)}) collective-permute-start(bf16[56,2560]{1,0:T(8,128)(2,1)S(1)} %collective-permute-done.8.f3), channel_id=1, source_target_pairs={{0,2},{2,4},{4,6},{6,8},{8,10},{10,12},{12,14},{14,0},{1,3},{3,5},... | collective-permute-start | bytes 860168 | tf_op jit(solution)/shard_map/ppermute | solution.py:20
  50.1 7.0 %collective-permute-start.11 = (bf16[512,1408]{1,0:T(8,128)(2,1)S(1)}, bf16[512,1408]{1,0:T(8,128)(2,1)S(1)}, u32[]{:S(2)}, u32[]{:S(2)}) collective-permute-start(bf16[512,1408]{1,0:T(8,128)(2,1)S(1)} %get-tuple-element.76), channel_id=1, source_target_pairs={{0,64},{64,0},{1,65},{65,1},{2,66},{66,2},{3,67},{67,3},{4,68},{68... | collective-permute-start | bytes 4325384 | tf_op jit(solution)/shard_map/ppermute | solution.py:20
  52.5 9.7 %collective-permute-start.18 = (bf16[56,2560]{1,0:T(8,128)(2,1)S(1)}, bf16[56,2560]{1,0:T(8,128)(2,1)S(1)}, u32[]{:S(2)}, u32[]{:S(2)}) collective-permute-start(bf16[56,2560]{1,0:T(8,128)(2,1)S(1)} %get-tuple-element.81.value), channel_id=1, source_target_pairs={{0,2},{2,4},{4,6},{6,8},{8,10},{10,12},{12,14},{14,0},{1,3},{3,5},... | collective-permute-start | bytes 860168 | tf_op jit(solution)/shard_map/ppermute | solution.py:20
  53.9 8.6 %collective-permute-start.19 = (bf16[56,2560]{1,0:T(8,128)(2,1)S(1)}, bf16[56,2560]{1,0:T(8,128)(2,1)S(1)}, u32[]{:S(2)}, u32[]{:S(2)}) collective-permute-start(bf16[56,2560]{1,0:T(8,128)(2,1)S(1)} %get-tuple-element.86), channel_id=1, source_target_pairs={{0,14},{2,0},{4,2},{6,4},{8,6},{10,8},{12,10},{14,12},{1,15},{3,1}... | collective-permute-start | bytes 860168 | tf_op jit(solution)/shard_map/ppermute | solution.py:20
  55.3 1.8 %collective-permute-start.14 = (bf16[56,1280]{1,0:T(8,128)(2,1)S(1)}, bf16[56,1280]{1,0:T(8,128)(2,1)S(1)}, u32[]{:S(2)}, u32[]{:S(2)}) collective-permute-start(bf16[56,1280]{1,0:T(8,128)(2,1)S(1)} %shard_map.82), channel_id=1, source_target_pairs={{0,64},{64,0},{1,65},{65,1},{2,66},{66,2},{3,67},{67,3},{4,68},{68... | collective-permute-start | bytes 430088 | tf_op jit(solution)/shard_map/ppermute | solution.py:20
  58.0 16.3 %collective-permute-start.15 = (bf16[128,1280]{1,0:T(8,128)(2,1)S(1)}, bf16[128,1280]{1,0:T(8,128)(2,1)S(1)}, u32[]{:S(2)}, u32[]{:S(2)}) collective-permute-start(bf16[128,1280]{1,0:T(8,128)(2,1)S(1)} %get-tuple-element.83), channel_id=1, source_target_pairs={{0,48},{16,0},{32,16},{48,32},{1,49},{17,1},{33,17},{49,33},{2,50}... | collective-permute-start | bytes 983048 | tf_op jit(solution)/shard_map/ppermute | solution.py:20
  59.8 14.5 %collective-permute-start.16 = (bf16[128,1280]{1,0:T(8,128)(2,1)S(1)}, bf16[128,1280]{1,0:T(8,128)(2,1)S(1)}, u32[]{:S(2)}, u32[]{:S(2)}) collective-permute-start(bf16[128,1280]{1,0:T(8,128)(2,1)S(1)} %get-tuple-element.84), channel_id=1, source_target_pairs={{0,32},{16,48},{32,0},{48,16},{1,33},{17,49},{33,1},{49,17},{2,34}... | collective-permute-start | bytes 983048 | tf_op jit(solution)/shard_map/ppermute | solution.py:20
  60.6 17.3 %collective-permute-start.17 = (bf16[128,1280]{1,0:T(8,128)(2,1)S(1)}, bf16[128,1280]{1,0:T(8,128)(2,1)S(1)}, u32[]{:S(2)}, u32[]{:S(2)}) collective-permute-start(bf16[128,1280]{1,0:T(8,128)(2,1)S(1)} %get-tuple-element.85), channel_id=1, source_target_pairs={{0,16},{16,32},{32,48},{48,0},{1,17},{17,33},{33,49},{49,1},{2,18}... | collective-permute-start | bytes 983048 | tf_op jit(solution)/shard_map/ppermute | solution.py:20
  62.7 8.7 %collective-permute-start.20 = (bf16[56,2560]{1,0:T(8,128)(2,1)S(1)}, bf16[56,2560]{1,0:T(8,128)(2,1)S(1)}, u32[]{:S(2)}, u32[]{:S(2)}) collective-permute-start(bf16[56,2560]{1,0:T(8,128)(2,1)S(1)} %get-tuple-element.89), channel_id=1, source_target_pairs={{0,2},{2,4},{4,6},{6,8},{8,10},{10,12},{12,14},{14,0},{1,3},{3,5},... | collective-permute-start | bytes 860168 | tf_op jit(solution)/shard_map/ppermute | solution.py:20
  64.0 7.3 %collective-permute-start.21 = (bf16[56,2560]{1,0:T(8,128)(2,1)S(1)}, bf16[56,2560]{1,0:T(8,128)(2,1)S(1)}, u32[]{:S(2)}, u32[]{:S(2)}) collective-permute-start(bf16[56,2560]{1,0:T(8,128)(2,1)S(1)} %get-tuple-element.90), channel_id=1, source_target_pairs={{0,14},{2,0},{4,2},{6,4},{8,6},{10,8},{12,10},{14,12},{1,15},{3,1}... | collective-permute-start | bytes 860168 | tf_op jit(solution)/shard_map/ppermute | solution.py:20
  71.5 8.5 %collective-permute-start.23 = (bf16[56,2560]{1,0:T(8,128)(2,1)S(1)}, bf16[56,2560]{1,0:T(8,128)(2,1)S(1)}, u32[]{:S(2)}, u32[]{:S(2)}) collective-permute-start(bf16[56,2560]{1,0:T(8,128)(2,1)S(1)} %get-tuple-element.99), channel_id=1, source_target_pairs={{0,2},{2,4},{4,6},{6,8},{8,10},{10,12},{12,14},{14,0},{1,3},{3,5},... | collective-permute-start | bytes 860168 | tf_op jit(solution)/shard_map/ppermute | solution.py:20
  71.6 8.4 %collective-permute-start.24 = (bf16[56,2560]{1,0:T(8,128)(2,1)S(1)}, bf16[56,2560]{1,0:T(8,128)(2,1)S(1)}, u32[]{:S(2)}, u32[]{:S(2)}) collective-permute-start(bf16[56,2560]{1,0:T(8,128)(2,1)S(1)} %get-tuple-element.100), channel_id=1, source_target_pairs={{0,14},{2,0},{4,2},{6,4},{8,6},{10,8},{12,10},{14,12},{1,15},{3,1}... | collective-permute-start | bytes 860168 | tf_op jit(solution)/shard_map/ppermute | solution.py:20
  78.1 11.4 %copy-start = (bf16[128,1728]{0,1:T(8,128)(2,1)S(1)}, bf16[128,1728]{0,1:T(8,128)(2,1)}, u32[]{:S(2)}) copy-start(bf16[128,1728]{0,1:T(8,128)(2,1)} %param.4) | copy-start | bytes 1327108
  78.1 11.4 %copy-start.1 = (bf16[128,1728]{0,1:T(8,128)(2,1)S(1)}, bf16[128,1728]{0,1:T(8,128)(2,1)}, u32[]{:S(2)}) copy-start(bf16[128,1728]{0,1:T(8,128)(2,1)} %param.5) | copy-start | bytes 1327108
  78.1 8.9 %collective-permute-start.22 = (bf16[128,1280]{1,0:T(8,128)(2,1)S(1)}, bf16[128,1280]{1,0:T(8,128)(2,1)S(1)}, u32[]{:S(2)}, u32[]{:S(2)}) collective-permute-start(bf16[128,1280]{1,0:T(8,128)(2,1)S(1)} %shard_map.87), channel_id=1, source_target_pairs={{0,128},{128,0},{1,129},{129,1},{2,130},{130,2},{3,131},{131,3},{4... | collective-permute-start | bytes 983048 | tf_op jit(solution)/shard_map/ppermute | solution.py:20
  78.6 10.9 %collective-permute-start.27 = (bf16[512,128]{1,0:T(8,128)(2,1)S(1)}, bf16[512,128]{1,0:T(8,128)(2,1)S(1)}, u32[]{:S(2)}, u32[]{:S(2)}) collective-permute-start(bf16[512,128]{1,0:T(8,128)(2,1)S(1)} %get-tuple-element.112), channel_id=1, source_target_pairs={{0,48},{16,0},{32,16},{48,32},{1,49},{17,1},{33,17},{49,33},{2,50}... | collective-permute-start | bytes 393224 | tf_op jit(solution)/shard_map/ppermute | solution.py:20
  78.6 10.9 %collective-permute-start.29 = (bf16[512,128]{1,0:T(8,128)(2,1)S(1)}, bf16[512,128]{1,0:T(8,128)(2,1)S(1)}, u32[]{:S(2)}, u32[]{:S(2)}) collective-permute-start(bf16[512,128]{1,0:T(8,128)(2,1)S(1)} %get-tuple-element.115), channel_id=1, source_target_pairs={{0,16},{16,32},{32,48},{48,0},{1,17},{17,33},{33,49},{49,1},{2,18}... | collective-permute-start | bytes 393224 | tf_op jit(solution)/shard_map/ppermute | solution.py:20
  80.3 10.6 %collective-permute-start.26 = (bf16[27,2560]{1,0:T(8,128)(2,1)S(1)}, bf16[27,2560]{1,0:T(8,128)(2,1)S(1)}, u32[]{:S(2)}, u32[]{:S(2)}) collective-permute-start(bf16[27,2560]{1,0:T(8,128)(2,1)S(1)} %get-tuple-element.106), channel_id=1, source_target_pairs={{0,1},{1,0},{2,3},{3,2},{4,5},{5,4},{6,7},{7,6},{8,9},{9,8},{10,11... | collective-permute-start | bytes 414728 | tf_op jit(solution)/shard_map/ppermute | solution.py:20
  82.0 7.5 %collective-permute-start.28 = (bf16[512,128]{1,0:T(8,128)(2,1)S(1)}, bf16[512,128]{1,0:T(8,128)(2,1)S(1)}, u32[]{:S(2)}, u32[]{:S(2)}) collective-permute-start(bf16[512,128]{1,0:T(8,128)(2,1)S(1)} %get-tuple-element.114), channel_id=1, source_target_pairs={{0,32},{16,48},{32,0},{48,16},{1,33},{17,49},{33,1},{49,17},{2,34}... | collective-permute-start | bytes 393224 | tf_op jit(solution)/shard_map/ppermute | solution.py:20
  87.1 3.9 %collective-permute-start.25 = (bf16[128,1280]{1,0:T(8,128)(2,1)S(1)}, bf16[128,1280]{1,0:T(8,128)(2,1)S(1)}, u32[]{:S(2)}, u32[]{:S(2)}) collective-permute-start(bf16[128,1280]{1,0:T(8,128)(2,1)S(1)} %add_convert_fusion.mine), channel_id=1, source_target_pairs={{0,64},{64,0},{1,65},{65,1},{2,66},{66,2},{3,67},{67,3},{4,68},{68... | collective-permute-start | bytes 983048 | tf_op jit(solution)/shard_map/ppermute | solution.py:20

commit v6 on v5

--- a/solution.py
+++ b/solution.py
@@ -123,10 +123,20 @@
 
 
 def add_up(own, h1, h2, h3, out):
-    total = own[...]
-    for got in (h1, h2, h3):
-        total = total + got[...].astype(F32)
-    out[...] = total.astype(BF16)
+    quarter = h2.shape[1]
+    low = lax.axis_index("yl") == 0
+    total = own[...] + h1[...].astype(F32) + h3[...].astype(F32)
+    more = h2[...].astype(F32)
+
+    @pl.when(low)
+    def _():
+        out[:, :quarter] = (total[:, :quarter] + more).astype(BF16)
+        out[:, quarter:] = total[:, quarter:].astype(BF16)
+
+    @pl.when(jnp.logical_not(low))
+    def _():
+        out[:, :quarter] = total[:, :quarter].astype(BF16)
+        out[:, quarter:] = (total[:, quarter:] + more).astype(BF16)
 
 
 def weight_gradient(scale, cot_own, hid_own, g1, g2, g3, far, pieces, to_bwd, cot, hid, hid_t):
@@ -192,8 +202,9 @@
     out[...] = block[:, out.shape[1] :]
 
 
-def output_parts(product, crossed, opposite, block, block_other, total, m1, m2, m3):
+def output_parts(product, crossed, opposite, block, block_other, total, m1, m3, keep, give, second):
     rows, half = total.shape
+    quarter = half // 2
     own, far = padded(block.at[:, :half]), padded(block_other)
     far_hidden = crossed[:, half : half + SLOT]
     for t in range(half // TILE):
@@ -202,12 +213,27 @@
         value = value + jnp.dot(opposite[...], own[:, here], preferred_element_type=F32)
         value = value + jnp.dot(far_hidden, far[:, here], preferred_element_type=F32)
         total[:, here] = value[:rows]
-        for k, out in enumerate((m1, m2, m3)):
-            out[:, here] = value[(k + 1) * rows : (k + 2) * rows].astype(BF16)
+        m1[:, here] = value[rows : 2 * rows].astype(BF16)
+        second[:, here] = value[2 * rows : 3 * rows]
+        m3[:, here] = value[3 * rows : 4 * rows].astype(BF16)
+
+    @pl.when(lax.axis_index("yl") == 0)
+    def _():
+        keep[...] = second[:, :quarter]
+        give[...] = second[:, quarter:].astype(BF16)
+
+    @pl.when(lax.axis_index("yl") != 0)
+    def _():
+        keep[...] = second[:, quarter:]
+        give[...] = second[:, :quarter].astype(BF16)
 
 
 def first_rows(value, out):
     out[...] = value[: out.shape[0], : out.shape[1]]
+
+
+def add_given(keep, given, out):
+    out[...] = (keep[...] + given[...].astype(F32)).astype(BF16)
 
 
 def back_parts(cot, weight, block, *parts):
@@ -360,19 +386,24 @@
 
     (mark,) = call(first_rows, [like((16, 128))], to_fwd, flops=2 * 10**9)
     (block_half,) = call(other_half, [like((SENT, half))], f4, mark, flops=14 * 10**9)
-    total, m1, m2, m3 = call(
+    total, m1, m3, keep2, give2 = call(
         output_parts,
-        [like((rows, half), F32)] + [like((rows, half))] * 3,
+        [like((rows, half), F32)] + [like((rows, half))] * 2
+        + [like((rows, half // 2), F32), like((rows, half // 2))],
         product, crossed, opposite, f4, shift(block_half, "core", 1),
+        scratch=[pltpu.VMEM((rows, half), F32)],
         flops=1 * 10**9,
         moved=0,
     )
-    got_out = [shift(m, "x", -k) for k, m in ((1, m1), (2, m2), (3, m3))]
+    given2 = shift(give2, "yl", 1)
+    got1, got3 = shift(m1, "x", -1), shift(m3, "x", -3)
+    (m2,) = call(add_given, [like((rows, half // 2))], keep2, given2, moved=0)
+    got_out = [got1, shift(m2, "x", -2), got3]
     back_own, *backs = call(
         back_parts, [like((slots, rows))] * NX, after(cot, m1), weight, f4, moved=0
     )
     back1, back2, back3 = backs
-    ring = after(ring, m1, m2, m3)
+    ring = after(ring, m1, m3)
     to_fwd, to_bwd = added(2, ring)
     ring = (shift(to_fwd, "z", 1), shift(to_bwd, "z", -1))
     *ring, back1, back2, back3 = lax.optimization_barrier((*ring, back1, back2, back3))

time: 92.1 us -> 90.4 us (0.982); the launches traced: 92 us -> 89 us
  waiting for transfers between devices: 25.1 us -> 17.2 us
  starting transfers between devices: 48.5 us -> 53.4 us
    ppermute x30 -> x31, waiting for transfers between devices: 25.1 us -> 17.2 us  [shift(): lax.ppermute(value, axis, [(i, (i + steps) % count) for i in range(count)])]
    ppermute x30 -> x31, starting transfers between devices: 48.5 us -> 53.4 us  [shift(): lax.ppermute(value, axis, [(i, (i + steps) % count) for i in range(count)])]
    pallas_call x16 -> x17, Pallas kernels: 16.5 us -> 16.7 us  [call(): pl.pallas_call(kernel, out_shape=outs, in_specs=[pl.BlockSpec(memory_spac...]
  transfers between devices with their start and end apart: 30 -> 31, of which waited for: 13 -> 11; matrix products, arithmetic and copies ran while one was open for 0% -> 0% of each run, Pallas kernels for 17% -> 18%
where the time goes in v6:
time: 90.4 us; the launch traced here: 89 us
  starting transfers between devices  53.4 us (59%)
  waiting for transfers between devices  17.2 us (19%)
  Pallas kernels  16.7 us (18%)
  local copies, waits for them, and re-layouts  0.94 us (1%)
    ppermute x31, starting transfers between devices, shift(): lax.ppermute(value, axis, [(i, (i + steps) % count) for i in range(count)])  53.4 us
    ppermute x31, waiting for transfers between devices, shift(): lax.ppermute(value, axis, [(i, (i + steps) % count) for i in range(count)])  17.2 us
    pallas_call x17, Pallas kernels, call(): pl.pallas_call(kernel, out_shape=outs, in_specs=[pl.BlockSpec(memory_spac...  16.7 us
  transfers between devices with their start and end apart: 31, of which 11 were waited for; matrix products, arithmetic and copies ran while one was open for 0% of the time, Pallas kernels for 18%

profile of v6, /device:TPU:1, one launch (start us, length us, event | category | flops | bytes accessed | tf_op | source)
XLA Modules:
  0.0 89.0 jit_solution(14528174027551536726)
XLA Ops:
  0.6 3.8 %collective-permute-start = (bf16[27,2560]{1,0:T(8,128)(2,1)}, bf16[27,2560]{1,0:T(8,128)(2,1)S(1)}, u32[]{:S(2)}, u32[]{:S(2)}) collective-permute-start(bf16[27,2560]{1,0:T(8,128)(2,1)} %mine.1), channel_id=1, source_target_pairs={{0,1},{1,0},{2,3},{3,2},{4,5},{5,4},{6,7},{7,6},{8,9},{9,8},{10,11... | collective-permute-start | bytes 414728 | tf_op jit(solution)/shard_map/ppermute | solution.py:20
  4.5 2.7 %shard_map.75 = (bf16[128,1792]{1,0:T(8,128)(2,1)}, bf16[128,1792]{1,0:T(8,128)(2,1)}, bf16[128,1792]{1,0:T(8,128)(2,1)}, bf16[512,128]{1,0:T(8,128)(2,1)}, bf16[128,2560]{1,0:T(8,128)(2,1)}) custom-call(bf16[1728,128]{1,0:T(8,128)(2,1)} %bitcast.4, bf16[1728,128]{1,0:T(8,128)(2,1)} %bitcast.6, bf16[128,2560]{1,0:T(8,128)(2,1)} %cot_hbm.1), custom_call_target="tpu_custom_call" | custom-call | bytes 3702784 | tf_op jit(solution)/shard_map/pallas_call | solution.py:30
  7.1 1.3 %collective-permute-start.5 = (bf16[128,1792]{1,0:T(8,128)(2,1)}, bf16[128,1792]{1,0:T(8,128)(2,1)S(1)}, u32[]{:S(2)}, u32[]{:S(2)}) collective-permute-start(bf16[128,1792]{1,0:T(8,128)(2,1)} %get-tuple-element.62), channel_id=1, source_target_pairs={{0,16},{16,32},{32,48},{48,0},{1,17},{17,33},{33,49},{49,1},{2,18}... | collective-permute-start | bytes 1376264 | tf_op jit(solution)/shard_map/ppermute | solution.py:20
  8.4 2.5 %collective-permute-start.6 = (bf16[128,1792]{1,0:T(8,128)(2,1)}, bf16[128,1792]{1,0:T(8,128)(2,1)S(1)}, u32[]{:S(2)}, u32[]{:S(2)}) collective-permute-start(bf16[128,1792]{1,0:T(8,128)(2,1)} %get-tuple-element.63), channel_id=1, source_target_pairs={{0,32},{16,48},{32,0},{48,16},{1,33},{17,49},{33,1},{49,17},{2,34}... | collective-permute-start | bytes 1376264 | tf_op jit(solution)/shard_map/ppermute | solution.py:20
  10.9 1.2 %collective-permute-start.7 = (bf16[128,1792]{1,0:T(8,128)(2,1)}, bf16[128,1792]{1,0:T(8,128)(2,1)S(1)}, u32[]{:S(2)}, u32[]{:S(2)}) collective-permute-start(bf16[128,1792]{1,0:T(8,128)(2,1)} %get-tuple-element.64), channel_id=1, source_target_pairs={{0,48},{16,0},{32,16},{48,32},{1,49},{17,1},{33,17},{49,33},{2,50}... | collective-permute-start | bytes 1376264 | tf_op jit(solution)/shard_map/ppermute | solution.py:20
  12.0 0.9 %copy-done.2 = bf16[27,2560]{1,0:T(8,128)(2,1)S(1)} copy-done((bf16[27,2560]{1,0:T(8,128)(2,1)S(1)}, bf16[27,2560]{1,0:T(8,128)(2,1)}, u32[]{:S(2)}) %copy-start.2) | copy-done | bytes 138264
  13.0 0.3 shard_map.76.w0
  13.3 0.0 copy-start.3
  13.3 0.0 copy-start.4
  13.3 1.7 %collective-permute-start.1 = (bf16[56,2560]{1,0:T(8,128)(2,1)S(1)}, bf16[56,2560]{1,0:T(8,128)(2,1)S(1)}, u32[]{:S(2)}, u32[]{:S(2)}) collective-permute-start(bf16[56,2560]{1,0:T(8,128)(2,1)S(1)} %shard_map.76.w0), channel_id=1, source_target_pairs={{0,2},{2,4},{4,6},{6,8},{8,10},{10,12},{12,14},{14,0},{1,3},{3,5},... | collective-permute-start | bytes 860168 | tf_op jit(solution)/shard_map/ppermute | solution.py:20
  15.0 4.0 %collective-permute-start.2 = (bf16[56,2560]{1,0:T(8,128)(2,1)S(1)}, bf16[56,2560]{1,0:T(8,128)(2,1)S(1)}, u32[]{:S(2)}, u32[]{:S(2)}) collective-permute-start(bf16[56,2560]{1,0:T(8,128)(2,1)S(1)} %shard_map.76.w0), channel_id=1, source_target_pairs={{0,14},{2,0},{4,2},{6,4},{8,6},{10,8},{12,10},{14,12},{1,15},{3,1}... | collective-permute-start | bytes 860168 | tf_op jit(solution)/shard_map/ppermute | solution.py:20
  19.1 5.3 %collective-permute-done.1.f1 = bf16[56,2560]{1,0:T(8,128)(2,1)S(1)} collective-permute-done((bf16[56,2560]{1,0:T(8,128)(2,1)S(1)}, bf16[56,2560]{1,0:T(8,128)(2,1)S(1)}, u32[]{:S(2)}, u32[]{:S(2)}) %collective-permute-start.1) | collective-permute-done | bytes 286752 | tf_op jit(solution)/shard_map/ppermute | solution.py:20
  24.3 2.7 %collective-permute-start.4 = (bf16[56,2560]{1,0:T(8,128)(2,1)S(1)}, bf16[56,2560]{1,0:T(8,128)(2,1)S(1)}, u32[]{:S(2)}, u32[]{:S(2)}) collective-permute-start(bf16[56,2560]{1,0:T(8,128)(2,1)S(1)} %collective-permute-done.2.b1), channel_id=1, source_target_pairs={{0,14},{2,0},{4,2},{6,4},{8,6},{10,8},{12,10},{14,12},{1,15},{3,1}... | collective-permute-start | bytes 860168 | tf_op jit(solution)/shard_map/ppermute | solution.py:20
  27.0 3.5 %collective-permute-done.6.g2 = bf16[128,1792]{1,0:T(8,128)(2,1)S(1)} collective-permute-done((bf16[128,1792]{1,0:T(8,128)(2,1)}, bf16[128,1792]{1,0:T(8,128)(2,1)S(1)}, u32[]{:S(2)}, u32[]{:S(2)}) %collective-permute-start.6) | collective-permute-done | bytes 458784 | tf_op jit(solution)/shard_map/ppermute | solution.py:20
  30.5 0.1 collective-permute-done.7.g3
  30.6 0.1 shard_map.77
  30.6 0.8 collective-permute-done.3.f2
  31.4 0.0 collective-permute-done.4.b2
  31.4 3.4 %collective-permute-start.10 = (bf16[384,1280]{1,0:T(8,128)(2,1)S(1)}, bf16[384,1280]{1,0:T(8,128)(2,1)S(1)}, u32[]{:S(2)}, u32[]{:S(2)}) collective-permute-start(bf16[384,1280]{1,0:T(8,128)(2,1)S(1)} %shard_map.77), channel_id=1, source_target_pairs={{0,64},{64,0},{1,65},{65,1},{2,66},{66,2},{3,67},{67,3},{4,68},{68... | collective-permute-start | bytes 2949128 | tf_op jit(solution)/shard_map/ppermute | solution.py:20
  34.8 2.0 %collective-permute-start.8 = (bf16[56,2560]{1,0:T(8,128)(2,1)S(1)}, bf16[56,2560]{1,0:T(8,128)(2,1)S(1)}, u32[]{:S(2)}, u32[]{:S(2)}) collective-permute-start(bf16[56,2560]{1,0:T(8,128)(2,1)S(1)} %collective-permute-done.3.f2), channel_id=1, source_target_pairs={{0,2},{2,4},{4,6},{6,8},{8,10},{10,12},{12,14},{14,0},{1,3},{3,5},... | collective-permute-start | bytes 860168 | tf_op jit(solution)/shard_map/ppermute | solution.py:20
  36.8 1.4 %collective-permute-start.9 = (bf16[56,2560]{1,0:T(8,128)(2,1)S(1)}, bf16[56,2560]{1,0:T(8,128)(2,1)S(1)}, u32[]{:S(2)}, u32[]{:S(2)}) collective-permute-start(bf16[56,2560]{1,0:T(8,128)(2,1)S(1)} %collective-permute-done.4.b2), channel_id=1, source_target_pairs={{0,14},{2,0},{4,2},{6,4},{8,6},{10,8},{12,10},{14,12},{1,15},{3,1}... | collective-permute-start | bytes 860168 | tf_op jit(solution)/shard_map/ppermute | solution.py:20
  38.2 0.0 collective-permute-done.10.far
  38.2 3.4 %shard_map.78 = (f32[8,56,2560]{2,1,0:T(8,128)S(1)}, bf16[56,2560]{1,0:T(8,128)(2,1)S(1)}, bf16[512,2560]{1,0:T(8,128)(2,1)S(1)}, bf16[512,512]{1,0:T(8,128)(2,1)S(1)}) custom-call(bf16[128,2560]{1,0:T(8,128)(2,1)S(1)} %copy-done.3, bf16[512,128]{1,0:T(8,128)(2,1)S(1)} %copy-done.4, bf16[128,1792]{1,0:T(8,128)(2,1)S(1)} %collective-permute-done.5.g1, ...), custom_call_target="tpu_custom_call" | custom-call | flops 1342177280 | bytes 11165696 | tf_op jit(solution)/shard_map/pallas_call | solution.py:30
  41.6 2.3 %collective-permute-start.13 = (bf16[56,2560]{1,0:T(8,128)(2,1)S(1)}, bf16[56,2560]{1,0:T(8,128)(2,1)S(1)}, u32[]{:S(2)}, u32[]{:S(2)}) collective-permute-start(bf16[56,2560]{1,0:T(8,128)(2,1)S(1)} %get-tuple-element.81), channel_id=1, source_target_pairs={{0,14},{2,0},{4,2},{6,4},{8,6},{10,8},{12,10},{14,12},{1,15},{3,1}... | collective-permute-start | bytes 860168 | tf_op jit(solution)/shard_map/ppermute | solution.py:20
  43.9 1.4 %collective-permute-done.8.f3 = bf16[56,2560]{1,0:T(8,128)(2,1)S(1)} collective-permute-done((bf16[56,2560]{1,0:T(8,128)(2,1)S(1)}, bf16[56,2560]{1,0:T(8,128)(2,1)S(1)}, u32[]{:S(2)}, u32[]{:S(2)}) %collective-permute-start.8) | collective-permute-done | bytes 286752 | tf_op jit(solution)/shard_map/ppermute | solution.py:20
  45.3 0.3 collective-permute-done.9.b3
  45.5 1.1 %collective-permute-start.12 = (bf16[56,2560]{1,0:T(8,128)(2,1)S(1)}, bf16[56,2560]{1,0:T(8,128)(2,1)S(1)}, u32[]{:S(2)}, u32[]{:S(2)}) collective-permute-start(bf16[56,2560]{1,0:T(8,128)(2,1)S(1)} %collective-permute-done.8.f3), channel_id=1, source_target_pairs={{0,2},{2,4},{4,6},{6,8},{8,10},{10,12},{12,14},{14,0},{1,3},{3,5},... | collective-permute-start | bytes 860168 | tf_op jit(solution)/shard_map/ppermute | solution.py:20
  46.7 3.4 %shard_map.79 = (bf16[8,64,2560]{2,1,0:T(8,128)(2,1)S(1)}, f32[512,2560]{1,0:T(8,128)S(1)}, bf16[512,64]{1,0:T(8,128)(2,1)S(1)}, bf16[512,1408]{1,0:T(8,128)(2,1)S(1)}, bf16[16,128]{1,0:T(8,128)(2,1)S(1)}) custom-call(bf16[56,2560]{1,0:T(8,128)(2,1)S(1)} %shard_map.76.w0, bf16[56,2560]{1,0:T(8,128)(2,1)S(1)} %collective-permute-done.1.f1, ...), custom_call_target="tpu_custom_call" | custom-call | tf_op jit(solution)/shard_map/pallas_call | solution.py:30
  50.1 2.3 %collective-permute-start.11 = (bf16[512,1408]{1,0:T(8,128)(2,1)S(1)}, bf16[512,1408]{1,0:T(8,128)(2,1)S(1)}, u32[]{:S(2)}, u32[]{:S(2)}) collective-permute-start(bf16[512,1408]{1,0:T(8,128)(2,1)S(1)} %get-tuple-element.77), channel_id=1, source_target_pairs={{0,64},{64,0},{1,65},{65,1},{2,66},{66,2},{3,67},{67,3},{4,68},{68... | collective-permute-start | bytes 4325384 | tf_op jit(solution)/shard_map/ppermute | solution.py:20
  52.4 0.0 collective-permute-done.13.refs_1_
  52.4 0.1 shard_map.80
  52.5 1.4 %collective-permute-start.19 = (bf16[56,2560]{1,0:T(8,128)(2,1)S(1)}, bf16[56,2560]{1,0:T(8,128)(2,1)S(1)}, u32[]{:S(2)}, u32[]{:S(2)}) collective-permute-start(bf16[56,2560]{1,0:T(8,128)(2,1)S(1)} %get-tuple-element.82.value), channel_id=1, source_target_pairs={{0,2},{2,4},{4,6},{6,8},{8,10},{10,12},{12,14},{14,0},{1,3},{3,5},... | collective-permute-start | bytes 860168 | tf_op jit(solution)/shard_map/ppermute | solution.py:20
  53.9 1.3 %collective-permute-start.20 = (bf16[56,2560]{1,0:T(8,128)(2,1)S(1)}, bf16[56,2560]{1,0:T(8,128)(2,1)S(1)}, u32[]{:S(2)}, u32[]{:S(2)}) collective-permute-start(bf16[56,2560]{1,0:T(8,128)(2,1)S(1)} %get-tuple-element.88), channel_id=1, source_target_pairs={{0,14},{2,0},{4,2},{6,4},{8,6},{10,8},{12,10},{14,12},{1,15},{3,1}... | collective-permute-start | bytes 860168 | tf_op jit(solution)/shard_map/ppermute | solution.py:20
  55.3 0.8 collective-permute-start.14
  56.1 1.0 %collective-permute-done.14.block_other = bf16[56,1280]{1,0:T(8,128)(2,1)S(1)} collective-permute-done((bf16[56,1280]{1,0:T(8,128)(2,1)S(1)}, bf16[56,1280]{1,0:T(8,128)(2,1)S(1)}, u32[]{:S(2)}, u32[]{:S(2)}) %collective-permute-start.14) | collective-permute-done | bytes 143392 | tf_op jit(solution)/shard_map/ppermute | solution.py:20
  57.1 0.9 %shard_map.83 = (f32[128,1280]{1,0:T(8,128)S(1)}, bf16[128,1280]{1,0:T(8,128)(2,1)S(1)}, bf16[128,1280]{1,0:T(8,128)(2,1)S(1)}, f32[128,640]{1,0:T(8,128)S(1)}, bf16[128,640]{1,0:T(8,128)(2,1)S(1)}) custom-call(f32[512,2560]{1,0:T(8,128)S(1)} %get-tuple-element.76.product, bf16[512,1408]{1,0:T(8,128)(2,1)S(1)} %collective-permute-done.11.crossed, ...), custom_call_target="tpu_custom_call" | custom-call | flops 1000000000 | tf_op jit(solution)/shard_map/pallas_call | solution.py:30
  58.0 0.5 collective-permute-start.16
  58.5 1.7 %collective-permute-start.15 = (bf16[128,1280]{1,0:T(8,128)(2,1)S(1)}, bf16[128,1280]{1,0:T(8,128)(2,1)S(1)}, u32[]{:S(2)}, u32[]{:S(2)}) collective-permute-start(bf16[128,1280]{1,0:T(8,128)(2,1)S(1)} %get-tuple-element.84), channel_id=1, source_target_pairs={{0,48},{16,0},{32,16},{48,32},{1,49},{17,1},{33,17},{49,33},{2,50}... | collective-permute-start | bytes 983048 | tf_op jit(solution)/shard_map/ppermute | solution.py:20
  60.2 0.0 collective-permute-start.18
  60.2 2.0 %collective-permute-done.19.refs_0_ = bf16[56,2560]{1,0:T(8,128)(2,1)S(1)} collective-permute-done((bf16[56,2560]{1,0:T(8,128)(2,1)S(1)}, bf16[56,2560]{1,0:T(8,128)(2,1)S(1)}, u32[]{:S(2)}, u32[]{:S(2)}) %collective-permute-start.19) | collective-permute-done | bytes 286752 | tf_op jit(solution)/shard_map/ppermute | solution.py:20
  62.2 0.3 collective-permute-done.20.refs_1_
  62.5 0.1 shard_map.85
  62.7 1.4 %collective-permute-start.21 = (bf16[56,2560]{1,0:T(8,128)(2,1)S(1)}, bf16[56,2560]{1,0:T(8,128)(2,1)S(1)}, u32[]{:S(2)}, u32[]{:S(2)}) collective-permute-start(bf16[56,2560]{1,0:T(8,128)(2,1)S(1)} %get-tuple-element.91), channel_id=1, source_target_pairs={{0,2},{2,4},{4,6},{6,8},{8,10},{10,12},{12,14},{14,0},{1,3},{3,5},... | collective-permute-start | bytes 860168 | tf_op jit(solution)/shard_map/ppermute | solution.py:20
  64.0 1.4 %collective-permute-start.22 = (bf16[56,2560]{1,0:T(8,128)(2,1)S(1)}, bf16[56,2560]{1,0:T(8,128)(2,1)S(1)}, u32[]{:S(2)}, u32[]{:S(2)}) collective-permute-start(bf16[56,2560]{1,0:T(8,128)(2,1)S(1)} %get-tuple-element.92), channel_id=1, source_target_pairs={{0,14},{2,0},{4,2},{6,4},{8,6},{10,8},{12,10},{14,12},{1,15},{3,1}... | collective-permute-start | bytes 860168 | tf_op jit(solution)/shard_map/ppermute | solution.py:20
  65.5 2.6 %collective-permute-start.17 = (bf16[128,640]{1,0:T(8,128)(2,1)S(1)}, bf16[128,640]{1,0:T(8,128)(2,1)S(1)}, u32[]{:S(2)}, u32[]{:S(2)}) collective-permute-start(bf16[128,640]{1,0:T(8,128)(2,1)S(1)} %shard_map.84), channel_id=1, source_target_pairs={{0,32},{16,48},{32,0},{48,16},{1,33},{17,49},{33,1},{49,17},{2,34}... | collective-permute-start | bytes 491528 | tf_op jit(solution)/shard_map/ppermute | solution.py:20
  68.1 2.6 %shard_map.86 = (bf16[512,128]{1,0:T(8,128)(2,1)S(1)}, bf16[512,128]{1,0:T(8,128)(2,1)S(1)}, bf16[512,128]{1,0:T(8,128)(2,1)S(1)}, bf16[512,128]{1,0:T(8,128)(2,1)S(1)}) custom-call(bf16[512,2560]{1,0:T(8,128)(2,1)S(1)} %get-tuple-element.94.cot, bf16[8,64,2560]{2,1,0:T(8,128)(2,1)S(1)} %get-tuple-element.95.weight, ...), custom_call_target="tpu_custom_call" | custom-call | tf_op jit(solution)/shard_map/pallas_call | solution.py:30
  70.7 0.6 collective-permute-done.21.refs_0_
  71.4 0.1 shard_map.87
  71.5 0.1 collective-permute-start.24
  71.6 2.7 %collective-permute-start.25 = (bf16[56,2560]{1,0:T(8,128)(2,1)S(1)}, bf16[56,2560]{1,0:T(8,128)(2,1)S(1)}, u32[]{:S(2)}, u32[]{:S(2)}) collective-permute-start(bf16[56,2560]{1,0:T(8,128)(2,1)S(1)} %get-tuple-element.102), channel_id=1, source_target_pairs={{0,14},{2,0},{4,2},{6,4},{8,6},{10,8},{12,10},{14,12},{1,15},{3,1}... | collective-permute-start | bytes 860168 | tf_op jit(solution)/shard_map/ppermute | solution.py:20
  74.3 0.2 shard_map.88
  74.5 0.0 copy-start
  74.5 0.0 copy-start.1
  74.5 0.5 collective-permute-start.23
  75.0 2.3 %collective-permute-start.28 = (bf16[512,128]{1,0:T(8,128)(2,1)S(1)}, bf16[512,128]{1,0:T(8,128)(2,1)S(1)}, u32[]{:S(2)}, u32[]{:S(2)}) collective-permute-start(bf16[512,128]{1,0:T(8,128)(2,1)S(1)} %get-tuple-element.114), channel_id=1, source_target_pairs={{0,48},{16,0},{32,16},{48,32},{1,49},{17,1},{33,17},{49,33},{2,50}... | collective-permute-start | bytes 393224 | tf_op jit(solution)/shard_map/ppermute | solution.py:20
  77.3 0.0 collective-permute-start.30
  77.3 1.9 %collective-permute-done.24.fwd = bf16[56,2560]{1,0:T(8,128)(2,1)S(1)} collective-permute-done((bf16[56,2560]{1,0:T(8,128)(2,1)S(1)}, bf16[56,2560]{1,0:T(8,128)(2,1)S(1)}, u32[]{:S(2)}, u32[]{:S(2)}) %collective-permute-start.24) | collective-permute-done | bytes 286752 | tf_op jit(solution)/shard_map/ppermute | solution.py:20
  79.2 0.3 shard_map.89
  79.5 0.2 collective-permute-start.27
  79.7 2.9 %collective-permute-start.29 = (bf16[512,128]{1,0:T(8,128)(2,1)S(1)}, bf16[512,128]{1,0:T(8,128)(2,1)S(1)}, u32[]{:S(2)}, u32[]{:S(2)}) collective-permute-start(bf16[512,128]{1,0:T(8,128)(2,1)S(1)} %get-tuple-element.116), channel_id=1, source_target_pairs={{0,32},{16,48},{32,0},{48,16},{1,33},{17,49},{33,1},{49,17},{2,34}... | collective-permute-start | bytes 393224 | tf_op jit(solution)/shard_map/ppermute | solution.py:20
  82.6 0.1 add_convert_fusion.mine
  82.7 3.9 %collective-permute-start.26 = (bf16[128,1280]{1,0:T(8,128)(2,1)S(1)}, bf16[128,1280]{1,0:T(8,128)(2,1)S(1)}, u32[]{:S(2)}, u32[]{:S(2)}) collective-permute-start(bf16[128,1280]{1,0:T(8,128)(2,1)S(1)} %add_convert_fusion.mine), channel_id=1, source_target_pairs={{0,64},{64,0},{1,65},{65,1},{2,66},{66,2},{3,67},{67,3},{4,68},{68... | collective-permute-start | bytes 983048 | tf_op jit(solution)/shard_map/ppermute | solution.py:20
  86.7 1.3 %shard_map.91 = (bf16[1728,128]{1,0:T(8,128)(2,1)}, bf16[1728,128]{1,0:T(8,128)(2,1)}) custom-call(bf16[1728,128]{1,0:T(8,128)(2,1)S(1)} %bitcast.5, bf16[1728,128]{1,0:T(8,128)(2,1)S(1)} %bitcast.7, bf16[512,128]{1,0:T(8,128)(2,1)S(1)} %get-tuple-element.113.b0, bf16[512,128]{1,0:T(8,128)(2,1)S(1)} %collective-permute-done.28.b1, ...), custom_call_target="tpu_custom_call" | custom-call | flops 4000000000 | tf_op jit(solution)/shard_map/pallas_call | solution.py:30
  88.0 1.0 %shard_map.90 = (bf16[128,2560]{1,0:T(8,128)(2,1)}, f32[27,2560]{1,0:T(8,128)}) custom-call(bf16[128,1280]{1,0:T(8,128)(2,1)S(1)} %add_convert_fusion.mine, bf16[128,1280]{1,0:T(8,128)(2,1)S(1)} %collective-permute-done.26.other, f32[27,2560]{1,0:T(8,128)S(1)} %get-tuple-element.110.keep, bf16[27,2560]{1,0:T(8,128)(2,1)S(1)} %collective-permute-done.27.taken), custom_call_target="tpu_custom_call" | custom-call | bytes 2001920 | tf_op jit(solution)/shard_map/pallas_call | solution.py:30
  (26 shorter events, 0.1 us)
Async XLA Ops:
  0.6 11.4 %collective-permute-start = (bf16[27,2560]{1,0:T(8,128)(2,1)}, bf16[27,2560]{1,0:T(8,128)(2,1)S(1)}, u32[]{:S(2)}, u32[]{:S(2)}) collective-permute-start(bf16[27,2560]{1,0:T(8,128)(2,1)} %mine.1), channel_id=1, source_target_pairs={{0,1},{1,0},{2,3},{3,2},{4,5},{5,4},{6,7},{7,6},{8,9},{9,8},{10,11... | collective-permute-start | bytes 414728 | tf_op jit(solution)/shard_map/ppermute | solution.py:20
  7.1 19.9 %collective-permute-start.5 = (bf16[128,1792]{1,0:T(8,128)(2,1)}, bf16[128,1792]{1,0:T(8,128)(2,1)S(1)}, u32[]{:S(2)}, u32[]{:S(2)}) collective-permute-start(bf16[128,1792]{1,0:T(8,128)(2,1)} %get-tuple-element.62), channel_id=1, source_target_pairs={{0,16},{16,32},{32,48},{48,0},{1,17},{17,33},{33,49},{49,1},{2,18}... | collective-permute-start | bytes 1376264 | tf_op jit(solution)/shard_map/ppermute | solution.py:20
  8.4 22.1 %collective-permute-start.6 = (bf16[128,1792]{1,0:T(8,128)(2,1)}, bf16[128,1792]{1,0:T(8,128)(2,1)S(1)}, u32[]{:S(2)}, u32[]{:S(2)}) collective-permute-start(bf16[128,1792]{1,0:T(8,128)(2,1)} %get-tuple-element.63), channel_id=1, source_target_pairs={{0,32},{16,48},{32,0},{48,16},{1,33},{17,49},{33,1},{49,17},{2,34}... | collective-permute-start | bytes 1376264 | tf_op jit(solution)/shard_map/ppermute | solution.py:20
  10.9 19.7 %collective-permute-start.7 = (bf16[128,1792]{1,0:T(8,128)(2,1)}, bf16[128,1792]{1,0:T(8,128)(2,1)S(1)}, u32[]{:S(2)}, u32[]{:S(2)}) collective-permute-start(bf16[128,1792]{1,0:T(8,128)(2,1)} %get-tuple-element.64), channel_id=1, source_target_pairs={{0,48},{16,0},{32,16},{48,32},{1,49},{17,1},{33,17},{49,33},{2,50}... | collective-permute-start | bytes 1376264 | tf_op jit(solution)/shard_map/ppermute | solution.py:20
  12.0 0.9 %copy-start.2 = (bf16[27,2560]{1,0:T(8,128)(2,1)S(1)}, bf16[27,2560]{1,0:T(8,128)(2,1)}, u32[]{:S(2)}) copy-start(bf16[27,2560]{1,0:T(8,128)(2,1)} %mine.1) | copy-start | bytes 414724
  13.3 24.9 %copy-start.3 = (bf16[128,2560]{1,0:T(8,128)(2,1)S(1)}, bf16[128,2560]{1,0:T(8,128)(2,1)}, u32[]{:S(2)}) copy-start(bf16[128,2560]{1,0:T(8,128)(2,1)} %get-tuple-element.72.cot_own) | copy-start | bytes 1966084
  13.3 24.9 %copy-start.4 = (bf16[512,128]{1,0:T(8,128)(2,1)S(1)}, bf16[512,128]{1,0:T(8,128)(2,1)}, u32[]{:S(2)}) copy-start(bf16[512,128]{1,0:T(8,128)(2,1)} %get-tuple-element.73.hid_own) | copy-start | bytes 393220
  13.3 11.0 %collective-permute-start.1 = (bf16[56,2560]{1,0:T(8,128)(2,1)S(1)}, bf16[56,2560]{1,0:T(8,128)(2,1)S(1)}, u32[]{:S(2)}, u32[]{:S(2)}) collective-permute-start(bf16[56,2560]{1,0:T(8,128)(2,1)S(1)} %shard_map.76.w0), channel_id=1, source_target_pairs={{0,2},{2,4},{4,6},{6,8},{8,10},{10,12},{12,14},{14,0},{1,3},{3,5},... | collective-permute-start | bytes 860168 | tf_op jit(solution)/shard_map/ppermute | solution.py:20
  15.0 9.3 %collective-permute-start.2 = (bf16[56,2560]{1,0:T(8,128)(2,1)S(1)}, bf16[56,2560]{1,0:T(8,128)(2,1)S(1)}, u32[]{:S(2)}, u32[]{:S(2)}) collective-permute-start(bf16[56,2560]{1,0:T(8,128)(2,1)S(1)} %shard_map.76.w0), channel_id=1, source_target_pairs={{0,14},{2,0},{4,2},{6,4},{8,6},{10,8},{12,10},{14,12},{1,15},{3,1}... | collective-permute-start | bytes 860168 | tf_op jit(solution)/shard_map/ppermute | solution.py:20
  24.3 7.1 %collective-permute-start.3 = (bf16[56,2560]{1,0:T(8,128)(2,1)S(1)}, bf16[56,2560]{1,0:T(8,128)(2,1)S(1)}, u32[]{:S(2)}, u32[]{:S(2)}) collective-permute-start(bf16[56,2560]{1,0:T(8,128)(2,1)S(1)} %collective-permute-done.1.f1), channel_id=1, source_target_pairs={{0,2},{2,4},{4,6},{6,8},{8,10},{10,12},{12,14},{14,0},{1,3},{3,5},... | collective-permute-start | bytes 860168 | tf_op jit(solution)/shard_map/ppermute | solution.py:20
  24.3 7.1 %collective-permute-start.4 = (bf16[56,2560]{1,0:T(8,128)(2,1)S(1)}, bf16[56,2560]{1,0:T(8,128)(2,1)S(1)}, u32[]{:S(2)}, u32[]{:S(2)}) collective-permute-start(bf16[56,2560]{1,0:T(8,128)(2,1)S(1)} %collective-permute-done.2.b1), channel_id=1, source_target_pairs={{0,14},{2,0},{4,2},{6,4},{8,6},{10,8},{12,10},{14,12},{1,15},{3,1}... | collective-permute-start | bytes 860168 | tf_op jit(solution)/shard_map/ppermute | solution.py:20
  31.4 6.7 %collective-permute-start.10 = (bf16[384,1280]{1,0:T(8,128)(2,1)S(1)}, bf16[384,1280]{1,0:T(8,128)(2,1)S(1)}, u32[]{:S(2)}, u32[]{:S(2)}) collective-permute-start(bf16[384,1280]{1,0:T(8,128)(2,1)S(1)} %shard_map.77), channel_id=1, source_target_pairs={{0,64},{64,0},{1,65},{65,1},{2,66},{66,2},{3,67},{67,3},{4,68},{68... | collective-permute-start | bytes 2949128 | tf_op jit(solution)/shard_map/ppermute | solution.py:20
  34.8 10.5 %collective-permute-start.8 = (bf16[56,2560]{1,0:T(8,128)(2,1)S(1)}, bf16[56,2560]{1,0:T(8,128)(2,1)S(1)}, u32[]{:S(2)}, u32[]{:S(2)}) collective-permute-start(bf16[56,2560]{1,0:T(8,128)(2,1)S(1)} %collective-permute-done.3.f2), channel_id=1, source_target_pairs={{0,2},{2,4},{4,6},{6,8},{8,10},{10,12},{12,14},{14,0},{1,3},{3,5},... | collective-permute-start | bytes 860168 | tf_op jit(solution)/shard_map/ppermute | solution.py:20
  36.8 8.7 %collective-permute-start.9 = (bf16[56,2560]{1,0:T(8,128)(2,1)S(1)}, bf16[56,2560]{1,0:T(8,128)(2,1)S(1)}, u32[]{:S(2)}, u32[]{:S(2)}) collective-permute-start(bf16[56,2560]{1,0:T(8,128)(2,1)S(1)} %collective-permute-done.4.b2), channel_id=1, source_target_pairs={{0,14},{2,0},{4,2},{6,4},{8,6},{10,8},{12,10},{14,12},{1,15},{3,1}... | collective-permute-start | bytes 860168 | tf_op jit(solution)/shard_map/ppermute | solution.py:20
  41.6 10.8 %collective-permute-start.13 = (bf16[56,2560]{1,0:T(8,128)(2,1)S(1)}, bf16[56,2560]{1,0:T(8,128)(2,1)S(1)}, u32[]{:S(2)}, u32[]{:S(2)}) collective-permute-start(bf16[56,2560]{1,0:T(8,128)(2,1)S(1)} %get-tuple-element.81), channel_id=1, source_target_pairs={{0,14},{2,0},{4,2},{6,4},{8,6},{10,8},{12,10},{14,12},{1,15},{3,1}... | collective-permute-start | bytes 860168 | tf_op jit(solution)/shard_map/ppermute | solution.py:20
  45.5 9.7 %collective-permute-start.12 = (bf16[56,2560]{1,0:T(8,128)(2,1)S(1)}, bf16[56,2560]{1,0:T(8,128)(2,1)S(1)}, u32[]{:S(2)}, u32[]{:S(2)}) collective-permute-start(bf16[56,2560]{1,0:T(8,128)(2,1)S(1)} %collective-permute-done.8.f3), channel_id=1, source_target_pairs={{0,2},{2,4},{4,6},{6,8},{8,10},{10,12},{12,14},{14,0},{1,3},{3,5},... | collective-permute-start | bytes 860168 | tf_op jit(solution)/shard_map/ppermute | solution.py:20
  50.1 7.0 %collective-permute-start.11 = (bf16[512,1408]{1,0:T(8,128)(2,1)S(1)}, bf16[512,1408]{1,0:T(8,128)(2,1)S(1)}, u32[]{:S(2)}, u32[]{:S(2)}) collective-permute-start(bf16[512,1408]{1,0:T(8,128)(2,1)S(1)} %get-tuple-element.77), channel_id=1, source_target_pairs={{0,64},{64,0},{1,65},{65,1},{2,66},{66,2},{3,67},{67,3},{4,68},{68... | collective-permute-start | bytes 4325384 | tf_op jit(solution)/shard_map/ppermute | solution.py:20
  52.5 9.7 %collective-permute-start.19 = (bf16[56,2560]{1,0:T(8,128)(2,1)S(1)}, bf16[56,2560]{1,0:T(8,128)(2,1)S(1)}, u32[]{:S(2)}, u32[]{:S(2)}) collective-permute-start(bf16[56,2560]{1,0:T(8,128)(2,1)S(1)} %get-tuple-element.82.value), channel_id=1, source_target_pairs={{0,2},{2,4},{4,6},{6,8},{8,10},{10,12},{12,14},{14,0},{1,3},{3,5},... | collective-permute-start | bytes 860168 | tf_op jit(solution)/shard_map/ppermute | solution.py:20
  53.9 8.6 %collective-permute-start.20 = (bf16[56,2560]{1,0:T(8,128)(2,1)S(1)}, bf16[56,2560]{1,0:T(8,128)(2,1)S(1)}, u32[]{:S(2)}, u32[]{:S(2)}) collective-permute-start(bf16[56,2560]{1,0:T(8,128)(2,1)S(1)} %get-tuple-element.88), channel_id=1, source_target_pairs={{0,14},{2,0},{4,2},{6,4},{8,6},{10,8},{12,10},{14,12},{1,15},{3,1}... | collective-permute-start | bytes 860168 | tf_op jit(solution)/shard_map/ppermute | solution.py:20
  55.3 1.8 %collective-permute-start.14 = (bf16[56,1280]{1,0:T(8,128)(2,1)S(1)}, bf16[56,1280]{1,0:T(8,128)(2,1)S(1)}, u32[]{:S(2)}, u32[]{:S(2)}) collective-permute-start(bf16[56,1280]{1,0:T(8,128)(2,1)S(1)} %shard_map.82), channel_id=1, source_target_pairs={{0,64},{64,0},{1,65},{65,1},{2,66},{66,2},{3,67},{67,3},{4,68},{68... | collective-permute-start | bytes 430088 | tf_op jit(solution)/shard_map/ppermute | solution.py:20
  58.0 7.4 %collective-permute-start.16 = (bf16[128,640]{1,0:T(8,128)(2,1)S(1)}, bf16[128,640]{1,0:T(8,128)(2,1)S(1)}, u32[]{:S(2)}, u32[]{:S(2)}) collective-permute-start(bf16[128,640]{1,0:T(8,128)(2,1)S(1)} %get-tuple-element.86), channel_id=1, source_target_pairs={{0,128},{128,0},{1,129},{129,1},{2,130},{130,2},{3,131},{131,3},{4... | collective-permute-start | bytes 491528 | tf_op jit(solution)/shard_map/ppermute | solution.py:20
  58.5 15.8 %collective-permute-start.15 = (bf16[128,1280]{1,0:T(8,128)(2,1)S(1)}, bf16[128,1280]{1,0:T(8,128)(2,1)S(1)}, u32[]{:S(2)}, u32[]{:S(2)}) collective-permute-start(bf16[128,1280]{1,0:T(8,128)(2,1)S(1)} %get-tuple-element.84), channel_id=1, source_target_pairs={{0,48},{16,0},{32,16},{48,32},{1,49},{17,1},{33,17},{49,33},{2,50}... | collective-permute-start | bytes 983048 | tf_op jit(solution)/shard_map/ppermute | solution.py:20
  60.2 14.1 %collective-permute-start.18 = (bf16[128,1280]{1,0:T(8,128)(2,1)S(1)}, bf16[128,1280]{1,0:T(8,128)(2,1)S(1)}, u32[]{:S(2)}, u32[]{:S(2)}) collective-permute-start(bf16[128,1280]{1,0:T(8,128)(2,1)S(1)} %get-tuple-element.87), channel_id=1, source_target_pairs={{0,16},{16,32},{32,48},{48,0},{1,17},{17,33},{33,49},{49,1},{2,18}... | collective-permute-start | bytes 983048 | tf_op jit(solution)/shard_map/ppermute | solution.py:20
  62.7 8.7 %collective-permute-start.21 = (bf16[56,2560]{1,0:T(8,128)(2,1)S(1)}, bf16[56,2560]{1,0:T(8,128)(2,1)S(1)}, u32[]{:S(2)}, u32[]{:S(2)}) collective-permute-start(bf16[56,2560]{1,0:T(8,128)(2,1)S(1)} %get-tuple-element.91), channel_id=1, source_target_pairs={{0,2},{2,4},{4,6},{6,8},{8,10},{10,12},{12,14},{14,0},{1,3},{3,5},... | collective-permute-start | bytes 860168 | tf_op jit(solution)/shard_map/ppermute | solution.py:20
  64.0 7.3 %collective-permute-start.22 = (bf16[56,2560]{1,0:T(8,128)(2,1)S(1)}, bf16[56,2560]{1,0:T(8,128)(2,1)S(1)}, u32[]{:S(2)}, u32[]{:S(2)}) collective-permute-start(bf16[56,2560]{1,0:T(8,128)(2,1)S(1)} %get-tuple-element.92), channel_id=1, source_target_pairs={{0,14},{2,0},{4,2},{6,4},{8,6},{10,8},{12,10},{14,12},{1,15},{3,1}... | collective-permute-start | bytes 860168 | tf_op jit(solution)/shard_map/ppermute | solution.py:20
  65.5 8.8 %collective-permute-start.17 = (bf16[128,640]{1,0:T(8,128)(2,1)S(1)}, bf16[128,640]{1,0:T(8,128)(2,1)S(1)}, u32[]{:S(2)}, u32[]{:S(2)}) collective-permute-start(bf16[128,640]{1,0:T(8,128)(2,1)S(1)} %shard_map.84), channel_id=1, source_target_pairs={{0,32},{16,48},{32,0},{48,16},{1,33},{17,49},{33,1},{49,17},{2,34}... | collective-permute-start | bytes 491528 | tf_op jit(solution)/shard_map/ppermute | solution.py:20
  71.5 7.7 %collective-permute-start.24 = (bf16[56,2560]{1,0:T(8,128)(2,1)S(1)}, bf16[56,2560]{1,0:T(8,128)(2,1)S(1)}, u32[]{:S(2)}, u32[]{:S(2)}) collective-permute-start(bf16[56,2560]{1,0:T(8,128)(2,1)S(1)} %get-tuple-element.101), channel_id=1, source_target_pairs={{0,2},{2,4},{4,6},{6,8},{8,10},{10,12},{12,14},{14,0},{1,3},{3,5},... | collective-permute-start | bytes 860168 | tf_op jit(solution)/shard_map/ppermute | solution.py:20
  71.6 7.6 %collective-permute-start.25 = (bf16[56,2560]{1,0:T(8,128)(2,1)S(1)}, bf16[56,2560]{1,0:T(8,128)(2,1)S(1)}, u32[]{:S(2)}, u32[]{:S(2)}) collective-permute-start(bf16[56,2560]{1,0:T(8,128)(2,1)S(1)} %get-tuple-element.102), channel_id=1, source_target_pairs={{0,14},{2,0},{4,2},{6,4},{8,6},{10,8},{12,10},{14,12},{1,15},{3,1}... | collective-permute-start | bytes 860168 | tf_op jit(solution)/shard_map/ppermute | solution.py:20
  74.5 12.2 %copy-start = (bf16[128,1728]{0,1:T(8,128)(2,1)S(1)}, bf16[128,1728]{0,1:T(8,128)(2,1)}, u32[]{:S(2)}) copy-start(bf16[128,1728]{0,1:T(8,128)(2,1)} %param.4) | copy-start | bytes 1327108
  74.5 12.2 %copy-start.1 = (bf16[128,1728]{0,1:T(8,128)(2,1)S(1)}, bf16[128,1728]{0,1:T(8,128)(2,1)}, u32[]{:S(2)}) copy-start(bf16[128,1728]{0,1:T(8,128)(2,1)} %param.5) | copy-start | bytes 1327108
  74.5 8.1 %collective-permute-start.23 = (bf16[128,1280]{1,0:T(8,128)(2,1)S(1)}, bf16[128,1280]{1,0:T(8,128)(2,1)S(1)}, u32[]{:S(2)}, u32[]{:S(2)}) collective-permute-start(bf16[128,1280]{1,0:T(8,128)(2,1)S(1)} %shard_map.88), channel_id=1, source_target_pairs={{0,128},{128,0},{1,129},{129,1},{2,130},{130,2},{3,131},{131,3},{4... | collective-permute-start | bytes 983048 | tf_op jit(solution)/shard_map/ppermute | solution.py:20
  75.0 11.6 %collective-permute-start.28 = (bf16[512,128]{1,0:T(8,128)(2,1)S(1)}, bf16[512,128]{1,0:T(8,128)(2,1)S(1)}, u32[]{:S(2)}, u32[]{:S(2)}) collective-permute-start(bf16[512,128]{1,0:T(8,128)(2,1)S(1)} %get-tuple-element.114), channel_id=1, source_target_pairs={{0,48},{16,0},{32,16},{48,32},{1,49},{17,1},{33,17},{49,33},{2,50}... | collective-permute-start | bytes 393224 | tf_op jit(solution)/shard_map/ppermute | solution.py:20
  77.3 9.4 %collective-permute-start.30 = (bf16[512,128]{1,0:T(8,128)(2,1)S(1)}, bf16[512,128]{1,0:T(8,128)(2,1)S(1)}, u32[]{:S(2)}, u32[]{:S(2)}) collective-permute-start(bf16[512,128]{1,0:T(8,128)(2,1)S(1)} %get-tuple-element.117), channel_id=1, source_target_pairs={{0,16},{16,32},{32,48},{48,0},{1,17},{17,33},{33,49},{49,1},{2,18}... | collective-permute-start | bytes 393224 | tf_op jit(solution)/shard_map/ppermute | solution.py:20
  79.5 8.5 %collective-permute-start.27 = (bf16[27,2560]{1,0:T(8,128)(2,1)S(1)}, bf16[27,2560]{1,0:T(8,128)(2,1)S(1)}, u32[]{:S(2)}, u32[]{:S(2)}) collective-permute-start(bf16[27,2560]{1,0:T(8,128)(2,1)S(1)} %get-tuple-element.108), channel_id=1, source_target_pairs={{0,1},{1,0},{2,3},{3,2},{4,5},{5,4},{6,7},{7,6},{8,9},{9,8},{10,11... | collective-permute-start | bytes 414728 | tf_op jit(solution)/shard_map/ppermute | solution.py:20
  79.7 7.0 %collective-permute-start.29 = (bf16[512,128]{1,0:T(8,128)(2,1)S(1)}, bf16[512,128]{1,0:T(8,128)(2,1)S(1)}, u32[]{:S(2)}, u32[]{:S(2)}) collective-permute-start(bf16[512,128]{1,0:T(8,128)(2,1)S(1)} %get-tuple-element.116), channel_id=1, source_target_pairs={{0,32},{16,48},{32,0},{48,16},{1,33},{17,49},{33,1},{49,17},{2,34}... | collective-permute-start | bytes 393224 | tf_op jit(solution)/shard_map/ppermute | solution.py:20
  82.7 5.3 %collective-permute-start.26 = (bf16[128,1280]{1,0:T(8,128)(2,1)S(1)}, bf16[128,1280]{1,0:T(8,128)(2,1)S(1)}, u32[]{:S(2)}, u32[]{:S(2)}) collective-permute-start(bf16[128,1280]{1,0:T(8,128)(2,1)S(1)} %add_convert_fusion.mine), channel_id=1, source_target_pairs={{0,64},{64,0},{1,65},{65,1},{2,66},{66,2},{3,67},{67,3},{4,68},{68... | collective-permute-start | bytes 983048 | tf_op jit(solution)/shard_map/ppermute | solution.py:20

commit v7 on v6

--- a/solution.py
+++ b/solution.py
@@ -92,8 +92,11 @@
         load.wait()
     mine = cot.at[:, pl.ds(pl.multiple_of(core * half, half), half)]
     other = cot.at[:, pl.ds(pl.multiple_of((1 - core) * half, half), half)]
-    for out in (m1, m2, m3, cot_own):
+    for out in (m1, m3, cot_own):
         copy(mine, out.at[:, pl.ds(0, half)])
+    quarter = half // 2
+    start = pl.multiple_of(core * half + lax.axis_index("yl") * quarter, quarter)
+    copy(cot.at[:, pl.ds(start, quarter)], m2.at[:, pl.ds(0, quarter)])
     copy(other, cot_own.at[:, pl.ds(half, half)])
     inside = lax.broadcasted_iota(jnp.int32, (SLOT, rows), 0) < used
     for s in range(NX):
@@ -108,7 +111,8 @@
             row, column = block * SLOT % rows, block * SLOT // rows * rows
             slots[s, row : row + SLOT, column : column + rows] = value
     for k, out in enumerate((m1, m2, m3)):
-        copy(slots.at[lax.rem(x + k + 1, NX)], out.at[:, pl.ds(half, NZ * SLOT)])
+        start = out.shape[1] - NZ * SLOT
+        copy(slots.at[lax.rem(x + k + 1, NX)], out.at[:, pl.ds(start, NZ * SLOT)])
     for i in range(NZ * SLOT // rows):
         here = pl.ds(i * rows, rows)
         copy(slots.at[x, :, here], hid_own.at[here])
@@ -116,10 +120,21 @@
         last.wait()
 
 
-def stack_halves(g1, g2, g3, out):
-    rows, half = g1.shape[0], out.shape[1]
-    for k, got in enumerate((g1, g2, g3)):
-        out[k * rows : (k + 1) * rows] = got[:, :half]
+def near_halves(g1, g2, g3, swapped2, n1, n2, n3):
+    half = n1.shape[1]
+    quarter = half // 2
+    n1[...] = g1[:, :half]
+    n3[...] = g3[:, :half]
+
+    @pl.when(lax.axis_index("yl") == 0)
+    def _():
+        n2[:, :quarter] = g2[:, :quarter]
+        n2[:, quarter:] = swapped2[:, :quarter]
+
+    @pl.when(lax.axis_index("yl") != 0)
+    def _():
+        n2[:, :quarter] = swapped2[:, :quarter]
+        n2[:, quarter:] = g2[:, :quarter]
 
 
 def add_up(own, h1, h2, h3, out):
@@ -139,16 +154,16 @@
         out[:, quarter:] = (total[:, quarter:] + more).astype(BF16)
 
 
-def weight_gradient(scale, cot_own, hid_own, g1, g2, g3, far, pieces, to_bwd, cot, hid, hid_t):
+def weight_gradient(scale, cot_own, hid_own, g1, g2, g3, n2, f1, f2, f3, pieces, to_bwd, cot, hid, hid_t):
     rows, half = cot_own.shape[0], cot_own.shape[1] // 2
     cot[:rows] = cot_own[...]
     hid_t[:, :rows] = hid_own[...]
-    for k, got in enumerate((g1, g2, g3)):
+    for k, (got, near, far) in enumerate(((g1, g1, f1), (g2, n2, f2), (g3, g3, f3))):
         here = slice((k + 1) * rows, (k + 2) * rows)
-        cot[here, :half] = got[:, :half]
-        cot[here, half:] = far[k * rows : (k + 1) * rows]
+        cot[here, :half] = near[:, :half]
+        cot[here, half:] = far[...]
         for i in range(NZ * SLOT // rows):
-            from_column = half + i * rows
+            from_column = got.shape[1] - NZ * SLOT + i * rows
             hid_t[i * rows : (i + 1) * rows, here] = got[:, from_column : from_column + rows]
     z = lax.axis_index("z")
 
@@ -331,7 +346,8 @@
     w_other = shift(down_weight, "yh", 1)
     m1, m2, m3, hid_own, cot_own = call(
         prepare,
-        [like((rows, wide))] * 3 + [like((slots, rows)), like((rows, width))],
+        [like((rows, wide)), like((rows, wide - half // 2)), like((rows, wide))]
+        + [like((slots, rows)), like((rows, width))],
         gate, up, cotangent,
         scratch=[pltpu.VMEM((rows, width), BF16)]
         + [pltpu.VMEM((units, rows), BF16)] * 2
@@ -342,34 +358,39 @@
         limit=56,
     )
     w_other = after(w_other, m1, m2, m3)
-    (w0,) = call(pack_weight, [like((SENT, width))], down_weight, w_other)
+    (w0,) = call(pack_weight, [like((SENT, width))], down_weight, w_other, flops=18 * 10**8)
     got = [shift(m, "x", k) for k, m in ((1, m1), (2, m2), (3, m3))]
 
-    (near,) = call(stack_halves, [like(((NX - 1) * rows, half))], *got, flops=2 * 10**9)
+    nears = call(
+        near_halves,
+        [like((rows, half))] * 3,
+        *got, shift(got[1], "yl", 1),
+        flops=200 * 10**6,
+        moved=0,
+    )
+    far = [shift(near, "core", 1) for near in nears]
 
     fwd, bwd = [w0], [w0]
     for step in range(3):
         f, b = shift(fwd[-1], "z", 1), shift(bwd[-1], "z", -1)
-        if step == 1:
-            f, b, near = lax.optimization_barrier((f, b, near))
-        else:
-            f, b = lax.optimization_barrier((f, b))
+        f, b = lax.optimization_barrier((f, b))
         fwd.append(f)
         bwd.append(b)
-    far = shift(near, "core", 1)
     scale = float(tokens * NZ * 2) ** (-0.5)
     pieces, to_bwd, cot, hid = call(
         functools.partial(weight_gradient, scale),
         [like((NZ, SENT, width), F32), like((SENT, width)), like((tokens, width)), like((tokens, slots))],
-        cot_own, hid_own, *got, far,
+        cot_own, hid_own, *got, nears[1], *far,
         scratch=[pltpu.VMEM((slots, tokens), BF16)],
-        flops=2 * slots * tokens * width,
+        flops=0,
+        moved=0,
     )
 
     def added(distance, ring, *others):
         kernel = functools.partial(add_pieces, distance, len(others))
         return call(kernel, [like((SENT, width))] * 2, pieces, *others, *ring, moved=0)
 
+    fwd[3], to_bwd = lax.optimization_barrier((fwd[3], to_bwd))
     f4 = shift(fwd[3], "z", 1)
     ring = (shift(to_bwd, "z", -1),)
 

time: 90.4 us -> 88.9 us (0.983)
  waiting for transfers between devices: 17.2 us -> 12.5 us
  starting transfers between devices: 53.4 us -> 56.3 us
    ppermute x31 -> x34, waiting for transfers between devices: 17.2 us -> 12.5 us  [shift(): lax.ppermute(value, axis, [(i, (i + steps) % count) for i in range(count)])]
    ppermute x31 -> x34, starting transfers between devices: 53.4 us -> 56.3 us  [shift(): lax.ppermute(value, axis, [(i, (i + steps) % count) for i in range(count)])]
  transfers between devices with their start and end apart: 31 -> 34, of which waited for: 11 -> 8; matrix products, arithmetic and copies ran while one was open for 0% -> 0% of each run, Pallas kernels for 18% -> 18%
where the time goes in v7:
time: 88.9 us; the launch traced here: 87.2 us
  starting transfers between devices  56.3 us (63%)
  Pallas kernels  16.6 us (19%)
  waiting for transfers between devices  12.5 us (14%)
  local copies, waits for them, and re-layouts  0.94 us (1%)
    ppermute x34, starting transfers between devices, shift(): lax.ppermute(value, axis, [(i, (i + steps) % count) for i in range(count)])  56.3 us
    pallas_call x17, Pallas kernels, call(): pl.pallas_call(kernel, out_shape=outs, in_specs=[pl.BlockSpec(memory_spac...  16.6 us
    ppermute x34, waiting for transfers between devices, shift(): lax.ppermute(value, axis, [(i, (i + steps) % count) for i in range(count)])  12.5 us
  transfers between devices with their start and end apart: 34, of which 8 were waited for; matrix products, arithmetic and copies ran while one was open for 0% of the time, Pallas kernels for 18%

profile of v7, /device:TPU:1, one launch (start us, length us, event | category | flops | bytes accessed | tf_op | source)
XLA Modules:
  0.0 87.2 jit_solution(4269994116738967952)
XLA Ops:
  0.6 3.8 %collective-permute-start = (bf16[27,2560]{1,0:T(8,128)(2,1)}, bf16[27,2560]{1,0:T(8,128)(2,1)S(1)}, u32[]{:S(2)}, u32[]{:S(2)}) collective-permute-start(bf16[27,2560]{1,0:T(8,128)(2,1)} %mine.1), channel_id=1, source_target_pairs={{0,1},{1,0},{2,3},{3,2},{4,5},{5,4},{6,7},{7,6},{8,9},{9,8},{10,11... | collective-permute-start | bytes 414728 | tf_op jit(solution)/shard_map/ppermute | solution.py:20
  4.5 2.6 %shard_map.75 = (bf16[128,1792]{1,0:T(8,128)(2,1)}, bf16[128,1152]{1,0:T(8,128)(2,1)}, bf16[128,1792]{1,0:T(8,128)(2,1)}, bf16[512,128]{1,0:T(8,128)(2,1)}, bf16[128,2560]{1,0:T(8,128)(2,1)}) custom-call(bf16[1728,128]{1,0:T(8,128)(2,1)} %bitcast.4, bf16[1728,128]{1,0:T(8,128)(2,1)} %bitcast.6, bf16[128,2560]{1,0:T(8,128)(2,1)} %cot_hbm.1), custom_call_target="tpu_custom_call" | custom-call | bytes 3538944 | tf_op jit(solution)/shard_map/pallas_call | solution.py:30
  7.1 2.8 %collective-permute-start.8 = (bf16[128,1152]{1,0:T(8,128)(2,1)}, bf16[128,1152]{1,0:T(8,128)(2,1)S(1)}, u32[]{:S(2)}, u32[]{:S(2)}) collective-permute-start(bf16[128,1152]{1,0:T(8,128)(2,1)} %get-tuple-element.67), channel_id=1, source_target_pairs={{0,32},{16,48},{32,0},{48,16},{1,33},{17,49},{33,1},{49,17},{2,34}... | collective-permute-start | bytes 884744 | tf_op jit(solution)/shard_map/ppermute | solution.py:20
  9.9 0.9 %copy-done.4 = bf16[27,2560]{1,0:T(8,128)(2,1)S(1)} copy-done((bf16[27,2560]{1,0:T(8,128)(2,1)S(1)}, bf16[27,2560]{1,0:T(8,128)(2,1)}, u32[]{:S(2)}) %copy-start.4) | copy-done | bytes 138264
  10.9 0.3 shard_map.76.w0
  11.2 1.7 %collective-permute-start.1 = (bf16[56,2560]{1,0:T(8,128)(2,1)S(1)}, bf16[56,2560]{1,0:T(8,128)(2,1)S(1)}, u32[]{:S(2)}, u32[]{:S(2)}) collective-permute-start(bf16[56,2560]{1,0:T(8,128)(2,1)S(1)} %shard_map.76.w0), channel_id=1, source_target_pairs={{0,2},{2,4},{4,6},{6,8},{8,10},{10,12},{12,14},{14,0},{1,3},{3,5},... | collective-permute-start | bytes 860168 | tf_op jit(solution)/shard_map/ppermute | solution.py:20
  12.9 4.0 %collective-permute-start.2 = (bf16[56,2560]{1,0:T(8,128)(2,1)S(1)}, bf16[56,2560]{1,0:T(8,128)(2,1)S(1)}, u32[]{:S(2)}, u32[]{:S(2)}) collective-permute-start(bf16[56,2560]{1,0:T(8,128)(2,1)S(1)} %shard_map.76.w0), channel_id=1, source_target_pairs={{0,14},{2,0},{4,2},{6,4},{8,6},{10,8},{12,10},{14,12},{1,15},{3,1}... | collective-permute-start | bytes 860168 | tf_op jit(solution)/shard_map/ppermute | solution.py:20
  16.9 0.3 collective-permute-start.7
  17.3 2.4 %collective-permute-start.9 = (bf16[128,1792]{1,0:T(8,128)(2,1)S(1)}, bf16[128,1792]{1,0:T(8,128)(2,1)S(1)}, u32[]{:S(2)}, u32[]{:S(2)}) collective-permute-start(bf16[128,1792]{1,0:T(8,128)(2,1)S(1)} %copy-done.5), channel_id=1, source_target_pairs={{0,48},{16,0},{32,16},{48,32},{1,49},{17,1},{33,17},{49,33},{2,50}... | collective-permute-start | bytes 1376264 | tf_op jit(solution)/shard_map/ppermute | solution.py:20
  19.6 0.0 collective-permute-done.8.g2
  19.6 0.4 collective-permute-start.10
  20.0 2.7 %collective-permute-done.1.f1 = bf16[56,2560]{1,0:T(8,128)(2,1)S(1)} collective-permute-done((bf16[56,2560]{1,0:T(8,128)(2,1)S(1)}, bf16[56,2560]{1,0:T(8,128)(2,1)S(1)}, u32[]{:S(2)}, u32[]{:S(2)}) %collective-permute-start.1) | collective-permute-done | bytes 286752 | tf_op jit(solution)/shard_map/ppermute | solution.py:20
  22.8 2.7 %collective-permute-start.4 = (bf16[56,2560]{1,0:T(8,128)(2,1)S(1)}, bf16[56,2560]{1,0:T(8,128)(2,1)S(1)}, u32[]{:S(2)}, u32[]{:S(2)}) collective-permute-start(bf16[56,2560]{1,0:T(8,128)(2,1)S(1)} %collective-permute-done.2.b1), channel_id=1, source_target_pairs={{0,14},{2,0},{4,2},{6,4},{8,6},{10,8},{12,10},{14,12},{1,15},{3,1}... | collective-permute-start | bytes 860168 | tf_op jit(solution)/shard_map/ppermute | solution.py:20
  25.4 3.2 %collective-permute-done.7.g1 = bf16[128,1792]{1,0:T(8,128)(2,1)S(1)} collective-permute-done((bf16[128,1792]{1,0:T(8,128)(2,1)S(1)}, bf16[128,1792]{1,0:T(8,128)(2,1)S(1)}, u32[]{:S(2)}, u32[]{:S(2)}) %collective-permute-start.7) | collective-permute-done | bytes 458784 | tf_op jit(solution)/shard_map/ppermute | solution.py:20
  28.6 0.0 collective-permute-done.9.g3
  28.6 0.0 collective-permute-done.10.swapped2
  28.6 0.1 shard_map.77
  28.7 2.5 %collective-permute-start.12 = (bf16[128,1280]{1,0:T(8,128)(2,1)S(1)}, bf16[128,1280]{1,0:T(8,128)(2,1)S(1)}, u32[]{:S(2)}, u32[]{:S(2)}) collective-permute-start(bf16[128,1280]{1,0:T(8,128)(2,1)S(1)} %get-tuple-element.77.n2), channel_id=1, source_target_pairs={{0,64},{64,0},{1,65},{65,1},{2,66},{66,2},{3,67},{67,3},{4,68},{68... | collective-permute-start | bytes 983048 | tf_op jit(solution)/shard_map/ppermute | solution.py:20
  31.2 0.1 collective-permute-start.11
  31.3 0.4 collective-permute-start.13
  31.8 0.0 collective-permute-start.5
  31.8 2.8 %collective-permute-start.6 = (bf16[56,2560]{1,0:T(8,128)(2,1)S(1)}, bf16[56,2560]{1,0:T(8,128)(2,1)S(1)}, u32[]{:S(2)}, u32[]{:S(2)}) collective-permute-start(bf16[56,2560]{1,0:T(8,128)(2,1)S(1)} %collective-permute-done.4.b2), channel_id=1, source_target_pairs={{0,14},{2,0},{4,2},{6,4},{8,6},{10,8},{12,10},{14,12},{1,15},{3,1}... | collective-permute-start | bytes 860168 | tf_op jit(solution)/shard_map/ppermute | solution.py:20
  34.6 3.4 %shard_map.78 = (f32[8,56,2560]{2,1,0:T(8,128)S(1)}, bf16[56,2560]{1,0:T(8,128)(2,1)S(1)}, bf16[512,2560]{1,0:T(8,128)(2,1)S(1)}, bf16[512,512]{1,0:T(8,128)(2,1)S(1)}) custom-call(bf16[128,2560]{1,0:T(8,128)(2,1)S(1)} %copy-done, bf16[512,128]{1,0:T(8,128)(2,1)S(1)} %copy-done.3, bf16[128,1792]{1,0:T(8,128)(2,1)S(1)} %collective-permute-done.7.g1, ...), custom_call_target="tpu_custom_call" | custom-call | tf_op jit(solution)/shard_map/pallas_call | solution.py:30
  38.1 1.9 %collective-permute-done.5.f3 = bf16[56,2560]{1,0:T(8,128)(2,1)S(1)} collective-permute-done((bf16[56,2560]{1,0:T(8,128)(2,1)S(1)}, bf16[56,2560]{1,0:T(8,128)(2,1)S(1)}, u32[]{:S(2)}, u32[]{:S(2)}) %collective-permute-start.5) | collective-permute-done | bytes 286752 | tf_op jit(solution)/shard_map/ppermute | solution.py:20
  40.0 0.0 collective-permute-done.6.b3
  40.0 2.6 %collective-permute-start.16 = (bf16[56,2560]{1,0:T(8,128)(2,1)S(1)}, bf16[56,2560]{1,0:T(8,128)(2,1)S(1)}, u32[]{:S(2)}, u32[]{:S(2)}) collective-permute-start(bf16[56,2560]{1,0:T(8,128)(2,1)S(1)} %get-tuple-element.89), channel_id=1, source_target_pairs={{0,14},{2,0},{4,2},{6,4},{8,6},{10,8},{12,10},{14,12},{1,15},{3,1}... | collective-permute-start | bytes 860168 | tf_op jit(solution)/shard_map/ppermute | solution.py:20
  42.5 0.0 collective-permute-start.15
  42.6 3.4 %shard_map.79 = (bf16[8,64,2560]{2,1,0:T(8,128)(2,1)S(1)}, f32[512,2560]{1,0:T(8,128)S(1)}, bf16[512,64]{1,0:T(8,128)(2,1)S(1)}, bf16[512,1408]{1,0:T(8,128)(2,1)S(1)}, bf16[16,128]{1,0:T(8,128)(2,1)S(1)}) custom-call(bf16[56,2560]{1,0:T(8,128)(2,1)S(1)} %shard_map.76.w0, bf16[56,2560]{1,0:T(8,128)(2,1)S(1)} %collective-permute-done.1.f1, ...), custom_call_target="tpu_custom_call" | custom-call | tf_op jit(solution)/shard_map/pallas_call | solution.py:30
  45.9 2.9 %collective-permute-start.14 = (bf16[512,1408]{1,0:T(8,128)(2,1)S(1)}, bf16[512,1408]{1,0:T(8,128)(2,1)S(1)}, u32[]{:S(2)}, u32[]{:S(2)}) collective-permute-start(bf16[512,1408]{1,0:T(8,128)(2,1)S(1)} %get-tuple-element.85), channel_id=1, source_target_pairs={{0,64},{64,0},{1,65},{65,1},{2,66},{66,2},{3,67},{67,3},{4,68},{68... | collective-permute-start | bytes 4325384 | tf_op jit(solution)/shard_map/ppermute | solution.py:20
  48.8 0.1 shard_map.80
  48.9 0.6 collective-permute-start.22
  49.5 2.6 %collective-permute-start.23 = (bf16[56,2560]{1,0:T(8,128)(2,1)S(1)}, bf16[56,2560]{1,0:T(8,128)(2,1)S(1)}, u32[]{:S(2)}, u32[]{:S(2)}) collective-permute-start(bf16[56,2560]{1,0:T(8,128)(2,1)S(1)} %get-tuple-element.96), channel_id=1, source_target_pairs={{0,14},{2,0},{4,2},{6,4},{8,6},{10,8},{12,10},{14,12},{1,15},{3,1}... | collective-permute-start | bytes 860168 | tf_op jit(solution)/shard_map/ppermute | solution.py:20
  52.1 0.0 collective-permute-done.15.block
  52.2 1.5 %collective-permute-start.17 = (bf16[56,1280]{1,0:T(8,128)(2,1)S(1)}, bf16[56,1280]{1,0:T(8,128)(2,1)S(1)}, u32[]{:S(2)}, u32[]{:S(2)}) collective-permute-start(bf16[56,1280]{1,0:T(8,128)(2,1)S(1)} %shard_map.82), channel_id=1, source_target_pairs={{0,64},{64,0},{1,65},{65,1},{2,66},{66,2},{3,67},{67,3},{4,68},{68... | collective-permute-start | bytes 430088 | tf_op jit(solution)/shard_map/ppermute | solution.py:20
  53.6 1.0 %collective-permute-done.17.block_other = bf16[56,1280]{1,0:T(8,128)(2,1)S(1)} collective-permute-done((bf16[56,1280]{1,0:T(8,128)(2,1)S(1)}, bf16[56,1280]{1,0:T(8,128)(2,1)S(1)}, u32[]{:S(2)}, u32[]{:S(2)}) %collective-permute-start.17) | collective-permute-done | bytes 143392 | tf_op jit(solution)/shard_map/ppermute | solution.py:20
  54.6 0.0 collective-permute-done.14.crossed
  54.6 0.9 %shard_map.83 = (f32[128,1280]{1,0:T(8,128)S(1)}, bf16[128,1280]{1,0:T(8,128)(2,1)S(1)}, bf16[128,1280]{1,0:T(8,128)(2,1)S(1)}, f32[128,640]{1,0:T(8,128)S(1)}, bf16[128,640]{1,0:T(8,128)(2,1)S(1)}) custom-call(f32[512,2560]{1,0:T(8,128)S(1)} %get-tuple-element.84.product, bf16[512,1408]{1,0:T(8,128)(2,1)S(1)} %collective-permute-done.14.crossed, ...), custom_call_target="tpu_custom_call" | custom-call | flops 1000000000 | tf_op jit(solution)/shard_map/pallas_call | solution.py:30
  55.6 0.4 collective-permute-start.19
  56.0 3.8 %collective-permute-start.18 = (bf16[128,1280]{1,0:T(8,128)(2,1)S(1)}, bf16[128,1280]{1,0:T(8,128)(2,1)S(1)}, u32[]{:S(2)}, u32[]{:S(2)}) collective-permute-start(bf16[128,1280]{1,0:T(8,128)(2,1)S(1)} %get-tuple-element.92), channel_id=1, source_target_pairs={{0,48},{16,0},{32,16},{48,32},{1,49},{17,1},{33,17},{49,33},{2,50}... | collective-permute-start | bytes 983048 | tf_op jit(solution)/shard_map/ppermute | solution.py:20
  59.8 0.0 collective-permute-done.22.refs_0_
  59.8 0.0 collective-permute-done.23.refs_1_
  59.8 0.1 shard_map.85
  60.0 0.1 collective-permute-start.24
  60.0 2.7 %collective-permute-start.25 = (bf16[56,2560]{1,0:T(8,128)(2,1)S(1)}, bf16[56,2560]{1,0:T(8,128)(2,1)S(1)}, u32[]{:S(2)}, u32[]{:S(2)}) collective-permute-start(bf16[56,2560]{1,0:T(8,128)(2,1)S(1)} %get-tuple-element.100), channel_id=1, source_target_pairs={{0,14},{2,0},{4,2},{6,4},{8,6},{10,8},{12,10},{14,12},{1,15},{3,1}... | collective-permute-start | bytes 860168 | tf_op jit(solution)/shard_map/ppermute | solution.py:20
  62.8 2.7 %collective-permute-start.20 = (bf16[128,640]{1,0:T(8,128)(2,1)S(1)}, bf16[128,640]{1,0:T(8,128)(2,1)S(1)}, u32[]{:S(2)}, u32[]{:S(2)}) collective-permute-start(bf16[128,640]{1,0:T(8,128)(2,1)S(1)} %shard_map.84), channel_id=1, source_target_pairs={{0,32},{16,48},{32,0},{48,16},{1,33},{17,49},{33,1},{49,17},{2,34}... | collective-permute-start | bytes 491528 | tf_op jit(solution)/shard_map/ppermute | solution.py:20
  65.5 2.6 %shard_map.86 = (bf16[512,128]{1,0:T(8,128)(2,1)S(1)}, bf16[512,128]{1,0:T(8,128)(2,1)S(1)}, bf16[512,128]{1,0:T(8,128)(2,1)S(1)}, bf16[512,128]{1,0:T(8,128)(2,1)S(1)}) custom-call(bf16[512,2560]{1,0:T(8,128)(2,1)S(1)} %get-tuple-element.102.cot, bf16[8,64,2560]{2,1,0:T(8,128)(2,1)S(1)} %get-tuple-element.103.weight, ...), custom_call_target="tpu_custom_call" | custom-call | tf_op jit(solution)/shard_map/pallas_call | solution.py:30
  68.1 0.5 collective-permute-done.24.refs_0_
  68.7 0.1 shard_map.87
  68.8 1.1 %collective-permute-start.27 = (bf16[56,2560]{1,0:T(8,128)(2,1)S(1)}, bf16[56,2560]{1,0:T(8,128)(2,1)S(1)}, u32[]{:S(2)}, u32[]{:S(2)}) collective-permute-start(bf16[56,2560]{1,0:T(8,128)(2,1)S(1)} %get-tuple-element.109), channel_id=1, source_target_pairs={{0,2},{2,4},{4,6},{6,8},{8,10},{10,12},{12,14},{14,0},{1,3},{3,5},... | collective-permute-start | bytes 860168 | tf_op jit(solution)/shard_map/ppermute | solution.py:20
  70.0 1.6 %collective-permute-start.28 = (bf16[56,2560]{1,0:T(8,128)(2,1)S(1)}, bf16[56,2560]{1,0:T(8,128)(2,1)S(1)}, u32[]{:S(2)}, u32[]{:S(2)}) collective-permute-start(bf16[56,2560]{1,0:T(8,128)(2,1)S(1)} %get-tuple-element.110), channel_id=1, source_target_pairs={{0,14},{2,0},{4,2},{6,4},{8,6},{10,8},{12,10},{14,12},{1,15},{3,1}... | collective-permute-start | bytes 860168 | tf_op jit(solution)/shard_map/ppermute | solution.py:20
  71.6 0.6 collective-permute-done.20.h2
  72.2 0.2 shard_map.88
  72.4 0.0 copy-start.1
  72.4 0.0 copy-start.2
  72.4 1.3 %collective-permute-start.26 = (bf16[128,1280]{1,0:T(8,128)(2,1)S(1)}, bf16[128,1280]{1,0:T(8,128)(2,1)S(1)}, u32[]{:S(2)}, u32[]{:S(2)}) collective-permute-start(bf16[128,1280]{1,0:T(8,128)(2,1)S(1)} %shard_map.88), channel_id=1, source_target_pairs={{0,128},{128,0},{1,129},{129,1},{2,130},{130,2},{3,131},{131,3},{4... | collective-permute-start | bytes 983048 | tf_op jit(solution)/shard_map/ppermute | solution.py:20
  73.8 2.0 %collective-permute-start.31 = (bf16[512,128]{1,0:T(8,128)(2,1)S(1)}, bf16[512,128]{1,0:T(8,128)(2,1)S(1)}, u32[]{:S(2)}, u32[]{:S(2)}) collective-permute-start(bf16[512,128]{1,0:T(8,128)(2,1)S(1)} %get-tuple-element.122), channel_id=1, source_target_pairs={{0,48},{16,0},{32,16},{48,32},{1,49},{17,1},{33,17},{49,33},{2,50}... | collective-permute-start | bytes 393224 | tf_op jit(solution)/shard_map/ppermute | solution.py:20
  75.7 0.9 %collective-permute-done.27.fwd = bf16[56,2560]{1,0:T(8,128)(2,1)S(1)} collective-permute-done((bf16[56,2560]{1,0:T(8,128)(2,1)S(1)}, bf16[56,2560]{1,0:T(8,128)(2,1)S(1)}, u32[]{:S(2)}, u32[]{:S(2)}) %collective-permute-start.27) | collective-permute-done | bytes 286752 | tf_op jit(solution)/shard_map/ppermute | solution.py:20
  76.6 0.3 shard_map.89
  76.9 1.1 %collective-permute-start.30 = (bf16[27,2560]{1,0:T(8,128)(2,1)S(1)}, bf16[27,2560]{1,0:T(8,128)(2,1)S(1)}, u32[]{:S(2)}, u32[]{:S(2)}) collective-permute-start(bf16[27,2560]{1,0:T(8,128)(2,1)S(1)} %get-tuple-element.116), channel_id=1, source_target_pairs={{0,1},{1,0},{2,3},{3,2},{4,5},{5,4},{6,7},{7,6},{8,9},{9,8},{10,11... | collective-permute-start | bytes 414728 | tf_op jit(solution)/shard_map/ppermute | solution.py:20
  78.0 1.5 %collective-permute-done.26 = bf16[128,1280]{1,0:T(8,128)(2,1)S(1)} collective-permute-done((bf16[128,1280]{1,0:T(8,128)(2,1)S(1)}, bf16[128,1280]{1,0:T(8,128)(2,1)S(1)}, u32[]{:S(2)}, u32[]{:S(2)}) %collective-permute-start.26) | collective-permute-done | bytes 327712 | tf_op jit(solution)/shard_map/ppermute | solution.py:20
  79.5 0.1 add_convert_fusion.mine
  79.6 5.2 %collective-permute-start.29 = (bf16[128,1280]{1,0:T(8,128)(2,1)S(1)}, bf16[128,1280]{1,0:T(8,128)(2,1)S(1)}, u32[]{:S(2)}, u32[]{:S(2)}) collective-permute-start(bf16[128,1280]{1,0:T(8,128)(2,1)S(1)} %add_convert_fusion.mine), channel_id=1, source_target_pairs={{0,64},{64,0},{1,65},{65,1},{2,66},{66,2},{3,67},{67,3},{4,68},{68... | collective-permute-start | bytes 983048 | tf_op jit(solution)/shard_map/ppermute | solution.py:20
  84.8 1.3 %shard_map.91 = (bf16[1728,128]{1,0:T(8,128)(2,1)}, bf16[1728,128]{1,0:T(8,128)(2,1)}) custom-call(bf16[1728,128]{1,0:T(8,128)(2,1)S(1)} %bitcast.5, bf16[1728,128]{1,0:T(8,128)(2,1)S(1)} %bitcast.7, bf16[512,128]{1,0:T(8,128)(2,1)S(1)} %get-tuple-element.121.b0, bf16[512,128]{1,0:T(8,128)(2,1)S(1)} %collective-permute-done.31.b1, ...), custom_call_target="tpu_custom_call" | custom-call | flops 4000000000 | tf_op jit(solution)/shard_map/pallas_call | solution.py:30
  86.2 1.0 %shard_map.90 = (bf16[128,2560]{1,0:T(8,128)(2,1)}, f32[27,2560]{1,0:T(8,128)}) custom-call(bf16[128,1280]{1,0:T(8,128)(2,1)S(1)} %add_convert_fusion.mine, bf16[128,1280]{1,0:T(8,128)(2,1)S(1)} %collective-permute-done.29.other, f32[27,2560]{1,0:T(8,128)S(1)} %get-tuple-element.118.keep, bf16[27,2560]{1,0:T(8,128)(2,1)S(1)} %collective-permute-done.30.taken), custom_call_target="tpu_custom_call" | custom-call | bytes 2001920 | tf_op jit(solution)/shard_map/pallas_call | solution.py:30
  (36 shorter events, 0.1 us)
Async XLA Ops:
  0.6 9.3 %collective-permute-start = (bf16[27,2560]{1,0:T(8,128)(2,1)}, bf16[27,2560]{1,0:T(8,128)(2,1)S(1)}, u32[]{:S(2)}, u32[]{:S(2)}) collective-permute-start(bf16[27,2560]{1,0:T(8,128)(2,1)} %mine.1), channel_id=1, source_target_pairs={{0,1},{1,0},{2,3},{3,2},{4,5},{5,4},{6,7},{7,6},{8,9},{9,8},{10,11... | collective-permute-start | bytes 414728 | tf_op jit(solution)/shard_map/ppermute | solution.py:20
  7.1 12.5 %collective-permute-start.8 = (bf16[128,1152]{1,0:T(8,128)(2,1)}, bf16[128,1152]{1,0:T(8,128)(2,1)S(1)}, u32[]{:S(2)}, u32[]{:S(2)}) collective-permute-start(bf16[128,1152]{1,0:T(8,128)(2,1)} %get-tuple-element.67), channel_id=1, source_target_pairs={{0,32},{16,48},{32,0},{48,16},{1,33},{17,49},{33,1},{49,17},{2,34}... | collective-permute-start | bytes 884744 | tf_op jit(solution)/shard_map/ppermute | solution.py:20
  9.9 0.9 %copy-start.4 = (bf16[27,2560]{1,0:T(8,128)(2,1)S(1)}, bf16[27,2560]{1,0:T(8,128)(2,1)}, u32[]{:S(2)}) copy-start(bf16[27,2560]{1,0:T(8,128)(2,1)} %mine.1) | copy-start | bytes 414724
  10.8 6.1 %copy-start.6 = (bf16[128,1792]{1,0:T(8,128)(2,1)S(1)}, bf16[128,1792]{1,0:T(8,128)(2,1)}, u32[]{:S(2)}) copy-start(bf16[128,1792]{1,0:T(8,128)(2,1)} %get-tuple-element.66) | copy-start | bytes 1376260
  10.8 6.4 %copy-start.5 = (bf16[128,1792]{1,0:T(8,128)(2,1)S(1)}, bf16[128,1792]{1,0:T(8,128)(2,1)}, u32[]{:S(2)}) copy-start(bf16[128,1792]{1,0:T(8,128)(2,1)} %get-tuple-element.68) | copy-start | bytes 1376260
  10.8 23.8 %copy-start = (bf16[128,2560]{1,0:T(8,128)(2,1)S(1)}, bf16[128,2560]{1,0:T(8,128)(2,1)}, u32[]{:S(2)}) copy-start(bf16[128,2560]{1,0:T(8,128)(2,1)} %get-tuple-element.75.cot_own) | copy-start | bytes 1966084
  10.8 23.8 %copy-start.3 = (bf16[512,128]{1,0:T(8,128)(2,1)S(1)}, bf16[512,128]{1,0:T(8,128)(2,1)}, u32[]{:S(2)}) copy-start(bf16[512,128]{1,0:T(8,128)(2,1)} %get-tuple-element.76.hid_own) | copy-start | bytes 393220
  11.2 11.6 %collective-permute-start.1 = (bf16[56,2560]{1,0:T(8,128)(2,1)S(1)}, bf16[56,2560]{1,0:T(8,128)(2,1)S(1)}, u32[]{:S(2)}, u32[]{:S(2)}) collective-permute-start(bf16[56,2560]{1,0:T(8,128)(2,1)S(1)} %shard_map.76.w0), channel_id=1, source_target_pairs={{0,2},{2,4},{4,6},{6,8},{8,10},{10,12},{12,14},{14,0},{1,3},{3,5},... | collective-permute-start | bytes 860168 | tf_op jit(solution)/shard_map/ppermute | solution.py:20
  12.9 9.8 %collective-permute-start.2 = (bf16[56,2560]{1,0:T(8,128)(2,1)S(1)}, bf16[56,2560]{1,0:T(8,128)(2,1)S(1)}, u32[]{:S(2)}, u32[]{:S(2)}) collective-permute-start(bf16[56,2560]{1,0:T(8,128)(2,1)S(1)} %shard_map.76.w0), channel_id=1, source_target_pairs={{0,14},{2,0},{4,2},{6,4},{8,6},{10,8},{12,10},{14,12},{1,15},{3,1}... | collective-permute-start | bytes 860168 | tf_op jit(solution)/shard_map/ppermute | solution.py:20
  16.9 11.7 %collective-permute-start.7 = (bf16[128,1792]{1,0:T(8,128)(2,1)S(1)}, bf16[128,1792]{1,0:T(8,128)(2,1)S(1)}, u32[]{:S(2)}, u32[]{:S(2)}) collective-permute-start(bf16[128,1792]{1,0:T(8,128)(2,1)S(1)} %copy-done.6), channel_id=1, source_target_pairs={{0,16},{16,32},{32,48},{48,0},{1,17},{17,33},{33,49},{49,1},{2,18}... | collective-permute-start | bytes 1376264 | tf_op jit(solution)/shard_map/ppermute | solution.py:20
  17.3 11.4 %collective-permute-start.9 = (bf16[128,1792]{1,0:T(8,128)(2,1)S(1)}, bf16[128,1792]{1,0:T(8,128)(2,1)S(1)}, u32[]{:S(2)}, u32[]{:S(2)}) collective-permute-start(bf16[128,1792]{1,0:T(8,128)(2,1)S(1)} %copy-done.5), channel_id=1, source_target_pairs={{0,48},{16,0},{32,16},{48,32},{1,49},{17,1},{33,17},{49,33},{2,50}... | collective-permute-start | bytes 1376264 | tf_op jit(solution)/shard_map/ppermute | solution.py:20
  19.6 9.0 %collective-permute-start.10 = (bf16[128,1152]{1,0:T(8,128)(2,1)S(1)}, bf16[128,1152]{1,0:T(8,128)(2,1)S(1)}, u32[]{:S(2)}, u32[]{:S(2)}) collective-permute-start(bf16[128,1152]{1,0:T(8,128)(2,1)S(1)} %collective-permute-done.8.g2), channel_id=1, source_target_pairs={{0,128},{128,0},{1,129},{129,1},{2,130},{130,2},{3,131},{131,3},{4... | collective-permute-start | bytes 884744 | tf_op jit(solution)/shard_map/ppermute | solution.py:20
  22.8 9.0 %collective-permute-start.3 = (bf16[56,2560]{1,0:T(8,128)(2,1)S(1)}, bf16[56,2560]{1,0:T(8,128)(2,1)S(1)}, u32[]{:S(2)}, u32[]{:S(2)}) collective-permute-start(bf16[56,2560]{1,0:T(8,128)(2,1)S(1)} %collective-permute-done.1.f1), channel_id=1, source_target_pairs={{0,2},{2,4},{4,6},{6,8},{8,10},{10,12},{12,14},{14,0},{1,3},{3,5},... | collective-permute-start | bytes 860168 | tf_op jit(solution)/shard_map/ppermute | solution.py:20
  22.8 9.0 %collective-permute-start.4 = (bf16[56,2560]{1,0:T(8,128)(2,1)S(1)}, bf16[56,2560]{1,0:T(8,128)(2,1)S(1)}, u32[]{:S(2)}, u32[]{:S(2)}) collective-permute-start(bf16[56,2560]{1,0:T(8,128)(2,1)S(1)} %collective-permute-done.2.b1), channel_id=1, source_target_pairs={{0,14},{2,0},{4,2},{6,4},{8,6},{10,8},{12,10},{14,12},{1,15},{3,1}... | collective-permute-start | bytes 860168 | tf_op jit(solution)/shard_map/ppermute | solution.py:20
  28.7 5.9 %collective-permute-start.12 = (bf16[128,1280]{1,0:T(8,128)(2,1)S(1)}, bf16[128,1280]{1,0:T(8,128)(2,1)S(1)}, u32[]{:S(2)}, u32[]{:S(2)}) collective-permute-start(bf16[128,1280]{1,0:T(8,128)(2,1)S(1)} %get-tuple-element.77.n2), channel_id=1, source_target_pairs={{0,64},{64,0},{1,65},{65,1},{2,66},{66,2},{3,67},{67,3},{4,68},{68... | collective-permute-start | bytes 983048 | tf_op jit(solution)/shard_map/ppermute | solution.py:20
  31.2 3.4 %collective-permute-start.11 = (bf16[128,1280]{1,0:T(8,128)(2,1)S(1)}, bf16[128,1280]{1,0:T(8,128)(2,1)S(1)}, u32[]{:S(2)}, u32[]{:S(2)}) collective-permute-start(bf16[128,1280]{1,0:T(8,128)(2,1)S(1)} %get-tuple-element.78), channel_id=1, source_target_pairs={{0,64},{64,0},{1,65},{65,1},{2,66},{66,2},{3,67},{67,3},{4,68},{68... | collective-permute-start | bytes 983048 | tf_op jit(solution)/shard_map/ppermute | solution.py:20
  31.3 3.3 %collective-permute-start.13 = (bf16[128,1280]{1,0:T(8,128)(2,1)S(1)}, bf16[128,1280]{1,0:T(8,128)(2,1)S(1)}, u32[]{:S(2)}, u32[]{:S(2)}) collective-permute-start(bf16[128,1280]{1,0:T(8,128)(2,1)S(1)} %get-tuple-element.79), channel_id=1, source_target_pairs={{0,64},{64,0},{1,65},{65,1},{2,66},{66,2},{3,67},{67,3},{4,68},{68... | collective-permute-start | bytes 983048 | tf_op jit(solution)/shard_map/ppermute | solution.py:20
  31.8 8.2 %collective-permute-start.5 = (bf16[56,2560]{1,0:T(8,128)(2,1)S(1)}, bf16[56,2560]{1,0:T(8,128)(2,1)S(1)}, u32[]{:S(2)}, u32[]{:S(2)}) collective-permute-start(bf16[56,2560]{1,0:T(8,128)(2,1)S(1)} %collective-permute-done.3.f2), channel_id=1, source_target_pairs={{0,2},{2,4},{4,6},{6,8},{8,10},{10,12},{12,14},{14,0},{1,3},{3,5},... | collective-permute-start | bytes 860168 | tf_op jit(solution)/shard_map/ppermute | solution.py:20
  31.8 8.2 %collective-permute-start.6 = (bf16[56,2560]{1,0:T(8,128)(2,1)S(1)}, bf16[56,2560]{1,0:T(8,128)(2,1)S(1)}, u32[]{:S(2)}, u32[]{:S(2)}) collective-permute-start(bf16[56,2560]{1,0:T(8,128)(2,1)S(1)} %collective-permute-done.4.b2), channel_id=1, source_target_pairs={{0,14},{2,0},{4,2},{6,4},{8,6},{10,8},{12,10},{14,12},{1,15},{3,1}... | collective-permute-start | bytes 860168 | tf_op jit(solution)/shard_map/ppermute | solution.py:20
  40.0 8.8 %collective-permute-start.16 = (bf16[56,2560]{1,0:T(8,128)(2,1)S(1)}, bf16[56,2560]{1,0:T(8,128)(2,1)S(1)}, u32[]{:S(2)}, u32[]{:S(2)}) collective-permute-start(bf16[56,2560]{1,0:T(8,128)(2,1)S(1)} %get-tuple-element.89), channel_id=1, source_target_pairs={{0,14},{2,0},{4,2},{6,4},{8,6},{10,8},{12,10},{14,12},{1,15},{3,1}... | collective-permute-start | bytes 860168 | tf_op jit(solution)/shard_map/ppermute | solution.py:20
  42.5 9.6 %collective-permute-start.15 = (bf16[56,2560]{1,0:T(8,128)(2,1)S(1)}, bf16[56,2560]{1,0:T(8,128)(2,1)S(1)}, u32[]{:S(2)}, u32[]{:S(2)}) collective-permute-start(bf16[56,2560]{1,0:T(8,128)(2,1)S(1)} %collective-permute-done.5.f3), channel_id=1, source_target_pairs={{0,2},{2,4},{4,6},{6,8},{8,10},{10,12},{12,14},{14,0},{1,3},{3,5},... | collective-permute-start | bytes 860168 | tf_op jit(solution)/shard_map/ppermute | solution.py:20
  45.9 8.7 %collective-permute-start.14 = (bf16[512,1408]{1,0:T(8,128)(2,1)S(1)}, bf16[512,1408]{1,0:T(8,128)(2,1)S(1)}, u32[]{:S(2)}, u32[]{:S(2)}) collective-permute-start(bf16[512,1408]{1,0:T(8,128)(2,1)S(1)} %get-tuple-element.85), channel_id=1, source_target_pairs={{0,64},{64,0},{1,65},{65,1},{2,66},{66,2},{3,67},{67,3},{4,68},{68... | collective-permute-start | bytes 4325384 | tf_op jit(solution)/shard_map/ppermute | solution.py:20
  48.9 10.9 %collective-permute-start.22 = (bf16[56,2560]{1,0:T(8,128)(2,1)S(1)}, bf16[56,2560]{1,0:T(8,128)(2,1)S(1)}, u32[]{:S(2)}, u32[]{:S(2)}) collective-permute-start(bf16[56,2560]{1,0:T(8,128)(2,1)S(1)} %get-tuple-element.90.value), channel_id=1, source_target_pairs={{0,2},{2,4},{4,6},{6,8},{8,10},{10,12},{12,14},{14,0},{1,3},{3,5},... | collective-permute-start | bytes 860168 | tf_op jit(solution)/shard_map/ppermute | solution.py:20
  49.5 10.3 %collective-permute-start.23 = (bf16[56,2560]{1,0:T(8,128)(2,1)S(1)}, bf16[56,2560]{1,0:T(8,128)(2,1)S(1)}, u32[]{:S(2)}, u32[]{:S(2)}) collective-permute-start(bf16[56,2560]{1,0:T(8,128)(2,1)S(1)} %get-tuple-element.96), channel_id=1, source_target_pairs={{0,14},{2,0},{4,2},{6,4},{8,6},{10,8},{12,10},{14,12},{1,15},{3,1}... | collective-permute-start | bytes 860168 | tf_op jit(solution)/shard_map/ppermute | solution.py:20
  52.2 2.5 %collective-permute-start.17 = (bf16[56,1280]{1,0:T(8,128)(2,1)S(1)}, bf16[56,1280]{1,0:T(8,128)(2,1)S(1)}, u32[]{:S(2)}, u32[]{:S(2)}) collective-permute-start(bf16[56,1280]{1,0:T(8,128)(2,1)S(1)} %shard_map.82), channel_id=1, source_target_pairs={{0,64},{64,0},{1,65},{65,1},{2,66},{66,2},{3,67},{67,3},{4,68},{68... | collective-permute-start | bytes 430088 | tf_op jit(solution)/shard_map/ppermute | solution.py:20
  55.6 7.2 %collective-permute-start.19 = (bf16[128,640]{1,0:T(8,128)(2,1)S(1)}, bf16[128,640]{1,0:T(8,128)(2,1)S(1)}, u32[]{:S(2)}, u32[]{:S(2)}) collective-permute-start(bf16[128,640]{1,0:T(8,128)(2,1)S(1)} %get-tuple-element.94), channel_id=1, source_target_pairs={{0,128},{128,0},{1,129},{129,1},{2,130},{130,2},{3,131},{131,3},{4... | collective-permute-start | bytes 491528 | tf_op jit(solution)/shard_map/ppermute | solution.py:20
  56.0 15.6 %collective-permute-start.18 = (bf16[128,1280]{1,0:T(8,128)(2,1)S(1)}, bf16[128,1280]{1,0:T(8,128)(2,1)S(1)}, u32[]{:S(2)}, u32[]{:S(2)}) collective-permute-start(bf16[128,1280]{1,0:T(8,128)(2,1)S(1)} %get-tuple-element.92), channel_id=1, source_target_pairs={{0,48},{16,0},{32,16},{48,32},{1,49},{17,1},{33,17},{49,33},{2,50}... | collective-permute-start | bytes 983048 | tf_op jit(solution)/shard_map/ppermute | solution.py:20
  59.8 11.8 %collective-permute-start.21 = (bf16[128,1280]{1,0:T(8,128)(2,1)S(1)}, bf16[128,1280]{1,0:T(8,128)(2,1)S(1)}, u32[]{:S(2)}, u32[]{:S(2)}) collective-permute-start(bf16[128,1280]{1,0:T(8,128)(2,1)S(1)} %get-tuple-element.95), channel_id=1, source_target_pairs={{0,16},{16,32},{32,48},{48,0},{1,17},{17,33},{33,49},{49,1},{2,18}... | collective-permute-start | bytes 983048 | tf_op jit(solution)/shard_map/ppermute | solution.py:20
  60.0 8.7 %collective-permute-start.24 = (bf16[56,2560]{1,0:T(8,128)(2,1)S(1)}, bf16[56,2560]{1,0:T(8,128)(2,1)S(1)}, u32[]{:S(2)}, u32[]{:S(2)}) collective-permute-start(bf16[56,2560]{1,0:T(8,128)(2,1)S(1)} %get-tuple-element.99), channel_id=1, source_target_pairs={{0,2},{2,4},{4,6},{6,8},{8,10},{10,12},{12,14},{14,0},{1,3},{3,5},... | collective-permute-start | bytes 860168 | tf_op jit(solution)/shard_map/ppermute | solution.py:20
  60.0 8.6 %collective-permute-start.25 = (bf16[56,2560]{1,0:T(8,128)(2,1)S(1)}, bf16[56,2560]{1,0:T(8,128)(2,1)S(1)}, u32[]{:S(2)}, u32[]{:S(2)}) collective-permute-start(bf16[56,2560]{1,0:T(8,128)(2,1)S(1)} %get-tuple-element.100), channel_id=1, source_target_pairs={{0,14},{2,0},{4,2},{6,4},{8,6},{10,8},{12,10},{14,12},{1,15},{3,1}... | collective-permute-start | bytes 860168 | tf_op jit(solution)/shard_map/ppermute | solution.py:20
  62.8 9.4 %collective-permute-start.20 = (bf16[128,640]{1,0:T(8,128)(2,1)S(1)}, bf16[128,640]{1,0:T(8,128)(2,1)S(1)}, u32[]{:S(2)}, u32[]{:S(2)}) collective-permute-start(bf16[128,640]{1,0:T(8,128)(2,1)S(1)} %shard_map.84), channel_id=1, source_target_pairs={{0,32},{16,48},{32,0},{48,16},{1,33},{17,49},{33,1},{49,17},{2,34}... | collective-permute-start | bytes 491528 | tf_op jit(solution)/shard_map/ppermute | solution.py:20
  68.8 7.8 %collective-permute-start.27 = (bf16[56,2560]{1,0:T(8,128)(2,1)S(1)}, bf16[56,2560]{1,0:T(8,128)(2,1)S(1)}, u32[]{:S(2)}, u32[]{:S(2)}) collective-permute-start(bf16[56,2560]{1,0:T(8,128)(2,1)S(1)} %get-tuple-element.109), channel_id=1, source_target_pairs={{0,2},{2,4},{4,6},{6,8},{8,10},{10,12},{12,14},{14,0},{1,3},{3,5},... | collective-permute-start | bytes 860168 | tf_op jit(solution)/shard_map/ppermute | solution.py:20
  70.0 6.7 %collective-permute-start.28 = (bf16[56,2560]{1,0:T(8,128)(2,1)S(1)}, bf16[56,2560]{1,0:T(8,128)(2,1)S(1)}, u32[]{:S(2)}, u32[]{:S(2)}) collective-permute-start(bf16[56,2560]{1,0:T(8,128)(2,1)S(1)} %get-tuple-element.110), channel_id=1, source_target_pairs={{0,14},{2,0},{4,2},{6,4},{8,6},{10,8},{12,10},{14,12},{1,15},{3,1}... | collective-permute-start | bytes 860168 | tf_op jit(solution)/shard_map/ppermute | solution.py:20
  72.4 12.4 %copy-start.1 = (bf16[128,1728]{0,1:T(8,128)(2,1)S(1)}, bf16[128,1728]{0,1:T(8,128)(2,1)}, u32[]{:S(2)}) copy-start(bf16[128,1728]{0,1:T(8,128)(2,1)} %param.4) | copy-start | bytes 1327108
  72.4 12.4 %copy-start.2 = (bf16[128,1728]{0,1:T(8,128)(2,1)S(1)}, bf16[128,1728]{0,1:T(8,128)(2,1)}, u32[]{:S(2)}) copy-start(bf16[128,1728]{0,1:T(8,128)(2,1)} %param.5) | copy-start | bytes 1327108
  72.4 7.1 %collective-permute-start.26 = (bf16[128,1280]{1,0:T(8,128)(2,1)S(1)}, bf16[128,1280]{1,0:T(8,128)(2,1)S(1)}, u32[]{:S(2)}, u32[]{:S(2)}) collective-permute-start(bf16[128,1280]{1,0:T(8,128)(2,1)S(1)} %shard_map.88), channel_id=1, source_target_pairs={{0,128},{128,0},{1,129},{129,1},{2,130},{130,2},{3,131},{131,3},{4... | collective-permute-start | bytes 983048 | tf_op jit(solution)/shard_map/ppermute | solution.py:20
  73.8 11.0 %collective-permute-start.31 = (bf16[512,128]{1,0:T(8,128)(2,1)S(1)}, bf16[512,128]{1,0:T(8,128)(2,1)S(1)}, u32[]{:S(2)}, u32[]{:S(2)}) collective-permute-start(bf16[512,128]{1,0:T(8,128)(2,1)S(1)} %get-tuple-element.122), channel_id=1, source_target_pairs={{0,48},{16,0},{32,16},{48,32},{1,49},{17,1},{33,17},{49,33},{2,50}... | collective-permute-start | bytes 393224 | tf_op jit(solution)/shard_map/ppermute | solution.py:20
  75.7 9.1 %collective-permute-start.33 = (bf16[512,128]{1,0:T(8,128)(2,1)S(1)}, bf16[512,128]{1,0:T(8,128)(2,1)S(1)}, u32[]{:S(2)}, u32[]{:S(2)}) collective-permute-start(bf16[512,128]{1,0:T(8,128)(2,1)S(1)} %get-tuple-element.125), channel_id=1, source_target_pairs={{0,16},{16,32},{32,48},{48,0},{1,17},{17,33},{33,49},{49,1},{2,18}... | collective-permute-start | bytes 393224 | tf_op jit(solution)/shard_map/ppermute | solution.py:20
  76.9 9.2 %collective-permute-start.30 = (bf16[27,2560]{1,0:T(8,128)(2,1)S(1)}, bf16[27,2560]{1,0:T(8,128)(2,1)S(1)}, u32[]{:S(2)}, u32[]{:S(2)}) collective-permute-start(bf16[27,2560]{1,0:T(8,128)(2,1)S(1)} %get-tuple-element.116), channel_id=1, source_target_pairs={{0,1},{1,0},{2,3},{3,2},{4,5},{5,4},{6,7},{7,6},{8,9},{9,8},{10,11... | collective-permute-start | bytes 414728 | tf_op jit(solution)/shard_map/ppermute | solution.py:20
  78.0 6.8 %collective-permute-start.32 = (bf16[512,128]{1,0:T(8,128)(2,1)S(1)}, bf16[512,128]{1,0:T(8,128)(2,1)S(1)}, u32[]{:S(2)}, u32[]{:S(2)}) collective-permute-start(bf16[512,128]{1,0:T(8,128)(2,1)S(1)} %get-tuple-element.124), channel_id=1, source_target_pairs={{0,32},{16,48},{32,0},{48,16},{1,33},{17,49},{33,1},{49,17},{2,34}... | collective-permute-start | bytes 393224 | tf_op jit(solution)/shard_map/ppermute | solution.py:20
  79.6 6.6 %collective-permute-start.29 = (bf16[128,1280]{1,0:T(8,128)(2,1)S(1)}, bf16[128,1280]{1,0:T(8,128)(2,1)S(1)}, u32[]{:S(2)}, u32[]{:S(2)}) collective-permute-start(bf16[128,1280]{1,0:T(8,128)(2,1)S(1)} %add_convert_fusion.mine), channel_id=1, source_target_pairs={{0,64},{64,0},{1,65},{65,1},{2,66},{66,2},{3,67},{67,3},{4,68},{68... | collective-permute-start | bytes 983048 | tf_op jit(solution)/shard_map/ppermute | solution.py:20

commit v8 on v7

--- a/solution.py
+++ b/solution.py
@@ -67,7 +67,7 @@
     store_swapped(lax.axis_index("core"), out, both.astype(BF16))
 
 
-def prepare(gate_hbm, up_hbm, cot_hbm, m1, m2, m3, hid_own, cot_own, cot, gate, up, hidden, slots, sems):
+def prepare(gate_hbm, up_hbm, cot_hbm, m1, m2, m3, hid_own, cot, gate, up, hidden, slots, sems):
     units, rows = gate.shape
     half = cot_hbm.shape[1] // 2
     part = units // NX
@@ -91,13 +91,11 @@
     for load in cot_loads:
         load.wait()
     mine = cot.at[:, pl.ds(pl.multiple_of(core * half, half), half)]
-    other = cot.at[:, pl.ds(pl.multiple_of((1 - core) * half, half), half)]
-    for out in (m1, m3, cot_own):
+    for out in (m1, m3):
         copy(mine, out.at[:, pl.ds(0, half)])
     quarter = half // 2
     start = pl.multiple_of(core * half + lax.axis_index("yl") * quarter, quarter)
     copy(cot.at[:, pl.ds(start, quarter)], m2.at[:, pl.ds(0, quarter)])
-    copy(other, cot_own.at[:, pl.ds(half, half)])
     inside = lax.broadcasted_iota(jnp.int32, (SLOT, rows), 0) < used
     for s in range(NX):
         for load in loads[s]:
@@ -156,7 +154,7 @@
 
 def weight_gradient(scale, cot_own, hid_own, g1, g2, g3, n2, f1, f2, f3, pieces, to_bwd, cot, hid, hid_t):
     rows, half = cot_own.shape[0], cot_own.shape[1] // 2
-    cot[:rows] = cot_own[...]
+    store_swapped(lax.axis_index("core"), cot.at[:rows], cot_own[...])
     hid_t[:, :rows] = hid_own[...]
     for k, (got, near, far) in enumerate(((g1, g1, f1), (g2, n2, f2), (g3, g3, f3))):
         here = slice((k + 1) * rows, (k + 2) * rows)
@@ -195,13 +193,15 @@
         else:
             weight[to] = padded(piece)
 
-    @pl.loop(0, width // TILE)
+    @pl.loop(0, half // TILE)
     def _(t):
-        columns = pl.ds(pl.multiple_of(t * TILE, TILE), TILE)
-        rhs = weight[:, :, columns].reshape(NZ * SLOT, TILE)
-        product[:, columns] = jnp.dot(hid[...], rhs, preferred_element_type=F32)
-
-    other[:, :half] = product[:, half:].astype(BF16)
+        here = pl.ds(pl.multiple_of(t * TILE, TILE), TILE)
+        there = pl.ds(pl.multiple_of(half + t * TILE, TILE), TILE)
+        rhs = weight[:, :, there].reshape(NZ * SLOT, TILE)
+        other[:, here] = jnp.dot(hid[...], rhs, preferred_element_type=F32).astype(BF16)
+        rhs = weight[:, :, here].reshape(NZ * SLOT, TILE)
+        product[:, here] = jnp.dot(hid[...], rhs, preferred_element_type=F32)
+
     for block in range(NZ):
 
         @pl.when(z == (block + NZ // 2) % NZ)
@@ -344,15 +344,15 @@
     wide = half + slots
 
     w_other = shift(down_weight, "yh", 1)
-    m1, m2, m3, hid_own, cot_own = call(
+    m1, m2, m3, hid_own = call(
         prepare,
         [like((rows, wide)), like((rows, wide - half // 2)), like((rows, wide))]
-        + [like((slots, rows)), like((rows, width))],
+        + [like((slots, rows))],
         gate, up, cotangent,
         scratch=[pltpu.VMEM((rows, width), BF16)]
         + [pltpu.VMEM((units, rows), BF16)] * 2
         + [pltpu.VMEM((units + SLOT, rows), F32), pltpu.VMEM((NX, rows, slots), BF16)]
-        + [pltpu.SemaphoreType.DMA((3 * NX + 8 + slots // rows,))],
+        + [pltpu.SemaphoreType.DMA((3 * NX + 6 + slots // rows,))],
         out_space=pltpu.HBM,
         space=pltpu.HBM,
         limit=56,
@@ -380,7 +380,7 @@
     pieces, to_bwd, cot, hid = call(
         functools.partial(weight_gradient, scale),
         [like((NZ, SENT, width), F32), like((SENT, width)), like((tokens, width)), like((tokens, slots))],
-        cot_own, hid_own, *got, nears[1], *far,
+        cotangent, hid_own, *got, nears[1], *far,
         scratch=[pltpu.VMEM((slots, tokens), BF16)],
         flops=0,
         moved=0,
@@ -390,13 +390,12 @@
         kernel = functools.partial(add_pieces, distance, len(others))
         return call(kernel, [like((SENT, width))] * 2, pieces, *others, *ring, moved=0)
 
-    fwd[3], to_bwd = lax.optimization_barrier((fwd[3], to_bwd))
     f4 = shift(fwd[3], "z", 1)
     ring = (shift(to_bwd, "z", -1),)
 
     weight, product, opposite, other, early = call(
         near_blocks,
-        [like((NZ, SLOT, width)), like((tokens, width), F32), like((tokens, SLOT))]
+        [like((NZ, SLOT, width)), like((tokens, half), F32), like((tokens, SLOT))]
         + [like((tokens, half + 2 * SLOT)), like((16, 128))],
         *fwd, *reversed(bwd[1:]), hid,
         moved=0,

time: 88.9 us -> 88 us (0.990)
  waiting for transfers between devices: 12.5 us -> 13.8 us
  Pallas kernels: 16.6 us -> 15.6 us
    ppermute x34, waiting for transfers between devices: 12.5 us -> 13.8 us  [shift(): lax.ppermute(value, axis, [(i, (i + steps) % count) for i in range(count)])]
    pallas_call x17, Pallas kernels: 16.6 us -> 15.6 us  [call(): pl.pallas_call(kernel, out_shape=outs, in_specs=[pl.BlockSpec(memory_spac...]
  transfers between devices with their start and end apart: 34 -> 34, of which waited for: 8 -> 9; matrix products, arithmetic and copies ran while one was open for 0% -> 0% of each run, Pallas kernels for 18% -> 17%
where the time goes in v8:
time: 88 us; the launch traced here: 87.1 us
  starting transfers between devices  55.9 us (64%)
  Pallas kernels  15.6 us (18%)
  waiting for transfers between devices  13.8 us (16%)
  local copies, waits for them, and re-layouts  0.94 us (1%)
    ppermute x34, starting transfers between devices, shift(): lax.ppermute(value, axis, [(i, (i + steps) % count) for i in range(count)])  55.9 us
    pallas_call x17, Pallas kernels, call(): pl.pallas_call(kernel, out_shape=outs, in_specs=[pl.BlockSpec(memory_spac...  15.6 us
    ppermute x34, waiting for transfers between devices, shift(): lax.ppermute(value, axis, [(i, (i + steps) % count) for i in range(count)])  13.8 us
  transfers between devices with their start and end apart: 34, of which 9 were waited for; matrix products, arithmetic and copies ran while one was open for 0% of the time, Pallas kernels for 17%

profile of v8, /device:TPU:1, one launch (start us, length us, event | category | flops | bytes accessed | tf_op | source)
XLA Modules:
  0.0 87.1 jit_solution(15314800689623634401)
XLA Ops:
  0.6 3.8 %collective-permute-start = (bf16[27,2560]{1,0:T(8,128)(2,1)}, bf16[27,2560]{1,0:T(8,128)(2,1)S(1)}, u32[]{:S(2)}, u32[]{:S(2)}) collective-permute-start(bf16[27,2560]{1,0:T(8,128)(2,1)} %mine.1), channel_id=1, source_target_pairs={{0,1},{1,0},{2,3},{3,2},{4,5},{5,4},{6,7},{7,6},{8,9},{9,8},{10,11... | collective-permute-start | bytes 414728 | tf_op jit(solution)/shard_map/ppermute | solution.py:20
  4.5 2.6 %shard_map.75 = (bf16[128,1792]{1,0:T(8,128)(2,1)}, bf16[128,1152]{1,0:T(8,128)(2,1)}, bf16[128,1792]{1,0:T(8,128)(2,1)}, bf16[512,128]{1,0:T(8,128)(2,1)}) custom-call(bf16[1728,128]{1,0:T(8,128)(2,1)} %bitcast.4, bf16[1728,128]{1,0:T(8,128)(2,1)} %bitcast.6, bf16[128,2560]{1,0:T(8,128)(2,1)} %cot_own.1), custom_call_target="tpu_custom_call" | custom-call | bytes 2883584 | tf_op jit(solution)/shard_map/pallas_call | solution.py:30
  7.0 2.8 %collective-permute-start.8 = (bf16[128,1152]{1,0:T(8,128)(2,1)}, bf16[128,1152]{1,0:T(8,128)(2,1)S(1)}, u32[]{:S(2)}, u32[]{:S(2)}) collective-permute-start(bf16[128,1152]{1,0:T(8,128)(2,1)} %get-tuple-element.64), channel_id=1, source_target_pairs={{0,32},{16,48},{32,0},{48,16},{1,33},{17,49},{33,1},{49,17},{2,34}... | collective-permute-start | bytes 884744 | tf_op jit(solution)/shard_map/ppermute | solution.py:20
  9.9 0.3 collective-permute-start.7
  10.2 2.4 %collective-permute-start.9 = (bf16[128,1792]{1,0:T(8,128)(2,1)}, bf16[128,1792]{1,0:T(8,128)(2,1)S(1)}, u32[]{:S(2)}, u32[]{:S(2)}) collective-permute-start(bf16[128,1792]{1,0:T(8,128)(2,1)} %get-tuple-element.65), channel_id=1, source_target_pairs={{0,48},{16,0},{32,16},{48,32},{1,49},{17,1},{33,17},{49,33},{2,50}... | collective-permute-start | bytes 1376264 | tf_op jit(solution)/shard_map/ppermute | solution.py:20
  12.5 0.0 collective-permute-done.other
  12.5 0.9 %copy-done.4 = bf16[27,2560]{1,0:T(8,128)(2,1)S(1)} copy-done((bf16[27,2560]{1,0:T(8,128)(2,1)S(1)}, bf16[27,2560]{1,0:T(8,128)(2,1)}, u32[]{:S(2)}) %copy-start.4) | copy-done | bytes 138264
  13.5 0.3 shard_map.76.w0
  13.8 1.7 %collective-permute-start.1 = (bf16[56,2560]{1,0:T(8,128)(2,1)S(1)}, bf16[56,2560]{1,0:T(8,128)(2,1)S(1)}, u32[]{:S(2)}, u32[]{:S(2)}) collective-permute-start(bf16[56,2560]{1,0:T(8,128)(2,1)S(1)} %shard_map.76.w0), channel_id=1, source_target_pairs={{0,2},{2,4},{4,6},{6,8},{8,10},{10,12},{12,14},{14,0},{1,3},{3,5},... | collective-permute-start | bytes 860168 | tf_op jit(solution)/shard_map/ppermute | solution.py:20
  15.5 4.0 %collective-permute-start.2 = (bf16[56,2560]{1,0:T(8,128)(2,1)S(1)}, bf16[56,2560]{1,0:T(8,128)(2,1)S(1)}, u32[]{:S(2)}, u32[]{:S(2)}) collective-permute-start(bf16[56,2560]{1,0:T(8,128)(2,1)S(1)} %shard_map.76.w0), channel_id=1, source_target_pairs={{0,14},{2,0},{4,2},{6,4},{8,6},{10,8},{12,10},{14,12},{1,15},{3,1}... | collective-permute-start | bytes 860168 | tf_op jit(solution)/shard_map/ppermute | solution.py:20
  19.5 0.4 collective-permute-start.10
  19.9 4.9 %collective-permute-done.1.f1 = bf16[56,2560]{1,0:T(8,128)(2,1)S(1)} collective-permute-done((bf16[56,2560]{1,0:T(8,128)(2,1)S(1)}, bf16[56,2560]{1,0:T(8,128)(2,1)S(1)}, u32[]{:S(2)}, u32[]{:S(2)}) %collective-permute-start.1) | collective-permute-done | bytes 286752 | tf_op jit(solution)/shard_map/ppermute | solution.py:20
  24.8 2.7 %collective-permute-start.4 = (bf16[56,2560]{1,0:T(8,128)(2,1)S(1)}, bf16[56,2560]{1,0:T(8,128)(2,1)S(1)}, u32[]{:S(2)}, u32[]{:S(2)}) collective-permute-start(bf16[56,2560]{1,0:T(8,128)(2,1)S(1)} %collective-permute-done.2.b1), channel_id=1, source_target_pairs={{0,14},{2,0},{4,2},{6,4},{8,6},{10,8},{12,10},{14,12},{1,15},{3,1}... | collective-permute-start | bytes 860168 | tf_op jit(solution)/shard_map/ppermute | solution.py:20
  27.5 0.1 collective-permute-done.7.g1
  27.6 0.0 collective-permute-done.9.g3
  27.6 0.0 collective-permute-done.10.swapped2
  27.6 0.1 shard_map.77
  27.7 3.0 %collective-permute-start.12 = (bf16[128,1280]{1,0:T(8,128)(2,1)S(1)}, bf16[128,1280]{1,0:T(8,128)(2,1)S(1)}, u32[]{:S(2)}, u32[]{:S(2)}) collective-permute-start(bf16[128,1280]{1,0:T(8,128)(2,1)S(1)} %get-tuple-element.74.n2), channel_id=1, source_target_pairs={{0,64},{64,0},{1,65},{65,1},{2,66},{66,2},{3,67},{67,3},{4,68},{68... | collective-permute-start | bytes 983048 | tf_op jit(solution)/shard_map/ppermute | solution.py:20
  30.6 0.1 collective-permute-start.11
  30.7 0.4 collective-permute-start.13
  31.2 0.7 collective-permute-done.3.f2
  31.9 0.0 collective-permute-done.4.b2
  31.9 1.5 %collective-permute-start.5 = (bf16[56,2560]{1,0:T(8,128)(2,1)S(1)}, bf16[56,2560]{1,0:T(8,128)(2,1)S(1)}, u32[]{:S(2)}, u32[]{:S(2)}) collective-permute-start(bf16[56,2560]{1,0:T(8,128)(2,1)S(1)} %collective-permute-done.3.f2), channel_id=1, source_target_pairs={{0,2},{2,4},{4,6},{6,8},{8,10},{10,12},{12,14},{14,0},{1,3},{3,5},... | collective-permute-start | bytes 860168 | tf_op jit(solution)/shard_map/ppermute | solution.py:20
  33.4 1.2 %collective-permute-start.6 = (bf16[56,2560]{1,0:T(8,128)(2,1)S(1)}, bf16[56,2560]{1,0:T(8,128)(2,1)S(1)}, u32[]{:S(2)}, u32[]{:S(2)}) collective-permute-start(bf16[56,2560]{1,0:T(8,128)(2,1)S(1)} %collective-permute-done.4.b2), channel_id=1, source_target_pairs={{0,14},{2,0},{4,2},{6,4},{8,6},{10,8},{12,10},{14,12},{1,15},{3,1}... | collective-permute-start | bytes 860168 | tf_op jit(solution)/shard_map/ppermute | solution.py:20
  34.6 0.0 collective-permute-done.12.f2
  34.6 3.5 %shard_map.78 = (f32[8,56,2560]{2,1,0:T(8,128)S(1)}, bf16[56,2560]{1,0:T(8,128)(2,1)S(1)}, bf16[512,2560]{1,0:T(8,128)(2,1)S(1)}, bf16[512,512]{1,0:T(8,128)(2,1)S(1)}) custom-call(bf16[128,2560]{1,0:T(8,128)(2,1)S(1)} %copy-done, bf16[512,128]{1,0:T(8,128)(2,1)S(1)} %copy-done.3, bf16[128,1792]{1,0:T(8,128)(2,1)S(1)} %collective-permute-done.7.g1, ...), custom_call_target="tpu_custom_call" | custom-call | tf_op jit(solution)/shard_map/pallas_call | solution.py:30
  38.1 1.6 %collective-permute-start.16 = (bf16[56,2560]{1,0:T(8,128)(2,1)S(1)}, bf16[56,2560]{1,0:T(8,128)(2,1)S(1)}, u32[]{:S(2)}, u32[]{:S(2)}) collective-permute-start(bf16[56,2560]{1,0:T(8,128)(2,1)S(1)} %get-tuple-element.83), channel_id=1, source_target_pairs={{0,14},{2,0},{4,2},{6,4},{8,6},{10,8},{12,10},{14,12},{1,15},{3,1}... | collective-permute-start | bytes 860168 | tf_op jit(solution)/shard_map/ppermute | solution.py:20
  39.7 1.0 %collective-permute-start.15 = (bf16[56,2560]{1,0:T(8,128)(2,1)S(1)}, bf16[56,2560]{1,0:T(8,128)(2,1)S(1)}, u32[]{:S(2)}, u32[]{:S(2)}) collective-permute-start(bf16[56,2560]{1,0:T(8,128)(2,1)S(1)} %collective-permute-done.5.f3), channel_id=1, source_target_pairs={{0,2},{2,4},{4,6},{6,8},{8,10},{10,12},{12,14},{14,0},{1,3},{3,5},... | collective-permute-start | bytes 860168 | tf_op jit(solution)/shard_map/ppermute | solution.py:20
  40.7 2.5 %shard_map.79 = (bf16[8,64,2560]{2,1,0:T(8,128)(2,1)S(1)}, f32[512,1280]{1,0:T(8,128)S(1)}, bf16[512,64]{1,0:T(8,128)(2,1)S(1)}, bf16[512,1408]{1,0:T(8,128)(2,1)S(1)}, bf16[16,128]{1,0:T(8,128)(2,1)S(1)}) custom-call(bf16[56,2560]{1,0:T(8,128)(2,1)S(1)} %shard_map.76.w0, bf16[56,2560]{1,0:T(8,128)(2,1)S(1)} %collective-permute-done.1.f1, ...), custom_call_target="tpu_custom_call" | custom-call | tf_op jit(solution)/shard_map/pallas_call | solution.py:30
  43.1 7.4 %collective-permute-start.14 = (bf16[512,1408]{1,0:T(8,128)(2,1)S(1)}, bf16[512,1408]{1,0:T(8,128)(2,1)S(1)}, u32[]{:S(2)}, u32[]{:S(2)}) collective-permute-start(bf16[512,1408]{1,0:T(8,128)(2,1)S(1)} %get-tuple-element.79), channel_id=1, source_target_pairs={{0,64},{64,0},{1,65},{65,1},{2,66},{66,2},{3,67},{67,3},{4,68},{68... | collective-permute-start | bytes 4325384 | tf_op jit(solution)/shard_map/ppermute | solution.py:20
  50.6 0.1 shard_map.80
  50.6 1.6 %collective-permute-start.22 = (bf16[56,2560]{1,0:T(8,128)(2,1)S(1)}, bf16[56,2560]{1,0:T(8,128)(2,1)S(1)}, u32[]{:S(2)}, u32[]{:S(2)}) collective-permute-start(bf16[56,2560]{1,0:T(8,128)(2,1)S(1)} %get-tuple-element.84.value), channel_id=1, source_target_pairs={{0,2},{2,4},{4,6},{6,8},{8,10},{10,12},{12,14},{14,0},{1,3},{3,5},... | collective-permute-start | bytes 860168 | tf_op jit(solution)/shard_map/ppermute | solution.py:20
  52.3 1.1 %collective-permute-start.23 = (bf16[56,2560]{1,0:T(8,128)(2,1)S(1)}, bf16[56,2560]{1,0:T(8,128)(2,1)S(1)}, u32[]{:S(2)}, u32[]{:S(2)}) collective-permute-start(bf16[56,2560]{1,0:T(8,128)(2,1)S(1)} %get-tuple-element.90), channel_id=1, source_target_pairs={{0,14},{2,0},{4,2},{6,4},{8,6},{10,8},{12,10},{14,12},{1,15},{3,1}... | collective-permute-start | bytes 860168 | tf_op jit(solution)/shard_map/ppermute | solution.py:20
  53.4 1.6 %collective-permute-start.17 = (bf16[56,1280]{1,0:T(8,128)(2,1)S(1)}, bf16[56,1280]{1,0:T(8,128)(2,1)S(1)}, u32[]{:S(2)}, u32[]{:S(2)}) collective-permute-start(bf16[56,1280]{1,0:T(8,128)(2,1)S(1)} %shard_map.82), channel_id=1, source_target_pairs={{0,64},{64,0},{1,65},{65,1},{2,66},{66,2},{3,67},{67,3},{4,68},{68... | collective-permute-start | bytes 430088 | tf_op jit(solution)/shard_map/ppermute | solution.py:20
  55.1 1.0 %collective-permute-done.17.block_other = bf16[56,1280]{1,0:T(8,128)(2,1)S(1)} collective-permute-done((bf16[56,1280]{1,0:T(8,128)(2,1)S(1)}, bf16[56,1280]{1,0:T(8,128)(2,1)S(1)}, u32[]{:S(2)}, u32[]{:S(2)}) %collective-permute-start.17) | collective-permute-done | bytes 143392 | tf_op jit(solution)/shard_map/ppermute | solution.py:20
  56.1 0.9 shard_map.83
  56.9 0.5 collective-permute-start.19
  57.4 1.5 %collective-permute-start.21 = (bf16[128,1280]{1,0:T(8,128)(2,1)S(1)}, bf16[128,1280]{1,0:T(8,128)(2,1)S(1)}, u32[]{:S(2)}, u32[]{:S(2)}) collective-permute-start(bf16[128,1280]{1,0:T(8,128)(2,1)S(1)} %get-tuple-element.89), channel_id=1, source_target_pairs={{0,16},{16,32},{32,48},{48,0},{1,17},{17,33},{33,49},{49,1},{2,18}... | collective-permute-start | bytes 983048 | tf_op jit(solution)/shard_map/ppermute | solution.py:20
  58.9 1.5 %collective-permute-done.22.refs_0_ = bf16[56,2560]{1,0:T(8,128)(2,1)S(1)} collective-permute-done((bf16[56,2560]{1,0:T(8,128)(2,1)S(1)}, bf16[56,2560]{1,0:T(8,128)(2,1)S(1)}, u32[]{:S(2)}, u32[]{:S(2)}) %collective-permute-start.22) | collective-permute-done | bytes 286752 | tf_op jit(solution)/shard_map/ppermute | solution.py:20
  60.4 0.1 collective-permute-done.23.refs_1_
  60.5 0.1 shard_map.85
  60.6 1.5 %collective-permute-start.24 = (bf16[56,2560]{1,0:T(8,128)(2,1)S(1)}, bf16[56,2560]{1,0:T(8,128)(2,1)S(1)}, u32[]{:S(2)}, u32[]{:S(2)}) collective-permute-start(bf16[56,2560]{1,0:T(8,128)(2,1)S(1)} %get-tuple-element.93), channel_id=1, source_target_pairs={{0,2},{2,4},{4,6},{6,8},{8,10},{10,12},{12,14},{14,0},{1,3},{3,5},... | collective-permute-start | bytes 860168 | tf_op jit(solution)/shard_map/ppermute | solution.py:20
  62.1 1.3 %collective-permute-start.25 = (bf16[56,2560]{1,0:T(8,128)(2,1)S(1)}, bf16[56,2560]{1,0:T(8,128)(2,1)S(1)}, u32[]{:S(2)}, u32[]{:S(2)}) collective-permute-start(bf16[56,2560]{1,0:T(8,128)(2,1)S(1)} %get-tuple-element.94), channel_id=1, source_target_pairs={{0,14},{2,0},{4,2},{6,4},{8,6},{10,8},{12,10},{14,12},{1,15},{3,1}... | collective-permute-start | bytes 860168 | tf_op jit(solution)/shard_map/ppermute | solution.py:20
  63.4 0.4 collective-permute-start.20
  63.8 2.6 %shard_map.86 = (bf16[512,128]{1,0:T(8,128)(2,1)S(1)}, bf16[512,128]{1,0:T(8,128)(2,1)S(1)}, bf16[512,128]{1,0:T(8,128)(2,1)S(1)}, bf16[512,128]{1,0:T(8,128)(2,1)S(1)}) custom-call(bf16[512,2560]{1,0:T(8,128)(2,1)S(1)} %get-tuple-element.96.cot, bf16[8,64,2560]{2,1,0:T(8,128)(2,1)S(1)} %get-tuple-element.97.weight, ...), custom_call_target="tpu_custom_call" | custom-call | tf_op jit(solution)/shard_map/pallas_call | solution.py:30
  66.5 2.7 %collective-permute-done.24.refs_0_ = bf16[56,2560]{1,0:T(8,128)(2,1)S(1)} collective-permute-done((bf16[56,2560]{1,0:T(8,128)(2,1)S(1)}, bf16[56,2560]{1,0:T(8,128)(2,1)S(1)}, u32[]{:S(2)}, u32[]{:S(2)}) %collective-permute-start.24) | collective-permute-done | bytes 286752 | tf_op jit(solution)/shard_map/ppermute | solution.py:20
  69.2 0.1 shard_map.87
  69.3 0.5 collective-permute-start.27
  69.8 2.3 %collective-permute-start.28 = (bf16[56,2560]{1,0:T(8,128)(2,1)S(1)}, bf16[56,2560]{1,0:T(8,128)(2,1)S(1)}, u32[]{:S(2)}, u32[]{:S(2)}) collective-permute-start(bf16[56,2560]{1,0:T(8,128)(2,1)S(1)} %get-tuple-element.104), channel_id=1, source_target_pairs={{0,14},{2,0},{4,2},{6,4},{8,6},{10,8},{12,10},{14,12},{1,15},{3,1}... | collective-permute-start | bytes 860168 | tf_op jit(solution)/shard_map/ppermute | solution.py:20
  72.1 0.2 shard_map.88
  72.3 0.0 copy-start.1
  72.3 0.0 copy-start.2
  72.3 0.7 collective-permute-start.26
  73.0 0.9 %collective-permute-start.31 = (bf16[512,128]{1,0:T(8,128)(2,1)S(1)}, bf16[512,128]{1,0:T(8,128)(2,1)S(1)}, u32[]{:S(2)}, u32[]{:S(2)}) collective-permute-start(bf16[512,128]{1,0:T(8,128)(2,1)S(1)} %get-tuple-element.116), channel_id=1, source_target_pairs={{0,48},{16,0},{32,16},{48,32},{1,49},{17,1},{33,17},{49,33},{2,50}... | collective-permute-start | bytes 393224 | tf_op jit(solution)/shard_map/ppermute | solution.py:20
  73.9 0.6 collective-permute-start.33
  74.4 2.3 %collective-permute-done.27.fwd = bf16[56,2560]{1,0:T(8,128)(2,1)S(1)} collective-permute-done((bf16[56,2560]{1,0:T(8,128)(2,1)S(1)}, bf16[56,2560]{1,0:T(8,128)(2,1)S(1)}, u32[]{:S(2)}, u32[]{:S(2)}) %collective-permute-start.27) | collective-permute-done | bytes 286752 | tf_op jit(solution)/shard_map/ppermute | solution.py:20
  76.7 0.3 shard_map.89
  77.0 0.1 collective-permute-start.30
  77.1 1.5 %collective-permute-start.32 = (bf16[512,128]{1,0:T(8,128)(2,1)S(1)}, bf16[512,128]{1,0:T(8,128)(2,1)S(1)}, u32[]{:S(2)}, u32[]{:S(2)}) collective-permute-start(bf16[512,128]{1,0:T(8,128)(2,1)S(1)} %get-tuple-element.118), channel_id=1, source_target_pairs={{0,32},{16,48},{32,0},{48,16},{1,33},{17,49},{33,1},{49,17},{2,34}... | collective-permute-start | bytes 393224 | tf_op jit(solution)/shard_map/ppermute | solution.py:20
  78.7 0.4 collective-permute-done.26
  79.1 0.1 add_convert_fusion.mine
  79.2 5.5 %collective-permute-start.29 = (bf16[128,1280]{1,0:T(8,128)(2,1)S(1)}, bf16[128,1280]{1,0:T(8,128)(2,1)S(1)}, u32[]{:S(2)}, u32[]{:S(2)}) collective-permute-start(bf16[128,1280]{1,0:T(8,128)(2,1)S(1)} %add_convert_fusion.mine), channel_id=1, source_target_pairs={{0,64},{64,0},{1,65},{65,1},{2,66},{66,2},{3,67},{67,3},{4,68},{68... | collective-permute-start | bytes 983048 | tf_op jit(solution)/shard_map/ppermute | solution.py:20
  84.7 1.3 %shard_map.91 = (bf16[1728,128]{1,0:T(8,128)(2,1)}, bf16[1728,128]{1,0:T(8,128)(2,1)}) custom-call(bf16[1728,128]{1,0:T(8,128)(2,1)S(1)} %bitcast.5, bf16[1728,128]{1,0:T(8,128)(2,1)S(1)} %bitcast.7, bf16[512,128]{1,0:T(8,128)(2,1)S(1)} %get-tuple-element.115.b0, bf16[512,128]{1,0:T(8,128)(2,1)S(1)} %collective-permute-done.31.b1, ...), custom_call_target="tpu_custom_call" | custom-call | flops 4000000000 | tf_op jit(solution)/shard_map/pallas_call | solution.py:30
  86.0 1.0 %shard_map.90 = (bf16[128,2560]{1,0:T(8,128)(2,1)}, f32[27,2560]{1,0:T(8,128)}) custom-call(bf16[128,1280]{1,0:T(8,128)(2,1)S(1)} %add_convert_fusion.mine, bf16[128,1280]{1,0:T(8,128)(2,1)S(1)} %collective-permute-done.29.other, f32[27,2560]{1,0:T(8,128)S(1)} %get-tuple-element.112.keep, bf16[27,2560]{1,0:T(8,128)(2,1)S(1)} %collective-permute-done.30.taken), custom_call_target="tpu_custom_call" | custom-call | bytes 2001920 | tf_op jit(solution)/shard_map/pallas_call | solution.py:30
  (32 shorter events, 0.1 us)
Async XLA Ops:
  0.6 11.9 %collective-permute-start = (bf16[27,2560]{1,0:T(8,128)(2,1)}, bf16[27,2560]{1,0:T(8,128)(2,1)S(1)}, u32[]{:S(2)}, u32[]{:S(2)}) collective-permute-start(bf16[27,2560]{1,0:T(8,128)(2,1)} %mine.1), channel_id=1, source_target_pairs={{0,1},{1,0},{2,3},{3,2},{4,5},{5,4},{6,7},{7,6},{8,9},{9,8},{10,11... | collective-permute-start | bytes 414728 | tf_op jit(solution)/shard_map/ppermute | solution.py:20
  7.0 12.5 %collective-permute-start.8 = (bf16[128,1152]{1,0:T(8,128)(2,1)}, bf16[128,1152]{1,0:T(8,128)(2,1)S(1)}, u32[]{:S(2)}, u32[]{:S(2)}) collective-permute-start(bf16[128,1152]{1,0:T(8,128)(2,1)} %get-tuple-element.64), channel_id=1, source_target_pairs={{0,32},{16,48},{32,0},{48,16},{1,33},{17,49},{33,1},{49,17},{2,34}... | collective-permute-start | bytes 884744 | tf_op jit(solution)/shard_map/ppermute | solution.py:20
  9.9 17.7 %collective-permute-start.7 = (bf16[128,1792]{1,0:T(8,128)(2,1)}, bf16[128,1792]{1,0:T(8,128)(2,1)S(1)}, u32[]{:S(2)}, u32[]{:S(2)}) collective-permute-start(bf16[128,1792]{1,0:T(8,128)(2,1)} %get-tuple-element.63), channel_id=1, source_target_pairs={{0,16},{16,32},{32,48},{48,0},{1,17},{17,33},{33,49},{49,1},{2,18}... | collective-permute-start | bytes 1376264 | tf_op jit(solution)/shard_map/ppermute | solution.py:20
  10.2 24.4 %copy-start = (bf16[128,2560]{1,0:T(8,128)(2,1)S(1)}, bf16[128,2560]{1,0:T(8,128)(2,1)}, u32[]{:S(2)}) copy-start(bf16[128,2560]{1,0:T(8,128)(2,1)} %cot_own.1) | copy-start | bytes 1966084
  10.2 24.4 %copy-start.3 = (bf16[512,128]{1,0:T(8,128)(2,1)S(1)}, bf16[512,128]{1,0:T(8,128)(2,1)}, u32[]{:S(2)}) copy-start(bf16[512,128]{1,0:T(8,128)(2,1)} %get-tuple-element.73.hid_own) | copy-start | bytes 393220
  10.2 17.4 %collective-permute-start.9 = (bf16[128,1792]{1,0:T(8,128)(2,1)}, bf16[128,1792]{1,0:T(8,128)(2,1)S(1)}, u32[]{:S(2)}, u32[]{:S(2)}) collective-permute-start(bf16[128,1792]{1,0:T(8,128)(2,1)} %get-tuple-element.65), channel_id=1, source_target_pairs={{0,48},{16,0},{32,16},{48,32},{1,49},{17,1},{33,17},{49,33},{2,50}... | collective-permute-start | bytes 1376264 | tf_op jit(solution)/shard_map/ppermute | solution.py:20
  12.5 0.9 %copy-start.4 = (bf16[27,2560]{1,0:T(8,128)(2,1)S(1)}, bf16[27,2560]{1,0:T(8,128)(2,1)}, u32[]{:S(2)}) copy-start(bf16[27,2560]{1,0:T(8,128)(2,1)} %mine.1) | copy-start | bytes 414724
  13.8 11.0 %collective-permute-start.1 = (bf16[56,2560]{1,0:T(8,128)(2,1)S(1)}, bf16[56,2560]{1,0:T(8,128)(2,1)S(1)}, u32[]{:S(2)}, u32[]{:S(2)}) collective-permute-start(bf16[56,2560]{1,0:T(8,128)(2,1)S(1)} %shard_map.76.w0), channel_id=1, source_target_pairs={{0,2},{2,4},{4,6},{6,8},{8,10},{10,12},{12,14},{14,0},{1,3},{3,5},... | collective-permute-start | bytes 860168 | tf_op jit(solution)/shard_map/ppermute | solution.py:20
  15.5 9.3 %collective-permute-start.2 = (bf16[56,2560]{1,0:T(8,128)(2,1)S(1)}, bf16[56,2560]{1,0:T(8,128)(2,1)S(1)}, u32[]{:S(2)}, u32[]{:S(2)}) collective-permute-start(bf16[56,2560]{1,0:T(8,128)(2,1)S(1)} %shard_map.76.w0), channel_id=1, source_target_pairs={{0,14},{2,0},{4,2},{6,4},{8,6},{10,8},{12,10},{14,12},{1,15},{3,1}... | collective-permute-start | bytes 860168 | tf_op jit(solution)/shard_map/ppermute | solution.py:20
  19.5 8.1 %collective-permute-start.10 = (bf16[128,1152]{1,0:T(8,128)(2,1)S(1)}, bf16[128,1152]{1,0:T(8,128)(2,1)S(1)}, u32[]{:S(2)}, u32[]{:S(2)}) collective-permute-start(bf16[128,1152]{1,0:T(8,128)(2,1)S(1)} %collective-permute-done.8.g2), channel_id=1, source_target_pairs={{0,128},{128,0},{1,129},{129,1},{2,130},{130,2},{3,131},{131,3},{4... | collective-permute-start | bytes 884744 | tf_op jit(solution)/shard_map/ppermute | solution.py:20
  24.8 7.1 %collective-permute-start.3 = (bf16[56,2560]{1,0:T(8,128)(2,1)S(1)}, bf16[56,2560]{1,0:T(8,128)(2,1)S(1)}, u32[]{:S(2)}, u32[]{:S(2)}) collective-permute-start(bf16[56,2560]{1,0:T(8,128)(2,1)S(1)} %collective-permute-done.1.f1), channel_id=1, source_target_pairs={{0,2},{2,4},{4,6},{6,8},{8,10},{10,12},{12,14},{14,0},{1,3},{3,5},... | collective-permute-start | bytes 860168 | tf_op jit(solution)/shard_map/ppermute | solution.py:20
  24.8 7.1 %collective-permute-start.4 = (bf16[56,2560]{1,0:T(8,128)(2,1)S(1)}, bf16[56,2560]{1,0:T(8,128)(2,1)S(1)}, u32[]{:S(2)}, u32[]{:S(2)}) collective-permute-start(bf16[56,2560]{1,0:T(8,128)(2,1)S(1)} %collective-permute-done.2.b1), channel_id=1, source_target_pairs={{0,14},{2,0},{4,2},{6,4},{8,6},{10,8},{12,10},{14,12},{1,15},{3,1}... | collective-permute-start | bytes 860168 | tf_op jit(solution)/shard_map/ppermute | solution.py:20
  27.7 6.9 %collective-permute-start.12 = (bf16[128,1280]{1,0:T(8,128)(2,1)S(1)}, bf16[128,1280]{1,0:T(8,128)(2,1)S(1)}, u32[]{:S(2)}, u32[]{:S(2)}) collective-permute-start(bf16[128,1280]{1,0:T(8,128)(2,1)S(1)} %get-tuple-element.74.n2), channel_id=1, source_target_pairs={{0,64},{64,0},{1,65},{65,1},{2,66},{66,2},{3,67},{67,3},{4,68},{68... | collective-permute-start | bytes 983048 | tf_op jit(solution)/shard_map/ppermute | solution.py:20
  30.6 3.9 %collective-permute-start.11 = (bf16[128,1280]{1,0:T(8,128)(2,1)S(1)}, bf16[128,1280]{1,0:T(8,128)(2,1)S(1)}, u32[]{:S(2)}, u32[]{:S(2)}) collective-permute-start(bf16[128,1280]{1,0:T(8,128)(2,1)S(1)} %get-tuple-element.75), channel_id=1, source_target_pairs={{0,64},{64,0},{1,65},{65,1},{2,66},{66,2},{3,67},{67,3},{4,68},{68... | collective-permute-start | bytes 983048 | tf_op jit(solution)/shard_map/ppermute | solution.py:20
  30.7 3.8 %collective-permute-start.13 = (bf16[128,1280]{1,0:T(8,128)(2,1)S(1)}, bf16[128,1280]{1,0:T(8,128)(2,1)S(1)}, u32[]{:S(2)}, u32[]{:S(2)}) collective-permute-start(bf16[128,1280]{1,0:T(8,128)(2,1)S(1)} %get-tuple-element.76), channel_id=1, source_target_pairs={{0,64},{64,0},{1,65},{65,1},{2,66},{66,2},{3,67},{67,3},{4,68},{68... | collective-permute-start | bytes 983048 | tf_op jit(solution)/shard_map/ppermute | solution.py:20
  31.9 7.8 %collective-permute-start.5 = (bf16[56,2560]{1,0:T(8,128)(2,1)S(1)}, bf16[56,2560]{1,0:T(8,128)(2,1)S(1)}, u32[]{:S(2)}, u32[]{:S(2)}) collective-permute-start(bf16[56,2560]{1,0:T(8,128)(2,1)S(1)} %collective-permute-done.3.f2), channel_id=1, source_target_pairs={{0,2},{2,4},{4,6},{6,8},{8,10},{10,12},{12,14},{14,0},{1,3},{3,5},... | collective-permute-start | bytes 860168 | tf_op jit(solution)/shard_map/ppermute | solution.py:20
  33.4 6.3 %collective-permute-start.6 = (bf16[56,2560]{1,0:T(8,128)(2,1)S(1)}, bf16[56,2560]{1,0:T(8,128)(2,1)S(1)}, u32[]{:S(2)}, u32[]{:S(2)}) collective-permute-start(bf16[56,2560]{1,0:T(8,128)(2,1)S(1)} %collective-permute-done.4.b2), channel_id=1, source_target_pairs={{0,14},{2,0},{4,2},{6,4},{8,6},{10,8},{12,10},{14,12},{1,15},{3,1}... | collective-permute-start | bytes 860168 | tf_op jit(solution)/shard_map/ppermute | solution.py:20
  38.1 12.5 %collective-permute-start.16 = (bf16[56,2560]{1,0:T(8,128)(2,1)S(1)}, bf16[56,2560]{1,0:T(8,128)(2,1)S(1)}, u32[]{:S(2)}, u32[]{:S(2)}) collective-permute-start(bf16[56,2560]{1,0:T(8,128)(2,1)S(1)} %get-tuple-element.83), channel_id=1, source_target_pairs={{0,14},{2,0},{4,2},{6,4},{8,6},{10,8},{12,10},{14,12},{1,15},{3,1}... | collective-permute-start | bytes 860168 | tf_op jit(solution)/shard_map/ppermute | solution.py:20
  39.7 13.7 %collective-permute-start.15 = (bf16[56,2560]{1,0:T(8,128)(2,1)S(1)}, bf16[56,2560]{1,0:T(8,128)(2,1)S(1)}, u32[]{:S(2)}, u32[]{:S(2)}) collective-permute-start(bf16[56,2560]{1,0:T(8,128)(2,1)S(1)} %collective-permute-done.5.f3), channel_id=1, source_target_pairs={{0,2},{2,4},{4,6},{6,8},{8,10},{10,12},{12,14},{14,0},{1,3},{3,5},... | collective-permute-start | bytes 860168 | tf_op jit(solution)/shard_map/ppermute | solution.py:20
  43.1 12.9 %collective-permute-start.14 = (bf16[512,1408]{1,0:T(8,128)(2,1)S(1)}, bf16[512,1408]{1,0:T(8,128)(2,1)S(1)}, u32[]{:S(2)}, u32[]{:S(2)}) collective-permute-start(bf16[512,1408]{1,0:T(8,128)(2,1)S(1)} %get-tuple-element.79), channel_id=1, source_target_pairs={{0,64},{64,0},{1,65},{65,1},{2,66},{66,2},{3,67},{67,3},{4,68},{68... | collective-permute-start | bytes 4325384 | tf_op jit(solution)/shard_map/ppermute | solution.py:20
  50.6 9.7 %collective-permute-start.22 = (bf16[56,2560]{1,0:T(8,128)(2,1)S(1)}, bf16[56,2560]{1,0:T(8,128)(2,1)S(1)}, u32[]{:S(2)}, u32[]{:S(2)}) collective-permute-start(bf16[56,2560]{1,0:T(8,128)(2,1)S(1)} %get-tuple-element.84.value), channel_id=1, source_target_pairs={{0,2},{2,4},{4,6},{6,8},{8,10},{10,12},{12,14},{14,0},{1,3},{3,5},... | collective-permute-start | bytes 860168 | tf_op jit(solution)/shard_map/ppermute | solution.py:20
  52.3 8.2 %collective-permute-start.23 = (bf16[56,2560]{1,0:T(8,128)(2,1)S(1)}, bf16[56,2560]{1,0:T(8,128)(2,1)S(1)}, u32[]{:S(2)}, u32[]{:S(2)}) collective-permute-start(bf16[56,2560]{1,0:T(8,128)(2,1)S(1)} %get-tuple-element.90), channel_id=1, source_target_pairs={{0,14},{2,0},{4,2},{6,4},{8,6},{10,8},{12,10},{14,12},{1,15},{3,1}... | collective-permute-start | bytes 860168 | tf_op jit(solution)/shard_map/ppermute | solution.py:20
  53.4 2.6 %collective-permute-start.17 = (bf16[56,1280]{1,0:T(8,128)(2,1)S(1)}, bf16[56,1280]{1,0:T(8,128)(2,1)S(1)}, u32[]{:S(2)}, u32[]{:S(2)}) collective-permute-start(bf16[56,1280]{1,0:T(8,128)(2,1)S(1)} %shard_map.82), channel_id=1, source_target_pairs={{0,64},{64,0},{1,65},{65,1},{2,66},{66,2},{3,67},{67,3},{4,68},{68... | collective-permute-start | bytes 430088 | tf_op jit(solution)/shard_map/ppermute | solution.py:20
  56.9 6.4 %collective-permute-start.19 = (bf16[128,640]{1,0:T(8,128)(2,1)S(1)}, bf16[128,640]{1,0:T(8,128)(2,1)S(1)}, u32[]{:S(2)}, u32[]{:S(2)}) collective-permute-start(bf16[128,640]{1,0:T(8,128)(2,1)S(1)} %get-tuple-element.88), channel_id=1, source_target_pairs={{0,128},{128,0},{1,129},{129,1},{2,130},{130,2},{3,131},{131,3},{4... | collective-permute-start | bytes 491528 | tf_op jit(solution)/shard_map/ppermute | solution.py:20
  57.4 14.6 %collective-permute-start.18 = (bf16[128,1280]{1,0:T(8,128)(2,1)S(1)}, bf16[128,1280]{1,0:T(8,128)(2,1)S(1)}, u32[]{:S(2)}, u32[]{:S(2)}) collective-permute-start(bf16[128,1280]{1,0:T(8,128)(2,1)S(1)} %get-tuple-element.86), channel_id=1, source_target_pairs={{0,48},{16,0},{32,16},{48,32},{1,49},{17,1},{33,17},{49,33},{2,50}... | collective-permute-start | bytes 983048 | tf_op jit(solution)/shard_map/ppermute | solution.py:20
  57.4 14.6 %collective-permute-start.21 = (bf16[128,1280]{1,0:T(8,128)(2,1)S(1)}, bf16[128,1280]{1,0:T(8,128)(2,1)S(1)}, u32[]{:S(2)}, u32[]{:S(2)}) collective-permute-start(bf16[128,1280]{1,0:T(8,128)(2,1)S(1)} %get-tuple-element.89), channel_id=1, source_target_pairs={{0,16},{16,32},{32,48},{48,0},{1,17},{17,33},{33,49},{49,1},{2,18}... | collective-permute-start | bytes 983048 | tf_op jit(solution)/shard_map/ppermute | solution.py:20
  60.6 8.5 %collective-permute-start.24 = (bf16[56,2560]{1,0:T(8,128)(2,1)S(1)}, bf16[56,2560]{1,0:T(8,128)(2,1)S(1)}, u32[]{:S(2)}, u32[]{:S(2)}) collective-permute-start(bf16[56,2560]{1,0:T(8,128)(2,1)S(1)} %get-tuple-element.93), channel_id=1, source_target_pairs={{0,2},{2,4},{4,6},{6,8},{8,10},{10,12},{12,14},{14,0},{1,3},{3,5},... | collective-permute-start | bytes 860168 | tf_op jit(solution)/shard_map/ppermute | solution.py:20
  62.1 7.1 %collective-permute-start.25 = (bf16[56,2560]{1,0:T(8,128)(2,1)S(1)}, bf16[56,2560]{1,0:T(8,128)(2,1)S(1)}, u32[]{:S(2)}, u32[]{:S(2)}) collective-permute-start(bf16[56,2560]{1,0:T(8,128)(2,1)S(1)} %get-tuple-element.94), channel_id=1, source_target_pairs={{0,14},{2,0},{4,2},{6,4},{8,6},{10,8},{12,10},{14,12},{1,15},{3,1}... | collective-permute-start | bytes 860168 | tf_op jit(solution)/shard_map/ppermute | solution.py:20
  63.4 8.6 %collective-permute-start.20 = (bf16[128,640]{1,0:T(8,128)(2,1)S(1)}, bf16[128,640]{1,0:T(8,128)(2,1)S(1)}, u32[]{:S(2)}, u32[]{:S(2)}) collective-permute-start(bf16[128,640]{1,0:T(8,128)(2,1)S(1)} %shard_map.84), channel_id=1, source_target_pairs={{0,32},{16,48},{32,0},{48,16},{1,33},{17,49},{33,1},{49,17},{2,34}... | collective-permute-start | bytes 491528 | tf_op jit(solution)/shard_map/ppermute | solution.py:20
  69.3 7.4 %collective-permute-start.27 = (bf16[56,2560]{1,0:T(8,128)(2,1)S(1)}, bf16[56,2560]{1,0:T(8,128)(2,1)S(1)}, u32[]{:S(2)}, u32[]{:S(2)}) collective-permute-start(bf16[56,2560]{1,0:T(8,128)(2,1)S(1)} %get-tuple-element.103), channel_id=1, source_target_pairs={{0,2},{2,4},{4,6},{6,8},{8,10},{10,12},{12,14},{14,0},{1,3},{3,5},... | collective-permute-start | bytes 860168 | tf_op jit(solution)/shard_map/ppermute | solution.py:20
  69.8 7.0 %collective-permute-start.28 = (bf16[56,2560]{1,0:T(8,128)(2,1)S(1)}, bf16[56,2560]{1,0:T(8,128)(2,1)S(1)}, u32[]{:S(2)}, u32[]{:S(2)}) collective-permute-start(bf16[56,2560]{1,0:T(8,128)(2,1)S(1)} %get-tuple-element.104), channel_id=1, source_target_pairs={{0,14},{2,0},{4,2},{6,4},{8,6},{10,8},{12,10},{14,12},{1,15},{3,1}... | collective-permute-start | bytes 860168 | tf_op jit(solution)/shard_map/ppermute | solution.py:20
  72.3 12.4 %copy-start.1 = (bf16[128,1728]{0,1:T(8,128)(2,1)S(1)}, bf16[128,1728]{0,1:T(8,128)(2,1)}, u32[]{:S(2)}) copy-start(bf16[128,1728]{0,1:T(8,128)(2,1)} %param.4) | copy-start | bytes 1327108
  72.3 12.4 %copy-start.2 = (bf16[128,1728]{0,1:T(8,128)(2,1)S(1)}, bf16[128,1728]{0,1:T(8,128)(2,1)}, u32[]{:S(2)}) copy-start(bf16[128,1728]{0,1:T(8,128)(2,1)} %param.5) | copy-start | bytes 1327108
  72.3 6.8 %collective-permute-start.26 = (bf16[128,1280]{1,0:T(8,128)(2,1)S(1)}, bf16[128,1280]{1,0:T(8,128)(2,1)S(1)}, u32[]{:S(2)}, u32[]{:S(2)}) collective-permute-start(bf16[128,1280]{1,0:T(8,128)(2,1)S(1)} %shard_map.88), channel_id=1, source_target_pairs={{0,128},{128,0},{1,129},{129,1},{2,130},{130,2},{3,131},{131,3},{4... | collective-permute-start | bytes 983048 | tf_op jit(solution)/shard_map/ppermute | solution.py:20
  73.0 11.7 %collective-permute-start.31 = (bf16[512,128]{1,0:T(8,128)(2,1)S(1)}, bf16[512,128]{1,0:T(8,128)(2,1)S(1)}, u32[]{:S(2)}, u32[]{:S(2)}) collective-permute-start(bf16[512,128]{1,0:T(8,128)(2,1)S(1)} %get-tuple-element.116), channel_id=1, source_target_pairs={{0,48},{16,0},{32,16},{48,32},{1,49},{17,1},{33,17},{49,33},{2,50}... | collective-permute-start | bytes 393224 | tf_op jit(solution)/shard_map/ppermute | solution.py:20
  73.9 10.8 %collective-permute-start.33 = (bf16[512,128]{1,0:T(8,128)(2,1)S(1)}, bf16[512,128]{1,0:T(8,128)(2,1)S(1)}, u32[]{:S(2)}, u32[]{:S(2)}) collective-permute-start(bf16[512,128]{1,0:T(8,128)(2,1)S(1)} %get-tuple-element.119), channel_id=1, source_target_pairs={{0,16},{16,32},{32,48},{48,0},{1,17},{17,33},{33,49},{49,1},{2,18}... | collective-permute-start | bytes 393224 | tf_op jit(solution)/shard_map/ppermute | solution.py:20
  77.0 9.0 %collective-permute-start.30 = (bf16[27,2560]{1,0:T(8,128)(2,1)S(1)}, bf16[27,2560]{1,0:T(8,128)(2,1)S(1)}, u32[]{:S(2)}, u32[]{:S(2)}) collective-permute-start(bf16[27,2560]{1,0:T(8,128)(2,1)S(1)} %get-tuple-element.110), channel_id=1, source_target_pairs={{0,1},{1,0},{2,3},{3,2},{4,5},{5,4},{6,7},{7,6},{8,9},{9,8},{10,11... | collective-permute-start | bytes 414728 | tf_op jit(solution)/shard_map/ppermute | solution.py:20
  77.1 7.5 %collective-permute-start.32 = (bf16[512,128]{1,0:T(8,128)(2,1)S(1)}, bf16[512,128]{1,0:T(8,128)(2,1)S(1)}, u32[]{:S(2)}, u32[]{:S(2)}) collective-permute-start(bf16[512,128]{1,0:T(8,128)(2,1)S(1)} %get-tuple-element.118), channel_id=1, source_target_pairs={{0,32},{16,48},{32,0},{48,16},{1,33},{17,49},{33,1},{49,17},{2,34}... | collective-permute-start | bytes 393224 | tf_op jit(solution)/shard_map/ppermute | solution.py:20
  79.2 6.9 %collective-permute-start.29 = (bf16[128,1280]{1,0:T(8,128)(2,1)S(1)}, bf16[128,1280]{1,0:T(8,128)(2,1)S(1)}, u32[]{:S(2)}, u32[]{:S(2)}) collective-permute-start(bf16[128,1280]{1,0:T(8,128)(2,1)S(1)} %add_convert_fusion.mine), channel_id=1, source_target_pairs={{0,64},{64,0},{1,65},{65,1},{2,66},{66,2},{3,67},{67,3},{4,68},{68... | collective-permute-start | bytes 983048 | tf_op jit(solution)/shard_map/ppermute | solution.py:20

commit v9 on v8

--- a/solution.py
+++ b/solution.py
@@ -427,7 +427,7 @@
     to_fwd, to_bwd = added(2, ring)
     ring = (shift(to_fwd, "z", 1), shift(to_bwd, "z", -1))
     *ring, back1, back2, back3 = lax.optimization_barrier((*ring, back1, back2, back3))
-    got_back1, got_back3 = shift(back1, "x", -1), shift(back3, "x", -3)
+    got_back1, got_back2 = shift(back1, "x", -1), shift(back2, "x", -2)
     to_fwd, to_bwd = added(1, ring)
     got_out = after(got_out, to_fwd, to_bwd)
     ring = (shift(to_fwd, "z", 1), shift(to_bwd, "z", -1))
@@ -443,7 +443,7 @@
         moved=0,
     )
     taken = shift(give, "yh", 1)
-    got_back2 = shift(after(back2, give), "x", -2)
+    got_back3 = shift(after(back3, give), "x", -3)
     grad_gate, grad_up = call(
         activation_gradients,
         [like((units, rows))] * 2,

time: 88 us -> 87.7 us (level)
  starting transfers between devices: 55.9 us -> 54.6 us
  waiting for transfers between devices: 13.8 us -> 15 us
    ppermute x34, starting transfers between devices: 55.9 us -> 54.6 us  [shift(): lax.ppermute(value, axis, [(i, (i + steps) % count) for i in range(count)])]
    ppermute x34, waiting for transfers between devices: 13.8 us -> 15 us  [shift(): lax.ppermute(value, axis, [(i, (i + steps) % count) for i in range(count)])]
where the time goes in v9:
time: 87.7 us; the launch traced here: 87.1 us
  starting transfers between devices  54.6 us (62%)
  Pallas kernels  15.6 us (18%)
  waiting for transfers between devices  15 us (17%)
  local copies, waits for them, and re-layouts  0.94 us (1%)
    ppermute x34, starting transfers between devices, shift(): lax.ppermute(value, axis, [(i, (i + steps) % count) for i in range(count)])  54.6 us
    pallas_call x17, Pallas kernels, call(): pl.pallas_call(kernel, out_shape=outs, in_specs=[pl.BlockSpec(memory_spac...  15.6 us
    ppermute x34, waiting for transfers between devices, shift(): lax.ppermute(value, axis, [(i, (i + steps) % count) for i in range(count)])  15 us
  transfers between devices with their start and end apart: 34, of which 9 were waited for; matrix products, arithmetic and copies ran while one was open for 0% of the time, Pallas kernels for 17%

profile of v9, /device:TPU:1, one launch (start us, length us, event | category | flops | bytes accessed | tf_op | source)
XLA Modules:
  0.0 87.1 jit_solution(17573959716085616135)
XLA Ops:
  0.6 3.8 %collective-permute-start = (bf16[27,2560]{1,0:T(8,128)(2,1)}, bf16[27,2560]{1,0:T(8,128)(2,1)S(1)}, u32[]{:S(2)}, u32[]{:S(2)}) collective-permute-start(bf16[27,2560]{1,0:T(8,128)(2,1)} %mine.1), channel_id=1, source_target_pairs={{0,1},{1,0},{2,3},{3,2},{4,5},{5,4},{6,7},{7,6},{8,9},{9,8},{10,11... | collective-permute-start | bytes 414728 | tf_op jit(solution)/shard_map/ppermute | solution.py:20
  4.5 2.6 %shard_map.75 = (bf16[128,1792]{1,0:T(8,128)(2,1)}, bf16[128,1152]{1,0:T(8,128)(2,1)}, bf16[128,1792]{1,0:T(8,128)(2,1)}, bf16[512,128]{1,0:T(8,128)(2,1)}) custom-call(bf16[1728,128]{1,0:T(8,128)(2,1)} %bitcast.4, bf16[1728,128]{1,0:T(8,128)(2,1)} %bitcast.6, bf16[128,2560]{1,0:T(8,128)(2,1)} %cot_own.1), custom_call_target="tpu_custom_call" | custom-call | bytes 2883584 | tf_op jit(solution)/shard_map/pallas_call | solution.py:30
  7.0 2.8 %collective-permute-start.8 = (bf16[128,1152]{1,0:T(8,128)(2,1)}, bf16[128,1152]{1,0:T(8,128)(2,1)S(1)}, u32[]{:S(2)}, u32[]{:S(2)}) collective-permute-start(bf16[128,1152]{1,0:T(8,128)(2,1)} %get-tuple-element.64), channel_id=1, source_target_pairs={{0,32},{16,48},{32,0},{48,16},{1,33},{17,49},{33,1},{49,17},{2,34}... | collective-permute-start | bytes 884744 | tf_op jit(solution)/shard_map/ppermute | solution.py:20
  9.9 0.3 collective-permute-start.7
  10.2 2.4 %collective-permute-start.9 = (bf16[128,1792]{1,0:T(8,128)(2,1)}, bf16[128,1792]{1,0:T(8,128)(2,1)S(1)}, u32[]{:S(2)}, u32[]{:S(2)}) collective-permute-start(bf16[128,1792]{1,0:T(8,128)(2,1)} %get-tuple-element.65), channel_id=1, source_target_pairs={{0,48},{16,0},{32,16},{48,32},{1,49},{17,1},{33,17},{49,33},{2,50}... | collective-permute-start | bytes 1376264 | tf_op jit(solution)/shard_map/ppermute | solution.py:20
  12.5 0.0 collective-permute-done.other
  12.5 0.9 %copy-done.4 = bf16[27,2560]{1,0:T(8,128)(2,1)S(1)} copy-done((bf16[27,2560]{1,0:T(8,128)(2,1)S(1)}, bf16[27,2560]{1,0:T(8,128)(2,1)}, u32[]{:S(2)}) %copy-start.4) | copy-done | bytes 138264
  13.5 0.3 shard_map.76.w0
  13.8 1.7 %collective-permute-start.1 = (bf16[56,2560]{1,0:T(8,128)(2,1)S(1)}, bf16[56,2560]{1,0:T(8,128)(2,1)S(1)}, u32[]{:S(2)}, u32[]{:S(2)}) collective-permute-start(bf16[56,2560]{1,0:T(8,128)(2,1)S(1)} %shard_map.76.w0), channel_id=1, source_target_pairs={{0,2},{2,4},{4,6},{6,8},{8,10},{10,12},{12,14},{14,0},{1,3},{3,5},... | collective-permute-start | bytes 860168 | tf_op jit(solution)/shard_map/ppermute | solution.py:20
  15.5 4.0 %collective-permute-start.2 = (bf16[56,2560]{1,0:T(8,128)(2,1)S(1)}, bf16[56,2560]{1,0:T(8,128)(2,1)S(1)}, u32[]{:S(2)}, u32[]{:S(2)}) collective-permute-start(bf16[56,2560]{1,0:T(8,128)(2,1)S(1)} %shard_map.76.w0), channel_id=1, source_target_pairs={{0,14},{2,0},{4,2},{6,4},{8,6},{10,8},{12,10},{14,12},{1,15},{3,1}... | collective-permute-start | bytes 860168 | tf_op jit(solution)/shard_map/ppermute | solution.py:20
  19.5 0.4 collective-permute-start.10
  19.9 4.9 %collective-permute-done.1.f1 = bf16[56,2560]{1,0:T(8,128)(2,1)S(1)} collective-permute-done((bf16[56,2560]{1,0:T(8,128)(2,1)S(1)}, bf16[56,2560]{1,0:T(8,128)(2,1)S(1)}, u32[]{:S(2)}, u32[]{:S(2)}) %collective-permute-start.1) | collective-permute-done | bytes 286752 | tf_op jit(solution)/shard_map/ppermute | solution.py:20
  24.8 2.7 %collective-permute-start.4 = (bf16[56,2560]{1,0:T(8,128)(2,1)S(1)}, bf16[56,2560]{1,0:T(8,128)(2,1)S(1)}, u32[]{:S(2)}, u32[]{:S(2)}) collective-permute-start(bf16[56,2560]{1,0:T(8,128)(2,1)S(1)} %collective-permute-done.2.b1), channel_id=1, source_target_pairs={{0,14},{2,0},{4,2},{6,4},{8,6},{10,8},{12,10},{14,12},{1,15},{3,1}... | collective-permute-start | bytes 860168 | tf_op jit(solution)/shard_map/ppermute | solution.py:20
  27.5 0.1 collective-permute-done.7.g1
  27.6 0.0 collective-permute-done.9.g3
  27.6 0.0 collective-permute-done.10.swapped2
  27.6 0.1 shard_map.77
  27.7 3.0 %collective-permute-start.12 = (bf16[128,1280]{1,0:T(8,128)(2,1)S(1)}, bf16[128,1280]{1,0:T(8,128)(2,1)S(1)}, u32[]{:S(2)}, u32[]{:S(2)}) collective-permute-start(bf16[128,1280]{1,0:T(8,128)(2,1)S(1)} %get-tuple-element.74.n2), channel_id=1, source_target_pairs={{0,64},{64,0},{1,65},{65,1},{2,66},{66,2},{3,67},{67,3},{4,68},{68... | collective-permute-start | bytes 983048 | tf_op jit(solution)/shard_map/ppermute | solution.py:20
  30.6 0.1 collective-permute-start.11
  30.7 0.4 collective-permute-start.13
  31.2 0.7 collective-permute-done.3.f2
  31.9 0.0 collective-permute-done.4.b2
  31.9 1.5 %collective-permute-start.5 = (bf16[56,2560]{1,0:T(8,128)(2,1)S(1)}, bf16[56,2560]{1,0:T(8,128)(2,1)S(1)}, u32[]{:S(2)}, u32[]{:S(2)}) collective-permute-start(bf16[56,2560]{1,0:T(8,128)(2,1)S(1)} %collective-permute-done.3.f2), channel_id=1, source_target_pairs={{0,2},{2,4},{4,6},{6,8},{8,10},{10,12},{12,14},{14,0},{1,3},{3,5},... | collective-permute-start | bytes 860168 | tf_op jit(solution)/shard_map/ppermute | solution.py:20
  33.4 1.2 %collective-permute-start.6 = (bf16[56,2560]{1,0:T(8,128)(2,1)S(1)}, bf16[56,2560]{1,0:T(8,128)(2,1)S(1)}, u32[]{:S(2)}, u32[]{:S(2)}) collective-permute-start(bf16[56,2560]{1,0:T(8,128)(2,1)S(1)} %collective-permute-done.4.b2), channel_id=1, source_target_pairs={{0,14},{2,0},{4,2},{6,4},{8,6},{10,8},{12,10},{14,12},{1,15},{3,1}... | collective-permute-start | bytes 860168 | tf_op jit(solution)/shard_map/ppermute | solution.py:20
  34.6 3.5 %shard_map.78 = (f32[8,56,2560]{2,1,0:T(8,128)S(1)}, bf16[56,2560]{1,0:T(8,128)(2,1)S(1)}, bf16[512,2560]{1,0:T(8,128)(2,1)S(1)}, bf16[512,512]{1,0:T(8,128)(2,1)S(1)}) custom-call(bf16[128,2560]{1,0:T(8,128)(2,1)S(1)} %copy-done, bf16[512,128]{1,0:T(8,128)(2,1)S(1)} %copy-done.3, bf16[128,1792]{1,0:T(8,128)(2,1)S(1)} %collective-permute-done.7.g1, ...), custom_call_target="tpu_custom_call" | custom-call | tf_op jit(solution)/shard_map/pallas_call | solution.py:30
  38.1 1.6 %collective-permute-start.16 = (bf16[56,2560]{1,0:T(8,128)(2,1)S(1)}, bf16[56,2560]{1,0:T(8,128)(2,1)S(1)}, u32[]{:S(2)}, u32[]{:S(2)}) collective-permute-start(bf16[56,2560]{1,0:T(8,128)(2,1)S(1)} %get-tuple-element.83), channel_id=1, source_target_pairs={{0,14},{2,0},{4,2},{6,4},{8,6},{10,8},{12,10},{14,12},{1,15},{3,1}... | collective-permute-start | bytes 860168 | tf_op jit(solution)/shard_map/ppermute | solution.py:20
  39.7 0.0 collective-permute-done.5.f3
  39.7 1.0 %collective-permute-start.15 = (bf16[56,2560]{1,0:T(8,128)(2,1)S(1)}, bf16[56,2560]{1,0:T(8,128)(2,1)S(1)}, u32[]{:S(2)}, u32[]{:S(2)}) collective-permute-start(bf16[56,2560]{1,0:T(8,128)(2,1)S(1)} %collective-permute-done.5.f3), channel_id=1, source_target_pairs={{0,2},{2,4},{4,6},{6,8},{8,10},{10,12},{12,14},{14,0},{1,3},{3,5},... | collective-permute-start | bytes 860168 | tf_op jit(solution)/shard_map/ppermute | solution.py:20
  40.7 2.5 %shard_map.79 = (bf16[8,64,2560]{2,1,0:T(8,128)(2,1)S(1)}, f32[512,1280]{1,0:T(8,128)S(1)}, bf16[512,64]{1,0:T(8,128)(2,1)S(1)}, bf16[512,1408]{1,0:T(8,128)(2,1)S(1)}, bf16[16,128]{1,0:T(8,128)(2,1)S(1)}) custom-call(bf16[56,2560]{1,0:T(8,128)(2,1)S(1)} %shard_map.76.w0, bf16[56,2560]{1,0:T(8,128)(2,1)S(1)} %collective-permute-done.1.f1, ...), custom_call_target="tpu_custom_call" | custom-call | tf_op jit(solution)/shard_map/pallas_call | solution.py:30
  43.1 7.4 %collective-permute-start.14 = (bf16[512,1408]{1,0:T(8,128)(2,1)S(1)}, bf16[512,1408]{1,0:T(8,128)(2,1)S(1)}, u32[]{:S(2)}, u32[]{:S(2)}) collective-permute-start(bf16[512,1408]{1,0:T(8,128)(2,1)S(1)} %get-tuple-element.79), channel_id=1, source_target_pairs={{0,64},{64,0},{1,65},{65,1},{2,66},{66,2},{3,67},{67,3},{4,68},{68... | collective-permute-start | bytes 4325384 | tf_op jit(solution)/shard_map/ppermute | solution.py:20
  50.6 0.1 shard_map.80
  50.6 1.6 %collective-permute-start.22 = (bf16[56,2560]{1,0:T(8,128)(2,1)S(1)}, bf16[56,2560]{1,0:T(8,128)(2,1)S(1)}, u32[]{:S(2)}, u32[]{:S(2)}) collective-permute-start(bf16[56,2560]{1,0:T(8,128)(2,1)S(1)} %get-tuple-element.84.value), channel_id=1, source_target_pairs={{0,2},{2,4},{4,6},{6,8},{8,10},{10,12},{12,14},{14,0},{1,3},{3,5},... | collective-permute-start | bytes 860168 | tf_op jit(solution)/shard_map/ppermute | solution.py:20
  52.3 1.1 %collective-permute-start.23 = (bf16[56,2560]{1,0:T(8,128)(2,1)S(1)}, bf16[56,2560]{1,0:T(8,128)(2,1)S(1)}, u32[]{:S(2)}, u32[]{:S(2)}) collective-permute-start(bf16[56,2560]{1,0:T(8,128)(2,1)S(1)} %get-tuple-element.90), channel_id=1, source_target_pairs={{0,14},{2,0},{4,2},{6,4},{8,6},{10,8},{12,10},{14,12},{1,15},{3,1}... | collective-permute-start | bytes 860168 | tf_op jit(solution)/shard_map/ppermute | solution.py:20
  53.4 1.6 %collective-permute-start.17 = (bf16[56,1280]{1,0:T(8,128)(2,1)S(1)}, bf16[56,1280]{1,0:T(8,128)(2,1)S(1)}, u32[]{:S(2)}, u32[]{:S(2)}) collective-permute-start(bf16[56,1280]{1,0:T(8,128)(2,1)S(1)} %shard_map.82), channel_id=1, source_target_pairs={{0,64},{64,0},{1,65},{65,1},{2,66},{66,2},{3,67},{67,3},{4,68},{68... | collective-permute-start | bytes 430088 | tf_op jit(solution)/shard_map/ppermute | solution.py:20
  55.1 1.0 %collective-permute-done.17.block_other = bf16[56,1280]{1,0:T(8,128)(2,1)S(1)} collective-permute-done((bf16[56,1280]{1,0:T(8,128)(2,1)S(1)}, bf16[56,1280]{1,0:T(8,128)(2,1)S(1)}, u32[]{:S(2)}, u32[]{:S(2)}) %collective-permute-start.17) | collective-permute-done | bytes 143392 | tf_op jit(solution)/shard_map/ppermute | solution.py:20
  56.1 0.9 shard_map.83
  56.9 0.5 collective-permute-start.19
  57.4 1.5 %collective-permute-start.21 = (bf16[128,1280]{1,0:T(8,128)(2,1)S(1)}, bf16[128,1280]{1,0:T(8,128)(2,1)S(1)}, u32[]{:S(2)}, u32[]{:S(2)}) collective-permute-start(bf16[128,1280]{1,0:T(8,128)(2,1)S(1)} %get-tuple-element.89), channel_id=1, source_target_pairs={{0,16},{16,32},{32,48},{48,0},{1,17},{17,33},{33,49},{49,1},{2,18}... | collective-permute-start | bytes 983048 | tf_op jit(solution)/shard_map/ppermute | solution.py:20
  58.9 1.5 %collective-permute-done.22.refs_0_ = bf16[56,2560]{1,0:T(8,128)(2,1)S(1)} collective-permute-done((bf16[56,2560]{1,0:T(8,128)(2,1)S(1)}, bf16[56,2560]{1,0:T(8,128)(2,1)S(1)}, u32[]{:S(2)}, u32[]{:S(2)}) %collective-permute-start.22) | collective-permute-done | bytes 286752 | tf_op jit(solution)/shard_map/ppermute | solution.py:20
  60.4 0.1 collective-permute-done.23.refs_1_
  60.5 0.1 shard_map.85
  60.6 1.5 %collective-permute-start.24 = (bf16[56,2560]{1,0:T(8,128)(2,1)S(1)}, bf16[56,2560]{1,0:T(8,128)(2,1)S(1)}, u32[]{:S(2)}, u32[]{:S(2)}) collective-permute-start(bf16[56,2560]{1,0:T(8,128)(2,1)S(1)} %get-tuple-element.93), channel_id=1, source_target_pairs={{0,2},{2,4},{4,6},{6,8},{8,10},{10,12},{12,14},{14,0},{1,3},{3,5},... | collective-permute-start | bytes 860168 | tf_op jit(solution)/shard_map/ppermute | solution.py:20
  62.1 1.3 %collective-permute-start.25 = (bf16[56,2560]{1,0:T(8,128)(2,1)S(1)}, bf16[56,2560]{1,0:T(8,128)(2,1)S(1)}, u32[]{:S(2)}, u32[]{:S(2)}) collective-permute-start(bf16[56,2560]{1,0:T(8,128)(2,1)S(1)} %get-tuple-element.94), channel_id=1, source_target_pairs={{0,14},{2,0},{4,2},{6,4},{8,6},{10,8},{12,10},{14,12},{1,15},{3,1}... | collective-permute-start | bytes 860168 | tf_op jit(solution)/shard_map/ppermute | solution.py:20
  63.4 0.4 collective-permute-start.20
  63.8 2.6 %shard_map.86 = (bf16[512,128]{1,0:T(8,128)(2,1)S(1)}, bf16[512,128]{1,0:T(8,128)(2,1)S(1)}, bf16[512,128]{1,0:T(8,128)(2,1)S(1)}, bf16[512,128]{1,0:T(8,128)(2,1)S(1)}) custom-call(bf16[512,2560]{1,0:T(8,128)(2,1)S(1)} %get-tuple-element.96.cot, bf16[8,64,2560]{2,1,0:T(8,128)(2,1)S(1)} %get-tuple-element.97.weight, ...), custom_call_target="tpu_custom_call" | custom-call | tf_op jit(solution)/shard_map/pallas_call | solution.py:30
  66.5 2.7 %collective-permute-done.24.refs_0_ = bf16[56,2560]{1,0:T(8,128)(2,1)S(1)} collective-permute-done((bf16[56,2560]{1,0:T(8,128)(2,1)S(1)}, bf16[56,2560]{1,0:T(8,128)(2,1)S(1)}, u32[]{:S(2)}, u32[]{:S(2)}) %collective-permute-start.24) | collective-permute-done | bytes 286752 | tf_op jit(solution)/shard_map/ppermute | solution.py:20
  69.2 0.1 shard_map.87
  69.3 0.5 collective-permute-start.27
  69.8 2.3 %collective-permute-start.28 = (bf16[56,2560]{1,0:T(8,128)(2,1)S(1)}, bf16[56,2560]{1,0:T(8,128)(2,1)S(1)}, u32[]{:S(2)}, u32[]{:S(2)}) collective-permute-start(bf16[56,2560]{1,0:T(8,128)(2,1)S(1)} %get-tuple-element.104), channel_id=1, source_target_pairs={{0,14},{2,0},{4,2},{6,4},{8,6},{10,8},{12,10},{14,12},{1,15},{3,1}... | collective-permute-start | bytes 860168 | tf_op jit(solution)/shard_map/ppermute | solution.py:20
  72.1 0.2 shard_map.88
  72.3 0.0 copy-start.1
  72.3 0.0 copy-start.2
  72.3 0.7 collective-permute-start.26
  73.0 0.9 %collective-permute-start.31 = (bf16[512,128]{1,0:T(8,128)(2,1)S(1)}, bf16[512,128]{1,0:T(8,128)(2,1)S(1)}, u32[]{:S(2)}, u32[]{:S(2)}) collective-permute-start(bf16[512,128]{1,0:T(8,128)(2,1)S(1)} %get-tuple-element.116), channel_id=1, source_target_pairs={{0,48},{16,0},{32,16},{48,32},{1,49},{17,1},{33,17},{49,33},{2,50}... | collective-permute-start | bytes 393224 | tf_op jit(solution)/shard_map/ppermute | solution.py:20
  73.9 0.8 collective-permute-start.32
  74.7 2.1 %collective-permute-done.27.fwd = bf16[56,2560]{1,0:T(8,128)(2,1)S(1)} collective-permute-done((bf16[56,2560]{1,0:T(8,128)(2,1)S(1)}, bf16[56,2560]{1,0:T(8,128)(2,1)S(1)}, u32[]{:S(2)}, u32[]{:S(2)}) %collective-permute-start.27) | collective-permute-done | bytes 286752 | tf_op jit(solution)/shard_map/ppermute | solution.py:20
  76.7 0.3 shard_map.89
  77.0 0.1 collective-permute-start.30
  77.1 0.1 collective-permute-start.33
  77.2 1.9 %collective-permute-done.26 = bf16[128,1280]{1,0:T(8,128)(2,1)S(1)} collective-permute-done((bf16[128,1280]{1,0:T(8,128)(2,1)S(1)}, bf16[128,1280]{1,0:T(8,128)(2,1)S(1)}, u32[]{:S(2)}, u32[]{:S(2)}) %collective-permute-start.26) | collective-permute-done | bytes 327712 | tf_op jit(solution)/shard_map/ppermute | solution.py:20
  79.1 0.1 add_convert_fusion.mine
  79.2 5.5 %collective-permute-start.29 = (bf16[128,1280]{1,0:T(8,128)(2,1)S(1)}, bf16[128,1280]{1,0:T(8,128)(2,1)S(1)}, u32[]{:S(2)}, u32[]{:S(2)}) collective-permute-start(bf16[128,1280]{1,0:T(8,128)(2,1)S(1)} %add_convert_fusion.mine), channel_id=1, source_target_pairs={{0,64},{64,0},{1,65},{65,1},{2,66},{66,2},{3,67},{67,3},{4,68},{68... | collective-permute-start | bytes 983048 | tf_op jit(solution)/shard_map/ppermute | solution.py:20
  84.7 1.3 %shard_map.91 = (bf16[1728,128]{1,0:T(8,128)(2,1)}, bf16[1728,128]{1,0:T(8,128)(2,1)}) custom-call(bf16[1728,128]{1,0:T(8,128)(2,1)S(1)} %bitcast.5, bf16[1728,128]{1,0:T(8,128)(2,1)S(1)} %bitcast.7, bf16[512,128]{1,0:T(8,128)(2,1)S(1)} %get-tuple-element.115.b0, bf16[512,128]{1,0:T(8,128)(2,1)S(1)} %collective-permute-done.31.b1, ...), custom_call_target="tpu_custom_call" | custom-call | flops 4000000000 | tf_op jit(solution)/shard_map/pallas_call | solution.py:30
  86.0 1.0 %shard_map.90 = (bf16[128,2560]{1,0:T(8,128)(2,1)}, f32[27,2560]{1,0:T(8,128)}) custom-call(bf16[128,1280]{1,0:T(8,128)(2,1)S(1)} %add_convert_fusion.mine, bf16[128,1280]{1,0:T(8,128)(2,1)S(1)} %collective-permute-done.29.other, f32[27,2560]{1,0:T(8,128)S(1)} %get-tuple-element.112.keep, bf16[27,2560]{1,0:T(8,128)(2,1)S(1)} %collective-permute-done.30.taken), custom_call_target="tpu_custom_call" | custom-call | bytes 2001920 | tf_op jit(solution)/shard_map/pallas_call | solution.py:30
  (32 shorter events, 0.1 us)
Async XLA Ops:
  0.6 11.9 %collective-permute-start = (bf16[27,2560]{1,0:T(8,128)(2,1)}, bf16[27,2560]{1,0:T(8,128)(2,1)S(1)}, u32[]{:S(2)}, u32[]{:S(2)}) collective-permute-start(bf16[27,2560]{1,0:T(8,128)(2,1)} %mine.1), channel_id=1, source_target_pairs={{0,1},{1,0},{2,3},{3,2},{4,5},{5,4},{6,7},{7,6},{8,9},{9,8},{10,11... | collective-permute-start | bytes 414728 | tf_op jit(solution)/shard_map/ppermute | solution.py:20
  7.0 12.5 %collective-permute-start.8 = (bf16[128,1152]{1,0:T(8,128)(2,1)}, bf16[128,1152]{1,0:T(8,128)(2,1)S(1)}, u32[]{:S(2)}, u32[]{:S(2)}) collective-permute-start(bf16[128,1152]{1,0:T(8,128)(2,1)} %get-tuple-element.64), channel_id=1, source_target_pairs={{0,32},{16,48},{32,0},{48,16},{1,33},{17,49},{33,1},{49,17},{2,34}... | collective-permute-start | bytes 884744 | tf_op jit(solution)/shard_map/ppermute | solution.py:20
  9.9 17.7 %collective-permute-start.7 = (bf16[128,1792]{1,0:T(8,128)(2,1)}, bf16[128,1792]{1,0:T(8,128)(2,1)S(1)}, u32[]{:S(2)}, u32[]{:S(2)}) collective-permute-start(bf16[128,1792]{1,0:T(8,128)(2,1)} %get-tuple-element.63), channel_id=1, source_target_pairs={{0,16},{16,32},{32,48},{48,0},{1,17},{17,33},{33,49},{49,1},{2,18}... | collective-permute-start | bytes 1376264 | tf_op jit(solution)/shard_map/ppermute | solution.py:20
  10.2 24.4 %copy-start = (bf16[128,2560]{1,0:T(8,128)(2,1)S(1)}, bf16[128,2560]{1,0:T(8,128)(2,1)}, u32[]{:S(2)}) copy-start(bf16[128,2560]{1,0:T(8,128)(2,1)} %cot_own.1) | copy-start | bytes 1966084
  10.2 24.4 %copy-start.3 = (bf16[512,128]{1,0:T(8,128)(2,1)S(1)}, bf16[512,128]{1,0:T(8,128)(2,1)}, u32[]{:S(2)}) copy-start(bf16[512,128]{1,0:T(8,128)(2,1)} %get-tuple-element.73.hid_own) | copy-start | bytes 393220
  10.2 17.4 %collective-permute-start.9 = (bf16[128,1792]{1,0:T(8,128)(2,1)}, bf16[128,1792]{1,0:T(8,128)(2,1)S(1)}, u32[]{:S(2)}, u32[]{:S(2)}) collective-permute-start(bf16[128,1792]{1,0:T(8,128)(2,1)} %get-tuple-element.65), channel_id=1, source_target_pairs={{0,48},{16,0},{32,16},{48,32},{1,49},{17,1},{33,17},{49,33},{2,50}... | collective-permute-start | bytes 1376264 | tf_op jit(solution)/shard_map/ppermute | solution.py:20
  12.5 0.9 %copy-start.4 = (bf16[27,2560]{1,0:T(8,128)(2,1)S(1)}, bf16[27,2560]{1,0:T(8,128)(2,1)}, u32[]{:S(2)}) copy-start(bf16[27,2560]{1,0:T(8,128)(2,1)} %mine.1) | copy-start | bytes 414724
  13.8 11.0 %collective-permute-start.1 = (bf16[56,2560]{1,0:T(8,128)(2,1)S(1)}, bf16[56,2560]{1,0:T(8,128)(2,1)S(1)}, u32[]{:S(2)}, u32[]{:S(2)}) collective-permute-start(bf16[56,2560]{1,0:T(8,128)(2,1)S(1)} %shard_map.76.w0), channel_id=1, source_target_pairs={{0,2},{2,4},{4,6},{6,8},{8,10},{10,12},{12,14},{14,0},{1,3},{3,5},... | collective-permute-start | bytes 860168 | tf_op jit(solution)/shard_map/ppermute | solution.py:20
  15.5 9.3 %collective-permute-start.2 = (bf16[56,2560]{1,0:T(8,128)(2,1)S(1)}, bf16[56,2560]{1,0:T(8,128)(2,1)S(1)}, u32[]{:S(2)}, u32[]{:S(2)}) collective-permute-start(bf16[56,2560]{1,0:T(8,128)(2,1)S(1)} %shard_map.76.w0), channel_id=1, source_target_pairs={{0,14},{2,0},{4,2},{6,4},{8,6},{10,8},{12,10},{14,12},{1,15},{3,1}... | collective-permute-start | bytes 860168 | tf_op jit(solution)/shard_map/ppermute | solution.py:20
  19.5 8.1 %collective-permute-start.10 = (bf16[128,1152]{1,0:T(8,128)(2,1)S(1)}, bf16[128,1152]{1,0:T(8,128)(2,1)S(1)}, u32[]{:S(2)}, u32[]{:S(2)}) collective-permute-start(bf16[128,1152]{1,0:T(8,128)(2,1)S(1)} %collective-permute-done.8.g2), channel_id=1, source_target_pairs={{0,128},{128,0},{1,129},{129,1},{2,130},{130,2},{3,131},{131,3},{4... | collective-permute-start | bytes 884744 | tf_op jit(solution)/shard_map/ppermute | solution.py:20
  24.8 7.1 %collective-permute-start.3 = (bf16[56,2560]{1,0:T(8,128)(2,1)S(1)}, bf16[56,2560]{1,0:T(8,128)(2,1)S(1)}, u32[]{:S(2)}, u32[]{:S(2)}) collective-permute-start(bf16[56,2560]{1,0:T(8,128)(2,1)S(1)} %collective-permute-done.1.f1), channel_id=1, source_target_pairs={{0,2},{2,4},{4,6},{6,8},{8,10},{10,12},{12,14},{14,0},{1,3},{3,5},... | collective-permute-start | bytes 860168 | tf_op jit(solution)/shard_map/ppermute | solution.py:20
  24.8 7.1 %collective-permute-start.4 = (bf16[56,2560]{1,0:T(8,128)(2,1)S(1)}, bf16[56,2560]{1,0:T(8,128)(2,1)S(1)}, u32[]{:S(2)}, u32[]{:S(2)}) collective-permute-start(bf16[56,2560]{1,0:T(8,128)(2,1)S(1)} %collective-permute-done.2.b1), channel_id=1, source_target_pairs={{0,14},{2,0},{4,2},{6,4},{8,6},{10,8},{12,10},{14,12},{1,15},{3,1}... | collective-permute-start | bytes 860168 | tf_op jit(solution)/shard_map/ppermute | solution.py:20
  27.7 6.9 %collective-permute-start.12 = (bf16[128,1280]{1,0:T(8,128)(2,1)S(1)}, bf16[128,1280]{1,0:T(8,128)(2,1)S(1)}, u32[]{:S(2)}, u32[]{:S(2)}) collective-permute-start(bf16[128,1280]{1,0:T(8,128)(2,1)S(1)} %get-tuple-element.74.n2), channel_id=1, source_target_pairs={{0,64},{64,0},{1,65},{65,1},{2,66},{66,2},{3,67},{67,3},{4,68},{68... | collective-permute-start | bytes 983048 | tf_op jit(solution)/shard_map/ppermute | solution.py:20
  30.6 3.9 %collective-permute-start.11 = (bf16[128,1280]{1,0:T(8,128)(2,1)S(1)}, bf16[128,1280]{1,0:T(8,128)(2,1)S(1)}, u32[]{:S(2)}, u32[]{:S(2)}) collective-permute-start(bf16[128,1280]{1,0:T(8,128)(2,1)S(1)} %get-tuple-element.75), channel_id=1, source_target_pairs={{0,64},{64,0},{1,65},{65,1},{2,66},{66,2},{3,67},{67,3},{4,68},{68... | collective-permute-start | bytes 983048 | tf_op jit(solution)/shard_map/ppermute | solution.py:20
  30.7 3.8 %collective-permute-start.13 = (bf16[128,1280]{1,0:T(8,128)(2,1)S(1)}, bf16[128,1280]{1,0:T(8,128)(2,1)S(1)}, u32[]{:S(2)}, u32[]{:S(2)}) collective-permute-start(bf16[128,1280]{1,0:T(8,128)(2,1)S(1)} %get-tuple-element.76), channel_id=1, source_target_pairs={{0,64},{64,0},{1,65},{65,1},{2,66},{66,2},{3,67},{67,3},{4,68},{68... | collective-permute-start | bytes 983048 | tf_op jit(solution)/shard_map/ppermute | solution.py:20
  31.9 7.8 %collective-permute-start.5 = (bf16[56,2560]{1,0:T(8,128)(2,1)S(1)}, bf16[56,2560]{1,0:T(8,128)(2,1)S(1)}, u32[]{:S(2)}, u32[]{:S(2)}) collective-permute-start(bf16[56,2560]{1,0:T(8,128)(2,1)S(1)} %collective-permute-done.3.f2), channel_id=1, source_target_pairs={{0,2},{2,4},{4,6},{6,8},{8,10},{10,12},{12,14},{14,0},{1,3},{3,5},... | collective-permute-start | bytes 860168 | tf_op jit(solution)/shard_map/ppermute | solution.py:20
  33.4 6.3 %collective-permute-start.6 = (bf16[56,2560]{1,0:T(8,128)(2,1)S(1)}, bf16[56,2560]{1,0:T(8,128)(2,1)S(1)}, u32[]{:S(2)}, u32[]{:S(2)}) collective-permute-start(bf16[56,2560]{1,0:T(8,128)(2,1)S(1)} %collective-permute-done.4.b2), channel_id=1, source_target_pairs={{0,14},{2,0},{4,2},{6,4},{8,6},{10,8},{12,10},{14,12},{1,15},{3,1}... | collective-permute-start | bytes 860168 | tf_op jit(solution)/shard_map/ppermute | solution.py:20
  38.1 12.5 %collective-permute-start.16 = (bf16[56,2560]{1,0:T(8,128)(2,1)S(1)}, bf16[56,2560]{1,0:T(8,128)(2,1)S(1)}, u32[]{:S(2)}, u32[]{:S(2)}) collective-permute-start(bf16[56,2560]{1,0:T(8,128)(2,1)S(1)} %get-tuple-element.83), channel_id=1, source_target_pairs={{0,14},{2,0},{4,2},{6,4},{8,6},{10,8},{12,10},{14,12},{1,15},{3,1}... | collective-permute-start | bytes 860168 | tf_op jit(solution)/shard_map/ppermute | solution.py:20
  39.7 13.7 %collective-permute-start.15 = (bf16[56,2560]{1,0:T(8,128)(2,1)S(1)}, bf16[56,2560]{1,0:T(8,128)(2,1)S(1)}, u32[]{:S(2)}, u32[]{:S(2)}) collective-permute-start(bf16[56,2560]{1,0:T(8,128)(2,1)S(1)} %collective-permute-done.5.f3), channel_id=1, source_target_pairs={{0,2},{2,4},{4,6},{6,8},{8,10},{10,12},{12,14},{14,0},{1,3},{3,5},... | collective-permute-start | bytes 860168 | tf_op jit(solution)/shard_map/ppermute | solution.py:20
  43.1 12.9 %collective-permute-start.14 = (bf16[512,1408]{1,0:T(8,128)(2,1)S(1)}, bf16[512,1408]{1,0:T(8,128)(2,1)S(1)}, u32[]{:S(2)}, u32[]{:S(2)}) collective-permute-start(bf16[512,1408]{1,0:T(8,128)(2,1)S(1)} %get-tuple-element.79), channel_id=1, source_target_pairs={{0,64},{64,0},{1,65},{65,1},{2,66},{66,2},{3,67},{67,3},{4,68},{68... | collective-permute-start | bytes 4325384 | tf_op jit(solution)/shard_map/ppermute | solution.py:20
  50.6 9.7 %collective-permute-start.22 = (bf16[56,2560]{1,0:T(8,128)(2,1)S(1)}, bf16[56,2560]{1,0:T(8,128)(2,1)S(1)}, u32[]{:S(2)}, u32[]{:S(2)}) collective-permute-start(bf16[56,2560]{1,0:T(8,128)(2,1)S(1)} %get-tuple-element.84.value), channel_id=1, source_target_pairs={{0,2},{2,4},{4,6},{6,8},{8,10},{10,12},{12,14},{14,0},{1,3},{3,5},... | collective-permute-start | bytes 860168 | tf_op jit(solution)/shard_map/ppermute | solution.py:20
  52.3 8.2 %collective-permute-start.23 = (bf16[56,2560]{1,0:T(8,128)(2,1)S(1)}, bf16[56,2560]{1,0:T(8,128)(2,1)S(1)}, u32[]{:S(2)}, u32[]{:S(2)}) collective-permute-start(bf16[56,2560]{1,0:T(8,128)(2,1)S(1)} %get-tuple-element.90), channel_id=1, source_target_pairs={{0,14},{2,0},{4,2},{6,4},{8,6},{10,8},{12,10},{14,12},{1,15},{3,1}... | collective-permute-start | bytes 860168 | tf_op jit(solution)/shard_map/ppermute | solution.py:20
  53.4 2.6 %collective-permute-start.17 = (bf16[56,1280]{1,0:T(8,128)(2,1)S(1)}, bf16[56,1280]{1,0:T(8,128)(2,1)S(1)}, u32[]{:S(2)}, u32[]{:S(2)}) collective-permute-start(bf16[56,1280]{1,0:T(8,128)(2,1)S(1)} %shard_map.82), channel_id=1, source_target_pairs={{0,64},{64,0},{1,65},{65,1},{2,66},{66,2},{3,67},{67,3},{4,68},{68... | collective-permute-start | bytes 430088 | tf_op jit(solution)/shard_map/ppermute | solution.py:20
  56.9 6.4 %collective-permute-start.19 = (bf16[128,640]{1,0:T(8,128)(2,1)S(1)}, bf16[128,640]{1,0:T(8,128)(2,1)S(1)}, u32[]{:S(2)}, u32[]{:S(2)}) collective-permute-start(bf16[128,640]{1,0:T(8,128)(2,1)S(1)} %get-tuple-element.88), channel_id=1, source_target_pairs={{0,128},{128,0},{1,129},{129,1},{2,130},{130,2},{3,131},{131,3},{4... | collective-permute-start | bytes 491528 | tf_op jit(solution)/shard_map/ppermute | solution.py:20
  57.4 14.6 %collective-permute-start.18 = (bf16[128,1280]{1,0:T(8,128)(2,1)S(1)}, bf16[128,1280]{1,0:T(8,128)(2,1)S(1)}, u32[]{:S(2)}, u32[]{:S(2)}) collective-permute-start(bf16[128,1280]{1,0:T(8,128)(2,1)S(1)} %get-tuple-element.86), channel_id=1, source_target_pairs={{0,48},{16,0},{32,16},{48,32},{1,49},{17,1},{33,17},{49,33},{2,50}... | collective-permute-start | bytes 983048 | tf_op jit(solution)/shard_map/ppermute | solution.py:20
  57.4 14.6 %collective-permute-start.21 = (bf16[128,1280]{1,0:T(8,128)(2,1)S(1)}, bf16[128,1280]{1,0:T(8,128)(2,1)S(1)}, u32[]{:S(2)}, u32[]{:S(2)}) collective-permute-start(bf16[128,1280]{1,0:T(8,128)(2,1)S(1)} %get-tuple-element.89), channel_id=1, source_target_pairs={{0,16},{16,32},{32,48},{48,0},{1,17},{17,33},{33,49},{49,1},{2,18}... | collective-permute-start | bytes 983048 | tf_op jit(solution)/shard_map/ppermute | solution.py:20
  60.6 8.5 %collective-permute-start.24 = (bf16[56,2560]{1,0:T(8,128)(2,1)S(1)}, bf16[56,2560]{1,0:T(8,128)(2,1)S(1)}, u32[]{:S(2)}, u32[]{:S(2)}) collective-permute-start(bf16[56,2560]{1,0:T(8,128)(2,1)S(1)} %get-tuple-element.93), channel_id=1, source_target_pairs={{0,2},{2,4},{4,6},{6,8},{8,10},{10,12},{12,14},{14,0},{1,3},{3,5},... | collective-permute-start | bytes 860168 | tf_op jit(solution)/shard_map/ppermute | solution.py:20
  62.1 7.1 %collective-permute-start.25 = (bf16[56,2560]{1,0:T(8,128)(2,1)S(1)}, bf16[56,2560]{1,0:T(8,128)(2,1)S(1)}, u32[]{:S(2)}, u32[]{:S(2)}) collective-permute-start(bf16[56,2560]{1,0:T(8,128)(2,1)S(1)} %get-tuple-element.94), channel_id=1, source_target_pairs={{0,14},{2,0},{4,2},{6,4},{8,6},{10,8},{12,10},{14,12},{1,15},{3,1}... | collective-permute-start | bytes 860168 | tf_op jit(solution)/shard_map/ppermute | solution.py:20
  63.4 8.6 %collective-permute-start.20 = (bf16[128,640]{1,0:T(8,128)(2,1)S(1)}, bf16[128,640]{1,0:T(8,128)(2,1)S(1)}, u32[]{:S(2)}, u32[]{:S(2)}) collective-permute-start(bf16[128,640]{1,0:T(8,128)(2,1)S(1)} %shard_map.84), channel_id=1, source_target_pairs={{0,32},{16,48},{32,0},{48,16},{1,33},{17,49},{33,1},{49,17},{2,34}... | collective-permute-start | bytes 491528 | tf_op jit(solution)/shard_map/ppermute | solution.py:20
  69.3 7.4 %collective-permute-start.27 = (bf16[56,2560]{1,0:T(8,128)(2,1)S(1)}, bf16[56,2560]{1,0:T(8,128)(2,1)S(1)}, u32[]{:S(2)}, u32[]{:S(2)}) collective-permute-start(bf16[56,2560]{1,0:T(8,128)(2,1)S(1)} %get-tuple-element.103), channel_id=1, source_target_pairs={{0,2},{2,4},{4,6},{6,8},{8,10},{10,12},{12,14},{14,0},{1,3},{3,5},... | collective-permute-start | bytes 860168 | tf_op jit(solution)/shard_map/ppermute | solution.py:20
  69.8 7.0 %collective-permute-start.28 = (bf16[56,2560]{1,0:T(8,128)(2,1)S(1)}, bf16[56,2560]{1,0:T(8,128)(2,1)S(1)}, u32[]{:S(2)}, u32[]{:S(2)}) collective-permute-start(bf16[56,2560]{1,0:T(8,128)(2,1)S(1)} %get-tuple-element.104), channel_id=1, source_target_pairs={{0,14},{2,0},{4,2},{6,4},{8,6},{10,8},{12,10},{14,12},{1,15},{3,1}... | collective-permute-start | bytes 860168 | tf_op jit(solution)/shard_map/ppermute | solution.py:20
  72.3 12.4 %copy-start.1 = (bf16[128,1728]{0,1:T(8,128)(2,1)S(1)}, bf16[128,1728]{0,1:T(8,128)(2,1)}, u32[]{:S(2)}) copy-start(bf16[128,1728]{0,1:T(8,128)(2,1)} %param.4) | copy-start | bytes 1327108
  72.3 12.4 %copy-start.2 = (bf16[128,1728]{0,1:T(8,128)(2,1)S(1)}, bf16[128,1728]{0,1:T(8,128)(2,1)}, u32[]{:S(2)}) copy-start(bf16[128,1728]{0,1:T(8,128)(2,1)} %param.5) | copy-start | bytes 1327108
  72.3 6.8 %collective-permute-start.26 = (bf16[128,1280]{1,0:T(8,128)(2,1)S(1)}, bf16[128,1280]{1,0:T(8,128)(2,1)S(1)}, u32[]{:S(2)}, u32[]{:S(2)}) collective-permute-start(bf16[128,1280]{1,0:T(8,128)(2,1)S(1)} %shard_map.88), channel_id=1, source_target_pairs={{0,128},{128,0},{1,129},{129,1},{2,130},{130,2},{3,131},{131,3},{4... | collective-permute-start | bytes 983048 | tf_op jit(solution)/shard_map/ppermute | solution.py:20
  73.0 11.7 %collective-permute-start.31 = (bf16[512,128]{1,0:T(8,128)(2,1)S(1)}, bf16[512,128]{1,0:T(8,128)(2,1)S(1)}, u32[]{:S(2)}, u32[]{:S(2)}) collective-permute-start(bf16[512,128]{1,0:T(8,128)(2,1)S(1)} %get-tuple-element.116), channel_id=1, source_target_pairs={{0,48},{16,0},{32,16},{48,32},{1,49},{17,1},{33,17},{49,33},{2,50}... | collective-permute-start | bytes 393224 | tf_op jit(solution)/shard_map/ppermute | solution.py:20
  73.9 10.8 %collective-permute-start.32 = (bf16[512,128]{1,0:T(8,128)(2,1)S(1)}, bf16[512,128]{1,0:T(8,128)(2,1)S(1)}, u32[]{:S(2)}, u32[]{:S(2)}) collective-permute-start(bf16[512,128]{1,0:T(8,128)(2,1)S(1)} %get-tuple-element.117), channel_id=1, source_target_pairs={{0,32},{16,48},{32,0},{48,16},{1,33},{17,49},{33,1},{49,17},{2,34}... | collective-permute-start | bytes 393224 | tf_op jit(solution)/shard_map/ppermute | solution.py:20
  77.0 9.0 %collective-permute-start.30 = (bf16[27,2560]{1,0:T(8,128)(2,1)S(1)}, bf16[27,2560]{1,0:T(8,128)(2,1)S(1)}, u32[]{:S(2)}, u32[]{:S(2)}) collective-permute-start(bf16[27,2560]{1,0:T(8,128)(2,1)S(1)} %get-tuple-element.110), channel_id=1, source_target_pairs={{0,1},{1,0},{2,3},{3,2},{4,5},{5,4},{6,7},{7,6},{8,9},{9,8},{10,11... | collective-permute-start | bytes 414728 | tf_op jit(solution)/shard_map/ppermute | solution.py:20
  77.1 7.5 %collective-permute-start.33 = (bf16[512,128]{1,0:T(8,128)(2,1)S(1)}, bf16[512,128]{1,0:T(8,128)(2,1)S(1)}, u32[]{:S(2)}, u32[]{:S(2)}) collective-permute-start(bf16[512,128]{1,0:T(8,128)(2,1)S(1)} %get-tuple-element.119), channel_id=1, source_target_pairs={{0,16},{16,32},{32,48},{48,0},{1,17},{17,33},{33,49},{49,1},{2,18}... | collective-permute-start | bytes 393224 | tf_op jit(solution)/shard_map/ppermute | solution.py:20
  79.2 6.9 %collective-permute-start.29 = (bf16[128,1280]{1,0:T(8,128)(2,1)S(1)}, bf16[128,1280]{1,0:T(8,128)(2,1)S(1)}, u32[]{:S(2)}, u32[]{:S(2)}) collective-permute-start(bf16[128,1280]{1,0:T(8,128)(2,1)S(1)} %add_convert_fusion.mine), channel_id=1, source_target_pairs={{0,64},{64,0},{1,65},{65,1},{2,66},{66,2},{3,67},{67,3},{4,68},{68... | collective-permute-start | bytes 983048 | tf_op jit(solution)/shard_map/ppermute | solution.py:20

commit v10 on v9

--- a/solution.py
+++ b/solution.py
@@ -273,8 +273,15 @@
         ].astype(BF16)
 
 
-def activation_gradients(gate, up, b0, b1, b2, b3, grad_gate, grad_up, back32):
-    units, rows = gate.shape
+def activation_factors(gate, up, of_gate, of_up):
+    gate32, up32 = gate[...].astype(F32), up[...].astype(F32)
+    sig = jax.nn.sigmoid(gate32)
+    of_gate[...] = up32 * (sig * (1.0 + gate32 * (1.0 - sig)))
+    of_up[...] = gate32 * sig
+
+
+def activation_gradients(of_gate, of_up, b0, b1, b2, b3, grad_gate, grad_up, back32):
+    units, rows = of_gate.shape
     used = units // (NX * NZ)
     for x in range(NX):
 
@@ -287,10 +294,8 @@
                     start = (s * NZ + block) * used
                     back32[start : start + used] = value[:used]
 
-    gate32, up32 = gate[...].astype(F32), up[...].astype(F32)
-    sig = jax.nn.sigmoid(gate32)
-    grad_gate[...] = (back32[...] * up32 * (sig * (1.0 + gate32 * (1.0 - sig)))).astype(BF16)
-    grad_up[...] = (back32[...] * (gate32 * sig)).astype(BF16)
+    grad_gate[...] = (back32[...] * of_gate[...]).astype(BF16)
+    grad_up[...] = (back32[...] * of_up[...]).astype(BF16)
 
 
 def add_pieces(distance, others, pieces, *refs):
@@ -426,7 +431,10 @@
     ring = after(ring, m1, m3)
     to_fwd, to_bwd = added(2, ring)
     ring = (shift(to_fwd, "z", 1), shift(to_bwd, "z", -1))
-    *ring, back1, back2, back3 = lax.optimization_barrier((*ring, back1, back2, back3))
+    of_gate, of_up = call(activation_factors, [like((units, rows), F32)] * 2, gate, up, moved=0)
+    *ring, back1, back2, back3, of_gate, of_up = lax.optimization_barrier(
+        (*ring, back1, back2, back3, of_gate, of_up)
+    )
     got_back1, got_back2 = shift(back1, "x", -1), shift(back2, "x", -2)
     to_fwd, to_bwd = added(1, ring)
     got_out = after(got_out, to_fwd, to_bwd)
@@ -447,7 +455,7 @@
     grad_gate, grad_up = call(
         activation_gradients,
         [like((units, rows))] * 2,
-        gate, up, back_own, got_back1, got_back2, got_back3,
+        of_gate, of_up, back_own, got_back1, got_back2, got_back3,
         scratch=[pltpu.VMEM((units, rows), F32)],
         flops=400 * 10**7,
         moved=0,

time: 87.7 us -> 87.5 us (level)
    pallas_call x17 -> x18, Pallas kernels: 15.6 us -> 15.7 us  [call(): pl.pallas_call(kernel, out_shape=outs, in_specs=[pl.BlockSpec(memory_spac...]
  transfers between devices with their start and end apart: 34 -> 34, of which waited for: 9 -> 10; matrix products, arithmetic and copies ran while one was open for 0% -> 0% of each run, Pallas kernels for 17% -> 17%
where the time goes in v10:
time: 87.5 us; the launch traced here: 86.9 us
  starting transfers between devices  54.6 us (62%)
  Pallas kernels  15.7 us (18%)
  waiting for transfers between devices  14.8 us (17%)
  local copies, waits for them, and re-layouts  0.93 us (1%)
    ppermute x34, starting transfers between devices, shift(): lax.ppermute(value, axis, [(i, (i + steps) % count) for i in range(count)])  54.6 us
    pallas_call x18, Pallas kernels, call(): pl.pallas_call(kernel, out_shape=outs, in_specs=[pl.BlockSpec(memory_spac...  15.7 us
    ppermute x34, waiting for transfers between devices, shift(): lax.ppermute(value, axis, [(i, (i + steps) % count) for i in range(count)])  14.8 us
  transfers between devices with their start and end apart: 34, of which 10 were waited for; matrix products, arithmetic and copies ran while one was open for 0% of the time, Pallas kernels for 17%

profile of v10, /device:TPU:1, one launch (start us, length us, event | category | flops | bytes accessed | tf_op | source)
XLA Modules:
  0.0 86.9 jit_solution(17645109552298595851)
XLA Ops:
  0.6 3.8 %collective-permute-start = (bf16[27,2560]{1,0:T(8,128)(2,1)}, bf16[27,2560]{1,0:T(8,128)(2,1)S(1)}, u32[]{:S(2)}, u32[]{:S(2)}) collective-permute-start(bf16[27,2560]{1,0:T(8,128)(2,1)} %mine.1), channel_id=1, source_target_pairs={{0,1},{1,0},{2,3},{3,2},{4,5},{5,4},{6,7},{7,6},{8,9},{9,8},{10,11... | collective-permute-start | bytes 414728 | tf_op jit(solution)/shard_map/ppermute | solution.py:20
  4.5 2.6 %shard_map.75 = (bf16[128,1792]{1,0:T(8,128)(2,1)}, bf16[128,1152]{1,0:T(8,128)(2,1)}, bf16[128,1792]{1,0:T(8,128)(2,1)}, bf16[512,128]{1,0:T(8,128)(2,1)}) custom-call(bf16[1728,128]{1,0:T(8,128)(2,1)} %bitcast.4, bf16[1728,128]{1,0:T(8,128)(2,1)} %bitcast.6, bf16[128,2560]{1,0:T(8,128)(2,1)} %cot_own.1), custom_call_target="tpu_custom_call" | custom-call | bytes 2883584 | tf_op jit(solution)/shard_map/pallas_call | solution.py:30
  7.0 2.8 %collective-permute-start.8 = (bf16[128,1152]{1,0:T(8,128)(2,1)}, bf16[128,1152]{1,0:T(8,128)(2,1)S(1)}, u32[]{:S(2)}, u32[]{:S(2)}) collective-permute-start(bf16[128,1152]{1,0:T(8,128)(2,1)} %get-tuple-element.68), channel_id=1, source_target_pairs={{0,32},{16,48},{32,0},{48,16},{1,33},{17,49},{33,1},{49,17},{2,34}... | collective-permute-start | bytes 884744 | tf_op jit(solution)/shard_map/ppermute | solution.py:20
  9.9 0.3 collective-permute-start.7
  10.2 2.4 %collective-permute-start.9 = (bf16[128,1792]{1,0:T(8,128)(2,1)}, bf16[128,1792]{1,0:T(8,128)(2,1)S(1)}, u32[]{:S(2)}, u32[]{:S(2)}) collective-permute-start(bf16[128,1792]{1,0:T(8,128)(2,1)} %get-tuple-element.69), channel_id=1, source_target_pairs={{0,48},{16,0},{32,16},{48,32},{1,49},{17,1},{33,17},{49,33},{2,50}... | collective-permute-start | bytes 1376264 | tf_op jit(solution)/shard_map/ppermute | solution.py:20
  12.5 0.0 collective-permute-done.other
  12.5 0.9 %copy-done.4 = bf16[27,2560]{1,0:T(8,128)(2,1)S(1)} copy-done((bf16[27,2560]{1,0:T(8,128)(2,1)S(1)}, bf16[27,2560]{1,0:T(8,128)(2,1)}, u32[]{:S(2)}) %copy-start.4) | copy-done | bytes 138264
  13.5 0.3 shard_map.76.w0
  13.8 1.7 %collective-permute-start.1 = (bf16[56,2560]{1,0:T(8,128)(2,1)S(1)}, bf16[56,2560]{1,0:T(8,128)(2,1)S(1)}, u32[]{:S(2)}, u32[]{:S(2)}) collective-permute-start(bf16[56,2560]{1,0:T(8,128)(2,1)S(1)} %shard_map.76.w0), channel_id=1, source_target_pairs={{0,2},{2,4},{4,6},{6,8},{8,10},{10,12},{12,14},{14,0},{1,3},{3,5},... | collective-permute-start | bytes 860168 | tf_op jit(solution)/shard_map/ppermute | solution.py:20
  15.5 4.0 %collective-permute-start.2 = (bf16[56,2560]{1,0:T(8,128)(2,1)S(1)}, bf16[56,2560]{1,0:T(8,128)(2,1)S(1)}, u32[]{:S(2)}, u32[]{:S(2)}) collective-permute-start(bf16[56,2560]{1,0:T(8,128)(2,1)S(1)} %shard_map.76.w0), channel_id=1, source_target_pairs={{0,14},{2,0},{4,2},{6,4},{8,6},{10,8},{12,10},{14,12},{1,15},{3,1}... | collective-permute-start | bytes 860168 | tf_op jit(solution)/shard_map/ppermute | solution.py:20
  19.5 0.0 collective-permute-done.8.g2
  19.5 0.4 collective-permute-start.10
  19.9 4.9 %collective-permute-done.1.f1 = bf16[56,2560]{1,0:T(8,128)(2,1)S(1)} collective-permute-done((bf16[56,2560]{1,0:T(8,128)(2,1)S(1)}, bf16[56,2560]{1,0:T(8,128)(2,1)S(1)}, u32[]{:S(2)}, u32[]{:S(2)}) %collective-permute-start.1) | collective-permute-done | bytes 286752 | tf_op jit(solution)/shard_map/ppermute | solution.py:20
  24.8 0.0 collective-permute-done.2.b1
  24.8 0.0 collective-permute-start.3
  24.8 2.7 %collective-permute-start.4 = (bf16[56,2560]{1,0:T(8,128)(2,1)S(1)}, bf16[56,2560]{1,0:T(8,128)(2,1)S(1)}, u32[]{:S(2)}, u32[]{:S(2)}) collective-permute-start(bf16[56,2560]{1,0:T(8,128)(2,1)S(1)} %collective-permute-done.2.b1), channel_id=1, source_target_pairs={{0,14},{2,0},{4,2},{6,4},{8,6},{10,8},{12,10},{14,12},{1,15},{3,1}... | collective-permute-start | bytes 860168 | tf_op jit(solution)/shard_map/ppermute | solution.py:20
  27.5 0.1 collective-permute-done.7.g1
  27.6 0.1 shard_map.77
  27.7 3.0 %collective-permute-start.12 = (bf16[128,1280]{1,0:T(8,128)(2,1)S(1)}, bf16[128,1280]{1,0:T(8,128)(2,1)S(1)}, u32[]{:S(2)}, u32[]{:S(2)}) collective-permute-start(bf16[128,1280]{1,0:T(8,128)(2,1)S(1)} %get-tuple-element.78.n2), channel_id=1, source_target_pairs={{0,64},{64,0},{1,65},{65,1},{2,66},{66,2},{3,67},{67,3},{4,68},{68... | collective-permute-start | bytes 983048 | tf_op jit(solution)/shard_map/ppermute | solution.py:20
  30.6 0.1 collective-permute-start.11
  30.7 0.4 collective-permute-start.13
  31.2 0.7 collective-permute-done.3.f2
  31.9 0.0 collective-permute-done.4.b2
  31.9 1.5 %collective-permute-start.5 = (bf16[56,2560]{1,0:T(8,128)(2,1)S(1)}, bf16[56,2560]{1,0:T(8,128)(2,1)S(1)}, u32[]{:S(2)}, u32[]{:S(2)}) collective-permute-start(bf16[56,2560]{1,0:T(8,128)(2,1)S(1)} %collective-permute-done.3.f2), channel_id=1, source_target_pairs={{0,2},{2,4},{4,6},{6,8},{8,10},{10,12},{12,14},{14,0},{1,3},{3,5},... | collective-permute-start | bytes 860168 | tf_op jit(solution)/shard_map/ppermute | solution.py:20
  33.4 1.2 %collective-permute-start.6 = (bf16[56,2560]{1,0:T(8,128)(2,1)S(1)}, bf16[56,2560]{1,0:T(8,128)(2,1)S(1)}, u32[]{:S(2)}, u32[]{:S(2)}) collective-permute-start(bf16[56,2560]{1,0:T(8,128)(2,1)S(1)} %collective-permute-done.4.b2), channel_id=1, source_target_pairs={{0,14},{2,0},{4,2},{6,4},{8,6},{10,8},{12,10},{14,12},{1,15},{3,1}... | collective-permute-start | bytes 860168 | tf_op jit(solution)/shard_map/ppermute | solution.py:20
  34.6 3.5 %shard_map.78 = (f32[8,56,2560]{2,1,0:T(8,128)S(1)}, bf16[56,2560]{1,0:T(8,128)(2,1)S(1)}, bf16[512,2560]{1,0:T(8,128)(2,1)S(1)}, bf16[512,512]{1,0:T(8,128)(2,1)S(1)}) custom-call(bf16[128,2560]{1,0:T(8,128)(2,1)S(1)} %copy-done, bf16[512,128]{1,0:T(8,128)(2,1)S(1)} %copy-done.3, bf16[128,1792]{1,0:T(8,128)(2,1)S(1)} %collective-permute-done.7.g1, ...), custom_call_target="tpu_custom_call" | custom-call | tf_op jit(solution)/shard_map/pallas_call | solution.py:30
  38.1 1.6 %collective-permute-start.16 = (bf16[56,2560]{1,0:T(8,128)(2,1)S(1)}, bf16[56,2560]{1,0:T(8,128)(2,1)S(1)}, u32[]{:S(2)}, u32[]{:S(2)}) collective-permute-start(bf16[56,2560]{1,0:T(8,128)(2,1)S(1)} %get-tuple-element.87), channel_id=1, source_target_pairs={{0,14},{2,0},{4,2},{6,4},{8,6},{10,8},{12,10},{14,12},{1,15},{3,1}... | collective-permute-start | bytes 860168 | tf_op jit(solution)/shard_map/ppermute | solution.py:20
  39.7 1.0 %collective-permute-start.15 = (bf16[56,2560]{1,0:T(8,128)(2,1)S(1)}, bf16[56,2560]{1,0:T(8,128)(2,1)S(1)}, u32[]{:S(2)}, u32[]{:S(2)}) collective-permute-start(bf16[56,2560]{1,0:T(8,128)(2,1)S(1)} %collective-permute-done.5.f3), channel_id=1, source_target_pairs={{0,2},{2,4},{4,6},{6,8},{8,10},{10,12},{12,14},{14,0},{1,3},{3,5},... | collective-permute-start | bytes 860168 | tf_op jit(solution)/shard_map/ppermute | solution.py:20
  40.7 2.5 %shard_map.79 = (bf16[8,64,2560]{2,1,0:T(8,128)(2,1)S(1)}, f32[512,1280]{1,0:T(8,128)S(1)}, bf16[512,64]{1,0:T(8,128)(2,1)S(1)}, bf16[512,1408]{1,0:T(8,128)(2,1)S(1)}, bf16[16,128]{1,0:T(8,128)(2,1)S(1)}) custom-call(bf16[56,2560]{1,0:T(8,128)(2,1)S(1)} %shard_map.76.w0, bf16[56,2560]{1,0:T(8,128)(2,1)S(1)} %collective-permute-done.1.f1, ...), custom_call_target="tpu_custom_call" | custom-call | tf_op jit(solution)/shard_map/pallas_call | solution.py:30
  43.1 7.4 %collective-permute-start.14 = (bf16[512,1408]{1,0:T(8,128)(2,1)S(1)}, bf16[512,1408]{1,0:T(8,128)(2,1)S(1)}, u32[]{:S(2)}, u32[]{:S(2)}) collective-permute-start(bf16[512,1408]{1,0:T(8,128)(2,1)S(1)} %get-tuple-element.83), channel_id=1, source_target_pairs={{0,64},{64,0},{1,65},{65,1},{2,66},{66,2},{3,67},{67,3},{4,68},{68... | collective-permute-start | bytes 4325384 | tf_op jit(solution)/shard_map/ppermute | solution.py:20
  50.6 0.1 shard_map.80
  50.6 1.6 %collective-permute-start.22 = (bf16[56,2560]{1,0:T(8,128)(2,1)S(1)}, bf16[56,2560]{1,0:T(8,128)(2,1)S(1)}, u32[]{:S(2)}, u32[]{:S(2)}) collective-permute-start(bf16[56,2560]{1,0:T(8,128)(2,1)S(1)} %get-tuple-element.88.value), channel_id=1, source_target_pairs={{0,2},{2,4},{4,6},{6,8},{8,10},{10,12},{12,14},{14,0},{1,3},{3,5},... | collective-permute-start | bytes 860168 | tf_op jit(solution)/shard_map/ppermute | solution.py:20
  52.3 1.1 %collective-permute-start.23 = (bf16[56,2560]{1,0:T(8,128)(2,1)S(1)}, bf16[56,2560]{1,0:T(8,128)(2,1)S(1)}, u32[]{:S(2)}, u32[]{:S(2)}) collective-permute-start(bf16[56,2560]{1,0:T(8,128)(2,1)S(1)} %get-tuple-element.94), channel_id=1, source_target_pairs={{0,14},{2,0},{4,2},{6,4},{8,6},{10,8},{12,10},{14,12},{1,15},{3,1}... | collective-permute-start | bytes 860168 | tf_op jit(solution)/shard_map/ppermute | solution.py:20
  53.4 1.6 %collective-permute-start.17 = (bf16[56,1280]{1,0:T(8,128)(2,1)S(1)}, bf16[56,1280]{1,0:T(8,128)(2,1)S(1)}, u32[]{:S(2)}, u32[]{:S(2)}) collective-permute-start(bf16[56,1280]{1,0:T(8,128)(2,1)S(1)} %shard_map.82), channel_id=1, source_target_pairs={{0,64},{64,0},{1,65},{65,1},{2,66},{66,2},{3,67},{67,3},{4,68},{68... | collective-permute-start | bytes 430088 | tf_op jit(solution)/shard_map/ppermute | solution.py:20
  55.1 1.0 %collective-permute-done.17.block_other = bf16[56,1280]{1,0:T(8,128)(2,1)S(1)} collective-permute-done((bf16[56,1280]{1,0:T(8,128)(2,1)S(1)}, bf16[56,1280]{1,0:T(8,128)(2,1)S(1)}, u32[]{:S(2)}, u32[]{:S(2)}) %collective-permute-start.17) | collective-permute-done | bytes 143392 | tf_op jit(solution)/shard_map/ppermute | solution.py:20
  56.1 0.9 shard_map.83
  56.9 0.5 collective-permute-start.19
  57.4 1.5 %collective-permute-start.21 = (bf16[128,1280]{1,0:T(8,128)(2,1)S(1)}, bf16[128,1280]{1,0:T(8,128)(2,1)S(1)}, u32[]{:S(2)}, u32[]{:S(2)}) collective-permute-start(bf16[128,1280]{1,0:T(8,128)(2,1)S(1)} %get-tuple-element.93), channel_id=1, source_target_pairs={{0,16},{16,32},{32,48},{48,0},{1,17},{17,33},{33,49},{49,1},{2,18}... | collective-permute-start | bytes 983048 | tf_op jit(solution)/shard_map/ppermute | solution.py:20
  58.9 1.5 %collective-permute-done.22.refs_0_ = bf16[56,2560]{1,0:T(8,128)(2,1)S(1)} collective-permute-done((bf16[56,2560]{1,0:T(8,128)(2,1)S(1)}, bf16[56,2560]{1,0:T(8,128)(2,1)S(1)}, u32[]{:S(2)}, u32[]{:S(2)}) %collective-permute-start.22) | collective-permute-done | bytes 286752 | tf_op jit(solution)/shard_map/ppermute | solution.py:20
  60.4 0.1 collective-permute-done.23.refs_1_
  60.5 0.1 shard_map.85
  60.7 1.5 %collective-permute-start.24 = (bf16[56,2560]{1,0:T(8,128)(2,1)S(1)}, bf16[56,2560]{1,0:T(8,128)(2,1)S(1)}, u32[]{:S(2)}, u32[]{:S(2)}) collective-permute-start(bf16[56,2560]{1,0:T(8,128)(2,1)S(1)} %get-tuple-element.97), channel_id=1, source_target_pairs={{0,2},{2,4},{4,6},{6,8},{8,10},{10,12},{12,14},{14,0},{1,3},{3,5},... | collective-permute-start | bytes 860168 | tf_op jit(solution)/shard_map/ppermute | solution.py:20
  62.1 1.3 %collective-permute-start.25 = (bf16[56,2560]{1,0:T(8,128)(2,1)S(1)}, bf16[56,2560]{1,0:T(8,128)(2,1)S(1)}, u32[]{:S(2)}, u32[]{:S(2)}) collective-permute-start(bf16[56,2560]{1,0:T(8,128)(2,1)S(1)} %get-tuple-element.98), channel_id=1, source_target_pairs={{0,14},{2,0},{4,2},{6,4},{8,6},{10,8},{12,10},{14,12},{1,15},{3,1}... | collective-permute-start | bytes 860168 | tf_op jit(solution)/shard_map/ppermute | solution.py:20
  63.4 0.4 collective-permute-start.20
  63.9 0.4 shard_map.87
  64.2 2.6 %shard_map.86 = (bf16[512,128]{1,0:T(8,128)(2,1)S(1)}, bf16[512,128]{1,0:T(8,128)(2,1)S(1)}, bf16[512,128]{1,0:T(8,128)(2,1)S(1)}, bf16[512,128]{1,0:T(8,128)(2,1)S(1)}) custom-call(bf16[512,2560]{1,0:T(8,128)(2,1)S(1)} %get-tuple-element.100.cot, bf16[8,64,2560]{2,1,0:T(8,128)(2,1)S(1)} %get-tuple-element.101.weight, ...), custom_call_target="tpu_custom_call" | custom-call | tf_op jit(solution)/shard_map/pallas_call | solution.py:30
  66.9 2.3 %collective-permute-done.24.refs_0_ = bf16[56,2560]{1,0:T(8,128)(2,1)S(1)} collective-permute-done((bf16[56,2560]{1,0:T(8,128)(2,1)S(1)}, bf16[56,2560]{1,0:T(8,128)(2,1)S(1)}, u32[]{:S(2)}, u32[]{:S(2)}) %collective-permute-start.24) | collective-permute-done | bytes 286752 | tf_op jit(solution)/shard_map/ppermute | solution.py:20
  69.2 0.1 shard_map.88
  69.3 0.5 collective-permute-start.27
  69.8 2.3 %collective-permute-start.28 = (bf16[56,2560]{1,0:T(8,128)(2,1)S(1)}, bf16[56,2560]{1,0:T(8,128)(2,1)S(1)}, u32[]{:S(2)}, u32[]{:S(2)}) collective-permute-start(bf16[56,2560]{1,0:T(8,128)(2,1)S(1)} %get-tuple-element.110), channel_id=1, source_target_pairs={{0,14},{2,0},{4,2},{6,4},{8,6},{10,8},{12,10},{14,12},{1,15},{3,1}... | collective-permute-start | bytes 860168 | tf_op jit(solution)/shard_map/ppermute | solution.py:20
  72.1 0.2 shard_map.89
  72.3 0.7 collective-permute-start.26
  73.0 0.9 %collective-permute-start.31 = (bf16[512,128]{1,0:T(8,128)(2,1)S(1)}, bf16[512,128]{1,0:T(8,128)(2,1)S(1)}, u32[]{:S(2)}, u32[]{:S(2)}) collective-permute-start(bf16[512,128]{1,0:T(8,128)(2,1)S(1)} %get-tuple-element.124), channel_id=1, source_target_pairs={{0,48},{16,0},{32,16},{48,32},{1,49},{17,1},{33,17},{49,33},{2,50}... | collective-permute-start | bytes 393224 | tf_op jit(solution)/shard_map/ppermute | solution.py:20
  73.9 0.8 collective-permute-start.32
  74.6 2.1 %collective-permute-done.27.fwd = bf16[56,2560]{1,0:T(8,128)(2,1)S(1)} collective-permute-done((bf16[56,2560]{1,0:T(8,128)(2,1)S(1)}, bf16[56,2560]{1,0:T(8,128)(2,1)S(1)}, u32[]{:S(2)}, u32[]{:S(2)}) %collective-permute-start.27) | collective-permute-done | bytes 286752 | tf_op jit(solution)/shard_map/ppermute | solution.py:20
  76.8 0.3 shard_map.90
  77.0 0.1 collective-permute-start.30
  77.1 0.1 collective-permute-start.33
  77.2 1.8 %collective-permute-done.26 = bf16[128,1280]{1,0:T(8,128)(2,1)S(1)} collective-permute-done((bf16[128,1280]{1,0:T(8,128)(2,1)S(1)}, bf16[128,1280]{1,0:T(8,128)(2,1)S(1)}, u32[]{:S(2)}, u32[]{:S(2)}) %collective-permute-start.26) | collective-permute-done | bytes 327712 | tf_op jit(solution)/shard_map/ppermute | solution.py:20
  79.1 0.1 add_convert_fusion.mine
  79.1 5.5 %collective-permute-start.29 = (bf16[128,1280]{1,0:T(8,128)(2,1)S(1)}, bf16[128,1280]{1,0:T(8,128)(2,1)S(1)}, u32[]{:S(2)}, u32[]{:S(2)}) collective-permute-start(bf16[128,1280]{1,0:T(8,128)(2,1)S(1)} %add_convert_fusion.mine), channel_id=1, source_target_pairs={{0,64},{64,0},{1,65},{65,1},{2,66},{66,2},{3,67},{67,3},{4,68},{68... | collective-permute-start | bytes 983048 | tf_op jit(solution)/shard_map/ppermute | solution.py:20
  84.7 1.1 %shard_map.92 = (bf16[1728,128]{1,0:T(8,128)(2,1)}, bf16[1728,128]{1,0:T(8,128)(2,1)}) custom-call(f32[1728,128]{1,0:T(8,128)S(1)} %get-tuple-element.121.of_gate, f32[1728,128]{1,0:T(8,128)S(1)} %get-tuple-element.122.of_up, bf16[512,128]{1,0:T(8,128)(2,1)S(1)} %get-tuple-element.123.b0, bf16[512,128]{1,0:T(8,128)(2,1)S(1)} %collective-permute-done.31.b1, ...), custom_call_target="tpu_custom_call" | custom-call | flops 4000000000 | tf_op jit(solution)/shard_map/pallas_call | solution.py:30
  85.8 0.1 collective-permute-done.29.other
  85.9 1.0 %shard_map.91 = (bf16[128,2560]{1,0:T(8,128)(2,1)}, f32[27,2560]{1,0:T(8,128)}) custom-call(bf16[128,1280]{1,0:T(8,128)(2,1)S(1)} %add_convert_fusion.mine, bf16[128,1280]{1,0:T(8,128)(2,1)S(1)} %collective-permute-done.29.other, f32[27,2560]{1,0:T(8,128)S(1)} %get-tuple-element.118.keep, bf16[27,2560]{1,0:T(8,128)(2,1)S(1)} %collective-permute-done.30.taken), custom_call_target="tpu_custom_call" | custom-call | bytes 2001920 | tf_op jit(solution)/shard_map/pallas_call | solution.py:30
  (33 shorter events, 0.1 us)
Async XLA Ops:
  0.6 11.9 %collective-permute-start = (bf16[27,2560]{1,0:T(8,128)(2,1)}, bf16[27,2560]{1,0:T(8,128)(2,1)S(1)}, u32[]{:S(2)}, u32[]{:S(2)}) collective-permute-start(bf16[27,2560]{1,0:T(8,128)(2,1)} %mine.1), channel_id=1, source_target_pairs={{0,1},{1,0},{2,3},{3,2},{4,5},{5,4},{6,7},{7,6},{8,9},{9,8},{10,11... | collective-permute-start | bytes 414728 | tf_op jit(solution)/shard_map/ppermute | solution.py:20
  7.0 12.5 %collective-permute-start.8 = (bf16[128,1152]{1,0:T(8,128)(2,1)}, bf16[128,1152]{1,0:T(8,128)(2,1)S(1)}, u32[]{:S(2)}, u32[]{:S(2)}) collective-permute-start(bf16[128,1152]{1,0:T(8,128)(2,1)} %get-tuple-element.68), channel_id=1, source_target_pairs={{0,32},{16,48},{32,0},{48,16},{1,33},{17,49},{33,1},{49,17},{2,34}... | collective-permute-start | bytes 884744 | tf_op jit(solution)/shard_map/ppermute | solution.py:20
  9.9 17.7 %collective-permute-start.7 = (bf16[128,1792]{1,0:T(8,128)(2,1)}, bf16[128,1792]{1,0:T(8,128)(2,1)S(1)}, u32[]{:S(2)}, u32[]{:S(2)}) collective-permute-start(bf16[128,1792]{1,0:T(8,128)(2,1)} %get-tuple-element.67), channel_id=1, source_target_pairs={{0,16},{16,32},{32,48},{48,0},{1,17},{17,33},{33,49},{49,1},{2,18}... | collective-permute-start | bytes 1376264 | tf_op jit(solution)/shard_map/ppermute | solution.py:20
  10.2 24.4 %copy-start = (bf16[128,2560]{1,0:T(8,128)(2,1)S(1)}, bf16[128,2560]{1,0:T(8,128)(2,1)}, u32[]{:S(2)}) copy-start(bf16[128,2560]{1,0:T(8,128)(2,1)} %cot_own.1) | copy-start | bytes 1966084
  10.2 24.4 %copy-start.3 = (bf16[512,128]{1,0:T(8,128)(2,1)S(1)}, bf16[512,128]{1,0:T(8,128)(2,1)}, u32[]{:S(2)}) copy-start(bf16[512,128]{1,0:T(8,128)(2,1)} %get-tuple-element.77.hid_own) | copy-start | bytes 393220
  10.2 17.4 %collective-permute-start.9 = (bf16[128,1792]{1,0:T(8,128)(2,1)}, bf16[128,1792]{1,0:T(8,128)(2,1)S(1)}, u32[]{:S(2)}, u32[]{:S(2)}) collective-permute-start(bf16[128,1792]{1,0:T(8,128)(2,1)} %get-tuple-element.69), channel_id=1, source_target_pairs={{0,48},{16,0},{32,16},{48,32},{1,49},{17,1},{33,17},{49,33},{2,50}... | collective-permute-start | bytes 1376264 | tf_op jit(solution)/shard_map/ppermute | solution.py:20
  12.5 0.9 %copy-start.4 = (bf16[27,2560]{1,0:T(8,128)(2,1)S(1)}, bf16[27,2560]{1,0:T(8,128)(2,1)}, u32[]{:S(2)}) copy-start(bf16[27,2560]{1,0:T(8,128)(2,1)} %mine.1) | copy-start | bytes 414724
  13.8 11.0 %collective-permute-start.1 = (bf16[56,2560]{1,0:T(8,128)(2,1)S(1)}, bf16[56,2560]{1,0:T(8,128)(2,1)S(1)}, u32[]{:S(2)}, u32[]{:S(2)}) collective-permute-start(bf16[56,2560]{1,0:T(8,128)(2,1)S(1)} %shard_map.76.w0), channel_id=1, source_target_pairs={{0,2},{2,4},{4,6},{6,8},{8,10},{10,12},{12,14},{14,0},{1,3},{3,5},... | collective-permute-start | bytes 860168 | tf_op jit(solution)/shard_map/ppermute | solution.py:20
  15.5 9.3 %collective-permute-start.2 = (bf16[56,2560]{1,0:T(8,128)(2,1)S(1)}, bf16[56,2560]{1,0:T(8,128)(2,1)S(1)}, u32[]{:S(2)}, u32[]{:S(2)}) collective-permute-start(bf16[56,2560]{1,0:T(8,128)(2,1)S(1)} %shard_map.76.w0), channel_id=1, source_target_pairs={{0,14},{2,0},{4,2},{6,4},{8,6},{10,8},{12,10},{14,12},{1,15},{3,1}... | collective-permute-start | bytes 860168 | tf_op jit(solution)/shard_map/ppermute | solution.py:20
  19.5 8.1 %collective-permute-start.10 = (bf16[128,1152]{1,0:T(8,128)(2,1)S(1)}, bf16[128,1152]{1,0:T(8,128)(2,1)S(1)}, u32[]{:S(2)}, u32[]{:S(2)}) collective-permute-start(bf16[128,1152]{1,0:T(8,128)(2,1)S(1)} %collective-permute-done.8.g2), channel_id=1, source_target_pairs={{0,128},{128,0},{1,129},{129,1},{2,130},{130,2},{3,131},{131,3},{4... | collective-permute-start | bytes 884744 | tf_op jit(solution)/shard_map/ppermute | solution.py:20
  24.8 7.1 %collective-permute-start.3 = (bf16[56,2560]{1,0:T(8,128)(2,1)S(1)}, bf16[56,2560]{1,0:T(8,128)(2,1)S(1)}, u32[]{:S(2)}, u32[]{:S(2)}) collective-permute-start(bf16[56,2560]{1,0:T(8,128)(2,1)S(1)} %collective-permute-done.1.f1), channel_id=1, source_target_pairs={{0,2},{2,4},{4,6},{6,8},{8,10},{10,12},{12,14},{14,0},{1,3},{3,5},... | collective-permute-start | bytes 860168 | tf_op jit(solution)/shard_map/ppermute | solution.py:20
  24.8 7.1 %collective-permute-start.4 = (bf16[56,2560]{1,0:T(8,128)(2,1)S(1)}, bf16[56,2560]{1,0:T(8,128)(2,1)S(1)}, u32[]{:S(2)}, u32[]{:S(2)}) collective-permute-start(bf16[56,2560]{1,0:T(8,128)(2,1)S(1)} %collective-permute-done.2.b1), channel_id=1, source_target_pairs={{0,14},{2,0},{4,2},{6,4},{8,6},{10,8},{12,10},{14,12},{1,15},{3,1}... | collective-permute-start | bytes 860168 | tf_op jit(solution)/shard_map/ppermute | solution.py:20
  27.7 6.9 %collective-permute-start.12 = (bf16[128,1280]{1,0:T(8,128)(2,1)S(1)}, bf16[128,1280]{1,0:T(8,128)(2,1)S(1)}, u32[]{:S(2)}, u32[]{:S(2)}) collective-permute-start(bf16[128,1280]{1,0:T(8,128)(2,1)S(1)} %get-tuple-element.78.n2), channel_id=1, source_target_pairs={{0,64},{64,0},{1,65},{65,1},{2,66},{66,2},{3,67},{67,3},{4,68},{68... | collective-permute-start | bytes 983048 | tf_op jit(solution)/shard_map/ppermute | solution.py:20
  30.6 3.9 %collective-permute-start.11 = (bf16[128,1280]{1,0:T(8,128)(2,1)S(1)}, bf16[128,1280]{1,0:T(8,128)(2,1)S(1)}, u32[]{:S(2)}, u32[]{:S(2)}) collective-permute-start(bf16[128,1280]{1,0:T(8,128)(2,1)S(1)} %get-tuple-element.79), channel_id=1, source_target_pairs={{0,64},{64,0},{1,65},{65,1},{2,66},{66,2},{3,67},{67,3},{4,68},{68... | collective-permute-start | bytes 983048 | tf_op jit(solution)/shard_map/ppermute | solution.py:20
  30.7 3.8 %collective-permute-start.13 = (bf16[128,1280]{1,0:T(8,128)(2,1)S(1)}, bf16[128,1280]{1,0:T(8,128)(2,1)S(1)}, u32[]{:S(2)}, u32[]{:S(2)}) collective-permute-start(bf16[128,1280]{1,0:T(8,128)(2,1)S(1)} %get-tuple-element.80), channel_id=1, source_target_pairs={{0,64},{64,0},{1,65},{65,1},{2,66},{66,2},{3,67},{67,3},{4,68},{68... | collective-permute-start | bytes 983048 | tf_op jit(solution)/shard_map/ppermute | solution.py:20
  31.9 7.8 %collective-permute-start.5 = (bf16[56,2560]{1,0:T(8,128)(2,1)S(1)}, bf16[56,2560]{1,0:T(8,128)(2,1)S(1)}, u32[]{:S(2)}, u32[]{:S(2)}) collective-permute-start(bf16[56,2560]{1,0:T(8,128)(2,1)S(1)} %collective-permute-done.3.f2), channel_id=1, source_target_pairs={{0,2},{2,4},{4,6},{6,8},{8,10},{10,12},{12,14},{14,0},{1,3},{3,5},... | collective-permute-start | bytes 860168 | tf_op jit(solution)/shard_map/ppermute | solution.py:20
  33.4 6.3 %collective-permute-start.6 = (bf16[56,2560]{1,0:T(8,128)(2,1)S(1)}, bf16[56,2560]{1,0:T(8,128)(2,1)S(1)}, u32[]{:S(2)}, u32[]{:S(2)}) collective-permute-start(bf16[56,2560]{1,0:T(8,128)(2,1)S(1)} %collective-permute-done.4.b2), channel_id=1, source_target_pairs={{0,14},{2,0},{4,2},{6,4},{8,6},{10,8},{12,10},{14,12},{1,15},{3,1}... | collective-permute-start | bytes 860168 | tf_op jit(solution)/shard_map/ppermute | solution.py:20
  38.1 12.5 %collective-permute-start.16 = (bf16[56,2560]{1,0:T(8,128)(2,1)S(1)}, bf16[56,2560]{1,0:T(8,128)(2,1)S(1)}, u32[]{:S(2)}, u32[]{:S(2)}) collective-permute-start(bf16[56,2560]{1,0:T(8,128)(2,1)S(1)} %get-tuple-element.87), channel_id=1, source_target_pairs={{0,14},{2,0},{4,2},{6,4},{8,6},{10,8},{12,10},{14,12},{1,15},{3,1}... | collective-permute-start | bytes 860168 | tf_op jit(solution)/shard_map/ppermute | solution.py:20
  39.7 13.7 %collective-permute-start.15 = (bf16[56,2560]{1,0:T(8,128)(2,1)S(1)}, bf16[56,2560]{1,0:T(8,128)(2,1)S(1)}, u32[]{:S(2)}, u32[]{:S(2)}) collective-permute-start(bf16[56,2560]{1,0:T(8,128)(2,1)S(1)} %collective-permute-done.5.f3), channel_id=1, source_target_pairs={{0,2},{2,4},{4,6},{6,8},{8,10},{10,12},{12,14},{14,0},{1,3},{3,5},... | collective-permute-start | bytes 860168 | tf_op jit(solution)/shard_map/ppermute | solution.py:20
  43.1 12.9 %collective-permute-start.14 = (bf16[512,1408]{1,0:T(8,128)(2,1)S(1)}, bf16[512,1408]{1,0:T(8,128)(2,1)S(1)}, u32[]{:S(2)}, u32[]{:S(2)}) collective-permute-start(bf16[512,1408]{1,0:T(8,128)(2,1)S(1)} %get-tuple-element.83), channel_id=1, source_target_pairs={{0,64},{64,0},{1,65},{65,1},{2,66},{66,2},{3,67},{67,3},{4,68},{68... | collective-permute-start | bytes 4325384 | tf_op jit(solution)/shard_map/ppermute | solution.py:20
  50.6 9.7 %collective-permute-start.22 = (bf16[56,2560]{1,0:T(8,128)(2,1)S(1)}, bf16[56,2560]{1,0:T(8,128)(2,1)S(1)}, u32[]{:S(2)}, u32[]{:S(2)}) collective-permute-start(bf16[56,2560]{1,0:T(8,128)(2,1)S(1)} %get-tuple-element.88.value), channel_id=1, source_target_pairs={{0,2},{2,4},{4,6},{6,8},{8,10},{10,12},{12,14},{14,0},{1,3},{3,5},... | collective-permute-start | bytes 860168 | tf_op jit(solution)/shard_map/ppermute | solution.py:20
  52.3 8.2 %collective-permute-start.23 = (bf16[56,2560]{1,0:T(8,128)(2,1)S(1)}, bf16[56,2560]{1,0:T(8,128)(2,1)S(1)}, u32[]{:S(2)}, u32[]{:S(2)}) collective-permute-start(bf16[56,2560]{1,0:T(8,128)(2,1)S(1)} %get-tuple-element.94), channel_id=1, source_target_pairs={{0,14},{2,0},{4,2},{6,4},{8,6},{10,8},{12,10},{14,12},{1,15},{3,1}... | collective-permute-start | bytes 860168 | tf_op jit(solution)/shard_map/ppermute | solution.py:20
  53.4 2.6 %collective-permute-start.17 = (bf16[56,1280]{1,0:T(8,128)(2,1)S(1)}, bf16[56,1280]{1,0:T(8,128)(2,1)S(1)}, u32[]{:S(2)}, u32[]{:S(2)}) collective-permute-start(bf16[56,1280]{1,0:T(8,128)(2,1)S(1)} %shard_map.82), channel_id=1, source_target_pairs={{0,64},{64,0},{1,65},{65,1},{2,66},{66,2},{3,67},{67,3},{4,68},{68... | collective-permute-start | bytes 430088 | tf_op jit(solution)/shard_map/ppermute | solution.py:20
  56.9 6.5 %collective-permute-start.19 = (bf16[128,640]{1,0:T(8,128)(2,1)S(1)}, bf16[128,640]{1,0:T(8,128)(2,1)S(1)}, u32[]{:S(2)}, u32[]{:S(2)}) collective-permute-start(bf16[128,640]{1,0:T(8,128)(2,1)S(1)} %get-tuple-element.92), channel_id=1, source_target_pairs={{0,128},{128,0},{1,129},{129,1},{2,130},{130,2},{3,131},{131,3},{4... | collective-permute-start | bytes 491528 | tf_op jit(solution)/shard_map/ppermute | solution.py:20
  57.4 14.6 %collective-permute-start.18 = (bf16[128,1280]{1,0:T(8,128)(2,1)S(1)}, bf16[128,1280]{1,0:T(8,128)(2,1)S(1)}, u32[]{:S(2)}, u32[]{:S(2)}) collective-permute-start(bf16[128,1280]{1,0:T(8,128)(2,1)S(1)} %get-tuple-element.90), channel_id=1, source_target_pairs={{0,48},{16,0},{32,16},{48,32},{1,49},{17,1},{33,17},{49,33},{2,50}... | collective-permute-start | bytes 983048 | tf_op jit(solution)/shard_map/ppermute | solution.py:20
  57.4 6.4 %copy-start.1 = (bf16[128,1728]{0,1:T(8,128)(2,1)S(1)}, bf16[128,1728]{0,1:T(8,128)(2,1)}, u32[]{:S(2)}) copy-start(bf16[128,1728]{0,1:T(8,128)(2,1)} %param.4) | copy-start | bytes 1327108
  57.4 6.4 %copy-start.2 = (bf16[128,1728]{0,1:T(8,128)(2,1)S(1)}, bf16[128,1728]{0,1:T(8,128)(2,1)}, u32[]{:S(2)}) copy-start(bf16[128,1728]{0,1:T(8,128)(2,1)} %param.5) | copy-start | bytes 1327108
  57.4 14.6 %collective-permute-start.21 = (bf16[128,1280]{1,0:T(8,128)(2,1)S(1)}, bf16[128,1280]{1,0:T(8,128)(2,1)S(1)}, u32[]{:S(2)}, u32[]{:S(2)}) collective-permute-start(bf16[128,1280]{1,0:T(8,128)(2,1)S(1)} %get-tuple-element.93), channel_id=1, source_target_pairs={{0,16},{16,32},{32,48},{48,0},{1,17},{17,33},{33,49},{49,1},{2,18}... | collective-permute-start | bytes 983048 | tf_op jit(solution)/shard_map/ppermute | solution.py:20
  60.7 8.6 %collective-permute-start.24 = (bf16[56,2560]{1,0:T(8,128)(2,1)S(1)}, bf16[56,2560]{1,0:T(8,128)(2,1)S(1)}, u32[]{:S(2)}, u32[]{:S(2)}) collective-permute-start(bf16[56,2560]{1,0:T(8,128)(2,1)S(1)} %get-tuple-element.97), channel_id=1, source_target_pairs={{0,2},{2,4},{4,6},{6,8},{8,10},{10,12},{12,14},{14,0},{1,3},{3,5},... | collective-permute-start | bytes 860168 | tf_op jit(solution)/shard_map/ppermute | solution.py:20
  62.1 7.1 %collective-permute-start.25 = (bf16[56,2560]{1,0:T(8,128)(2,1)S(1)}, bf16[56,2560]{1,0:T(8,128)(2,1)S(1)}, u32[]{:S(2)}, u32[]{:S(2)}) collective-permute-start(bf16[56,2560]{1,0:T(8,128)(2,1)S(1)} %get-tuple-element.98), channel_id=1, source_target_pairs={{0,14},{2,0},{4,2},{6,4},{8,6},{10,8},{12,10},{14,12},{1,15},{3,1}... | collective-permute-start | bytes 860168 | tf_op jit(solution)/shard_map/ppermute | solution.py:20
  63.4 8.6 %collective-permute-start.20 = (bf16[128,640]{1,0:T(8,128)(2,1)S(1)}, bf16[128,640]{1,0:T(8,128)(2,1)S(1)}, u32[]{:S(2)}, u32[]{:S(2)}) collective-permute-start(bf16[128,640]{1,0:T(8,128)(2,1)S(1)} %shard_map.84), channel_id=1, source_target_pairs={{0,32},{16,48},{32,0},{48,16},{1,33},{17,49},{33,1},{49,17},{2,34}... | collective-permute-start | bytes 491528 | tf_op jit(solution)/shard_map/ppermute | solution.py:20
  69.3 7.4 %collective-permute-start.27 = (bf16[56,2560]{1,0:T(8,128)(2,1)S(1)}, bf16[56,2560]{1,0:T(8,128)(2,1)S(1)}, u32[]{:S(2)}, u32[]{:S(2)}) collective-permute-start(bf16[56,2560]{1,0:T(8,128)(2,1)S(1)} %get-tuple-element.109), channel_id=1, source_target_pairs={{0,2},{2,4},{4,6},{6,8},{8,10},{10,12},{12,14},{14,0},{1,3},{3,5},... | collective-permute-start | bytes 860168 | tf_op jit(solution)/shard_map/ppermute | solution.py:20
  69.8 7.0 %collective-permute-start.28 = (bf16[56,2560]{1,0:T(8,128)(2,1)S(1)}, bf16[56,2560]{1,0:T(8,128)(2,1)S(1)}, u32[]{:S(2)}, u32[]{:S(2)}) collective-permute-start(bf16[56,2560]{1,0:T(8,128)(2,1)S(1)} %get-tuple-element.110), channel_id=1, source_target_pairs={{0,14},{2,0},{4,2},{6,4},{8,6},{10,8},{12,10},{14,12},{1,15},{3,1}... | collective-permute-start | bytes 860168 | tf_op jit(solution)/shard_map/ppermute | solution.py:20
  72.3 6.8 %collective-permute-start.26 = (bf16[128,1280]{1,0:T(8,128)(2,1)S(1)}, bf16[128,1280]{1,0:T(8,128)(2,1)S(1)}, u32[]{:S(2)}, u32[]{:S(2)}) collective-permute-start(bf16[128,1280]{1,0:T(8,128)(2,1)S(1)} %shard_map.89), channel_id=1, source_target_pairs={{0,128},{128,0},{1,129},{129,1},{2,130},{130,2},{3,131},{131,3},{4... | collective-permute-start | bytes 983048 | tf_op jit(solution)/shard_map/ppermute | solution.py:20
  73.0 11.7 %collective-permute-start.31 = (bf16[512,128]{1,0:T(8,128)(2,1)S(1)}, bf16[512,128]{1,0:T(8,128)(2,1)S(1)}, u32[]{:S(2)}, u32[]{:S(2)}) collective-permute-start(bf16[512,128]{1,0:T(8,128)(2,1)S(1)} %get-tuple-element.124), channel_id=1, source_target_pairs={{0,48},{16,0},{32,16},{48,32},{1,49},{17,1},{33,17},{49,33},{2,50}... | collective-permute-start | bytes 393224 | tf_op jit(solution)/shard_map/ppermute | solution.py:20
  73.9 10.8 %collective-permute-start.32 = (bf16[512,128]{1,0:T(8,128)(2,1)S(1)}, bf16[512,128]{1,0:T(8,128)(2,1)S(1)}, u32[]{:S(2)}, u32[]{:S(2)}) collective-permute-start(bf16[512,128]{1,0:T(8,128)(2,1)S(1)} %get-tuple-element.125), channel_id=1, source_target_pairs={{0,32},{16,48},{32,0},{48,16},{1,33},{17,49},{33,1},{49,17},{2,34}... | collective-permute-start | bytes 393224 | tf_op jit(solution)/shard_map/ppermute | solution.py:20
  77.0 8.8 %collective-permute-start.30 = (bf16[27,2560]{1,0:T(8,128)(2,1)S(1)}, bf16[27,2560]{1,0:T(8,128)(2,1)S(1)}, u32[]{:S(2)}, u32[]{:S(2)}) collective-permute-start(bf16[27,2560]{1,0:T(8,128)(2,1)S(1)} %get-tuple-element.116), channel_id=1, source_target_pairs={{0,1},{1,0},{2,3},{3,2},{4,5},{5,4},{6,7},{7,6},{8,9},{9,8},{10,11... | collective-permute-start | bytes 414728 | tf_op jit(solution)/shard_map/ppermute | solution.py:20
  77.1 7.5 %collective-permute-start.33 = (bf16[512,128]{1,0:T(8,128)(2,1)S(1)}, bf16[512,128]{1,0:T(8,128)(2,1)S(1)}, u32[]{:S(2)}, u32[]{:S(2)}) collective-permute-start(bf16[512,128]{1,0:T(8,128)(2,1)S(1)} %get-tuple-element.127), channel_id=1, source_target_pairs={{0,16},{16,32},{32,48},{48,0},{1,17},{17,33},{33,49},{49,1},{2,18}... | collective-permute-start | bytes 393224 | tf_op jit(solution)/shard_map/ppermute | solution.py:20
  79.1 6.8 %collective-permute-start.29 = (bf16[128,1280]{1,0:T(8,128)(2,1)S(1)}, bf16[128,1280]{1,0:T(8,128)(2,1)S(1)}, u32[]{:S(2)}, u32[]{:S(2)}) collective-permute-start(bf16[128,1280]{1,0:T(8,128)(2,1)S(1)} %add_convert_fusion.mine), channel_id=1, source_target_pairs={{0,64},{64,0},{1,65},{65,1},{2,66},{66,2},{3,67},{67,3},{4,68},{68... | collective-permute-start | bytes 983048 | tf_op jit(solution)/shard_map/ppermute | solution.py:20
